TPU v7x, 32 devices: a whole 2x2x4 slice. The times are simulated.
32 devices in a mesh: parts: 2 (over x), row: 16 (over z, y, core).
Axes of the slice: x: 2, y: 2, z: 4, core: 2. Of those that a mesh axis runs over, the one named last changes fastest.
Arguments:
- features: bfloat16 [16384, 128], P(('parts', 'row')), parts along dimension 0, may hold values from -6 to 6
- tiles: bfloat16 [1920, 128, 128], P(('parts', 'row')), parts along dimension 0, as said below
- tile_row: int32 [1920], P(('parts', 'row')), parts along dimension 0, may hold values from 0 to 63, as said below
- tile_col: int32 [1920], P(('parts', 'row')), parts along dimension 0, may hold values from -1 to 63, as said below
- degree: int32 [16384], P(('parts', 'row')), parts along dimension 0, may hold values from 16 to 64
- train_mask: int32 [16384], P(('parts', 'row')), parts along dimension 0, may hold values 0 or 1
- w_self: bfloat16 [128, 256], replicated, may hold values from -0.5 to 0.5
- w_neigh: bfloat16 [128, 256], replicated, may hold values from -0.5 to 0.5
- cotangent: bfloat16 [16384, 256], P(('parts', 'row')), parts along dimension 0, may hold values from -6 to 6
Outputs:
- embedded: bfloat16 [16384, 256], P(('parts', 'row')), parts along dimension 0
- grad_input: bfloat16 [16384, 128], P(('parts', 'row')), parts along dimension 0
- grad_self: float32 [256, 256], P('parts'), parts along dimension 0
- grad_neigh: float32 [256, 256], P('parts'), parts along dimension 0
There are 2 independent parts, one for each index of `parts`. A program takes and returns all parts, laid end to end along the dimension named above; an argument that names none is the same for every part. Nothing has to cross between parts.
Inputs may be any that keep to these rules, and one draw needn't show every extreme that they name: `tile_row`: the tile slots of the device that holds nodes 128 b to 128 b + 127 name only row blocks of that device's 512 // 128 blocks. `tile_col`: -1 marks an empty slot; empty slots stand after the live ones of a device; every device has 30 live slots or more, and in every draw some device has all its slots live. The live slots of one device name column blocks held by any one other device at most 4 times, and in every draw some device does so exactly 4 times. A pair of blocks may appear in several slots. `tiles`: nonnegative edge weights.
All inputs are finite; a program needn't handle non-finite values. No bound on the sum of `train_mask` on one device may be relied on, other than what follows from the above.
Results may differ from a plain program's by a relative error of at most 0.0029.
Values may be sent and summed in bfloat16 or wider, within the bound.
No kernel may reach another device: no remote copies, remote signals or barrier semaphores. Data moves between devices by JAX's collectives and lax.ppermute only.
A program may use at most 128 MiB of HBM per device.

v0:
```python
import jax
import jax.numpy as jnp
from jax import lax
from jax.sharding import PartitionSpec as P


def pack_slots(contrib, col_block, is_live, block_local):
    device_count = lax.axis_size("row")
    myself = lax.axis_index("row")
    tiles_dev = contrib.shape[0]
    capacity = (tiles_dev + device_count - 2) // (device_count - 1)
    owner = col_block // block_local
    target = col_block % block_local
    remote = is_live & (owner != myself)
    home = is_live & (owner == myself)
    order = jnp.arange(tiles_dev)
    earlier = (
        (owner[:, None] == owner[None, :]) & remote[None, :] & (order[None, :] < order[:, None])
    )
    rank = jnp.sum(earlier.astype(jnp.int32), axis=1)
    slot = jnp.where(remote, owner * capacity + rank, device_count * capacity)
    outgoing = jnp.zeros((device_count * capacity,) + contrib.shape[1:], jnp.float32)
    outgoing = outgoing.at[slot].set(contrib, mode="drop")
    slot_target = (
        jnp.full((device_count * capacity,), -1, jnp.int32).at[slot].set(target, mode="drop")
    )
    home_map = (home[:, None] & (target[:, None] == jnp.arange(block_local)[None, :])).astype(
        jnp.float32
    )
    home_sum = jnp.einsum("tb,tif->bif", home_map, contrib, precision=lax.Precision.HIGHEST)
    return (outgoing, slot_target, home_sum)


def unpack_slots(incoming, slot_target, home_sum, block_local):
    place_map = (slot_target[:, None] == jnp.arange(block_local)[None, :]).astype(jnp.float32)
    total = home_sum + jnp.einsum(
        "sb,sif->bif", place_map, incoming, precision=lax.Precision.HIGHEST
    )
    return total.reshape(block_local * 128, incoming.shape[2])


def body(features, tiles, tile_row, tile_col, degree, train_mask, w_self, w_neigh, cotangent):
    node_count, feat_in = features.shape
    block_local = node_count // 128
    first_block = lax.axis_index("row") * block_local
    is_live = tile_col >= 0
    col_block = jnp.where(is_live, tile_col, 0)
    local_block = jnp.clip(tile_row - first_block, 0, block_local - 1)
    live_tiles = tiles * is_live.astype(jnp.bfloat16)[:, None, None]
    gathered = lax.all_gather(features, "row", axis=0, tiled=True)
    picked = jnp.take(gathered.reshape(-1, 128, feat_in), col_block, axis=0)
    products = jnp.einsum("tij,tjf->tif", live_tiles, picked, preferred_element_type=jnp.float32)
    owner_map = (local_block[:, None] == jnp.arange(block_local)[None, :]).astype(jnp.float32)
    raw = jnp.einsum("tb,tif->bif", owner_map, products, precision=lax.Precision.HIGHEST).reshape(
        node_count, feat_in
    )
    scaled_degree = degree.astype(jnp.float32)[:, None]
    neighbour_mean = raw / scaled_degree
    pre_act = jnp.dot(features, w_self, preferred_element_type=jnp.float32) + jnp.dot(
        neighbour_mean, w_neigh.astype(jnp.float32), precision=lax.Precision.HIGHEST
    )
    sigmoid_val = jax.nn.sigmoid(pre_act)
    embedded = (pre_act * sigmoid_val).astype(jnp.bfloat16)
    upstream = cotangent.astype(jnp.float32) * train_mask.astype(jnp.float32)[:, None]
    grad_pre = upstream * sigmoid_val * (1.0 + pre_act * (1.0 - sigmoid_val))
    scaled_grad = (grad_pre / scaled_degree).astype(jnp.bfloat16)
    feat_wide = features.astype(jnp.float32)
    grad_self = jnp.dot(feat_wide.T, grad_pre, precision=lax.Precision.HIGHEST)
    picked_grad = jnp.take(scaled_grad.reshape(block_local, 128, -1), local_block, axis=0)
    contrib = jnp.einsum(
        "tji,tjf->tif", live_tiles, picked_grad, preferred_element_type=jnp.float32
    )
    outgoing, slot_target, home_sum = pack_slots(contrib, col_block, is_live, block_local)
    incoming, arrived_target = (
        lax.all_to_all(outgoing, "row", split_axis=0, concat_axis=0, tiled=True),
        lax.all_to_all(slot_target, "row", split_axis=0, concat_axis=0, tiled=True),
    )
    spread = unpack_slots(incoming, arrived_target, home_sum, block_local)
    neighbour_grad = jnp.dot(spread, w_neigh.astype(jnp.float32).T, precision=lax.Precision.HIGHEST)
    grad_neigh = jnp.dot(feat_wide.T, spread, precision=lax.Precision.HIGHEST)
    grad_self, grad_neigh = lax.psum((grad_self, grad_neigh), "row")
    grad_input = (
        jnp.dot(grad_pre, w_self.astype(jnp.float32).T, precision=lax.Precision.HIGHEST)
        + neighbour_grad
    ).astype(jnp.bfloat16)
    return (embedded, grad_input, grad_self, grad_neigh)


def solution(mesh):
    placed = (
        P(("parts", "row"), None),
        P(("parts", "row"), None, None),
        P(("parts", "row")),
        P(("parts", "row")),
        P(("parts", "row")),
        P(("parts", "row")),
        P(),
        P(),
        P(("parts", "row"), None),
    )
    return jax.shard_map(
        body,
        mesh=mesh,
        in_specs=placed,
        out_specs=(
            P(("parts", "row"), None),
            P(("parts", "row"), None),
            P("parts", None),
            P("parts", None),
        ),
        check_vma=False,
    )
```

profile of v0, /device:TPU:0, one launch (start us, length us, event | category | flops | bytes accessed | tf_op | source)
XLA Modules:
  0.0 403.3 jit_solution(2922326971102392463)
XLA Ops:
  7.2 0.0 copy-start
  7.2 0.0 copy-start.1
  7.2 0.0 all-gather.2.cloned.1.call-start
  7.2 0.7 all-gather.2.cloned.1.call-update
  7.9 0.7 compare_and_fusion.1
  8.6 0.7 compare_and_fusion.3
  9.3 0.2 convert_reduce_fusion
  9.5 0.8 scatter_custom_fusion
  10.3 0.7 all_to_all.9
  10.9 7.4 %all-to-all-start = ((s32[16,4,1]{1,2,0:T(1,128)}), s32[16,4,1]{1,2,0:T(1,128)S(1)}, u32[]{:S(2)}, u32[]{:S(2)}) async-start(s32[16,4,1]{1,2,0:T(1,128)} %bitcast.5), calls=%async_computation | async-start | bytes 16384 | tf_op jit(solution)/shard_map/all_to_all | solution.py:76
  18.3 0.7 convert_element_type.32
  19.0 0.7 convert_element_type.35
  19.7 34.6 %all-gather.2.cloned.1.call-done = bf16[8192,128]{1,0:T(8,128)(2,1)} async-done(((bf16[512,128]{1,0:T(8,128)(2,1)}), bf16[8192,128]{1,0:T(8,128)(2,1)}) %all-gather.2.cloned.1.call-update) | async-done | bytes 2097168 | tf_op jit(solution)/shard_map/all_gather | solution.py:50
  54.3 3.7 gather_fusion
  58.0 0.0 copy-done.1
  58.0 2.3 fusion.10
  60.3 0.0 copy-start.3
  60.3 0.0 copy-start.2
  60.3 0.0 copy-start.4
  60.3 3.7 fusion.4
  64.0 0.1 bitcast_divide_fusion
  64.2 0.0 copy-done.3
  64.2 0.4 fusion.39
  64.5 0.0 copy-done
  64.5 0.0 copy-done.2
  64.6 1.1 divide_convert_fusion
  65.7 2.7 gather_fusion.1
  68.4 6.9 %fusion.6 = f32[60,128,256]{2,1,0:T(8,128)} fusion(bf16[60,128,256]{2,1,0:T(8,128)(2,1)} %gather_fusion.1, pred[60]{0:T(512)(128)(4,1)S(1)} %get-tuple-element.25, bf16[60,128,128]{2,1,0:T(8,128)(2,1)S(1)} %copy-done.1, bf16[60]{0:T(256)(128)(2,1)S(1)} %get-tuple-element.34), kind=kOutput, calls=%fused_computation.10 | convolution fusion | flops 506265600 | bytes 13762740 | tf_op jit(solution)/shard_map/tji,tjf->tif/dot_general | solution.py:70
  75.3 4.3 %broadcast_in_dim.60 = f32[64,128,256]{2,1,0:T(8,128)} broadcast(f32[]{:T(128)} %constant.69.clone.1), dimensions={} | broadcast | bytes 8388612 | tf_op jit(solution)/shard_map/broadcast_in_dim | solution.py:22
  79.5 15.4 %scatter_fusion = f32[64,128,256]{2,1,0:T(8,128)} fusion(f32[64,128,256]{2,1,0:T(8,128)} %broadcast_in_dim.60, s32[60]{0:T(128)S(1)} %compare_select_fusion, f32[60,128,256]{2,1,0:T(8,128)} %fusion.6), kind=kCustom, calls=%fused_computation.3 | custom fusion | bytes 23593200 | tf_op jit(solution)/shard_map/scatter | solution.py:23
  95.0 0.0 all-to-all-done
  95.0 4.7 %all-to-all-start.1 = ((f32[64,128,256]{2,1,0:T(8,128)}), f32[64,128,256]{2,1,0:T(8,128)}, u32[]{:S(2)}, u32[]{:S(2)}) async-start(f32[64,128,256]{2,1,0:T(8,128)} %scatter_fusion), calls=%async_computation.1 | async-start | bytes 16777216 | tf_op jit(solution)/shard_map/all_to_all | solution.py:75
  99.7 0.2 all-reduce.3.cloned.1.call-start
  100.0 0.5 broadcast.43
  100.5 0.7 reduce.3
  101.1 0.1 eq.73
  101.2 1.3 convolution_bitcast_fusion.1
  102.5 0.4 fusion.40
  102.9 147.5 %all-to-all-done.1 = f32[64,128,256]{2,1,0:T(8,128)} async-done(((f32[64,128,256]{2,1,0:T(8,128)}), f32[64,128,256]{2,1,0:T(8,128)}, u32[]{:S(2)}, u32[]{:S(2)}) %all-to-all-start.1) | async-done | bytes 8388640 | tf_op jit(solution)/shard_map/all_to_all | solution.py:75
  250.3 10.4 %fusion = f32[4,128,256]{2,0,1:T(4,128)S(1)} fusion(f32[64,128,256]{2,1,0:T(8,128)} %all-to-all-done.1, s32[64]{0:T(128)S(1)} %eq.73), kind=kOutput, calls=%fused_computation.4 | convolution fusion | flops 100663552 | bytes 8913152 | tf_op jit(solution)/shard_map/sb,sif->bif/dot_general | solution.py:36
  260.8 10.3 %fusion.15 = f32[4,128,256]{2,0,1:T(4,128)S(1)} fusion(f32[4,128,256]{2,0,1:T(4,128)S(1)} %fusion, f32[60,128,256]{2,1,0:T(8,128)} %fusion.6, s32[60]{0:T(128)S(1)} %and_select_fusion, pred[60]{0:T(512)(128)(4,1)S(1)} %get-tuple-element.35), kind=kOutput, calls=%fused_computation.19 | convolution fusion | flops 94503392 | bytes 8913196 | tf_op jit(solution)/shard_map/tb,tif->bif/dot_general | solution.py:30
  271.0 0.1 copy.39
  271.1 1.3 convolution_bitcast_fusion
  272.4 0.0 all-reduce.3.cloned.1.call-update
  272.4 1.0 fusion.18
  273.4 119.7 %all-reduce.3.cloned.1.call-done = (f32[128,256]{0,1:T(8,128)}, f32[128,256]{0,1:T(8,128)}) async-done(((f32[128,256]{0,1:T(8,128)}, f32[128,256]{0,1:T(8,128)}), (f32[128,256]{0,1:T(8,128)}, f32[128,256]{0,1:T(8,128)})) %all-reduce.3.cloned.1.call-update) | async-done | bytes 262160 | tf_op jit(solution)/shard_map/psum | solution.py:81
  393.1 1.7 copy.40
  394.8 1.7 copy.41
  (7 shorter events, 0.0 us)
Async XLA Ops:
  7.2 57.4 %copy-start = (bf16[128,256]{1,0:T(8,128)(2,1)S(1)}, bf16[128,256]{1,0:T(8,128)(2,1)}, u32[]{:S(2)}) copy-start(bf16[128,256]{1,0:T(8,128)(2,1)} %param.15) | copy-start | bytes 196612
  7.2 50.8 %copy-start.1 = (bf16[60,128,128]{2,1,0:T(8,128)(2,1)S(1)}, bf16[60,128,128]{2,1,0:T(8,128)(2,1)}, u32[]{:S(2)}) copy-start(bf16[60,128,128]{2,1,0:T(8,128)(2,1)} %param.10) | copy-start | bytes 5898244
  7.2 47.1 %all-gather.2.cloned.1.call-start = ((), (), s32[]{:S(2)}) async-start(), calls=%async_computation.2 | async-start | bytes 2228224 | tf_op jit(solution)/shard_map/all_gather | solution.py:50
  10.9 84.0 %all-to-all-start = ((s32[16,4,1]{1,2,0:T(1,128)}), s32[16,4,1]{1,2,0:T(1,128)S(1)}, u32[]{:S(2)}, u32[]{:S(2)}) async-start(s32[16,4,1]{1,2,0:T(1,128)} %bitcast.5), calls=%async_computation | async-start | bytes 16384 | tf_op jit(solution)/shard_map/all_to_all | solution.py:76
  60.3 3.9 copy-start.3
  60.3 4.3 %copy-start.2 = (bf16[512,128]{1,0:T(8,128)(2,1)S(1)}, bf16[512,128]{1,0:T(8,128)(2,1)}, u32[]{:S(2)}) copy-start(bf16[512,128]{1,0:T(8,128)(2,1)} %param.9) | copy-start | bytes 393220
  60.3 4.3 %copy-start.4 = (bf16[512,256]{1,0:T(8,128)(2,1)S(1)}, bf16[512,256]{1,0:T(8,128)(2,1)}, u32[]{:S(2)}) copy-start(bf16[512,256]{1,0:T(8,128)(2,1)} %param.17) | copy-start | bytes 786436
  95.0 155.4 %all-to-all-start.1 = ((f32[64,128,256]{2,1,0:T(8,128)}), f32[64,128,256]{2,1,0:T(8,128)}, u32[]{:S(2)}, u32[]{:S(2)}) async-start(f32[64,128,256]{2,1,0:T(8,128)} %scatter_fusion), calls=%async_computation.1 | async-start | bytes 16777216 | tf_op jit(solution)/shard_map/all_to_all | solution.py:75
  99.7 293.4 %all-reduce.3.cloned.1.call-start = ((), (), s32[]{:S(2)}) async-start(), calls=%async_computation.3 | async-start | bytes 524288 | tf_op jit(solution)/shard_map/psum | solution.py:81
Sparse Core Ops, SparseCore 0:
  10.2 44.0 all-gather.1
  272.5 120.5 all-reduce.2
where the time goes:
time: 404 us; the launch traced here: 403 us
  waiting for transfers between devices  302 us (75%)
  matrix products  38.9 us (10%)
  local copies, waits for them, and re-layouts  31.6 us (8%)
  between operations  14.2 us (4%)
  starting transfers between devices  12.4 us (3%)
    all_to_all x1, waiting for transfers between devices, body(): lax.all_to_all(outgoing, 'row', split_axis=0, concat_axis=0, tiled=True)  147 us
    psum x1, waiting for transfers between devices, body(): grad_self, grad_neigh = lax.psum((grad_self, grad_neigh), 'row')  120 us
    all_gather x1, waiting for transfers between devices, body(): gathered = lax.all_gather(features, 'row', axis=0, tiled=True)  34.6 us
    scatter x1, local copies, waits for them, and re-layouts, pack_slots(): outgoing = outgoing.at[slot].set(contrib, mode='drop')  15.4 us
    dot_general x1, matrix products, unpack_slots(): jnp.einsum('sb,sif->bif', place_map, incoming, precision=lax.Precision.HI...  10.4 us
    dot_general x1, matrix products, pack_slots(): jnp.einsum('tb,tif->bif', home_map, contrib, precision=lax.Precision.HIGH...  10.3 us
  transfers between devices with their start and end apart: 4, of which 3 were waited for; matrix products, arithmetic and copies ran while one was open for 12% of the time, Pallas kernels for 0%

commit v1 on v0

v1 whole, which is shorter than its diff:
```python
import functools

import jax
import jax.numpy as jnp
from jax import lax
from jax.experimental import pallas as pl
from jax.experimental.pallas import tpu as pltpu
from jax.sharding import PartitionSpec as P

BLOCK = 128
F32, BF16 = jnp.float32, jnp.bfloat16
VMEM = pl.BlockSpec(memory_space=pltpu.VMEM)
SMEM = pl.BlockSpec(memory_space=pltpu.SMEM)
ANY = pl.BlockSpec(memory_space=pl.ANY)
VMEM_LIMIT = 56 * 1024 * 1024


def swap(x, n, offset):
    return lax.ppermute(x, "row", [(i, i ^ offset) for i in range(n)])


def gather_by_xor(x, n):
    blocks = {0: x}
    bits = [1 << b for b in range(n.bit_length() - 2, -1, -1)]
    while bits:
        if len(bits) >= 4:
            hi, lo, bits = bits[0], bits[1], bits[2:]
            offsets = (hi, lo, hi | lo)
        else:
            offsets, bits = (bits[0],), bits[1:]
        blocks |= {k ^ o: swap(v, n, o) for o in offsets for k, v in blocks.items()}
    return [blocks[k] for k in range(n)]


def split_bf16(x):
    high = x.astype(BF16)
    return high, (x - high.astype(F32)).astype(BF16)


def dot(a, b, dims=((1,), (0,))):
    return lax.dot_general(a, b, (dims, ((), ())), preferred_element_type=F32)


def dot_wide(a, b, dims=((1,), (0,))):
    high, low = split_bf16(a)
    return dot(high, b, dims) + dot(low, b, dims)


def rows_to_lanes(row):
    return jnp.transpose(jnp.broadcast_to(row, (BLOCK, BLOCK)))


def local_kernel(n, group, me_ref, trow_ref, tcol_ref, tiles_ref, deg_ref, mask_ref, ws_ref,
                 wn_ref, cot_ref, own_ref, *refs):
    feat_refs, refs = refs[:n], refs[n:]
    (emb_ref, base_ref, wkeep_ref, wsend_ref, keep_ref, send_ref,
     feats, raw, gt, acc, wsum, sem) = refs
    block_local = own_ref.shape[0] // BLOCK
    tile_count = tiles_ref.shape[0]
    me = me_ref[0]

    copies = [
        pltpu.make_async_copy(feat_refs[k], feats.at[pl.ds(k * block_local, block_local)],
                              sem.at[k])
        for k in range(n)
    ]
    for copy in copies:
        copy.start()
    raw[...] = jnp.zeros_like(raw)
    acc[...] = jnp.zeros_like(acc)
    for copy in copies:
        copy.wait()

    def place(t):
        col = tcol_ref[t]
        live = col >= 0
        col = jnp.maximum(col, 0)
        position = ((col // block_local) ^ me) * block_local + col % block_local
        row = jnp.clip(trow_ref[t] - me * block_local, 0, block_local - 1)
        return live, row, position

    def forward(step, carry):
        rows, products = [], []
        for u in range(group):
            t = step * group + u
            live, row, position = place(t)
            rows.append(jnp.where(live, row, block_local))
            products.append(dot(tiles_ref[t], feats[position]))
        for row, product in zip(rows, products):
            raw[row] += product
        return carry

    lax.fori_loop(0, tile_count // group, forward, 0)

    wn = wn_ref[...]
    ws = ws_ref[...]
    for b in range(block_local):
        span = pl.ds(b * BLOCK, BLOCK)
        degree = rows_to_lanes(deg_ref[pl.ds(b, 1), :].astype(F32))
        mask = rows_to_lanes(mask_ref[pl.ds(b, 1), :].astype(F32))
        degree2 = jnp.concatenate([degree, degree], axis=1)
        mask2 = jnp.concatenate([mask, mask], axis=1)
        feat = own_ref[span, :]
        raw_b = raw[b]
        pre = dot(feat, ws) + dot_wide(raw_b / degree, wn)
        sig = jax.nn.sigmoid(pre)
        emb_ref[span, :] = (pre * sig).astype(BF16)
        upstream = cot_ref[span, :].astype(F32) * mask2
        grad_pre = upstream * sig * (1.0 + pre * (1.0 - sig))
        scaled = (grad_pre / degree2).astype(BF16)
        gp_high, gp_low = split_bf16(grad_pre)
        feat_t = jnp.transpose(feat.astype(F32)).astype(BF16)
        grad_self = dot(feat_t, gp_high) + dot(feat_t, gp_low)
        grad_neigh = dot_wide(jnp.transpose(raw_b), scaled)
        if b == 0:
            wsum[0], wsum[1] = grad_self, grad_neigh
        else:
            wsum[0] += grad_self
            wsum[1] += grad_neigh
        last = ((1,), (1,))
        base_ref[span, :] = dot(gp_high, ws, last) + dot(gp_low, ws, last)
        high, low = split_bf16(dot(wn, scaled, last))
        gt[b, :BLOCK, :] = high
        gt[b, BLOCK:, :] = low

    core = me % 2
    wkeep_ref[...] = wsum[core]
    wsend_ref[...] = wsum[1 - core]

    def backward(step, carry):
        places, products = [], []
        for u in range(group):
            t = step * group + u
            live, row, position = place(t)
            places.append(jnp.where(live, position, n * block_local))
            both = dot(gt[row], tiles_ref[t])
            products.append(both[:BLOCK] + both[BLOCK:])
        for position, product in zip(places, products):
            acc[position] += product
        return carry

    lax.fori_loop(0, tile_count // group, backward, 0)

    for k in range(n):
        for b in range(block_local):
            target = send_ref if k % 2 else keep_ref
            target[k // 2, pl.ds(b * BLOCK, BLOCK), :] = acc[k * block_local + b]


def pair_kernel(chips, keep_ref, got_ref, own_ref, *out_refs):
    own_ref[...] = keep_ref[0] + got_ref[0]
    for j in range(1, chips):
        out_refs[j - 1][...] = (keep_ref[j] + got_ref[j]).astype(BF16)


def last_kernel(chips, base_ref, own_ref, *refs):
    got_refs, out_ref = refs[:chips - 1], refs[chips - 1]
    for b in range(base_ref.shape[0] // BLOCK):
        span = pl.ds(b * BLOCK, BLOCK)
        total = own_ref[span, :]
        for got in got_refs:
            total = total + got[span, :].astype(F32)
        out_ref[span, :] = (base_ref[span, :] + jnp.transpose(total)).astype(BF16)


def body(features, tiles, tile_row, tile_col, degree, train_mask, w_self, w_neigh, cotangent):
    n = lax.axis_size("row")
    me = lax.axis_index("row")
    chips = n // 2
    nodes, feat_in = features.shape
    hidden = w_self.shape[1]
    block_local = nodes // BLOCK
    tile_count = tiles.shape[0]
    group = max(g for g in range(1, 7) if tile_count % g == 0)
    params = pltpu.CompilerParams(vmem_limit_bytes=VMEM_LIMIT)

    gathered = gather_by_xor(features, n)
    half = jax.ShapeDtypeStruct((chips, nodes, feat_in), F32)
    weight = jax.ShapeDtypeStruct((feat_in, hidden), F32)
    embedded, base, wkeep, wsend, keep, send = pl.pallas_call(
        functools.partial(local_kernel, n, group),
        out_shape=(
            jax.ShapeDtypeStruct((nodes, hidden), BF16),
            jax.ShapeDtypeStruct((nodes, feat_in), F32),
            weight, weight, half, half,
        ),
        in_specs=[SMEM] * 3 + [VMEM] * 7 + [ANY] * n,
        out_specs=(VMEM,) * 6,
        scratch_shapes=[
            pltpu.VMEM((n * block_local, BLOCK, feat_in), BF16),
            pltpu.VMEM((block_local + 1, BLOCK, feat_in), F32),
            pltpu.VMEM((block_local, 2 * feat_in, BLOCK), BF16),
            pltpu.VMEM((n * block_local + 1, feat_in, BLOCK), F32),
            pltpu.VMEM((2, feat_in, hidden), F32),
            pltpu.SemaphoreType.DMA((n,)),
        ],
        compiler_params=params,
        name="local_layer",
    )(
        me.astype(jnp.int32).reshape(1), tile_row, tile_col, tiles,
        degree.reshape(block_local, BLOCK), train_mask.reshape(block_local, BLOCK),
        w_self, w_neigh, cotangent, features,
        *[g.reshape(block_local, BLOCK, feat_in) for g in gathered],
    )

    got = swap(send, n, 1)
    own, *outgoing = pl.pallas_call(
        functools.partial(pair_kernel, chips),
        out_shape=[jax.ShapeDtypeStruct((nodes, feat_in), F32)]
        + [jax.ShapeDtypeStruct((nodes, feat_in), BF16)] * (chips - 1),
        in_specs=[VMEM] * 2,
        out_specs=[VMEM] * chips,
        compiler_params=params,
        name="pair_sum",
    )(keep, got)
    arrived = [swap(x, n, 2 * (j + 1)) for j, x in enumerate(outgoing)]

    groups = [[2 * i + c for i in range(chips)] for c in range(2)]

    def exchange(x):
        return lax.all_to_all(x, "row", 0, 0, axis_index_groups=groups, tiled=True)

    pair = (wkeep + swap(wsend, n, 1)).reshape(chips, feat_in // chips, hidden)
    chunk = jnp.sum(exchange(pair), axis=0)
    mine = exchange(jnp.broadcast_to(chunk[None], pair.shape)).reshape(feat_in, hidden)
    other = swap(mine, n, 1)
    first = me % 2 == 0
    grad_self = jnp.where(first, mine, other)
    grad_neigh = jnp.where(first, other, mine)

    grad_input = pl.pallas_call(
        functools.partial(last_kernel, chips),
        out_shape=jax.ShapeDtypeStruct((nodes, feat_in), BF16),
        in_specs=[VMEM] * (chips + 1),
        out_specs=VMEM,
        compiler_params=params,
        name="grad_input_sum",
    )(base, own, *arrived)
    return (embedded, grad_input, grad_self, grad_neigh)


def solution(mesh):
    placed = (
        P(("parts", "row"), None),
        P(("parts", "row"), None, None),
        P(("parts", "row")),
        P(("parts", "row")),
        P(("parts", "row")),
        P(("parts", "row")),
        P(),
        P(),
        P(("parts", "row"), None),
    )
    return jax.shard_map(
        body,
        mesh=mesh,
        in_specs=placed,
        out_specs=(
            P(("parts", "row"), None),
            P(("parts", "row"), None),
            P("parts", None),
            P("parts", None),
        ),
        check_vma=False,
    )
```

time: 404 us -> 100 us (0.25)
  the two profiles are of different devices: /device:TPU:0 before, /device:TPU:14 now
where the time goes in v1:
time: 100 us
  waiting for transfers between devices  39.1 us (39%)
  blocking collectives  22.2 us (22%)
  Pallas kernels  17.5 us (18%)
  starting transfers between devices  16.1 us (16%)
  local copies, waits for them, and re-layouts  2.58 us (3%)
  other arithmetic  1.66 us (2%)
    ppermute x25, waiting for transfers between devices, swap(): return lax.ppermute(x, 'row', [(i, i ^ offset) for i in range(n)])  39.1 us
    all_to_all x2, blocking collectives, exchange(): return lax.all_to_all(x, 'row', 0, 0, axis_index_groups=groups, tiled=True)  22.2 us
    ppermute x25, starting transfers between devices, swap(): return lax.ppermute(x, 'row', [(i, i ^ offset) for i in range(n)])  16.1 us
    pallas_call x1, Pallas kernels, body(): pl.pallas_call(functools.partial(local_kernel, n, group), out_shape=(jax....  12 us
    pallas_call x1, Pallas kernels, body(): pl.pallas_call(functools.partial(pair_kernel, chips), out_shape=[jax.Shap...  3.28 us
    unnamed x46, local copies, waits for them, and re-layouts  2.56 us
    pallas_call x1, Pallas kernels, body(): pl.pallas_call(functools.partial(last_kernel, chips), out_shape=jax.Shape...  2.19 us
  transfers between devices with their start and end apart: 25, of which 14 were waited for; matrix products, arithmetic and copies ran while one was open for 2% of the time, Pallas kernels for 3%

profile of v1, /device:TPU:14, one launch (start us, length us, event | category | flops | bytes accessed | tf_op | source)
XLA Modules:
  0.0 100.0 jit_solution(11926526265396265175)
XLA Ops:
  0.6 2.7 %collective-permute-start.7 = (bf16[512,128]{1,0:T(8,128)(2,1)}, bf16[512,128]{1,0:T(8,128)(2,1)S(1)}, u32[]{:S(2)}, u32[]{:S(2)}) collective-permute-start(bf16[512,128]{1,0:T(8,128)(2,1)} %own_ref.1), channel_id=1, source_target_pairs={{0,8},{1,9},{2,10},{3,11},{4,12},{5,13},{6,14},{7,15},{8,0},{9,1},... | collective-permute-start | bytes 393224 | tf_op jit(solution)/shard_map/ppermute | solution.py:19
  3.3 0.4 collective-permute-start.3
  3.7 0.5 collective-permute-start.1
  4.2 0.5 collective-permute-start.11
  4.7 5.4 %collective-permute-done.7 = bf16[512,128]{1,0:T(8,128)(2,1)S(1)} collective-permute-done((bf16[512,128]{1,0:T(8,128)(2,1)}, bf16[512,128]{1,0:T(8,128)(2,1)S(1)}, u32[]{:S(2)}, u32[]{:S(2)}) %collective-permute-start.7) | collective-permute-done | bytes 131104 | tf_op jit(solution)/shard_map/ppermute | solution.py:19
  10.1 0.5 collective-permute-start.9
  10.6 0.6 collective-permute-done.3
  11.1 0.0 collective-permute-start.8
  11.1 0.0 copy-start.3
  11.1 1.0 %collective-permute-start.5 = (bf16[512,128]{1,0:T(8,128)(2,1)S(1)}, bf16[512,128]{1,0:T(8,128)(2,1)S(1)}, u32[]{:S(2)}, u32[]{:S(2)}) collective-permute-start(bf16[512,128]{1,0:T(8,128)(2,1)S(1)} %collective-permute-done.3), channel_id=1, source_target_pairs={{0,2},{1,3},{2,0},{3,1},{4,6},{5,7},{6,4},{7,5},{8,10},{9,11},{10,... | collective-permute-start | bytes 393224 | tf_op jit(solution)/shard_map/ppermute | solution.py:19
  12.2 0.2 collective-permute-start.4
  12.3 2.3 %collective-permute-done.11 = bf16[512,128]{1,0:T(8,128)(2,1)S(1)} collective-permute-done((bf16[512,128]{1,0:T(8,128)(2,1)}, bf16[512,128]{1,0:T(8,128)(2,1)S(1)}, u32[]{:S(2)}, u32[]{:S(2)}) %collective-permute-start.11) | collective-permute-done | bytes 131104 | tf_op jit(solution)/shard_map/ppermute | solution.py:19
  14.7 0.5 collective-permute-start.13
  15.2 0.7 collective-permute-done.9
  15.9 0.0 collective-permute-start.12
  15.9 0.0 collective-permute-done.8
  15.9 0.5 collective-permute-start.2
  16.4 1.9 %collective-permute-done.5 = bf16[512,128]{1,0:T(8,128)(2,1)S(1)} collective-permute-done((bf16[512,128]{1,0:T(8,128)(2,1)S(1)}, bf16[512,128]{1,0:T(8,128)(2,1)S(1)}, u32[]{:S(2)}, u32[]{:S(2)}) %collective-permute-start.5) | collective-permute-done | bytes 131104 | tf_op jit(solution)/shard_map/ppermute | solution.py:19
  18.3 0.5 collective-permute-start.6
  18.8 1.8 %collective-permute-done.13 = bf16[512,128]{1,0:T(8,128)(2,1)S(1)} collective-permute-done((bf16[512,128]{1,0:T(8,128)(2,1)S(1)}, bf16[512,128]{1,0:T(8,128)(2,1)S(1)}, u32[]{:S(2)}, u32[]{:S(2)}) %collective-permute-start.13) | collective-permute-done | bytes 131104 | tf_op jit(solution)/shard_map/ppermute | solution.py:19
  20.7 0.0 copy-start.14
  20.7 1.3 %collective-permute-done.14 = bf16[512,128]{1,0:T(8,128)(2,1)S(1)} collective-permute-done((bf16[512,128]{1,0:T(8,128)(2,1)S(1)}, bf16[512,128]{1,0:T(8,128)(2,1)S(1)}, u32[]{:S(2)}, u32[]{:S(2)}) %collective-permute-start.14) | collective-permute-done | bytes 131104 | tf_op jit(solution)/shard_map/ppermute | solution.py:19
  22.1 0.5 copy-done.21
  22.7 12.0 %local_layer.1 = (bf16[512,256]{1,0:T(8,128)(2,1)}, f32[512,128]{1,0:T(8,128)}, f32[128,256]{1,0:T(8,128)}, f32[128,256]{1,0:T(8,128)}, f32[8,512,128]{2,1,0:T(8,128)}, /*index=5*/f32[8,512,128]{2,1,0:T(8,128)}) custom-call(s32[1]{0:T(128)} %bitcast.me_ref, s32[60]{0:T(128)} %trow_ref.1, s32[60]{0:T(128)} %tcol_ref.1, bf16[60,128,128]{2,1,0:T(8,128)(2,1)} %tiles_ref.1, ...), custom_call_target="tpu_custom_call" | custom-call | tf_op jit(solution)/shard_map/local_layer/pallas_call | solution.py:180
  34.7 0.2 collective-permute-start.15
  34.9 0.4 collective-permute-start.23
  35.2 4.0 %collective-permute-done.23 = f32[128,256]{1,0:T(8,128)S(1)} collective-permute-done((f32[128,256]{1,0:T(8,128)}, f32[128,256]{1,0:T(8,128)S(1)}, u32[]{:S(2)}, u32[]{:S(2)}) %collective-permute-start.23) | collective-permute-done | bytes 131104 | tf_op jit(solution)/shard_map/ppermute | solution.py:19
  39.3 0.9 add.8
  40.2 12.4 %all_to_all.10 = f32[8,16,256]{2,1,0:T(8,128)S(1)} all-to-all(f32[8,16,256]{2,1,0:T(8,128)S(1)} %bitcast.25), channel_id=1, replica_groups={{0,2,4,6,8,10,12,14},{1,3,5,7,9,11,13,15},{16,18,20,22,24,26,28,30},{17..., dimensions={0} | all-to-all | bytes 262144 | tf_op jit(solution)/shard_map/all_to_all | solution.py:221
  52.6 9.8 %all_to_all.11 = f32[8,16,256]{2,1,0:T(8,128)S(1)} all-to-all(f32[8,16,256]{2,1,0:T(8,128)S(1)} %broadcast_in_dim.2), channel_id=1, replica_groups={{0,2,4,6,8,10,12,14},{1,3,5,7,9,11,13,15},{16,18,20,22,24,26,28,30},{17..., dimensions={0} | all-to-all | bytes 262144 | tf_op jit(solution)/shard_map/all_to_all | solution.py:221
  62.4 1.3 %copy-done = f32[8,512,128]{2,1,0:T(8,128)} copy-done((f32[8,512,128]{2,1,0:T(8,128)}, f32[8,512,128]{2,1,0:T(8,128)S(1)}, u32[]{:S(2)}) %copy-start) | copy-done | bytes 2097176
  63.7 3.3 %pair_sum.1 = (f32[512,128]{1,0:T(8,128)}, bf16[512,128]{1,0:T(8,128)(2,1)}, bf16[512,128]{1,0:T(8,128)(2,1)}, bf16[512,128]{1,0:T(8,128)(2,1)}, bf16[512,128]{1...) custom-call(f32[8,512,128]{2,1,0:T(8,128)} %get-tuple-element.20.keep_ref, ...), custom_call_target="tpu_custom_call" | custom-call | tf_op jit(solution)/shard_map/pair_sum/pallas_call | solution.py:207
  67.0 0.6 collective-permute-start.16
  67.6 2.2 %collective-permute-start.17 = (bf16[512,128]{1,0:T(8,128)(2,1)}, bf16[512,128]{1,0:T(8,128)(2,1)S(1)}, u32[]{:S(2)}, u32[]{:S(2)}) collective-permute-start(bf16[512,128]{1,0:T(8,128)(2,1)} %get-tuple-element.24), channel_id=1, source_target_pairs={{0,4},{1,5},{2,6},{3,7},{4,0},{5,1},{6,2},{7,3},{8,12},{9,13},{10,... | collective-permute-start | bytes 393224 | tf_op jit(solution)/shard_map/ppermute | solution.py:19
  69.8 0.7 collective-permute-start.18
  70.5 0.9 collective-permute-start.19
  71.4 2.2 %collective-permute-start.20 = (bf16[512,128]{1,0:T(8,128)(2,1)}, bf16[512,128]{1,0:T(8,128)(2,1)S(1)}, u32[]{:S(2)}, u32[]{:S(2)}) collective-permute-start(bf16[512,128]{1,0:T(8,128)(2,1)} %get-tuple-element.27), channel_id=1, source_target_pairs={{0,10},{1,11},{2,8},{3,9},{4,14},{5,15},{6,12},{7,13},{8,2},{9,3},... | collective-permute-start | bytes 393224 | tf_op jit(solution)/shard_map/ppermute | solution.py:19
  73.6 0.9 collective-permute-start.21
  74.6 2.6 %collective-permute-done.17.refs_1_ = bf16[512,128]{1,0:T(8,128)(2,1)S(1)} collective-permute-done((bf16[512,128]{1,0:T(8,128)(2,1)}, bf16[512,128]{1,0:T(8,128)(2,1)S(1)}, u32[]{:S(2)}, u32[]{:S(2)}) %collective-permute-start.17) | collective-permute-done | bytes 131104 | tf_op jit(solution)/shard_map/ppermute | solution.py:19
  77.2 0.7 collective-permute-start.22
  77.9 0.7 broadcast_select_fusion
  78.7 0.8 collective-permute-done.18.refs_2_
  79.5 0.9 collective-permute-done.19.refs_3_
  80.4 8.7 %collective-permute-done.20.refs_4_ = bf16[512,128]{1,0:T(8,128)(2,1)S(1)} collective-permute-done((bf16[512,128]{1,0:T(8,128)(2,1)}, bf16[512,128]{1,0:T(8,128)(2,1)S(1)}, u32[]{:S(2)}, u32[]{:S(2)}) %collective-permute-start.20) | collective-permute-done | bytes 131104 | tf_op jit(solution)/shard_map/ppermute | solution.py:19
  89.1 5.2 %collective-permute-done.21.refs_5_ = bf16[512,128]{1,0:T(8,128)(2,1)S(1)} collective-permute-done((bf16[512,128]{1,0:T(8,128)(2,1)}, bf16[512,128]{1,0:T(8,128)(2,1)S(1)}, u32[]{:S(2)}, u32[]{:S(2)}) %collective-permute-start.21) | collective-permute-done | bytes 131104 | tf_op jit(solution)/shard_map/ppermute | solution.py:19
  94.4 2.8 %collective-permute-done.22.refs_6_ = bf16[512,128]{1,0:T(8,128)(2,1)S(1)} collective-permute-done((bf16[512,128]{1,0:T(8,128)(2,1)}, bf16[512,128]{1,0:T(8,128)(2,1)S(1)}, u32[]{:S(2)}, u32[]{:S(2)}) %collective-permute-start.22) | collective-permute-done | bytes 131104 | tf_op jit(solution)/shard_map/ppermute | solution.py:19
  97.2 0.6 copy-done.22
  97.8 2.2 %grad_input_sum.1 = bf16[512,128]{1,0:T(8,128)(2,1)} custom-call(f32[512,128]{1,0:T(8,128)} %get-tuple-element.19.base_ref, f32[512,128]{1,0:T(8,128)} %get-tuple-element.22.own_ref, bf16[512,128]{1,0:T(8,128)(2,1)} %copy-done.7, bf16[512,128]{1,0:T(8,128)(2,1)} %copy-done.9, bf16[512,128]{1,0:T(8,128)(2,1)} %copy-done.15, bf16[512,128]{1,0:T(8,128)(2,1)} %copy-done.16, ...), custom_call_target="tpu_custom_call" | custom-call | tf_op jit(solution)/shard_map/grad_input_sum/pallas_call | solution.py:231
  (57 shorter events, 0.1 us)
Async XLA Ops:
  0.6 9.4 %collective-permute-start.7 = (bf16[512,128]{1,0:T(8,128)(2,1)}, bf16[512,128]{1,0:T(8,128)(2,1)S(1)}, u32[]{:S(2)}, u32[]{:S(2)}) collective-permute-start(bf16[512,128]{1,0:T(8,128)(2,1)} %own_ref.1), channel_id=1, source_target_pairs={{0,8},{1,9},{2,10},{3,11},{4,12},{5,13},{6,14},{7,15},{8,0},{9,1},... | collective-permute-start | bytes 393224 | tf_op jit(solution)/shard_map/ppermute | solution.py:19
  3.3 7.8 %collective-permute-start.3 = (bf16[512,128]{1,0:T(8,128)(2,1)}, bf16[512,128]{1,0:T(8,128)(2,1)S(1)}, u32[]{:S(2)}, u32[]{:S(2)}) collective-permute-start(bf16[512,128]{1,0:T(8,128)(2,1)} %own_ref.1), channel_id=1, source_target_pairs={{0,4},{1,5},{2,6},{3,7},{4,0},{5,1},{6,2},{7,3},{8,12},{9,13},{10,... | collective-permute-start | bytes 393224 | tf_op jit(solution)/shard_map/ppermute | solution.py:19
  3.7 7.4 %collective-permute-start.1 = (bf16[512,128]{1,0:T(8,128)(2,1)}, bf16[512,128]{1,0:T(8,128)(2,1)S(1)}, u32[]{:S(2)}, u32[]{:S(2)}) collective-permute-start(bf16[512,128]{1,0:T(8,128)(2,1)} %own_ref.1), channel_id=1, source_target_pairs={{0,2},{1,3},{2,0},{3,1},{4,6},{5,7},{6,4},{7,5},{8,10},{9,11},{10,... | collective-permute-start | bytes 393224 | tf_op jit(solution)/shard_map/ppermute | solution.py:19
  4.2 7.9 %collective-permute-start = (bf16[512,128]{1,0:T(8,128)(2,1)}, bf16[512,128]{1,0:T(8,128)(2,1)S(1)}, u32[]{:S(2)}, u32[]{:S(2)}) collective-permute-start(bf16[512,128]{1,0:T(8,128)(2,1)} %own_ref.1), channel_id=1, source_target_pairs={{0,1},{1,0},{2,3},{3,2},{4,5},{5,4},{6,7},{7,6},{8,9},{9,8},{10,11... | collective-permute-start | bytes 393224 | tf_op jit(solution)/shard_map/ppermute | solution.py:19
  4.2 10.4 %collective-permute-start.11 = (bf16[512,128]{1,0:T(8,128)(2,1)}, bf16[512,128]{1,0:T(8,128)(2,1)S(1)}, u32[]{:S(2)}, u32[]{:S(2)}) collective-permute-start(bf16[512,128]{1,0:T(8,128)(2,1)} %own_ref.1), channel_id=1, source_target_pairs={{0,12},{1,13},{2,14},{3,15},{4,8},{5,9},{6,10},{7,11},{8,4},{9,5},... | collective-permute-start | bytes 393224 | tf_op jit(solution)/shard_map/ppermute | solution.py:19
  10.1 11.9 %copy-start.1 = (bf16[512,128]{1,0:T(8,128)(2,1)}, bf16[512,128]{1,0:T(8,128)(2,1)S(1)}, u32[]{:S(2)}) copy-start(bf16[512,128]{1,0:T(8,128)(2,1)S(1)} %collective-permute-done.7) | copy-start | bytes 393220
  10.1 5.8 %collective-permute-start.9 = (bf16[512,128]{1,0:T(8,128)(2,1)S(1)}, bf16[512,128]{1,0:T(8,128)(2,1)S(1)}, u32[]{:S(2)}, u32[]{:S(2)}) collective-permute-start(bf16[512,128]{1,0:T(8,128)(2,1)S(1)} %collective-permute-done.7), channel_id=1, source_target_pairs={{0,2},{1,3},{2,0},{3,1},{4,6},{5,7},{6,4},{7,5},{8,10},{9,11},{10,... | collective-permute-start | bytes 393224 | tf_op jit(solution)/shard_map/ppermute | solution.py:19
  11.1 10.9 %copy-start.2 = (bf16[512,128]{1,0:T(8,128)(2,1)}, bf16[512,128]{1,0:T(8,128)(2,1)S(1)}, u32[]{:S(2)}) copy-start(bf16[512,128]{1,0:T(8,128)(2,1)S(1)} %collective-permute-done.3) | copy-start | bytes 393220
  11.1 4.7 %collective-permute-start.8 = (bf16[512,128]{1,0:T(8,128)(2,1)S(1)}, bf16[512,128]{1,0:T(8,128)(2,1)S(1)}, u32[]{:S(2)}, u32[]{:S(2)}) collective-permute-start(bf16[512,128]{1,0:T(8,128)(2,1)S(1)} %collective-permute-done.7), channel_id=1, source_target_pairs={{0,1},{1,0},{2,3},{3,2},{4,5},{5,4},{6,7},{7,6},{8,9},{9,8},{10,11... | collective-permute-start | bytes 393224 | tf_op jit(solution)/shard_map/ppermute | solution.py:19
  11.1 10.9 %copy-start.3 = (bf16[512,128]{1,0:T(8,128)(2,1)}, bf16[512,128]{1,0:T(8,128)(2,1)S(1)}, u32[]{:S(2)}) copy-start(bf16[512,128]{1,0:T(8,128)(2,1)S(1)} %collective-permute-done.1) | copy-start | bytes 393220
  11.1 7.2 %collective-permute-start.5 = (bf16[512,128]{1,0:T(8,128)(2,1)S(1)}, bf16[512,128]{1,0:T(8,128)(2,1)S(1)}, u32[]{:S(2)}, u32[]{:S(2)}) collective-permute-start(bf16[512,128]{1,0:T(8,128)(2,1)S(1)} %collective-permute-done.3), channel_id=1, source_target_pairs={{0,2},{1,3},{2,0},{3,1},{4,6},{5,7},{6,4},{7,5},{8,10},{9,11},{10,... | collective-permute-start | bytes 393224 | tf_op jit(solution)/shard_map/ppermute | solution.py:19
  12.2 9.8 %copy-start.4 = (bf16[512,128]{1,0:T(8,128)(2,1)}, bf16[512,128]{1,0:T(8,128)(2,1)S(1)}, u32[]{:S(2)}) copy-start(bf16[512,128]{1,0:T(8,128)(2,1)S(1)} %collective-permute-done) | copy-start | bytes 393220
  12.2 6.1 %collective-permute-start.4 = (bf16[512,128]{1,0:T(8,128)(2,1)S(1)}, bf16[512,128]{1,0:T(8,128)(2,1)S(1)}, u32[]{:S(2)}, u32[]{:S(2)}) collective-permute-start(bf16[512,128]{1,0:T(8,128)(2,1)S(1)} %collective-permute-done.3), channel_id=1, source_target_pairs={{0,1},{1,0},{2,3},{3,2},{4,5},{5,4},{6,7},{7,6},{8,9},{9,8},{10,11... | collective-permute-start | bytes 393224 | tf_op jit(solution)/shard_map/ppermute | solution.py:19
  14.7 7.3 %copy-start.5 = (bf16[512,128]{1,0:T(8,128)(2,1)}, bf16[512,128]{1,0:T(8,128)(2,1)S(1)}, u32[]{:S(2)}) copy-start(bf16[512,128]{1,0:T(8,128)(2,1)S(1)} %collective-permute-done.11) | copy-start | bytes 393220
  14.7 6.0 %collective-permute-start.13 = (bf16[512,128]{1,0:T(8,128)(2,1)S(1)}, bf16[512,128]{1,0:T(8,128)(2,1)S(1)}, u32[]{:S(2)}, u32[]{:S(2)}) collective-permute-start(bf16[512,128]{1,0:T(8,128)(2,1)S(1)} %collective-permute-done.11), channel_id=1, source_target_pairs={{0,2},{1,3},{2,0},{3,1},{4,6},{5,7},{6,4},{7,5},{8,10},{9,11},{10,... | collective-permute-start | bytes 393224 | tf_op jit(solution)/shard_map/ppermute | solution.py:19
  15.9 6.2 %copy-start.6 = (bf16[512,128]{1,0:T(8,128)(2,1)}, bf16[512,128]{1,0:T(8,128)(2,1)S(1)}, u32[]{:S(2)}) copy-start(bf16[512,128]{1,0:T(8,128)(2,1)S(1)} %collective-permute-done.9) | copy-start | bytes 393220
  15.9 4.8 %collective-permute-start.12 = (bf16[512,128]{1,0:T(8,128)(2,1)S(1)}, bf16[512,128]{1,0:T(8,128)(2,1)S(1)}, u32[]{:S(2)}, u32[]{:S(2)}) collective-permute-start(bf16[512,128]{1,0:T(8,128)(2,1)S(1)} %collective-permute-done.11), channel_id=1, source_target_pairs={{0,1},{1,0},{2,3},{3,2},{4,5},{5,4},{6,7},{7,6},{8,9},{9,8},{10,11... | collective-permute-start | bytes 393224 | tf_op jit(solution)/shard_map/ppermute | solution.py:19
  15.9 6.2 %copy-start.8 = (bf16[512,128]{1,0:T(8,128)(2,1)}, bf16[512,128]{1,0:T(8,128)(2,1)S(1)}, u32[]{:S(2)}) copy-start(bf16[512,128]{1,0:T(8,128)(2,1)S(1)} %collective-permute-done.8) | copy-start | bytes 393220
  15.9 4.8 %collective-permute-start.2 = (bf16[512,128]{1,0:T(8,128)(2,1)S(1)}, bf16[512,128]{1,0:T(8,128)(2,1)S(1)}, u32[]{:S(2)}, u32[]{:S(2)}) collective-permute-start(bf16[512,128]{1,0:T(8,128)(2,1)S(1)} %collective-permute-done.1), channel_id=1, source_target_pairs={{0,1},{1,0},{2,3},{3,2},{4,5},{5,4},{6,7},{7,6},{8,9},{9,8},{10,11... | collective-permute-start | bytes 393224 | tf_op jit(solution)/shard_map/ppermute | solution.py:19
  18.3 3.7 %copy-start.10 = (bf16[512,128]{1,0:T(8,128)(2,1)}, bf16[512,128]{1,0:T(8,128)(2,1)S(1)}, u32[]{:S(2)}) copy-start(bf16[512,128]{1,0:T(8,128)(2,1)S(1)} %collective-permute-done.5) | copy-start | bytes 393220
  18.3 2.4 %collective-permute-start.10 = (bf16[512,128]{1,0:T(8,128)(2,1)S(1)}, bf16[512,128]{1,0:T(8,128)(2,1)S(1)}, u32[]{:S(2)}, u32[]{:S(2)}) collective-permute-start(bf16[512,128]{1,0:T(8,128)(2,1)S(1)} %collective-permute-done.9), channel_id=1, source_target_pairs={{0,1},{1,0},{2,3},{3,2},{4,5},{5,4},{6,7},{7,6},{8,9},{9,8},{10,11... | collective-permute-start | bytes 393224 | tf_op jit(solution)/shard_map/ppermute | solution.py:19
  18.3 3.7 %copy-start.11 = (bf16[512,128]{1,0:T(8,128)(2,1)}, bf16[512,128]{1,0:T(8,128)(2,1)S(1)}, u32[]{:S(2)}) copy-start(bf16[512,128]{1,0:T(8,128)(2,1)S(1)} %collective-permute-done.4) | copy-start | bytes 393220
  18.3 2.4 %collective-permute-start.6 = (bf16[512,128]{1,0:T(8,128)(2,1)S(1)}, bf16[512,128]{1,0:T(8,128)(2,1)S(1)}, u32[]{:S(2)}, u32[]{:S(2)}) collective-permute-start(bf16[512,128]{1,0:T(8,128)(2,1)S(1)} %collective-permute-done.5), channel_id=1, source_target_pairs={{0,1},{1,0},{2,3},{3,2},{4,5},{5,4},{6,7},{7,6},{8,9},{9,8},{10,11... | collective-permute-start | bytes 393224 | tf_op jit(solution)/shard_map/ppermute | solution.py:19
  20.6 1.4 %copy-start.12 = (bf16[512,128]{1,0:T(8,128)(2,1)}, bf16[512,128]{1,0:T(8,128)(2,1)S(1)}, u32[]{:S(2)}) copy-start(bf16[512,128]{1,0:T(8,128)(2,1)S(1)} %collective-permute-done.13) | copy-start | bytes 393220
  20.6 1.3 %collective-permute-start.14 = (bf16[512,128]{1,0:T(8,128)(2,1)S(1)}, bf16[512,128]{1,0:T(8,128)(2,1)S(1)}, u32[]{:S(2)}, u32[]{:S(2)}) collective-permute-start(bf16[512,128]{1,0:T(8,128)(2,1)S(1)} %collective-permute-done.13), channel_id=1, source_target_pairs={{0,1},{1,0},{2,3},{3,2},{4,5},{5,4},{6,7},{7,6},{8,9},{9,8},{10,11... | collective-permute-start | bytes 393224 | tf_op jit(solution)/shard_map/ppermute | solution.py:19
  20.7 1.4 %copy-start.14 = (bf16[512,128]{1,0:T(8,128)(2,1)}, bf16[512,128]{1,0:T(8,128)(2,1)S(1)}, u32[]{:S(2)}) copy-start(bf16[512,128]{1,0:T(8,128)(2,1)S(1)} %collective-permute-done.2) | copy-start | bytes 393220
  20.7 1.4 %copy-start.13 = (bf16[512,128]{1,0:T(8,128)(2,1)}, bf16[512,128]{1,0:T(8,128)(2,1)S(1)}, u32[]{:S(2)}) copy-start(bf16[512,128]{1,0:T(8,128)(2,1)S(1)} %collective-permute-done.12) | copy-start | bytes 393220
  20.7 1.4 %copy-start.17 = (bf16[512,128]{1,0:T(8,128)(2,1)}, bf16[512,128]{1,0:T(8,128)(2,1)S(1)}, u32[]{:S(2)}) copy-start(bf16[512,128]{1,0:T(8,128)(2,1)S(1)} %collective-permute-done.10) | copy-start | bytes 393220
  20.7 1.4 %copy-start.19 = (bf16[512,128]{1,0:T(8,128)(2,1)}, bf16[512,128]{1,0:T(8,128)(2,1)S(1)}, u32[]{:S(2)}) copy-start(bf16[512,128]{1,0:T(8,128)(2,1)S(1)} %collective-permute-done.6) | copy-start | bytes 393220
  22.0 0.7 copy-start.21
  34.7 27.8 %collective-permute-start.15 = (f32[8,512,128]{2,1,0:T(8,128)}, f32[8,512,128]{2,1,0:T(8,128)S(1)}, u32[]{:S(2)}, u32[]{:S(2)}) collective-permute-start(f32[8,512,128]{2,1,0:T(8,128)} %get-tuple-element.21), channel_id=1, source_target_pairs={{0,1},{1,0},{2,3},{3,2},{4,5},{5,4},{6,7},{7,6},{8,9},{9,8},{10,11... | collective-permute-start | bytes 6291464 | tf_op jit(solution)/shard_map/ppermute | solution.py:19
  34.9 4.4 %collective-permute-start.23 = (f32[128,256]{1,0:T(8,128)}, f32[128,256]{1,0:T(8,128)S(1)}, u32[]{:S(2)}, u32[]{:S(2)}) collective-permute-start(f32[128,256]{1,0:T(8,128)} %get-tuple-element.31), channel_id=1, source_target_pairs={{0,1},{1,0},{2,3},{3,2},{4,5},{5,4},{6,7},{7,6},{8,9},{9,8},{10,11... | collective-permute-start | bytes 393224 | tf_op jit(solution)/shard_map/ppermute | solution.py:19
  62.4 9.0 %collective-permute-start.24 = (f32[128,256]{1,0:T(8,128)S(1)}, f32[128,256]{1,0:T(8,128)S(1)}, u32[]{:S(2)}, u32[]{:S(2)}) collective-permute-start(f32[128,256]{1,0:T(8,128)S(1)} %bitcast.24), channel_id=1, source_target_pairs={{0,1},{1,0},{2,3},{3,2},{4,5},{5,4},{6,7},{7,6},{8,9},{9,8},{10,11... | collective-permute-start | bytes 393224 | tf_op jit(solution)/shard_map/ppermute | solution.py:19
  62.4 1.3 %copy-start = (f32[8,512,128]{2,1,0:T(8,128)}, f32[8,512,128]{2,1,0:T(8,128)S(1)}, u32[]{:S(2)}) copy-start(f32[8,512,128]{2,1,0:T(8,128)S(1)} %collective-permute-done.15.got_ref) | copy-start | bytes 6291460
  67.0 6.6 %collective-permute-start.16 = (bf16[512,128]{1,0:T(8,128)(2,1)}, bf16[512,128]{1,0:T(8,128)(2,1)S(1)}, u32[]{:S(2)}, u32[]{:S(2)}) collective-permute-start(bf16[512,128]{1,0:T(8,128)(2,1)} %get-tuple-element.23), channel_id=1, source_target_pairs={{0,2},{1,3},{2,0},{3,1},{4,6},{5,7},{6,4},{7,5},{8,10},{9,11},{10,... | collective-permute-start | bytes 393224 | tf_op jit(solution)/shard_map/ppermute | solution.py:19
  67.6 9.6 %collective-permute-start.17 = (bf16[512,128]{1,0:T(8,128)(2,1)}, bf16[512,128]{1,0:T(8,128)(2,1)S(1)}, u32[]{:S(2)}, u32[]{:S(2)}) collective-permute-start(bf16[512,128]{1,0:T(8,128)(2,1)} %get-tuple-element.24), channel_id=1, source_target_pairs={{0,4},{1,5},{2,6},{3,7},{4,0},{5,1},{6,2},{7,3},{8,12},{9,13},{10,... | collective-permute-start | bytes 393224 | tf_op jit(solution)/shard_map/ppermute | solution.py:19
  69.8 9.7 %collective-permute-start.18 = (bf16[512,128]{1,0:T(8,128)(2,1)}, bf16[512,128]{1,0:T(8,128)(2,1)S(1)}, u32[]{:S(2)}, u32[]{:S(2)}) collective-permute-start(bf16[512,128]{1,0:T(8,128)(2,1)} %get-tuple-element.25), channel_id=1, source_target_pairs={{0,6},{1,7},{2,4},{3,5},{4,2},{5,3},{6,0},{7,1},{8,14},{9,15},{10,... | collective-permute-start | bytes 393224 | tf_op jit(solution)/shard_map/ppermute | solution.py:19
  70.5 9.9 %collective-permute-start.19 = (bf16[512,128]{1,0:T(8,128)(2,1)}, bf16[512,128]{1,0:T(8,128)(2,1)S(1)}, u32[]{:S(2)}, u32[]{:S(2)}) collective-permute-start(bf16[512,128]{1,0:T(8,128)(2,1)} %get-tuple-element.26), channel_id=1, source_target_pairs={{0,8},{1,9},{2,10},{3,11},{4,12},{5,13},{6,14},{7,15},{8,0},{9,1},... | collective-permute-start | bytes 393224 | tf_op jit(solution)/shard_map/ppermute | solution.py:19
  71.4 17.7 %collective-permute-start.20 = (bf16[512,128]{1,0:T(8,128)(2,1)}, bf16[512,128]{1,0:T(8,128)(2,1)S(1)}, u32[]{:S(2)}, u32[]{:S(2)}) collective-permute-start(bf16[512,128]{1,0:T(8,128)(2,1)} %get-tuple-element.27), channel_id=1, source_target_pairs={{0,10},{1,11},{2,8},{3,9},{4,14},{5,15},{6,12},{7,13},{8,2},{9,3},... | collective-permute-start | bytes 393224 | tf_op jit(solution)/shard_map/ppermute | solution.py:19
  73.6 23.5 %copy-start.7 = (bf16[512,128]{1,0:T(8,128)(2,1)}, bf16[512,128]{1,0:T(8,128)(2,1)S(1)}, u32[]{:S(2)}) copy-start(bf16[512,128]{1,0:T(8,128)(2,1)S(1)} %collective-permute-done.16.refs_0_) | copy-start | bytes 393220
  73.6 20.7 %collective-permute-start.21 = (bf16[512,128]{1,0:T(8,128)(2,1)}, bf16[512,128]{1,0:T(8,128)(2,1)S(1)}, u32[]{:S(2)}, u32[]{:S(2)}) collective-permute-start(bf16[512,128]{1,0:T(8,128)(2,1)} %get-tuple-element.28), channel_id=1, source_target_pairs={{0,12},{1,13},{2,14},{3,15},{4,8},{5,9},{6,10},{7,11},{8,4},{9,5},... | collective-permute-start | bytes 393224 | tf_op jit(solution)/shard_map/ppermute | solution.py:19
  77.2 19.9 %copy-start.9 = (bf16[512,128]{1,0:T(8,128)(2,1)}, bf16[512,128]{1,0:T(8,128)(2,1)S(1)}, u32[]{:S(2)}) copy-start(bf16[512,128]{1,0:T(8,128)(2,1)S(1)} %collective-permute-done.17.refs_1_) | copy-start | bytes 393220
  77.2 19.9 %collective-permute-start.22 = (bf16[512,128]{1,0:T(8,128)(2,1)}, bf16[512,128]{1,0:T(8,128)(2,1)S(1)}, u32[]{:S(2)}, u32[]{:S(2)}) collective-permute-start(bf16[512,128]{1,0:T(8,128)(2,1)} %get-tuple-element.29), channel_id=1, source_target_pairs={{0,14},{1,15},{2,12},{3,13},{4,10},{5,11},{6,8},{7,9},{8,6},{9,7},... | collective-permute-start | bytes 393224 | tf_op jit(solution)/shard_map/ppermute | solution.py:19
  79.5 17.7 %copy-start.15 = (bf16[512,128]{1,0:T(8,128)(2,1)}, bf16[512,128]{1,0:T(8,128)(2,1)S(1)}, u32[]{:S(2)}) copy-start(bf16[512,128]{1,0:T(8,128)(2,1)S(1)} %collective-permute-done.18.refs_2_) | copy-start | bytes 393220
  80.4 16.7 %copy-start.16 = (bf16[512,128]{1,0:T(8,128)(2,1)}, bf16[512,128]{1,0:T(8,128)(2,1)S(1)}, u32[]{:S(2)}) copy-start(bf16[512,128]{1,0:T(8,128)(2,1)S(1)} %collective-permute-done.19.refs_3_) | copy-start | bytes 393220
  89.1 8.0 %copy-start.18 = (bf16[512,128]{1,0:T(8,128)(2,1)}, bf16[512,128]{1,0:T(8,128)(2,1)S(1)}, u32[]{:S(2)}) copy-start(bf16[512,128]{1,0:T(8,128)(2,1)S(1)} %collective-permute-done.20.refs_4_) | copy-start | bytes 393220
  94.4 2.8 %copy-start.20 = (bf16[512,128]{1,0:T(8,128)(2,1)}, bf16[512,128]{1,0:T(8,128)(2,1)S(1)}, u32[]{:S(2)}) copy-start(bf16[512,128]{1,0:T(8,128)(2,1)S(1)} %collective-permute-done.21.refs_5_) | copy-start | bytes 393220
  97.1 0.6 copy-start.22

commit v2 on v1

v2 whole, which is shorter than its diff:
```python
import functools

import jax
import jax.numpy as jnp
from jax import lax
from jax.experimental import pallas as pl
from jax.experimental.pallas import tpu as pltpu
from jax.sharding import PartitionSpec as P

BLOCK = 128
F32, BF16 = jnp.float32, jnp.bfloat16
VMEM = pl.BlockSpec(memory_space=pltpu.VMEM)
SMEM = pl.BlockSpec(memory_space=pltpu.SMEM)
MIB = 1024 * 1024


def swap(x, n, offset):
    return lax.ppermute(x, "row", [(i, i ^ offset) for i in range(n)])


def gather_by_xor(x, n):
    blocks = {0: x}
    for bit in range(n.bit_length() - 2, -1, -1):
        blocks |= {k ^ (1 << bit): swap(v, n, 1 << bit) for k, v in blocks.items()}
    return [blocks[k] for k in range(n)]


def split_bf16(x):
    high = x.astype(BF16)
    return high, (x - high.astype(F32)).astype(BF16)


def dot(a, b, dims=((1,), (0,))):
    return lax.dot_general(a, b, (dims, ((), ())), preferred_element_type=F32)


def dot_wide(a, b, dims=((1,), (0,))):
    high, low = split_bf16(a)
    return dot(high, b, dims) + dot(low, b, dims)


def rows_to_lanes(row):
    return jnp.transpose(jnp.broadcast_to(row, (BLOCK, BLOCK)))


def place(t, n, block_local, me, trow_ref, tcol_ref):
    col = tcol_ref[t]
    live = col >= 0
    col = jnp.maximum(col, 0)
    position = ((col // block_local) ^ me) * block_local + col % block_local
    row = jnp.clip(trow_ref[t] - me * block_local, 0, block_local - 1)
    return live, row, position


def forward_kernel(n, group, me_ref, trow_ref, tcol_ref, tiles_ref, deg_ref, mask_ref, ws_ref,
                   wn_ref, cot_ref, *refs):
    feat_refs, refs = refs[:n], refs[n:]
    emb_ref, base_ref, wkeep_ref, wsend_ref, gt_ref, feats, raw, wsum = refs
    own_ref = feat_refs[0]
    block_local = own_ref.shape[0] // BLOCK
    tile_count = tiles_ref.shape[0]
    me = me_ref[0]

    raw[...] = jnp.zeros_like(raw)
    for k in range(n):
        for b in range(block_local):
            feats[k * block_local + b] = feat_refs[k][pl.ds(b * BLOCK, BLOCK), :]

    def forward(step, carry):
        rows, products = [], []
        for u in range(group):
            t = step * group + u
            live, row, position = place(t, n, block_local, me, trow_ref, tcol_ref)
            rows.append(jnp.where(live, row, block_local))
            products.append(dot(tiles_ref[t], feats[position]))
        for row, product in zip(rows, products):
            raw[row] += product
        return carry

    lax.fori_loop(0, tile_count // group, forward, 0)

    wn = wn_ref[...]
    ws = ws_ref[...]
    for b in range(block_local):
        span = pl.ds(b * BLOCK, BLOCK)
        degree = rows_to_lanes(deg_ref[pl.ds(b, 1), :].astype(F32))
        mask = rows_to_lanes(mask_ref[pl.ds(b, 1), :].astype(F32))
        degree2 = jnp.concatenate([degree, degree], axis=1)
        mask2 = jnp.concatenate([mask, mask], axis=1)
        feat = own_ref[span, :]
        raw_b = raw[b]
        pre = dot(feat, ws) + dot_wide(raw_b / degree, wn)
        sig = jax.nn.sigmoid(pre)
        emb_ref[span, :] = (pre * sig).astype(BF16)
        upstream = cot_ref[span, :].astype(F32) * mask2
        grad_pre = upstream * sig * (1.0 + pre * (1.0 - sig))
        scaled = (grad_pre / degree2).astype(BF16)
        gp_high, gp_low = split_bf16(grad_pre)
        feat_t = jnp.transpose(feat.astype(F32)).astype(BF16)
        grad_self = dot(feat_t, gp_high) + dot(feat_t, gp_low)
        grad_neigh = dot_wide(jnp.transpose(raw_b), scaled)
        if b == 0:
            wsum[0], wsum[1] = grad_self, grad_neigh
        else:
            wsum[0] += grad_self
            wsum[1] += grad_neigh
        last = ((1,), (1,))
        base_ref[span, :] = dot(gp_high, ws, last) + dot(gp_low, ws, last)
        high, low = split_bf16(dot(wn, scaled, last))
        gt_ref[b, :BLOCK, :] = high
        gt_ref[b, BLOCK:, :] = low

    core = me % 2
    wkeep_ref[...] = wsum[core]
    wsend_ref[...] = wsum[1 - core]


def backward_kernel(n, group, me_ref, trow_ref, tcol_ref, tiles_ref, gt_ref,
                    send_odd_ref, send_even_ref, keep_odd_ref, keep_even_ref, acc):
    block_local = gt_ref.shape[0]
    tile_count = tiles_ref.shape[0]
    me = me_ref[0]
    acc[...] = jnp.zeros_like(acc)

    def backward(step, carry):
        places, products = [], []
        for u in range(group):
            t = step * group + u
            live, row, position = place(t, n, block_local, me, trow_ref, tcol_ref)
            places.append(jnp.where(live, position, n * block_local))
            both = dot(gt_ref[row], tiles_ref[t])
            products.append(both[:BLOCK] + both[BLOCK:])
        for position, product in zip(places, products):
            acc[position] += product
        return carry

    lax.fori_loop(0, tile_count // group, backward, 0)

    targets = ((keep_even_ref, keep_odd_ref), (send_even_ref, send_odd_ref))
    for k in range(n):
        j = k // 2
        for b in range(block_local):
            targets[k % 2][j % 2][j // 2, pl.ds(b * BLOCK, BLOCK), :] = acc[k * block_local + b]


def odd_kernel(count, keep_ref, got_ref, *out_refs):
    for j in range(count):
        out_refs[j][...] = (keep_ref[j] + got_ref[j]).astype(BF16)


def even_kernel(count, keep_ref, got_ref, *out_refs):
    for j in range(count):
        out_refs[j][...] = keep_ref[j] + got_ref[j]


def add_kernel(own_ref, got_ref, out_ref):
    out_ref[...] = (own_ref[...] + got_ref[...].astype(F32)).astype(BF16)


def last_kernel(count, base_ref, own_ref, *refs):
    got_refs, out_ref = refs[:count], refs[count]
    for b in range(base_ref.shape[0] // BLOCK):
        span = pl.ds(b * BLOCK, BLOCK)
        total = own_ref[span, :]
        for got in got_refs:
            total = total + got[span, :].astype(F32)
        out_ref[span, :] = (base_ref[span, :] + jnp.transpose(total)).astype(BF16)


def body(features, tiles, tile_row, tile_col, degree, train_mask, w_self, w_neigh, cotangent):
    n = lax.axis_size("row")
    me = lax.axis_index("row")
    lines = n // 4
    nodes, feat_in = features.shape
    hidden = w_self.shape[1]
    block_local = nodes // BLOCK
    tile_count = tiles.shape[0]
    group = max(g for g in range(1, 7) if tile_count % g == 0)
    small = n * nodes * feat_in * 4 <= 4 * MIB
    limit = (24 if small else 56) * MIB

    def near(x):
        return pltpu.with_memory_space_constraint(x, pltpu.VMEM) if small else x

    def result(shape, dtype, stays=True):
        kind = pltpu.VMEM if small and stays else jax.ShapeDtypeStruct
        return kind(shape, dtype)

    def call(kernel, name, out_shape, scalars, arrays, scratch=()):
        return pl.pallas_call(
            kernel,
            out_shape=out_shape,
            in_specs=[SMEM] * len(scalars) + [VMEM] * len(arrays),
            out_specs=jax.tree.map(lambda _: VMEM, out_shape),
            scratch_shapes=list(scratch),
            compiler_params=pltpu.CompilerParams(vmem_limit_bytes=limit),
            name=name,
        )(*scalars, *[near(x) for x in arrays])

    scalars = (me.astype(jnp.int32).reshape(1), tile_row, tile_col)
    gathered = gather_by_xor(features, n)
    embedded, base, wkeep, wsend, gt = call(
        functools.partial(forward_kernel, n, group),
        "forward_layer",
        (
            result((nodes, hidden), BF16, False),
            result((nodes, feat_in), F32),
            result((feat_in, hidden), F32),
            result((feat_in, hidden), F32),
            result((block_local, 2 * feat_in, BLOCK), BF16),
        ),
        scalars,
        (
            tiles, degree.reshape(block_local, BLOCK), train_mask.reshape(block_local, BLOCK),
            w_self, w_neigh, cotangent, *gathered,
        ),
        [
            pltpu.VMEM((n * block_local, BLOCK, feat_in), BF16),
            pltpu.VMEM((block_local + 1, BLOCK, feat_in), F32),
            pltpu.VMEM((2, feat_in, hidden), F32),
        ],
    )

    quarter = result((lines, nodes, feat_in), F32)
    send_odd, send_even, keep_odd, keep_even = call(
        functools.partial(backward_kernel, n, group),
        "backward_tiles",
        (quarter,) * 4,
        scalars,
        (tiles, gt),
        [pltpu.VMEM((n * block_local + 1, feat_in, BLOCK), F32)],
    )

    piece = result((nodes, feat_in), BF16)
    wide = result((nodes, feat_in), F32)
    to_y = call(
        functools.partial(odd_kernel, lines), "pair_sum_y", (piece,) * lines, (),
        (keep_odd, swap(send_odd, n, 1)),
    )
    from_y = [swap(x, n, 2) for x in to_y]
    here = call(
        functools.partial(even_kernel, lines), "pair_sum_z", (wide,) * lines, (),
        (keep_even, swap(send_even, n, 1)),
    )
    from_z = []
    for line in range(lines - 1, 0, -1):
        total = call(add_kernel, "line_sum", piece, (), (here[line], from_y[line]))
        from_z.append(swap(total, n, 4 * line))

    mine = wkeep + swap(wsend, n, 1)
    for bit in range(1, n.bit_length() - 1):
        mine = mine + swap(mine, n, 1 << bit)
    other = swap(mine, n, 1)
    first = me % 2 == 0
    grad_self = jnp.where(first, mine, other)
    grad_neigh = jnp.where(first, other, mine)

    grad_input = call(
        functools.partial(last_kernel, lines), "grad_input_sum",
        result((nodes, feat_in), BF16, False), (),
        (base, here[0], from_y[0], *from_z),
    )
    return (embedded, grad_input, grad_self, grad_neigh)


def solution(mesh):
    placed = (
        P(("parts", "row"), None),
        P(("parts", "row"), None, None),
        P(("parts", "row")),
        P(("parts", "row")),
        P(("parts", "row")),
        P(("parts", "row")),
        P(),
        P(),
        P(("parts", "row"), None),
    )
    return jax.shard_map(
        body,
        mesh=mesh,
        in_specs=placed,
        out_specs=(
            P(("parts", "row"), None),
            P(("parts", "row"), None),
            P("parts", None),
            P("parts", None),
        ),
        check_vma=False,
    )
```

time: 100 us -> 80.1 us (0.80)
  the two profiles are of different devices: /device:TPU:14 before, /device:TPU:0 now
where the time goes in v2:
time: 80.1 us; the launch traced here: 79.8 us
  waiting for transfers between devices  32.7 us (41%)
  starting transfers between devices  27 us (34%)
  Pallas kernels  10.7 us (13%)
  local copies, waits for them, and re-layouts  7.75 us (10%)
    ppermute x29, waiting for transfers between devices, swap(): return lax.ppermute(x, 'row', [(i, i ^ offset) for i in range(n)])  32.7 us
    ppermute x29, starting transfers between devices, swap(): return lax.ppermute(x, 'row', [(i, i ^ offset) for i in range(n)])  27 us
    pallas_call x8, Pallas kernels, call(): pl.pallas_call(kernel, out_shape=out_shape, in_specs=[SMEM] * len(scalars...  10.7 us
    unnamed x18, local copies, waits for them, and re-layouts  7.75 us
  transfers between devices with their start and end apart: 29, of which 14 were waited for; matrix products, arithmetic and copies ran while one was open for 1% of the time, Pallas kernels for 0%

profile of v2, /device:TPU:0, one launch (start us, length us, event | category | flops | bytes accessed | tf_op | source)
XLA Modules:
  0.0 79.8 jit_solution(12089615982576868651)
XLA Ops:
  0.6 4.1 %collective-permute-start.7 = (bf16[512,128]{1,0:T(8,128)(2,1)}, bf16[512,128]{1,0:T(8,128)(2,1)S(1)}, u32[]{:S(2)}, u32[]{:S(2)}) collective-permute-start(bf16[512,128]{1,0:T(8,128)(2,1)} %refs_0_.1), channel_id=1, source_target_pairs={{0,8},{1,9},{2,10},{3,11},{4,12},{5,13},{6,14},{7,15},{8,0},{9,1},... | collective-permute-start | bytes 393224 | tf_op jit(solution)/shard_map/ppermute | solution.py:18
  4.7 1.6 %collective-permute-start.3 = (bf16[512,128]{1,0:T(8,128)(2,1)}, bf16[512,128]{1,0:T(8,128)(2,1)S(1)}, u32[]{:S(2)}, u32[]{:S(2)}) collective-permute-start(bf16[512,128]{1,0:T(8,128)(2,1)} %refs_0_.1), channel_id=1, source_target_pairs={{0,4},{1,5},{2,6},{3,7},{4,0},{5,1},{6,2},{7,3},{8,12},{9,13},{10,... | collective-permute-start | bytes 393224 | tf_op jit(solution)/shard_map/ppermute | solution.py:18
  6.3 1.5 %collective-permute-start.1 = (bf16[512,128]{1,0:T(8,128)(2,1)}, bf16[512,128]{1,0:T(8,128)(2,1)S(1)}, u32[]{:S(2)}, u32[]{:S(2)}) collective-permute-start(bf16[512,128]{1,0:T(8,128)(2,1)} %refs_0_.1), channel_id=1, source_target_pairs={{0,2},{1,3},{2,0},{3,1},{4,6},{5,7},{6,4},{7,5},{8,10},{9,11},{10,... | collective-permute-start | bytes 393224 | tf_op jit(solution)/shard_map/ppermute | solution.py:18
  7.8 3.5 %collective-permute-done.7.refs_8_ = bf16[512,128]{1,0:T(8,128)(2,1)S(1)} collective-permute-done((bf16[512,128]{1,0:T(8,128)(2,1)}, bf16[512,128]{1,0:T(8,128)(2,1)S(1)}, u32[]{:S(2)}, u32[]{:S(2)}) %collective-permute-start.7) | collective-permute-done | bytes 131104 | tf_op jit(solution)/shard_map/ppermute | solution.py:18
  11.4 0.7 collective-permute-start.11
  12.1 1.5 %collective-permute-start.5 = (bf16[512,128]{1,0:T(8,128)(2,1)S(1)}, bf16[512,128]{1,0:T(8,128)(2,1)S(1)}, u32[]{:S(2)}, u32[]{:S(2)}) collective-permute-start(bf16[512,128]{1,0:T(8,128)(2,1)S(1)} %collective-permute-done.3.refs_4_), channel_id=1, source_target_pairs={{0,2},{1,3},{2,0},{3,1},{4,6},{5,7},{6,4},{7,5},{8,10},{9,11},{10,... | collective-permute-start | bytes 393224 | tf_op jit(solution)/shard_map/ppermute | solution.py:18
  13.6 0.5 collective-permute-start.2
  14.1 0.5 collective-permute-start.9
  14.6 1.7 %collective-permute-done.11.refs_12_ = bf16[512,128]{1,0:T(8,128)(2,1)S(1)} collective-permute-done((bf16[512,128]{1,0:T(8,128)(2,1)S(1)}, bf16[512,128]{1,0:T(8,128)(2,1)S(1)}, u32[]{:S(2)}, u32[]{:S(2)}) %collective-permute-start.11) | collective-permute-done | bytes 131104 | tf_op jit(solution)/shard_map/ppermute | solution.py:18
  16.3 1.6 %collective-permute-start.13 = (bf16[512,128]{1,0:T(8,128)(2,1)S(1)}, bf16[512,128]{1,0:T(8,128)(2,1)S(1)}, u32[]{:S(2)}, u32[]{:S(2)}) collective-permute-start(bf16[512,128]{1,0:T(8,128)(2,1)S(1)} %collective-permute-done.11.refs_12_), channel_id=1, source_target_pairs={{0,2},{1,3},{2,0},{3,1},{4,6},{5,7},{6,4},{7,5},{8,10},{9,11},{10,... | collective-permute-start | bytes 393224 | tf_op jit(solution)/shard_map/ppermute | solution.py:18
  17.9 0.5 collective-permute-start.12
  18.5 2.0 %collective-permute-done.9.refs_10_ = bf16[512,128]{1,0:T(8,128)(2,1)S(1)} collective-permute-done((bf16[512,128]{1,0:T(8,128)(2,1)S(1)}, bf16[512,128]{1,0:T(8,128)(2,1)S(1)}, u32[]{:S(2)}, u32[]{:S(2)}) %collective-permute-start.9) | collective-permute-done | bytes 131104 | tf_op jit(solution)/shard_map/ppermute | solution.py:18
  20.5 2.4 %collective-permute-done.13.refs_14_ = bf16[512,128]{1,0:T(8,128)(2,1)S(1)} collective-permute-done((bf16[512,128]{1,0:T(8,128)(2,1)S(1)}, bf16[512,128]{1,0:T(8,128)(2,1)S(1)}, u32[]{:S(2)}, u32[]{:S(2)}) %collective-permute-start.13) | collective-permute-done | bytes 131104 | tf_op jit(solution)/shard_map/ppermute | solution.py:18
  22.9 1.3 %collective-permute-done.14.refs_15_ = bf16[512,128]{1,0:T(8,128)(2,1)S(1)} collective-permute-done((bf16[512,128]{1,0:T(8,128)(2,1)S(1)}, bf16[512,128]{1,0:T(8,128)(2,1)S(1)}, u32[]{:S(2)}, u32[]{:S(2)}) %collective-permute-start.14) | collective-permute-done | bytes 131104 | tf_op jit(solution)/shard_map/ppermute | solution.py:18
  24.2 1.5 %copy-done = bf16[60,128,128]{2,1,0:T(8,128)(2,1)S(1)} copy-done((bf16[60,128,128]{2,1,0:T(8,128)(2,1)S(1)}, bf16[60,128,128]{2,1,0:T(8,128)(2,1)}, u32[]{:S(2)}) %copy-start) | copy-done | bytes 1966104
  25.7 0.9 %copy-done.1 = bf16[512,256]{1,0:T(8,128)(2,1)S(1)} copy-done((bf16[512,256]{1,0:T(8,128)(2,1)S(1)}, bf16[512,256]{1,0:T(8,128)(2,1)}, u32[]{:S(2)}) %copy-start.1) | copy-done | bytes 262168
  26.7 0.9 %copy-done.2 = bf16[512,128]{1,0:T(8,128)(2,1)S(1)} copy-done((bf16[512,128]{1,0:T(8,128)(2,1)S(1)}, bf16[512,128]{1,0:T(8,128)(2,1)}, u32[]{:S(2)}) %copy-start.2) | copy-done | bytes 131096
  27.6 0.8 %copy-done.3 = bf16[128,256]{1,0:T(8,128)(2,1)S(1)} copy-done((bf16[128,256]{1,0:T(8,128)(2,1)S(1)}, bf16[128,256]{1,0:T(8,128)(2,1)}, u32[]{:S(2)}) %copy-start.3) | copy-done | bytes 65560
  28.4 0.8 %copy-done.4 = bf16[128,256]{1,0:T(8,128)(2,1)S(1)} copy-done((bf16[128,256]{1,0:T(8,128)(2,1)S(1)}, bf16[128,256]{1,0:T(8,128)(2,1)}, u32[]{:S(2)}) %copy-start.4) | copy-done | bytes 65560
  29.3 0.7 copy-done.5
  30.0 0.7 copy-done.6
  30.6 0.7 copy-done.7
  31.3 0.7 copy-done.8
  31.9 5.0 %forward_layer.1 = (bf16[512,256]{1,0:T(8,128)(2,1)}, f32[512,128]{1,0:T(8,128)S(1)}, f32[128,256]{1,0:T(8,128)S(1)}, f32[128,256]{1,0:T(8,128)S(1)}, bf16[4,256,128]{2,1,0:T(8,128)(2,1)S(1)}) custom-call(s32[1]{0:T(128)} %bitcast.me_ref, s32[60]{0:T(128)S(1)} %copy-done.7, s32[60]{0:T(128)S(1)} %copy-done.8, bf16[60,128,128]{2,1,0:T(8,128)(2,1)S(1)} %copy-done, ...), custom_call_target="tpu_custom_call" | custom-call | tf_op jit(solution)/shard_map/forward_layer/pallas_call | solution.py:190
  37.0 4.6 %backward_tiles.1 = (f32[4,512,128]{2,1,0:T(8,128)S(1)}, f32[4,512,128]{2,1,0:T(8,128)}, f32[4,512,128]{2,1,0:T(8,128)S(1)}, f32[4,512,128]{2,1,0:T(8,128)S(1)}) custom-call(s32[1]{0:T(128)} %bitcast.me_ref, s32[60]{0:T(128)S(1)} %copy-done.7, s32[60]{0:T(128)S(1)} %copy-done.8, bf16[60,128,128]{2,1,0:T(8,128)(2,1)S(1)} %copy-done, ...), custom_call_target="tpu_custom_call" | custom-call | tf_op jit(solution)/shard_map/backward_tiles/pallas_call | solution.py:190
  41.7 0.4 collective-permute-start.15
  42.0 0.1 collective-permute-start.24
  42.2 2.5 %collective-permute-done.24 = f32[128,256]{1,0:T(8,128)S(1)} collective-permute-done((f32[128,256]{1,0:T(8,128)S(1)}, f32[128,256]{1,0:T(8,128)S(1)}, u32[]{:S(2)}, u32[]{:S(2)}) %collective-permute-start.24) | collective-permute-done | bytes 131104 | tf_op jit(solution)/shard_map/ppermute | solution.py:18
  44.7 1.6 %collective-permute-start.25 = (f32[128,256]{1,0:T(8,128)S(1)}, f32[128,256]{1,0:T(8,128)S(1)}, u32[]{:S(2)}, u32[]{:S(2)}) collective-permute-start(f32[128,256]{1,0:T(8,128)S(1)} %add.17), channel_id=1, source_target_pairs={{0,2},{1,3},{2,0},{3,1},{4,6},{5,7},{6,4},{7,5},{8,10},{9,11},{10,... | collective-permute-start | bytes 393224 | tf_op jit(solution)/shard_map/ppermute | solution.py:18
  46.2 4.0 %collective-permute-done.25 = f32[128,256]{1,0:T(8,128)S(1)} collective-permute-done((f32[128,256]{1,0:T(8,128)S(1)}, f32[128,256]{1,0:T(8,128)S(1)}, u32[]{:S(2)}, u32[]{:S(2)}) %collective-permute-start.25) | collective-permute-done | bytes 131104 | tf_op jit(solution)/shard_map/ppermute | solution.py:18
  50.3 1.1 %collective-permute-start.26 = (f32[128,256]{1,0:T(8,128)S(1)}, f32[128,256]{1,0:T(8,128)S(1)}, u32[]{:S(2)}, u32[]{:S(2)}) collective-permute-start(f32[128,256]{1,0:T(8,128)S(1)} %add.18), channel_id=1, source_target_pairs={{0,4},{1,5},{2,6},{3,7},{4,0},{5,1},{6,2},{7,3},{8,12},{9,13},{10,... | collective-permute-start | bytes 393224 | tf_op jit(solution)/shard_map/ppermute | solution.py:18
  51.4 3.9 %collective-permute-done.26 = f32[128,256]{1,0:T(8,128)S(1)} collective-permute-done((f32[128,256]{1,0:T(8,128)S(1)}, f32[128,256]{1,0:T(8,128)S(1)}, u32[]{:S(2)}, u32[]{:S(2)}) %collective-permute-start.26) | collective-permute-done | bytes 131104 | tf_op jit(solution)/shard_map/ppermute | solution.py:18
  55.4 3.7 %collective-permute-start.27 = (f32[128,256]{1,0:T(8,128)S(1)}, f32[128,256]{1,0:T(8,128)S(1)}, u32[]{:S(2)}, u32[]{:S(2)}) collective-permute-start(f32[128,256]{1,0:T(8,128)S(1)} %add.19), channel_id=1, source_target_pairs={{0,8},{1,9},{2,10},{3,11},{4,12},{5,13},{6,14},{7,15},{8,0},{9,1},... | collective-permute-start | bytes 393224 | tf_op jit(solution)/shard_map/ppermute | solution.py:18
  59.0 0.2 pair_sum_y.1
  59.2 1.5 %collective-permute-start.18 = (bf16[512,128]{1,0:T(8,128)(2,1)S(1)}, bf16[512,128]{1,0:T(8,128)(2,1)S(1)}, u32[]{:S(2)}, u32[]{:S(2)}) collective-permute-start(bf16[512,128]{1,0:T(8,128)(2,1)S(1)} %get-tuple-element.31), channel_id=1, source_target_pairs={{0,2},{1,3},{2,0},{3,1},{4,6},{5,7},{6,4},{7,5},{8,10},{9,11},{10,... | collective-permute-start | bytes 393224 | tf_op jit(solution)/shard_map/ppermute | solution.py:18
  60.7 0.6 collective-permute-start.20
  61.3 1.4 %collective-permute-start.22 = (bf16[512,128]{1,0:T(8,128)(2,1)S(1)}, bf16[512,128]{1,0:T(8,128)(2,1)S(1)}, u32[]{:S(2)}, u32[]{:S(2)}) collective-permute-start(bf16[512,128]{1,0:T(8,128)(2,1)S(1)} %get-tuple-element.35), channel_id=1, source_target_pairs={{0,2},{1,3},{2,0},{3,1},{4,6},{5,7},{6,4},{7,5},{8,10},{9,11},{10,... | collective-permute-start | bytes 393224 | tf_op jit(solution)/shard_map/ppermute | solution.py:18
  62.7 0.5 collective-permute-done.27
  63.3 1.6 %collective-permute-start.17 = (bf16[512,128]{1,0:T(8,128)(2,1)S(1)}, bf16[512,128]{1,0:T(8,128)(2,1)S(1)}, u32[]{:S(2)}, u32[]{:S(2)}) collective-permute-start(bf16[512,128]{1,0:T(8,128)(2,1)S(1)} %get-tuple-element.29), channel_id=1, source_target_pairs={{0,2},{1,3},{2,0},{3,1},{4,6},{5,7},{6,4},{7,5},{8,10},{9,11},{10,... | collective-permute-start | bytes 393224 | tf_op jit(solution)/shard_map/ppermute | solution.py:18
  65.1 1.0 %collective-permute-start.19 = (bf16[512,128]{1,0:T(8,128)(2,1)S(1)}, bf16[512,128]{1,0:T(8,128)(2,1)S(1)}, u32[]{:S(2)}, u32[]{:S(2)}) collective-permute-start(bf16[512,128]{1,0:T(8,128)(2,1)S(1)} %line_sum.3), channel_id=1, source_target_pairs={{0,12},{1,13},{2,14},{3,15},{4,8},{5,9},{6,10},{7,11},{8,4},{9,5},... | collective-permute-start | bytes 393224 | tf_op jit(solution)/shard_map/ppermute | solution.py:18
  66.1 0.2 collective-permute-done.20.got_ref
  66.4 0.5 collective-permute-start.21
  66.9 2.1 %collective-permute-done.22.got_ref = bf16[512,128]{1,0:T(8,128)(2,1)S(1)} collective-permute-done((bf16[512,128]{1,0:T(8,128)(2,1)S(1)}, bf16[512,128]{1,0:T(8,128)(2,1)S(1)}, u32[]{:S(2)}, u32[]{:S(2)}) %collective-permute-start.22) | collective-permute-done | bytes 131104 | tf_op jit(solution)/shard_map/ppermute | solution.py:18
  69.1 0.7 collective-permute-start.23
  69.8 0.7 broadcast_select_fusion
  70.6 2.8 %collective-permute-done.19.refs_1_ = bf16[512,128]{1,0:T(8,128)(2,1)S(1)} collective-permute-done((bf16[512,128]{1,0:T(8,128)(2,1)S(1)}, bf16[512,128]{1,0:T(8,128)(2,1)S(1)}, u32[]{:S(2)}, u32[]{:S(2)}) %collective-permute-start.19) | collective-permute-done | bytes 131104 | tf_op jit(solution)/shard_map/ppermute | solution.py:18
  73.4 5.5 %collective-permute-done.21.refs_2_ = bf16[512,128]{1,0:T(8,128)(2,1)S(1)} collective-permute-done((bf16[512,128]{1,0:T(8,128)(2,1)S(1)}, bf16[512,128]{1,0:T(8,128)(2,1)S(1)}, u32[]{:S(2)}, u32[]{:S(2)}) %collective-permute-start.21) | collective-permute-done | bytes 131104 | tf_op jit(solution)/shard_map/ppermute | solution.py:18
  79.0 0.8 %grad_input_sum.1 = bf16[512,128]{1,0:T(8,128)(2,1)} custom-call(f32[512,128]{1,0:T(8,128)S(1)} %get-tuple-element.22.base_ref, f32[512,128]{1,0:T(8,128)S(1)} %get-tuple-element.26.own_ref, bf16[512,128]{1,0:T(8,128)(2,1)S(1)} %collective-permute-done.17.refs_0_, bf16[512,128]{1,0:T(8,128)(2,1)S(1)} %collective-permute-done.19.refs_1_, ...), custom_call_target="tpu_custom_call" | custom-call | tf_op jit(solution)/shard_map/grad_input_sum/pallas_call | solution.py:190
  (41 shorter events, 0.7 us)
Async XLA Ops:
  0.6 10.7 %collective-permute-start.7 = (bf16[512,128]{1,0:T(8,128)(2,1)}, bf16[512,128]{1,0:T(8,128)(2,1)S(1)}, u32[]{:S(2)}, u32[]{:S(2)}) collective-permute-start(bf16[512,128]{1,0:T(8,128)(2,1)} %refs_0_.1), channel_id=1, source_target_pairs={{0,8},{1,9},{2,10},{3,11},{4,12},{5,13},{6,14},{7,15},{8,0},{9,1},... | collective-permute-start | bytes 393224 | tf_op jit(solution)/shard_map/ppermute | solution.py:18
  4.7 7.3 %collective-permute-start.3 = (bf16[512,128]{1,0:T(8,128)(2,1)}, bf16[512,128]{1,0:T(8,128)(2,1)S(1)}, u32[]{:S(2)}, u32[]{:S(2)}) collective-permute-start(bf16[512,128]{1,0:T(8,128)(2,1)} %refs_0_.1), channel_id=1, source_target_pairs={{0,4},{1,5},{2,6},{3,7},{4,0},{5,1},{6,2},{7,3},{8,12},{9,13},{10,... | collective-permute-start | bytes 393224 | tf_op jit(solution)/shard_map/ppermute | solution.py:18
  6.3 7.3 %collective-permute-start.1 = (bf16[512,128]{1,0:T(8,128)(2,1)}, bf16[512,128]{1,0:T(8,128)(2,1)S(1)}, u32[]{:S(2)}, u32[]{:S(2)}) collective-permute-start(bf16[512,128]{1,0:T(8,128)(2,1)} %refs_0_.1), channel_id=1, source_target_pairs={{0,2},{1,3},{2,0},{3,1},{4,6},{5,7},{6,4},{7,5},{8,10},{9,11},{10,... | collective-permute-start | bytes 393224 | tf_op jit(solution)/shard_map/ppermute | solution.py:18
  7.8 6.3 %collective-permute-start = (bf16[512,128]{1,0:T(8,128)(2,1)}, bf16[512,128]{1,0:T(8,128)(2,1)S(1)}, u32[]{:S(2)}, u32[]{:S(2)}) collective-permute-start(bf16[512,128]{1,0:T(8,128)(2,1)} %refs_0_.1), channel_id=1, source_target_pairs={{0,1},{1,0},{2,3},{3,2},{4,5},{5,4},{6,7},{7,6},{8,9},{9,8},{10,11... | collective-permute-start | bytes 393224 | tf_op jit(solution)/shard_map/ppermute | solution.py:18
  11.4 5.0 %collective-permute-start.11 = (bf16[512,128]{1,0:T(8,128)(2,1)S(1)}, bf16[512,128]{1,0:T(8,128)(2,1)S(1)}, u32[]{:S(2)}, u32[]{:S(2)}) collective-permute-start(bf16[512,128]{1,0:T(8,128)(2,1)S(1)} %collective-permute-done.7.refs_8_), channel_id=1, source_target_pairs={{0,4},{1,5},{2,6},{3,7},{4,0},{5,1},{6,2},{7,3},{8,12},{9,13},{10,... | collective-permute-start | bytes 393224 | tf_op jit(solution)/shard_map/ppermute | solution.py:18
  12.1 5.8 %collective-permute-start.5 = (bf16[512,128]{1,0:T(8,128)(2,1)S(1)}, bf16[512,128]{1,0:T(8,128)(2,1)S(1)}, u32[]{:S(2)}, u32[]{:S(2)}) collective-permute-start(bf16[512,128]{1,0:T(8,128)(2,1)S(1)} %collective-permute-done.3.refs_4_), channel_id=1, source_target_pairs={{0,2},{1,3},{2,0},{3,1},{4,6},{5,7},{6,4},{7,5},{8,10},{9,11},{10,... | collective-permute-start | bytes 393224 | tf_op jit(solution)/shard_map/ppermute | solution.py:18
  13.6 4.3 %collective-permute-start.4 = (bf16[512,128]{1,0:T(8,128)(2,1)S(1)}, bf16[512,128]{1,0:T(8,128)(2,1)S(1)}, u32[]{:S(2)}, u32[]{:S(2)}) collective-permute-start(bf16[512,128]{1,0:T(8,128)(2,1)S(1)} %collective-permute-done.3.refs_4_), channel_id=1, source_target_pairs={{0,1},{1,0},{2,3},{3,2},{4,5},{5,4},{6,7},{7,6},{8,9},{9,8},{10,11... | collective-permute-start | bytes 393224 | tf_op jit(solution)/shard_map/ppermute | solution.py:18
  13.6 4.8 %collective-permute-start.2 = (bf16[512,128]{1,0:T(8,128)(2,1)S(1)}, bf16[512,128]{1,0:T(8,128)(2,1)S(1)}, u32[]{:S(2)}, u32[]{:S(2)}) collective-permute-start(bf16[512,128]{1,0:T(8,128)(2,1)S(1)} %collective-permute-done.1.refs_2_), channel_id=1, source_target_pairs={{0,1},{1,0},{2,3},{3,2},{4,5},{5,4},{6,7},{7,6},{8,9},{9,8},{10,11... | collective-permute-start | bytes 393224 | tf_op jit(solution)/shard_map/ppermute | solution.py:18
  14.1 6.4 %collective-permute-start.9 = (bf16[512,128]{1,0:T(8,128)(2,1)S(1)}, bf16[512,128]{1,0:T(8,128)(2,1)S(1)}, u32[]{:S(2)}, u32[]{:S(2)}) collective-permute-start(bf16[512,128]{1,0:T(8,128)(2,1)S(1)} %collective-permute-done.7.refs_8_), channel_id=1, source_target_pairs={{0,2},{1,3},{2,0},{3,1},{4,6},{5,7},{6,4},{7,5},{8,10},{9,11},{10,... | collective-permute-start | bytes 393224 | tf_op jit(solution)/shard_map/ppermute | solution.py:18
  16.3 6.5 %collective-permute-start.13 = (bf16[512,128]{1,0:T(8,128)(2,1)S(1)}, bf16[512,128]{1,0:T(8,128)(2,1)S(1)}, u32[]{:S(2)}, u32[]{:S(2)}) collective-permute-start(bf16[512,128]{1,0:T(8,128)(2,1)S(1)} %collective-permute-done.11.refs_12_), channel_id=1, source_target_pairs={{0,2},{1,3},{2,0},{3,1},{4,6},{5,7},{6,4},{7,5},{8,10},{9,11},{10,... | collective-permute-start | bytes 393224 | tf_op jit(solution)/shard_map/ppermute | solution.py:18
  17.9 4.9 %collective-permute-start.8 = (bf16[512,128]{1,0:T(8,128)(2,1)S(1)}, bf16[512,128]{1,0:T(8,128)(2,1)S(1)}, u32[]{:S(2)}, u32[]{:S(2)}) collective-permute-start(bf16[512,128]{1,0:T(8,128)(2,1)S(1)} %collective-permute-done.7.refs_8_), channel_id=1, source_target_pairs={{0,1},{1,0},{2,3},{3,2},{4,5},{5,4},{6,7},{7,6},{8,9},{9,8},{10,11... | collective-permute-start | bytes 393224 | tf_op jit(solution)/shard_map/ppermute | solution.py:18
  17.9 4.9 %collective-permute-start.12 = (bf16[512,128]{1,0:T(8,128)(2,1)S(1)}, bf16[512,128]{1,0:T(8,128)(2,1)S(1)}, u32[]{:S(2)}, u32[]{:S(2)}) collective-permute-start(bf16[512,128]{1,0:T(8,128)(2,1)S(1)} %collective-permute-done.11.refs_12_), channel_id=1, source_target_pairs={{0,1},{1,0},{2,3},{3,2},{4,5},{5,4},{6,7},{7,6},{8,9},{9,8},{10,11... | collective-permute-start | bytes 393224 | tf_op jit(solution)/shard_map/ppermute | solution.py:18
  18.4 4.4 %collective-permute-start.6 = (bf16[512,128]{1,0:T(8,128)(2,1)S(1)}, bf16[512,128]{1,0:T(8,128)(2,1)S(1)}, u32[]{:S(2)}, u32[]{:S(2)}) collective-permute-start(bf16[512,128]{1,0:T(8,128)(2,1)S(1)} %collective-permute-done.5.refs_6_), channel_id=1, source_target_pairs={{0,1},{1,0},{2,3},{3,2},{4,5},{5,4},{6,7},{7,6},{8,9},{9,8},{10,11... | collective-permute-start | bytes 393224 | tf_op jit(solution)/shard_map/ppermute | solution.py:18
  20.5 2.4 %collective-permute-start.10 = (bf16[512,128]{1,0:T(8,128)(2,1)S(1)}, bf16[512,128]{1,0:T(8,128)(2,1)S(1)}, u32[]{:S(2)}, u32[]{:S(2)}) collective-permute-start(bf16[512,128]{1,0:T(8,128)(2,1)S(1)} %collective-permute-done.9.refs_10_), channel_id=1, source_target_pairs={{0,1},{1,0},{2,3},{3,2},{4,5},{5,4},{6,7},{7,6},{8,9},{9,8},{10,11... | collective-permute-start | bytes 393224 | tf_op jit(solution)/shard_map/ppermute | solution.py:18
  22.8 1.3 %collective-permute-start.14 = (bf16[512,128]{1,0:T(8,128)(2,1)S(1)}, bf16[512,128]{1,0:T(8,128)(2,1)S(1)}, u32[]{:S(2)}, u32[]{:S(2)}) collective-permute-start(bf16[512,128]{1,0:T(8,128)(2,1)S(1)} %collective-permute-done.13.refs_14_), channel_id=1, source_target_pairs={{0,1},{1,0},{2,3},{3,2},{4,5},{5,4},{6,7},{7,6},{8,9},{9,8},{10,11... | collective-permute-start | bytes 393224 | tf_op jit(solution)/shard_map/ppermute | solution.py:18
  24.2 1.5 %copy-start = (bf16[60,128,128]{2,1,0:T(8,128)(2,1)S(1)}, bf16[60,128,128]{2,1,0:T(8,128)(2,1)}, u32[]{:S(2)}) copy-start(bf16[60,128,128]{2,1,0:T(8,128)(2,1)} %tiles_ref.3) | copy-start | bytes 5898244
  25.7 0.9 %copy-start.1 = (bf16[512,256]{1,0:T(8,128)(2,1)S(1)}, bf16[512,256]{1,0:T(8,128)(2,1)}, u32[]{:S(2)}) copy-start(bf16[512,256]{1,0:T(8,128)(2,1)} %cot_ref.1) | copy-start | bytes 786436
  26.7 0.9 %copy-start.2 = (bf16[512,128]{1,0:T(8,128)(2,1)S(1)}, bf16[512,128]{1,0:T(8,128)(2,1)}, u32[]{:S(2)}) copy-start(bf16[512,128]{1,0:T(8,128)(2,1)} %refs_0_.1) | copy-start | bytes 393220
  27.6 0.8 %copy-start.3 = (bf16[128,256]{1,0:T(8,128)(2,1)S(1)}, bf16[128,256]{1,0:T(8,128)(2,1)}, u32[]{:S(2)}) copy-start(bf16[128,256]{1,0:T(8,128)(2,1)} %ws_ref.1) | copy-start | bytes 196612
  28.4 0.8 %copy-start.4 = (bf16[128,256]{1,0:T(8,128)(2,1)S(1)}, bf16[128,256]{1,0:T(8,128)(2,1)}, u32[]{:S(2)}) copy-start(bf16[128,256]{1,0:T(8,128)(2,1)} %wn_ref.1) | copy-start | bytes 196612
  29.3 0.7 copy-start.5
  30.0 0.7 copy-start.6
  30.6 0.7 copy-start.7
  31.3 0.7 copy-start.8
  41.5 17.5 %collective-permute-start.16 = (f32[4,512,128]{2,1,0:T(8,128)S(1)}, f32[4,512,128]{2,1,0:T(8,128)S(1)}, u32[]{:S(2)}, u32[]{:S(2)}) collective-permute-start(f32[4,512,128]{2,1,0:T(8,128)S(1)} %get-tuple-element.28), channel_id=1, source_target_pairs={{0,1},{1,0},{2,3},{3,2},{4,5},{5,4},{6,7},{7,6},{8,9},{9,8},{10,11... | collective-permute-start | bytes 3145736 | tf_op jit(solution)/shard_map/ppermute | solution.py:18
  41.7 21.7 %collective-permute-start.15 = (f32[4,512,128]{2,1,0:T(8,128)}, f32[4,512,128]{2,1,0:T(8,128)S(1)}, u32[]{:S(2)}, u32[]{:S(2)}) collective-permute-start(f32[4,512,128]{2,1,0:T(8,128)} %get-tuple-element.25), channel_id=1, source_target_pairs={{0,1},{1,0},{2,3},{3,2},{4,5},{5,4},{6,7},{7,6},{8,9},{9,8},{10,11... | collective-permute-start | bytes 3145736 | tf_op jit(solution)/shard_map/ppermute | solution.py:18
  42.0 2.6 %collective-permute-start.24 = (f32[128,256]{1,0:T(8,128)S(1)}, f32[128,256]{1,0:T(8,128)S(1)}, u32[]{:S(2)}, u32[]{:S(2)}) collective-permute-start(f32[128,256]{1,0:T(8,128)S(1)} %get-tuple-element.37), channel_id=1, source_target_pairs={{0,1},{1,0},{2,3},{3,2},{4,5},{5,4},{6,7},{7,6},{8,9},{9,8},{10,11... | collective-permute-start | bytes 393224 | tf_op jit(solution)/shard_map/ppermute | solution.py:18
  44.7 5.6 %collective-permute-start.25 = (f32[128,256]{1,0:T(8,128)S(1)}, f32[128,256]{1,0:T(8,128)S(1)}, u32[]{:S(2)}, u32[]{:S(2)}) collective-permute-start(f32[128,256]{1,0:T(8,128)S(1)} %add.17), channel_id=1, source_target_pairs={{0,2},{1,3},{2,0},{3,1},{4,6},{5,7},{6,4},{7,5},{8,10},{9,11},{10,... | collective-permute-start | bytes 393224 | tf_op jit(solution)/shard_map/ppermute | solution.py:18
  50.3 5.0 %collective-permute-start.26 = (f32[128,256]{1,0:T(8,128)S(1)}, f32[128,256]{1,0:T(8,128)S(1)}, u32[]{:S(2)}, u32[]{:S(2)}) collective-permute-start(f32[128,256]{1,0:T(8,128)S(1)} %add.18), channel_id=1, source_target_pairs={{0,4},{1,5},{2,6},{3,7},{4,0},{5,1},{6,2},{7,3},{8,12},{9,13},{10,... | collective-permute-start | bytes 393224 | tf_op jit(solution)/shard_map/ppermute | solution.py:18
  55.4 7.9 %collective-permute-start.27 = (f32[128,256]{1,0:T(8,128)S(1)}, f32[128,256]{1,0:T(8,128)S(1)}, u32[]{:S(2)}, u32[]{:S(2)}) collective-permute-start(f32[128,256]{1,0:T(8,128)S(1)} %add.19), channel_id=1, source_target_pairs={{0,8},{1,9},{2,10},{3,11},{4,12},{5,13},{6,14},{7,15},{8,0},{9,1},... | collective-permute-start | bytes 393224 | tf_op jit(solution)/shard_map/ppermute | solution.py:18
  59.2 5.8 %collective-permute-start.18 = (bf16[512,128]{1,0:T(8,128)(2,1)S(1)}, bf16[512,128]{1,0:T(8,128)(2,1)S(1)}, u32[]{:S(2)}, u32[]{:S(2)}) collective-permute-start(bf16[512,128]{1,0:T(8,128)(2,1)S(1)} %get-tuple-element.31), channel_id=1, source_target_pairs={{0,2},{1,3},{2,0},{3,1},{4,6},{5,7},{6,4},{7,5},{8,10},{9,11},{10,... | collective-permute-start | bytes 393224 | tf_op jit(solution)/shard_map/ppermute | solution.py:18
  60.7 5.7 %collective-permute-start.20 = (bf16[512,128]{1,0:T(8,128)(2,1)S(1)}, bf16[512,128]{1,0:T(8,128)(2,1)S(1)}, u32[]{:S(2)}, u32[]{:S(2)}) collective-permute-start(bf16[512,128]{1,0:T(8,128)(2,1)S(1)} %get-tuple-element.33), channel_id=1, source_target_pairs={{0,2},{1,3},{2,0},{3,1},{4,6},{5,7},{6,4},{7,5},{8,10},{9,11},{10,... | collective-permute-start | bytes 393224 | tf_op jit(solution)/shard_map/ppermute | solution.py:18
  61.3 7.7 %collective-permute-start.22 = (bf16[512,128]{1,0:T(8,128)(2,1)S(1)}, bf16[512,128]{1,0:T(8,128)(2,1)S(1)}, u32[]{:S(2)}, u32[]{:S(2)}) collective-permute-start(bf16[512,128]{1,0:T(8,128)(2,1)S(1)} %get-tuple-element.35), channel_id=1, source_target_pairs={{0,2},{1,3},{2,0},{3,1},{4,6},{5,7},{6,4},{7,5},{8,10},{9,11},{10,... | collective-permute-start | bytes 393224 | tf_op jit(solution)/shard_map/ppermute | solution.py:18
  63.2 6.5 %collective-permute-start.28 = (f32[128,256]{1,0:T(8,128)S(1)}, f32[128,256]{1,0:T(8,128)S(1)}, u32[]{:S(2)}, u32[]{:S(2)}) collective-permute-start(f32[128,256]{1,0:T(8,128)S(1)} %add.20), channel_id=1, source_target_pairs={{0,1},{1,0},{2,3},{3,2},{4,5},{5,4},{6,7},{7,6},{8,9},{9,8},{10,11... | collective-permute-start | bytes 393224 | tf_op jit(solution)/shard_map/ppermute | solution.py:18
  63.3 7.2 %collective-permute-start.17 = (bf16[512,128]{1,0:T(8,128)(2,1)S(1)}, bf16[512,128]{1,0:T(8,128)(2,1)S(1)}, u32[]{:S(2)}, u32[]{:S(2)}) collective-permute-start(bf16[512,128]{1,0:T(8,128)(2,1)S(1)} %get-tuple-element.29), channel_id=1, source_target_pairs={{0,2},{1,3},{2,0},{3,1},{4,6},{5,7},{6,4},{7,5},{8,10},{9,11},{10,... | collective-permute-start | bytes 393224 | tf_op jit(solution)/shard_map/ppermute | solution.py:18
  65.1 8.3 %collective-permute-start.19 = (bf16[512,128]{1,0:T(8,128)(2,1)S(1)}, bf16[512,128]{1,0:T(8,128)(2,1)S(1)}, u32[]{:S(2)}, u32[]{:S(2)}) collective-permute-start(bf16[512,128]{1,0:T(8,128)(2,1)S(1)} %line_sum.3), channel_id=1, source_target_pairs={{0,12},{1,13},{2,14},{3,15},{4,8},{5,9},{6,10},{7,11},{8,4},{9,5},... | collective-permute-start | bytes 393224 | tf_op jit(solution)/shard_map/ppermute | solution.py:18
  66.4 12.6 %collective-permute-start.21 = (bf16[512,128]{1,0:T(8,128)(2,1)S(1)}, bf16[512,128]{1,0:T(8,128)(2,1)S(1)}, u32[]{:S(2)}, u32[]{:S(2)}) collective-permute-start(bf16[512,128]{1,0:T(8,128)(2,1)S(1)} %line_sum.4), channel_id=1, source_target_pairs={{0,8},{1,9},{2,10},{3,11},{4,12},{5,13},{6,14},{7,15},{8,0},{9,1},... | collective-permute-start | bytes 393224 | tf_op jit(solution)/shard_map/ppermute | solution.py:18
  69.1 9.9 %collective-permute-start.23 = (bf16[512,128]{1,0:T(8,128)(2,1)S(1)}, bf16[512,128]{1,0:T(8,128)(2,1)S(1)}, u32[]{:S(2)}, u32[]{:S(2)}) collective-permute-start(bf16[512,128]{1,0:T(8,128)(2,1)S(1)} %line_sum.5), channel_id=1, source_target_pairs={{0,4},{1,5},{2,6},{3,7},{4,0},{5,1},{6,2},{7,3},{8,12},{9,13},{10,... | collective-permute-start | bytes 393224 | tf_op jit(solution)/shard_map/ppermute | solution.py:18

commit v3 on v2

v3 whole, which is shorter than its diff:
```python
import functools

import jax
import jax.numpy as jnp
from jax import lax
from jax.experimental import pallas as pl
from jax.experimental.pallas import tpu as pltpu
from jax.sharding import PartitionSpec as P

BLOCK = 128
F32, BF16 = jnp.float32, jnp.bfloat16
VMEM = pl.BlockSpec(memory_space=pltpu.VMEM)
SMEM = pl.BlockSpec(memory_space=pltpu.SMEM)
ANY = pl.BlockSpec(memory_space=pl.ANY)
MIB = 1024 * 1024
LAST = ((1,), (1,))


def swap(x, n, offset):
    return lax.ppermute(x, "row", [(i, i ^ offset) for i in range(n)])


def gather_by_xor(x, n, call, pack):
    blocks = [x]
    bit = n // 2
    while bit >= 8:
        blocks = blocks + [swap(v, n, bit) for v in blocks]
        bit //= 2
    offsets = [0]
    bit = n // 2
    while bit >= 8:
        offsets = offsets + [o ^ bit for o in offsets]
        bit //= 2
    blocks = [v for _, v in sorted(zip(offsets, blocks), key=lambda pair: pair[0])]
    same = []
    for v in blocks:
        square = (v, *[swap(v, n, offset) for offset in (2, 4, 6)])
        same.append(call(pack_kernel, "pack_square", pack, square))
    return same, [swap(v, n, 1) for v in same]


def split_bf16(x):
    high = x.astype(BF16)
    return high, (x - high.astype(F32)).astype(BF16)


def dot(a, b, dims=((1,), (0,))):
    return lax.dot_general(a, b, (dims, ((), ())), preferred_element_type=F32)


def dot_wide(a, b, dims=((1,), (0,))):
    high, low = split_bf16(a)
    return dot(high, b, dims) + dot(low, b, dims)


def rows_to_lanes(row):
    return jnp.transpose(jnp.broadcast_to(row, (BLOCK, BLOCK)))


def rows_of(b):
    return pl.ds(b * BLOCK, BLOCK)


def pack_kernel(*refs):
    for i, ref in enumerate(refs[:-1]):
        refs[-1][i] = ref[...]


def stage_kernel(me_ref, trow_ref, tcol_ref, deg_ref, mask_ref, ws_ref, wn_ref, feat_ref, cot_ref,
                 tiles_ref, tiles_out, ws_out, wn_out, deg_out, up_out, pre_out, featt_out,
                 index_out, sem):
    copy = pltpu.make_async_copy(tiles_ref, tiles_out, sem)
    copy.start()
    block_local = feat_ref.shape[0] // BLOCK
    tile_count = trow_ref.shape[0]
    me = me_ref[0]
    index_out[2 * tile_count] = me

    def place(t, carry):
        col = tcol_ref[t]
        live = col >= 0
        col = jnp.maximum(col, 0)
        position = ((col // block_local) ^ me) * block_local + col % block_local
        row = jnp.clip(trow_ref[t] - me * block_local, 0, block_local - 1)
        index_out[t] = jnp.where(live, row, block_local)
        index_out[tile_count + t] = position
        return carry

    lax.fori_loop(0, tile_count, place, 0)
    ws_out[...] = ws_ref[...]
    wn_out[...] = wn_ref[...]
    ws = ws_ref[...]
    for b in range(block_local):
        degree = rows_to_lanes(deg_ref[pl.ds(b, 1), :].astype(F32))
        mask = rows_to_lanes(mask_ref[pl.ds(b, 1), :].astype(F32))
        deg_out[b] = degree
        feat = feat_ref[rows_of(b), :]
        featt_out[b] = jnp.transpose(feat.astype(F32)).astype(BF16)
        pre_out[rows_of(b), :] = dot(feat, ws)
        up_out[rows_of(b), :] = cot_ref[rows_of(b), :].astype(F32) * jnp.concatenate(
            [mask, mask], axis=1)
    copy.wait()


def forward_kernel(n, group, index_ref, tiles_ref, ws_ref, wn_ref, deg_ref, up_ref, pre_ref,
                   featt_ref, *refs):
    squares = n // 8
    feat_refs, refs = refs[:2 * squares], refs[2 * squares:]
    emb_ref, base_ref, wkeep_ref, wsend_ref, gt_ref, feats, raw, wsum = refs
    block_local = deg_ref.shape[0]
    tile_count = tiles_ref.shape[0]

    raw[...] = jnp.zeros_like(raw)
    for s in range(squares):
        for q in range(4):
            for core in range(2):
                for b in range(block_local):
                    spot = (8 * s + 2 * q + core) * block_local + b
                    feats[spot] = feat_refs[core * squares + s][q, rows_of(b), :]

    def forward(step, carry):
        rows, products = [], []
        for u in range(group):
            t = step * group + u
            rows.append(index_ref[t])
            products.append(dot(tiles_ref[t], feats[index_ref[tile_count + t]]))
        for row, product in zip(rows, products):
            raw[row] += product
        return carry

    lax.fori_loop(0, tile_count // group, forward, 0)

    wn = wn_ref[...]
    ws = ws_ref[...]
    for b in range(block_local):
        degree = deg_ref[b]
        raw_b = raw[b]
        pre = pre_ref[rows_of(b), :] + dot_wide(raw_b / degree, wn)
        sig = jax.nn.sigmoid(pre)
        emb_ref[rows_of(b), :] = (pre * sig).astype(BF16)
        grad_pre = up_ref[rows_of(b), :] * sig * (1.0 + pre * (1.0 - sig))
        scaled = (grad_pre / jnp.concatenate([degree, degree], axis=1)).astype(BF16)
        gp_high, gp_low = split_bf16(grad_pre)
        feat_t = featt_ref[b]
        grad_self = dot(feat_t, gp_high) + dot(feat_t, gp_low)
        grad_neigh = dot_wide(jnp.transpose(raw_b), scaled)
        if b == 0:
            wsum[0], wsum[1] = grad_self, grad_neigh
        else:
            wsum[0] += grad_self
            wsum[1] += grad_neigh
        base_ref[rows_of(b), :] = dot(gp_high, ws, LAST) + dot(gp_low, ws, LAST)
        high, low = split_bf16(dot(wn, scaled, LAST))
        gt_ref[b, :BLOCK, :] = high
        gt_ref[b, BLOCK:, :] = low

    core = index_ref[2 * tile_count] % 2
    wkeep_ref[...] = wsum[core]
    wsend_ref[...] = wsum[1 - core]


def add_tiles(first, last, group, index_ref, tiles_ref, gt_ref, acc):
    block_local = gt_ref.shape[0]
    tile_count = tiles_ref.shape[0]
    dump = acc.shape[0] - 1

    def backward(step, carry):
        places, products = [], []
        for u in range(group):
            t = first + step * group + u
            row = index_ref[t]
            places.append(jnp.where(row < block_local, index_ref[tile_count + t], dump))
            both = dot(gt_ref[jnp.minimum(row, block_local - 1)], tiles_ref[t])
            products.append(both[:BLOCK] + both[BLOCK:])
        for position, product in zip(places, products):
            acc[position] += product
        return carry

    lax.fori_loop(0, (last - first) // group, backward, 0)


def backward_first_kernel(last, group, index_ref, tiles_ref, gt_ref, acc_ref):
    acc_ref[...] = jnp.zeros_like(acc_ref)
    add_tiles(0, last, group, index_ref, tiles_ref, gt_ref, acc_ref)


def backward_second_kernel(n, first, group, index_ref, tiles_ref, gt_ref, wkeep_ref, wgot_ref,
                           before_ref, *refs):
    far_send, near_send, far_keep, near_keep, w0, w1, w2, w3, acc = refs
    block_local = gt_ref.shape[0]
    tile_count = tiles_ref.shape[0]
    rows = w0.shape[0]
    chip = index_ref[2 * tile_count] // 2 % 4
    for p, ref in enumerate((w0, w1, w2, w3)):
        span = pl.ds(pl.multiple_of((chip ^ p) * rows, rows), rows)
        ref[...] = wkeep_ref[span, :] + wgot_ref[span, :]
    acc[...] = jnp.zeros_like(acc)
    add_tiles(first, tile_count, group, index_ref, tiles_ref, gt_ref, acc)
    for k in range(n):
        square, q = k // 8, k // 2 % 4
        near, far = (near_send, far_send) if k % 2 else (near_keep, far_keep)
        for b in range(block_local):
            spot = k * block_local + b
            total = acc[spot] + before_ref[spot]
            if square:
                far[square - 1, q, rows_of(b), :] = total
            else:
                near[0, q, rows_of(b), :] = total


def pair_kernel(squares, keep_ref, got_ref, *refs):
    for s in range(squares):
        refs[4 * s][...] = keep_ref[s, 0] + got_ref[s, 0]
        for q in range(1, 4):
            refs[4 * s + q][...] = (keep_ref[s, q] + got_ref[s, q]).astype(BF16)


def pair_far_kernel(squares, w0, w1, w2, w3, *refs):
    refs[-1][...] = (w0[...] + w1[...]) + (w2[...] + w3[...])
    pair_kernel(squares, *refs[:-1])


def add_kernel(own_ref, *refs):
    total = own_ref[...]
    for got_ref in refs[:-1]:
        total = total + got_ref[...].astype(F32)
    refs[-1][...] = total.astype(BF16)


def add_both_kernel(weight_ref, wgot_ref, own_ref, *refs):
    refs[-1][...] = weight_ref[...] + wgot_ref[...]
    add_kernel(own_ref, *refs[:-1])


def last_kernel(index_ref, weight_ref, other_ref, base_ref, own_ref, *refs):
    got_refs, (out_ref, self_ref, neigh_ref) = refs[:-3], refs[-3:]
    for b in range(base_ref.shape[0] // BLOCK):
        total = own_ref[rows_of(b), :]
        for got_ref in got_refs:
            total = total + got_ref[rows_of(b), :].astype(F32)
        out_ref[rows_of(b), :] = (base_ref[rows_of(b), :] + jnp.transpose(total)).astype(BF16)
    me = index_ref[index_ref.shape[0] - 1]
    first = me % 2 == 0
    chip = me // 2 % 4
    rows = weight_ref.shape[1]
    for p in range(4):
        span = pl.ds(pl.multiple_of((chip ^ p) * rows, rows), rows)
        mine, other = weight_ref[p], other_ref[p]
        self_ref[span, :] = jnp.where(first, mine, other)
        neigh_ref[span, :] = jnp.where(first, other, mine)


def body(features, tiles, tile_row, tile_col, degree, train_mask, w_self, w_neigh, cotangent):
    n = lax.axis_size("row")
    me = lax.axis_index("row").astype(jnp.int32).reshape(1)
    squares = n // 8
    nodes, feat_in = features.shape
    hidden = w_self.shape[1]
    block_local = nodes // BLOCK
    tile_count = tiles.shape[0]
    half = tile_count // 2
    group = max(g for g in range(1, 7) if half % g == 0)
    small = n * nodes * feat_in * 4 <= 4 * MIB
    limit = (24 if small else 56) * MIB

    def result(shape, dtype, stays=True):
        kind = pltpu.VMEM if small and stays else jax.ShapeDtypeStruct
        return kind(shape, dtype)

    def placed(x, spec):
        if spec is SMEM or not small:
            return x
        return pltpu.with_memory_space_constraint(x, pltpu.HBM if spec is ANY else pltpu.VMEM)

    def call(kernel, name, out_shape, operands, in_specs=None, out_specs=None, cost_us=0.2, **more):
        specs = in_specs or [VMEM] * len(operands)
        return pl.pallas_call(
            kernel,
            out_shape=out_shape,
            in_specs=specs,
            out_specs=out_specs or jax.tree.map(lambda _: VMEM, out_shape),
            compiler_params=pltpu.CompilerParams(vmem_limit_bytes=limit),
            cost_estimate=pl.CostEstimate(
                flops=0, bytes_accessed=int(cost_us * 3.6e6), transcendentals=0),
            name=name,
            **more,
        )(*[placed(x, spec) for x, spec in zip(operands, specs)])

    wide, piece = result((nodes, feat_in), F32), result((nodes, feat_in), BF16)
    weight = result((feat_in, hidden), F32)
    chunk = result((feat_in // 4, hidden), F32)
    by_block = (block_local, BLOCK, feat_in)

    own_arguments = (
        degree.reshape(block_local, BLOCK), train_mask.reshape(block_local, BLOCK),
        w_self, w_neigh, features, cotangent,
    )
    if small:
        own_arguments = [pltpu.with_memory_space_constraint(x, pltpu.HBM) for x in own_arguments]
    tiles_near, ws, wn, degree_wide, upstream, pre_self, feat_t, index = pl.pallas_call(
        stage_kernel,
        out_shape=(
            result(tiles.shape, BF16),
            result(w_self.shape, BF16),
            result(w_neigh.shape, BF16),
            result(by_block, F32),
            result((nodes, hidden), F32),
            result((nodes, hidden), F32),
            result(by_block, BF16),
            jax.ShapeDtypeStruct((2 * tile_count + 1,), jnp.int32),
        ),
        in_specs=[SMEM] * 3 + [VMEM] * 6 + [ANY],
        out_specs=(VMEM,) * 7 + (SMEM,),
        scratch_shapes=[pltpu.SemaphoreType.DMA],
        compiler_params=pltpu.CompilerParams(vmem_limit_bytes=limit),
        cost_estimate=pl.CostEstimate(flops=0, bytes_accessed=int(3 * 3.6e6), transcendentals=0),
        name="stage_arguments",
    )(me, tile_row, tile_col, *own_arguments, placed(tiles, ANY))

    same, other = gather_by_xor(features, n, call, result((4, nodes, feat_in), BF16))
    operands = (index, tiles_near, ws, wn, degree_wide, upstream, pre_self, feat_t, *same, *other)
    embedded, base, wkeep, wsend, gt = call(
        functools.partial(forward_kernel, n, group),
        "forward_layer",
        (
            result((nodes, hidden), BF16, False), wide, weight, weight,
            result((block_local, 2 * feat_in, BLOCK), BF16),
        ),
        operands,
        [SMEM] + [VMEM] * (len(operands) - 1),
        cost_us=5,
        scratch_shapes=[
            pltpu.VMEM((n * block_local, BLOCK, feat_in), BF16),
            pltpu.VMEM((block_local + 1, BLOCK, feat_in), F32),
            pltpu.VMEM((2, feat_in, hidden), F32),
        ],
    )

    wgot = swap(wsend, n, 1)
    acc_shape = (n * block_local + 1, feat_in, BLOCK)
    acc = call(
        functools.partial(backward_first_kernel, half, group),
        "backward_first", result(acc_shape, F32), (index, tiles_near, gt), [SMEM, VMEM, VMEM],
        cost_us=2.5,
    )
    far = result((max(squares - 1, 1), 4, nodes, feat_in), F32)
    near = result((1, 4, nodes, feat_in), F32)
    far_send, near_send, far_keep, near_keep, *w = call(
        functools.partial(backward_second_kernel, n, half, group),
        "backward_second", (far, near, far, near) + (chunk,) * 4,
        (index, tiles_near, gt, wkeep, wgot, acc), [SMEM] + [VMEM] * 5, cost_us=2.5,
        scratch_shapes=[pltpu.VMEM(acc_shape, F32)],
    )

    count = squares - 1
    *far_sums, wsum = call(
        functools.partial(pair_far_kernel, count), "pair_sum_far",
        (wide, piece, piece, piece) * count + (chunk,),
        (w[0], *[swap(w[p], n, 2 * p) for p in (1, 2, 3)], far_keep, swap(far_send, n, 1)),
    )
    near_sums = call(
        functools.partial(pair_kernel, 1), "pair_sum_near", (wide, piece, piece, piece),
        (near_keep, swap(near_send, n, 1)),
    )
    sums = [*near_sums, *far_sums]
    terms = [
        [sums[4 * s], *[swap(sums[4 * s + q], n, 2 * q) for q in (1, 2, 3)]]
        for s in range(squares)
    ]
    distance = 1
    while distance < squares:
        wgot = swap(wsum, n, 8 * distance)
        for s in range(squares - distance, 0, -2 * distance):
            if s == squares - distance:
                total, wsum = call(
                    add_both_kernel, "square_sum", (piece, chunk), (wsum, wgot, *terms[s]))
            else:
                total = call(add_kernel, "square_sum", piece, terms[s])
            terms[s - distance].append(swap(total, n, 8 * distance))
        distance *= 2

    mine = call(
        pack_kernel, "pack_weights", result((4, feat_in // 4, hidden), F32),
        (wsum, *[swap(wsum, n, 2 * p) for p in (1, 2, 3)]),
    )
    grad_input, grad_self, grad_neigh = call(
        last_kernel, "grad_input_sum",
        (
            result((nodes, feat_in), BF16, False), result((feat_in, hidden), F32, False),
            result((feat_in, hidden), F32, False),
        ),
        (index, mine, swap(mine, n, 1), base, *terms[0]),
        [SMEM] + [VMEM] * (3 + len(terms[0])),
    )
    return (embedded, grad_input, grad_self, grad_neigh)


def solution(mesh):
    placed = (
        P(("parts", "row"), None),
        P(("parts", "row"), None, None),
        P(("parts", "row")),
        P(("parts", "row")),
        P(("parts", "row")),
        P(("parts", "row")),
        P(),
        P(),
        P(("parts", "row"), None),
    )
    return jax.shard_map(
        body,
        mesh=mesh,
        in_specs=placed,
        out_specs=(
            P(("parts", "row"), None),
            P(("parts", "row"), None),
            P("parts", None),
            P("parts", None),
        ),
        check_vma=False,
    )
```

time: 80.1 us -> 68.6 us (0.86)
  waiting for transfers between devices: 32.7 us -> 19.9 us
  local copies, waits for them, and re-layouts: 7.75 us -> 0.91 us
  starting transfers between devices: 27 us -> 32 us
  Pallas kernels: 10.7 us -> 14.9 us
    ppermute x29 -> x27, waiting for transfers between devices: 32.7 us -> 19.9 us  [swap(): return lax.ppermute(x, 'row', [(i, i ^ offset) for i in range(n)])]
    unnamed x18 -> x6, local copies, waits for them, and re-layouts: 7.75 us -> 0.91 us
    ppermute x29 -> x27, starting transfers between devices: 27 us -> 32 us  [swap(): return lax.ppermute(x, 'row', [(i, i ^ offset) for i in range(n)])]
    pallas_call x8 -> x11, Pallas kernels: 10.7 us -> 14.9 us  [the longest x10 11.6 us: call(): pl.pallas_call(kernel, out_shape=out_shape, in_specs=specs, out_specs=out...]
  transfers between devices with their start and end apart: 29 -> 27, of which waited for: 14 -> 12; matrix products, arithmetic and copies ran while one was open for 1% -> 0% of each run, Pallas kernels for 0% -> 8%
where the time goes in v3:
time: 68.6 us; the launch traced here: 68.4 us
  starting transfers between devices  32 us (47%)
  waiting for transfers between devices  19.9 us (29%)
  Pallas kernels  14.9 us (22%)
  local copies, waits for them, and re-layouts  0.91 us (1%)
  between operations  0.78 us (1%)
    ppermute x27, starting transfers between devices, swap(): return lax.ppermute(x, 'row', [(i, i ^ offset) for i in range(n)])  32 us
    ppermute x27, waiting for transfers between devices, swap(): return lax.ppermute(x, 'row', [(i, i ^ offset) for i in range(n)])  19.9 us
    pallas_call x10, Pallas kernels, call(): pl.pallas_call(kernel, out_shape=out_shape, in_specs=specs, out_specs=out...  11.6 us
    pallas_call x1, Pallas kernels, body(): pl.pallas_call(stage_kernel, out_shape=(result(tiles.shape, BF16), result...  3.28 us
  transfers between devices with their start and end apart: 27, of which 12 were waited for; matrix products, arithmetic and copies ran while one was open for 0% of the time, Pallas kernels for 8%

profile of v3, /device:TPU:0, one launch (start us, length us, event | category | flops | bytes accessed | tf_op | source)
XLA Modules:
  0.0 68.4 jit_solution(8816805922710192952)
XLA Ops:
  0.6 4.1 %collective-permute-start.3 = (bf16[512,128]{1,0:T(8,128)(2,1)}, bf16[512,128]{1,0:T(8,128)(2,1)S(1)}, u32[]{:S(2)}, u32[]{:S(2)}) collective-permute-start(bf16[512,128]{1,0:T(8,128)(2,1)} %refs_0_.1), channel_id=1, source_target_pairs={{0,8},{1,9},{2,10},{3,11},{4,12},{5,13},{6,14},{7,15},{8,0},{9,1},... | collective-permute-start | bytes 393224 | tf_op jit(solution)/shard_map/ppermute | solution.py:20
  4.7 2.5 %collective-permute-start.2 = (bf16[512,128]{1,0:T(8,128)(2,1)}, bf16[512,128]{1,0:T(8,128)(2,1)S(1)}, u32[]{:S(2)}, u32[]{:S(2)}) collective-permute-start(bf16[512,128]{1,0:T(8,128)(2,1)} %refs_0_.1), channel_id=1, source_target_pairs={{0,6},{1,7},{2,4},{3,5},{4,2},{5,3},{6,0},{7,1},{8,14},{9,15},{10,... | collective-permute-start | bytes 393224 | tf_op jit(solution)/shard_map/ppermute | solution.py:20
  7.3 0.4 collective-permute-start.1
  7.7 0.5 collective-permute-start
  8.2 3.1 %collective-permute-done.3.refs_0_ = bf16[512,128]{1,0:T(8,128)(2,1)S(1)} collective-permute-done((bf16[512,128]{1,0:T(8,128)(2,1)}, bf16[512,128]{1,0:T(8,128)(2,1)S(1)}, u32[]{:S(2)}, u32[]{:S(2)}) %collective-permute-start.3) | collective-permute-done | bytes 131104 | tf_op jit(solution)/shard_map/ppermute | solution.py:20
  11.3 1.7 %collective-permute-start.6 = (bf16[512,128]{1,0:T(8,128)(2,1)S(1)}, bf16[512,128]{1,0:T(8,128)(2,1)S(1)}, u32[]{:S(2)}, u32[]{:S(2)}) collective-permute-start(bf16[512,128]{1,0:T(8,128)(2,1)S(1)} %collective-permute-done.3.refs_0_), channel_id=1, source_target_pairs={{0,6},{1,7},{2,4},{3,5},{4,2},{5,3},{6,0},{7,1},{8,14},{9,15},{10,... | collective-permute-start | bytes 393224 | tf_op jit(solution)/shard_map/ppermute | solution.py:20
  13.1 1.3 %collective-permute-start.5 = (bf16[512,128]{1,0:T(8,128)(2,1)S(1)}, bf16[512,128]{1,0:T(8,128)(2,1)S(1)}, u32[]{:S(2)}, u32[]{:S(2)}) collective-permute-start(bf16[512,128]{1,0:T(8,128)(2,1)S(1)} %collective-permute-done.3.refs_0_), channel_id=1, source_target_pairs={{0,4},{1,5},{2,6},{3,7},{4,0},{5,1},{6,2},{7,3},{8,12},{9,13},{10,... | collective-permute-start | bytes 393224 | tf_op jit(solution)/shard_map/ppermute | solution.py:20
  14.4 0.6 collective-permute-start.4
  15.0 1.3 %collective-permute-done.1.refs_2_ = bf16[512,128]{1,0:T(8,128)(2,1)S(1)} collective-permute-done((bf16[512,128]{1,0:T(8,128)(2,1)}, bf16[512,128]{1,0:T(8,128)(2,1)S(1)}, u32[]{:S(2)}, u32[]{:S(2)}) %collective-permute-start.1) | collective-permute-done | bytes 131104 | tf_op jit(solution)/shard_map/ppermute | solution.py:20
  16.3 0.9 %copy-done = bf16[512,128]{1,0:T(8,128)(2,1)S(1)} copy-done((bf16[512,128]{1,0:T(8,128)(2,1)S(1)}, bf16[512,128]{1,0:T(8,128)(2,1)}, u32[]{:S(2)}) %copy-start) | copy-done | bytes 131096
  17.3 0.1 collective-permute-start.7
  17.4 2.1 %collective-permute-done.6.refs_3_ = bf16[512,128]{1,0:T(8,128)(2,1)S(1)} collective-permute-done((bf16[512,128]{1,0:T(8,128)(2,1)S(1)}, bf16[512,128]{1,0:T(8,128)(2,1)S(1)}, u32[]{:S(2)}, u32[]{:S(2)}) %collective-permute-start.6) | collective-permute-done | bytes 131104 | tf_op jit(solution)/shard_map/ppermute | solution.py:20
  19.4 1.5 %collective-permute-done.5.refs_2_ = bf16[512,128]{1,0:T(8,128)(2,1)S(1)} collective-permute-done((bf16[512,128]{1,0:T(8,128)(2,1)S(1)}, bf16[512,128]{1,0:T(8,128)(2,1)S(1)}, u32[]{:S(2)}, u32[]{:S(2)}) %collective-permute-start.5) | collective-permute-done | bytes 131104 | tf_op jit(solution)/shard_map/ppermute | solution.py:20
  21.0 0.1 collective-permute-start.8
  21.1 3.3 %stage_arguments.1 = (bf16[60,128,128]{2,1,0:T(8,128)(2,1)S(1)}, bf16[128,256]{1,0:T(8,128)(2,1)S(1)}, bf16[128,256]{1,0:T(8,128)(2,1)S(1)}, f32[4,128,128]{2,1,...) custom-call(s32[1]{0:T(128)} %bitcast.me_ref, ...), custom_call_target="tpu_custom_call" | custom-call | bytes 10800000 | tf_op jit(solution)/shard_map/stage_arguments/pallas_call | solution.py:300
  24.4 5.0 %forward_layer.1 = (bf16[512,256]{1,0:T(8,128)(2,1)}, f32[512,128]{1,0:T(8,128)S(1)}, f32[128,256]{1,0:T(8,128)S(1)}, f32[128,256]{1,0:T(8,128)S(1)}, bf16[4,256,128]{2,1,0:T(8,128)(2,1)S(1)}) custom-call(s32[121]{0:T(128)S(1)} %get-tuple-element.39.index_ref, bf16[60,128,128]{2,1,0:T(8,128)(2,1)S(1)} %get-tuple-element.40.tiles_ref, ...), custom_call_target="tpu_custom_call" | custom-call | bytes 18000000 | tf_op jit(solution)/shard_map/forward_layer/pallas_call | solution.py:277
  29.4 0.5 collective-permute-start.9
  29.9 2.1 %backward_first.1.before_ref = f32[65,128,128]{2,1,0:T(8,128)S(1)} custom-call(s32[121]{0:T(128)S(1)} %get-tuple-element.39.index_ref, bf16[60,128,128]{2,1,0:T(8,128)(2,1)S(1)} %get-tuple-element.40.tiles_ref, bf16[4,256,128]{2,1,0:T(8,128)(2,1)S(1)} %get-tuple-element.48.gt_ref), custom_call_target="tpu_custom_call" | custom-call | bytes 9000000 | tf_op jit(solution)/shard_map/backward_first/pallas_call | solution.py:277
  32.0 2.7 %backward_second.1 = (f32[1,4,512,128]{3,2,1,0:T(8,128)S(1)}, f32[1,4,512,128]{3,2,1,0:T(8,128)S(1)}, f32[1,4,512,128]{3,2,1,0:T(8,128)S(1)}, f32[1,4,512,128]{3...) custom-call(s32[121]{0:T(128)S(1)} %get-tuple-element.39.index_ref, ...), custom_call_target="tpu_custom_call" | custom-call | bytes 9000000 | tf_op jit(solution)/shard_map/backward_second/pallas_call | solution.py:277
  34.7 0.1 collective-permute-start.13
  34.9 0.5 collective-permute-start.22
  35.3 0.6 collective-permute-start.10
  35.9 1.5 %collective-permute-start.11 = (f32[32,256]{1,0:T(8,128)S(1)}, f32[32,256]{1,0:T(8,128)S(1)}, u32[]{:S(2)}, u32[]{:S(2)}) collective-permute-start(f32[32,256]{1,0:T(8,128)S(1)} %get-tuple-element.53), channel_id=1, source_target_pairs={{0,4},{1,5},{2,6},{3,7},{4,0},{5,1},{6,2},{7,3},{8,12},{9,13},{10,... | collective-permute-start | bytes 98312 | tf_op jit(solution)/shard_map/ppermute | solution.py:20
  37.4 1.4 %collective-permute-start.12 = (f32[32,256]{1,0:T(8,128)S(1)}, f32[32,256]{1,0:T(8,128)S(1)}, u32[]{:S(2)}, u32[]{:S(2)}) collective-permute-start(f32[32,256]{1,0:T(8,128)S(1)} %get-tuple-element.54), channel_id=1, source_target_pairs={{0,6},{1,7},{2,4},{3,5},{4,2},{5,3},{6,0},{7,1},{8,14},{9,15},{10,... | collective-permute-start | bytes 98312 | tf_op jit(solution)/shard_map/ppermute | solution.py:20
  38.8 0.4 collective-permute-done.10.w1
  39.2 0.6 collective-permute-done.11.w2
  39.8 2.4 %collective-permute-done.12.w3 = f32[32,256]{1,0:T(8,128)S(1)} collective-permute-done((f32[32,256]{1,0:T(8,128)S(1)}, f32[32,256]{1,0:T(8,128)S(1)}, u32[]{:S(2)}, u32[]{:S(2)}) %collective-permute-start.12) | collective-permute-done | bytes 32800 | tf_op jit(solution)/shard_map/ppermute | solution.py:20
  42.2 0.1 pair_sum_far.1
  42.3 1.2 %collective-permute-start.15 = (bf16[512,128]{1,0:T(8,128)(2,1)S(1)}, bf16[512,128]{1,0:T(8,128)(2,1)S(1)}, u32[]{:S(2)}, u32[]{:S(2)}) collective-permute-start(bf16[512,128]{1,0:T(8,128)(2,1)S(1)} %get-tuple-element.59), channel_id=1, source_target_pairs={{0,2},{1,3},{2,0},{3,1},{4,6},{5,7},{6,4},{7,5},{8,10},{9,11},{10,... | collective-permute-start | bytes 393224 | tf_op jit(solution)/shard_map/ppermute | solution.py:20
  43.4 0.9 %collective-permute-start.16 = (bf16[512,128]{1,0:T(8,128)(2,1)S(1)}, bf16[512,128]{1,0:T(8,128)(2,1)S(1)}, u32[]{:S(2)}, u32[]{:S(2)}) collective-permute-start(bf16[512,128]{1,0:T(8,128)(2,1)S(1)} %get-tuple-element.60), channel_id=1, source_target_pairs={{0,4},{1,5},{2,6},{3,7},{4,0},{5,1},{6,2},{7,3},{8,12},{9,13},{10,... | collective-permute-start | bytes 393224 | tf_op jit(solution)/shard_map/ppermute | solution.py:20
  44.4 1.5 %collective-permute-start.17 = (bf16[512,128]{1,0:T(8,128)(2,1)S(1)}, bf16[512,128]{1,0:T(8,128)(2,1)S(1)}, u32[]{:S(2)}, u32[]{:S(2)}) collective-permute-start(bf16[512,128]{1,0:T(8,128)(2,1)S(1)} %get-tuple-element.61), channel_id=1, source_target_pairs={{0,6},{1,7},{2,4},{3,5},{4,2},{5,3},{6,0},{7,1},{8,14},{9,15},{10,... | collective-permute-start | bytes 393224 | tf_op jit(solution)/shard_map/ppermute | solution.py:20
  45.8 3.1 %collective-permute-start.14 = (f32[32,256]{1,0:T(8,128)S(1)}, f32[32,256]{1,0:T(8,128)S(1)}, u32[]{:S(2)}, u32[]{:S(2)}) collective-permute-start(f32[32,256]{1,0:T(8,128)S(1)} %get-tuple-element.57.weight_ref), channel_id=1, source_target_pairs={{0,8},{1,9},{2,10},{3,11},{4,12},{5,13},{6,14},{7,15},{8,0},{9,1},... | collective-permute-start | bytes 98312 | tf_op jit(solution)/shard_map/ppermute | solution.py:20
  48.9 1.9 %collective-permute-done.14.wgot_ref = f32[32,256]{1,0:T(8,128)S(1)} collective-permute-done((f32[32,256]{1,0:T(8,128)S(1)}, f32[32,256]{1,0:T(8,128)S(1)}, u32[]{:S(2)}, u32[]{:S(2)}) %collective-permute-start.14) | collective-permute-done | bytes 32800 | tf_op jit(solution)/shard_map/ppermute | solution.py:20
  50.8 0.0 collective-permute-done.17.refs_2_
  50.8 0.1 square_sum.1
  50.9 3.1 %collective-permute-start.20 = (f32[32,256]{1,0:T(8,128)S(1)}, f32[32,256]{1,0:T(8,128)S(1)}, u32[]{:S(2)}, u32[]{:S(2)}) collective-permute-start(f32[32,256]{1,0:T(8,128)S(1)} %get-tuple-element.62.refs_0_), channel_id=1, source_target_pairs={{0,6},{1,7},{2,4},{3,5},{4,2},{5,3},{6,0},{7,1},{8,14},{9,15},{10,... | collective-permute-start | bytes 98312 | tf_op jit(solution)/shard_map/ppermute | solution.py:20
  54.0 0.6 collective-permute-start.18
  54.7 0.1 pair_sum_near.1
  54.8 1.5 %collective-permute-start.23 = (bf16[512,128]{1,0:T(8,128)(2,1)S(1)}, bf16[512,128]{1,0:T(8,128)(2,1)S(1)}, u32[]{:S(2)}, u32[]{:S(2)}) collective-permute-start(bf16[512,128]{1,0:T(8,128)(2,1)S(1)} %get-tuple-element.67), channel_id=1, source_target_pairs={{0,2},{1,3},{2,0},{3,1},{4,6},{5,7},{6,4},{7,5},{8,10},{9,11},{10,... | collective-permute-start | bytes 393224 | tf_op jit(solution)/shard_map/ppermute | solution.py:20
  56.2 2.0 %collective-permute-start.24 = (bf16[512,128]{1,0:T(8,128)(2,1)S(1)}, bf16[512,128]{1,0:T(8,128)(2,1)S(1)}, u32[]{:S(2)}, u32[]{:S(2)}) collective-permute-start(bf16[512,128]{1,0:T(8,128)(2,1)S(1)} %get-tuple-element.68), channel_id=1, source_target_pairs={{0,4},{1,5},{2,6},{3,7},{4,0},{5,1},{6,2},{7,3},{8,12},{9,13},{10,... | collective-permute-start | bytes 393224 | tf_op jit(solution)/shard_map/ppermute | solution.py:20
  58.3 0.9 %collective-permute-start.25 = (bf16[512,128]{1,0:T(8,128)(2,1)S(1)}, bf16[512,128]{1,0:T(8,128)(2,1)S(1)}, u32[]{:S(2)}, u32[]{:S(2)}) collective-permute-start(bf16[512,128]{1,0:T(8,128)(2,1)S(1)} %get-tuple-element.69), channel_id=1, source_target_pairs={{0,6},{1,7},{2,4},{3,5},{4,2},{5,3},{6,0},{7,1},{8,14},{9,15},{10,... | collective-permute-start | bytes 393224 | tf_op jit(solution)/shard_map/ppermute | solution.py:20
  59.2 0.6 collective-permute-done.19.refs_2_
  59.8 1.3 %collective-permute-start.26 = (bf16[512,128]{1,0:T(8,128)(2,1)S(1)}, bf16[512,128]{1,0:T(8,128)(2,1)S(1)}, u32[]{:S(2)}, u32[]{:S(2)}) collective-permute-start(bf16[512,128]{1,0:T(8,128)(2,1)S(1)} %get-tuple-element.70), channel_id=1, source_target_pairs={{0,8},{1,9},{2,10},{3,11},{4,12},{5,13},{6,14},{7,15},{8,0},{9,1},... | collective-permute-start | bytes 393224 | tf_op jit(solution)/shard_map/ppermute | solution.py:20
  61.1 0.1 collective-permute-start.21
  61.1 0.1 collective-permute-done.24.refs_1_
  61.2 4.3 %collective-permute-done.25.refs_2_ = bf16[512,128]{1,0:T(8,128)(2,1)S(1)} collective-permute-done((bf16[512,128]{1,0:T(8,128)(2,1)S(1)}, bf16[512,128]{1,0:T(8,128)(2,1)S(1)}, u32[]{:S(2)}, u32[]{:S(2)}) %collective-permute-start.25) | collective-permute-done | bytes 131104 | tf_op jit(solution)/shard_map/ppermute | solution.py:20
  65.5 1.5 %collective-permute-done.26.refs_3_ = bf16[512,128]{1,0:T(8,128)(2,1)S(1)} collective-permute-done((bf16[512,128]{1,0:T(8,128)(2,1)S(1)}, bf16[512,128]{1,0:T(8,128)(2,1)S(1)}, u32[]{:S(2)}, u32[]{:S(2)}) %collective-permute-start.26) | collective-permute-done | bytes 131104 | tf_op jit(solution)/shard_map/ppermute | solution.py:20
  67.0 1.4 %grad_input_sum.1 = (bf16[512,128]{1,0:T(8,128)(2,1)}, f32[128,256]{1,0:T(8,128)}, f32[128,256]{1,0:T(8,128)}) custom-call(s32[121]{0:T(128)S(1)} %get-tuple-element.39.index_ref, f32[4,32,256]{2,1,0:T(8,128)S(1)} %pack_weights.1.weight_ref, f32[4,32,256]{2,1,0:T(8,128)S(1)} %collective-permute-done.21.other_ref, f32[512,128]{1,0:T(8,128)S(1)} %get-tuple-element.63.base_ref, ...), custom_call_target="tpu_custom_call" | custom-call | bytes 720000 | tf_op jit(solution)/shard_map/grad_input_sum/pallas_call | solution.py:277
  (23 shorter events, 0.1 us)
Async XLA Ops:
  0.6 10.7 %collective-permute-start.3 = (bf16[512,128]{1,0:T(8,128)(2,1)}, bf16[512,128]{1,0:T(8,128)(2,1)S(1)}, u32[]{:S(2)}, u32[]{:S(2)}) collective-permute-start(bf16[512,128]{1,0:T(8,128)(2,1)} %refs_0_.1), channel_id=1, source_target_pairs={{0,8},{1,9},{2,10},{3,11},{4,12},{5,13},{6,14},{7,15},{8,0},{9,1},... | collective-permute-start | bytes 393224 | tf_op jit(solution)/shard_map/ppermute | solution.py:20
  4.7 9.7 %collective-permute-start.2 = (bf16[512,128]{1,0:T(8,128)(2,1)}, bf16[512,128]{1,0:T(8,128)(2,1)S(1)}, u32[]{:S(2)}, u32[]{:S(2)}) collective-permute-start(bf16[512,128]{1,0:T(8,128)(2,1)} %refs_0_.1), channel_id=1, source_target_pairs={{0,6},{1,7},{2,4},{3,5},{4,2},{5,3},{6,0},{7,1},{8,14},{9,15},{10,... | collective-permute-start | bytes 393224 | tf_op jit(solution)/shard_map/ppermute | solution.py:20
  7.3 9.1 %collective-permute-start.1 = (bf16[512,128]{1,0:T(8,128)(2,1)}, bf16[512,128]{1,0:T(8,128)(2,1)S(1)}, u32[]{:S(2)}, u32[]{:S(2)}) collective-permute-start(bf16[512,128]{1,0:T(8,128)(2,1)} %refs_0_.1), channel_id=1, source_target_pairs={{0,4},{1,5},{2,6},{3,7},{4,0},{5,1},{6,2},{7,3},{8,12},{9,13},{10,... | collective-permute-start | bytes 393224 | tf_op jit(solution)/shard_map/ppermute | solution.py:20
  7.7 8.6 %collective-permute-start = (bf16[512,128]{1,0:T(8,128)(2,1)}, bf16[512,128]{1,0:T(8,128)(2,1)S(1)}, u32[]{:S(2)}, u32[]{:S(2)}) collective-permute-start(bf16[512,128]{1,0:T(8,128)(2,1)} %refs_0_.1), channel_id=1, source_target_pairs={{0,2},{1,3},{2,0},{3,1},{4,6},{5,7},{6,4},{7,5},{8,10},{9,11},{10,... | collective-permute-start | bytes 393224 | tf_op jit(solution)/shard_map/ppermute | solution.py:20
  11.3 8.1 %collective-permute-start.6 = (bf16[512,128]{1,0:T(8,128)(2,1)S(1)}, bf16[512,128]{1,0:T(8,128)(2,1)S(1)}, u32[]{:S(2)}, u32[]{:S(2)}) collective-permute-start(bf16[512,128]{1,0:T(8,128)(2,1)S(1)} %collective-permute-done.3.refs_0_), channel_id=1, source_target_pairs={{0,6},{1,7},{2,4},{3,5},{4,2},{5,3},{6,0},{7,1},{8,14},{9,15},{10,... | collective-permute-start | bytes 393224 | tf_op jit(solution)/shard_map/ppermute | solution.py:20
  13.1 7.9 %collective-permute-start.5 = (bf16[512,128]{1,0:T(8,128)(2,1)S(1)}, bf16[512,128]{1,0:T(8,128)(2,1)S(1)}, u32[]{:S(2)}, u32[]{:S(2)}) collective-permute-start(bf16[512,128]{1,0:T(8,128)(2,1)S(1)} %collective-permute-done.3.refs_0_), channel_id=1, source_target_pairs={{0,4},{1,5},{2,6},{3,7},{4,0},{5,1},{6,2},{7,3},{8,12},{9,13},{10,... | collective-permute-start | bytes 393224 | tf_op jit(solution)/shard_map/ppermute | solution.py:20
  14.4 6.5 %collective-permute-start.4 = (bf16[512,128]{1,0:T(8,128)(2,1)S(1)}, bf16[512,128]{1,0:T(8,128)(2,1)S(1)}, u32[]{:S(2)}, u32[]{:S(2)}) collective-permute-start(bf16[512,128]{1,0:T(8,128)(2,1)S(1)} %collective-permute-done.3.refs_0_), channel_id=1, source_target_pairs={{0,2},{1,3},{2,0},{3,1},{4,6},{5,7},{6,4},{7,5},{8,10},{9,11},{10,... | collective-permute-start | bytes 393224 | tf_op jit(solution)/shard_map/ppermute | solution.py:20
  16.3 0.9 %copy-start = (bf16[512,128]{1,0:T(8,128)(2,1)S(1)}, bf16[512,128]{1,0:T(8,128)(2,1)}, u32[]{:S(2)}) copy-start(bf16[512,128]{1,0:T(8,128)(2,1)} %refs_0_.1) | copy-start | bytes 393220
  17.2 3.8 %copy-start.1 = (s32[60]{0:T(128)S(1)}, s32[60]{0:T(128)}, u32[]{:S(2)}) copy-start(s32[60]{0:T(128)} %trow_ref.1) | copy-start | bytes 724
  17.2 3.8 %copy-start.2 = (s32[60]{0:T(128)S(1)}, s32[60]{0:T(128)}, u32[]{:S(2)}) copy-start(s32[60]{0:T(128)} %tcol_ref.1) | copy-start | bytes 724
  17.3 7.1 %collective-permute-start.7 = (bf16[4,512,128]{2,1,0:T(8,128)(2,1)S(1)}, bf16[4,512,128]{2,1,0:T(8,128)(2,1)S(1)}, u32[]{:S(2)}, u32[]{:S(2)}) collective-permute-start(bf16[4,512,128]{2,1,0:T(8,128)(2,1)S(1)} %pack_square.2.refs_0_), channel_id=1, source_target_pairs={{0,1},{1,0},{2,3},{3,2},{4,5},{5,4},{6,7},{7,6},{8,9},{9,8},{10,11... | collective-permute-start | bytes 1572872 | tf_op jit(solution)/shard_map/ppermute | solution.py:20
  21.0 3.4 %collective-permute-start.8 = (bf16[4,512,128]{2,1,0:T(8,128)(2,1)S(1)}, bf16[4,512,128]{2,1,0:T(8,128)(2,1)S(1)}, u32[]{:S(2)}, u32[]{:S(2)}) collective-permute-start(bf16[4,512,128]{2,1,0:T(8,128)(2,1)S(1)} %pack_square.3.refs_1_), channel_id=1, source_target_pairs={{0,1},{1,0},{2,3},{3,2},{4,5},{5,4},{6,7},{7,6},{8,9},{9,8},{10,11... | collective-permute-start | bytes 1572872 | tf_op jit(solution)/shard_map/ppermute | solution.py:20
  29.4 2.6 %collective-permute-start.9 = (f32[128,256]{1,0:T(8,128)S(1)}, f32[128,256]{1,0:T(8,128)S(1)}, u32[]{:S(2)}, u32[]{:S(2)}) collective-permute-start(f32[128,256]{1,0:T(8,128)S(1)} %get-tuple-element.50), channel_id=1, source_target_pairs={{0,1},{1,0},{2,3},{3,2},{4,5},{5,4},{6,7},{7,6},{8,9},{9,8},{10,11... | collective-permute-start | bytes 393224 | tf_op jit(solution)/shard_map/ppermute | solution.py:20
  34.7 7.4 %collective-permute-start.13 = (f32[1,4,512,128]{3,2,1,0:T(8,128)S(1)}, f32[1,4,512,128]{3,2,1,0:T(8,128)S(1)}, u32[]{:S(2)}, u32[]{:S(2)}) collective-permute-start(f32[1,4,512,128]{3,2,1,0:T(8,128)S(1)} %get-tuple-element.56), channel_id=1, source_target_pairs={{0,1},{1,0},{2,3},{3,2},{4,5},{5,4},{6,7},{7,6},{8,9},{9,8},{10,11... | collective-permute-start | bytes 3145736 | tf_op jit(solution)/shard_map/ppermute | solution.py:20
  34.9 19.8 %collective-permute-start.22 = (f32[1,4,512,128]{3,2,1,0:T(8,128)S(1)}, f32[1,4,512,128]{3,2,1,0:T(8,128)S(1)}, u32[]{:S(2)}, u32[]{:S(2)}) collective-permute-start(f32[1,4,512,128]{3,2,1,0:T(8,128)S(1)} %get-tuple-element.65), channel_id=1, source_target_pairs={{0,1},{1,0},{2,3},{3,2},{4,5},{5,4},{6,7},{7,6},{8,9},{9,8},{10,11... | collective-permute-start | bytes 3145736 | tf_op jit(solution)/shard_map/ppermute | solution.py:20
  35.3 3.9 %collective-permute-start.10 = (f32[32,256]{1,0:T(8,128)S(1)}, f32[32,256]{1,0:T(8,128)S(1)}, u32[]{:S(2)}, u32[]{:S(2)}) collective-permute-start(f32[32,256]{1,0:T(8,128)S(1)} %get-tuple-element.52), channel_id=1, source_target_pairs={{0,2},{1,3},{2,0},{3,1},{4,6},{5,7},{6,4},{7,5},{8,10},{9,11},{10,... | collective-permute-start | bytes 98312 | tf_op jit(solution)/shard_map/ppermute | solution.py:20
  35.9 3.9 %collective-permute-start.11 = (f32[32,256]{1,0:T(8,128)S(1)}, f32[32,256]{1,0:T(8,128)S(1)}, u32[]{:S(2)}, u32[]{:S(2)}) collective-permute-start(f32[32,256]{1,0:T(8,128)S(1)} %get-tuple-element.53), channel_id=1, source_target_pairs={{0,4},{1,5},{2,6},{3,7},{4,0},{5,1},{6,2},{7,3},{8,12},{9,13},{10,... | collective-permute-start | bytes 98312 | tf_op jit(solution)/shard_map/ppermute | solution.py:20
  37.4 4.8 %collective-permute-start.12 = (f32[32,256]{1,0:T(8,128)S(1)}, f32[32,256]{1,0:T(8,128)S(1)}, u32[]{:S(2)}, u32[]{:S(2)}) collective-permute-start(f32[32,256]{1,0:T(8,128)S(1)} %get-tuple-element.54), channel_id=1, source_target_pairs={{0,6},{1,7},{2,4},{3,5},{4,2},{5,3},{6,0},{7,1},{8,14},{9,15},{10,... | collective-permute-start | bytes 98312 | tf_op jit(solution)/shard_map/ppermute | solution.py:20
  42.3 8.5 %collective-permute-start.15 = (bf16[512,128]{1,0:T(8,128)(2,1)S(1)}, bf16[512,128]{1,0:T(8,128)(2,1)S(1)}, u32[]{:S(2)}, u32[]{:S(2)}) collective-permute-start(bf16[512,128]{1,0:T(8,128)(2,1)S(1)} %get-tuple-element.59), channel_id=1, source_target_pairs={{0,2},{1,3},{2,0},{3,1},{4,6},{5,7},{6,4},{7,5},{8,10},{9,11},{10,... | collective-permute-start | bytes 393224 | tf_op jit(solution)/shard_map/ppermute | solution.py:20
  43.4 7.4 %collective-permute-start.16 = (bf16[512,128]{1,0:T(8,128)(2,1)S(1)}, bf16[512,128]{1,0:T(8,128)(2,1)S(1)}, u32[]{:S(2)}, u32[]{:S(2)}) collective-permute-start(bf16[512,128]{1,0:T(8,128)(2,1)S(1)} %get-tuple-element.60), channel_id=1, source_target_pairs={{0,4},{1,5},{2,6},{3,7},{4,0},{5,1},{6,2},{7,3},{8,12},{9,13},{10,... | collective-permute-start | bytes 393224 | tf_op jit(solution)/shard_map/ppermute | solution.py:20
  44.4 6.5 %collective-permute-start.17 = (bf16[512,128]{1,0:T(8,128)(2,1)S(1)}, bf16[512,128]{1,0:T(8,128)(2,1)S(1)}, u32[]{:S(2)}, u32[]{:S(2)}) collective-permute-start(bf16[512,128]{1,0:T(8,128)(2,1)S(1)} %get-tuple-element.61), channel_id=1, source_target_pairs={{0,6},{1,7},{2,4},{3,5},{4,2},{5,3},{6,0},{7,1},{8,14},{9,15},{10,... | collective-permute-start | bytes 393224 | tf_op jit(solution)/shard_map/ppermute | solution.py:20
  45.8 5.0 %collective-permute-start.14 = (f32[32,256]{1,0:T(8,128)S(1)}, f32[32,256]{1,0:T(8,128)S(1)}, u32[]{:S(2)}, u32[]{:S(2)}) collective-permute-start(f32[32,256]{1,0:T(8,128)S(1)} %get-tuple-element.57.weight_ref), channel_id=1, source_target_pairs={{0,8},{1,9},{2,10},{3,11},{4,12},{5,13},{6,14},{7,15},{8,0},{9,1},... | collective-permute-start | bytes 98312 | tf_op jit(solution)/shard_map/ppermute | solution.py:20
  50.9 7.4 %collective-permute-start.20 = (f32[32,256]{1,0:T(8,128)S(1)}, f32[32,256]{1,0:T(8,128)S(1)}, u32[]{:S(2)}, u32[]{:S(2)}) collective-permute-start(f32[32,256]{1,0:T(8,128)S(1)} %get-tuple-element.62.refs_0_), channel_id=1, source_target_pairs={{0,6},{1,7},{2,4},{3,5},{4,2},{5,3},{6,0},{7,1},{8,14},{9,15},{10,... | collective-permute-start | bytes 98312 | tf_op jit(solution)/shard_map/ppermute | solution.py:20
  54.0 5.7 %collective-permute-start.19 = (f32[32,256]{1,0:T(8,128)S(1)}, f32[32,256]{1,0:T(8,128)S(1)}, u32[]{:S(2)}, u32[]{:S(2)}) collective-permute-start(f32[32,256]{1,0:T(8,128)S(1)} %get-tuple-element.62.refs_0_), channel_id=1, source_target_pairs={{0,4},{1,5},{2,6},{3,7},{4,0},{5,1},{6,2},{7,3},{8,12},{9,13},{10,... | collective-permute-start | bytes 98312 | tf_op jit(solution)/shard_map/ppermute | solution.py:20
  54.0 7.0 %collective-permute-start.18 = (f32[32,256]{1,0:T(8,128)S(1)}, f32[32,256]{1,0:T(8,128)S(1)}, u32[]{:S(2)}, u32[]{:S(2)}) collective-permute-start(f32[32,256]{1,0:T(8,128)S(1)} %get-tuple-element.62.refs_0_), channel_id=1, source_target_pairs={{0,2},{1,3},{2,0},{3,1},{4,6},{5,7},{6,4},{7,5},{8,10},{9,11},{10,... | collective-permute-start | bytes 98312 | tf_op jit(solution)/shard_map/ppermute | solution.py:20
  54.8 6.3 %collective-permute-start.23 = (bf16[512,128]{1,0:T(8,128)(2,1)S(1)}, bf16[512,128]{1,0:T(8,128)(2,1)S(1)}, u32[]{:S(2)}, u32[]{:S(2)}) collective-permute-start(bf16[512,128]{1,0:T(8,128)(2,1)S(1)} %get-tuple-element.67), channel_id=1, source_target_pairs={{0,2},{1,3},{2,0},{3,1},{4,6},{5,7},{6,4},{7,5},{8,10},{9,11},{10,... | collective-permute-start | bytes 393224 | tf_op jit(solution)/shard_map/ppermute | solution.py:20
  56.2 5.0 %collective-permute-start.24 = (bf16[512,128]{1,0:T(8,128)(2,1)S(1)}, bf16[512,128]{1,0:T(8,128)(2,1)S(1)}, u32[]{:S(2)}, u32[]{:S(2)}) collective-permute-start(bf16[512,128]{1,0:T(8,128)(2,1)S(1)} %get-tuple-element.68), channel_id=1, source_target_pairs={{0,4},{1,5},{2,6},{3,7},{4,0},{5,1},{6,2},{7,3},{8,12},{9,13},{10,... | collective-permute-start | bytes 393224 | tf_op jit(solution)/shard_map/ppermute | solution.py:20
  58.3 7.3 %collective-permute-start.25 = (bf16[512,128]{1,0:T(8,128)(2,1)S(1)}, bf16[512,128]{1,0:T(8,128)(2,1)S(1)}, u32[]{:S(2)}, u32[]{:S(2)}) collective-permute-start(bf16[512,128]{1,0:T(8,128)(2,1)S(1)} %get-tuple-element.69), channel_id=1, source_target_pairs={{0,6},{1,7},{2,4},{3,5},{4,2},{5,3},{6,0},{7,1},{8,14},{9,15},{10,... | collective-permute-start | bytes 393224 | tf_op jit(solution)/shard_map/ppermute | solution.py:20
  59.8 7.3 %collective-permute-start.26 = (bf16[512,128]{1,0:T(8,128)(2,1)S(1)}, bf16[512,128]{1,0:T(8,128)(2,1)S(1)}, u32[]{:S(2)}, u32[]{:S(2)}) collective-permute-start(bf16[512,128]{1,0:T(8,128)(2,1)S(1)} %get-tuple-element.70), channel_id=1, source_target_pairs={{0,8},{1,9},{2,10},{3,11},{4,12},{5,13},{6,14},{7,15},{8,0},{9,1},... | collective-permute-start | bytes 393224 | tf_op jit(solution)/shard_map/ppermute | solution.py:20
  61.1 6.0 %collective-permute-start.21 = (f32[4,32,256]{2,1,0:T(8,128)S(1)}, f32[4,32,256]{2,1,0:T(8,128)S(1)}, u32[]{:S(2)}, u32[]{:S(2)}) collective-permute-start(f32[4,32,256]{2,1,0:T(8,128)S(1)} %pack_weights.1.weight_ref), channel_id=1, source_target_pairs={{0,1},{1,0},{2,3},{3,2},{4,5},{5,4},{6,7},{7,6},{8,9},{9,8},{10,11... | collective-permute-start | bytes 393224 | tf_op jit(solution)/shard_map/ppermute | solution.py:20

commit v4 on v3

--- a/solution.py
+++ b/solution.py
@@ -14,13 +14,14 @@
 ANY = pl.BlockSpec(memory_space=pl.ANY)
 MIB = 1024 * 1024
 LAST = ((1,), (1,))
+NEAR_COST, SQUARE_COST, WEIGHT_COST = 1, 4, 8
 
 
 def swap(x, n, offset):
     return lax.ppermute(x, "row", [(i, i ^ offset) for i in range(n)])
 
 
-def gather_by_xor(x, n, call, pack):
+def gather_by_xor(x, own, n, call, pack):
     blocks = [x]
     bit = n // 2
     while bit >= 8:
@@ -34,7 +35,7 @@
     blocks = [v for _, v in sorted(zip(offsets, blocks), key=lambda pair: pair[0])]
     same = []
     for v in blocks:
-        square = (v, *[swap(v, n, offset) for offset in (2, 4, 6)])
+        square = (own if v is x else v, *[swap(v, n, offset) for offset in (2, 4, 6)])
         same.append(call(pack_kernel, "pack_square", pack, square))
     return same, [swap(v, n, 1) for v in same]
 
@@ -68,7 +69,7 @@
 
 def stage_kernel(me_ref, trow_ref, tcol_ref, deg_ref, mask_ref, ws_ref, wn_ref, feat_ref, cot_ref,
                  tiles_ref, tiles_out, ws_out, wn_out, deg_out, up_out, pre_out, featt_out,
-                 index_out, sem):
+                 own_out, index_out, sem):
     copy = pltpu.make_async_copy(tiles_ref, tiles_out, sem)
     copy.start()
     block_local = feat_ref.shape[0] // BLOCK
@@ -87,6 +88,7 @@
         return carry
 
     lax.fori_loop(0, tile_count, place, 0)
+    own_out[...] = feat_ref[...]
     ws_out[...] = ws_ref[...]
     wn_out[...] = wn_ref[...]
     ws = ws_ref[...]
@@ -159,65 +161,75 @@
     wsend_ref[...] = wsum[1 - core]
 
 
-def add_tiles(first, last, group, index_ref, tiles_ref, gt_ref, acc):
+def backward_kernel(group, index_ref, tiles_ref, gt_ref, acc_ref):
     block_local = gt_ref.shape[0]
     tile_count = tiles_ref.shape[0]
-    dump = acc.shape[0] - 1
+    dump = acc_ref.shape[0] - 1
+    acc_ref[...] = jnp.zeros_like(acc_ref)
 
     def backward(step, carry):
         places, products = [], []
         for u in range(group):
-            t = first + step * group + u
+            t = step * group + u
             row = index_ref[t]
             places.append(jnp.where(row < block_local, index_ref[tile_count + t], dump))
             both = dot(gt_ref[jnp.minimum(row, block_local - 1)], tiles_ref[t])
             products.append(both[:BLOCK] + both[BLOCK:])
         for position, product in zip(places, products):
-            acc[position] += product
+            acc_ref[position] += product
         return carry
 
-    lax.fori_loop(0, (last - first) // group, backward, 0)
-
-
-def backward_first_kernel(last, group, index_ref, tiles_ref, gt_ref, acc_ref):
-    acc_ref[...] = jnp.zeros_like(acc_ref)
-    add_tiles(0, last, group, index_ref, tiles_ref, gt_ref, acc_ref)
-
-
-def backward_second_kernel(n, first, group, index_ref, tiles_ref, gt_ref, wkeep_ref, wgot_ref,
-                           before_ref, *refs):
-    far_send, near_send, far_keep, near_keep, w0, w1, w2, w3, acc = refs
-    block_local = gt_ref.shape[0]
-    tile_count = tiles_ref.shape[0]
-    rows = w0.shape[0]
-    chip = index_ref[2 * tile_count] // 2 % 4
-    for p, ref in enumerate((w0, w1, w2, w3)):
+    lax.fori_loop(0, tile_count // group, backward, 0)
+
+
+def split_kernel(n, block_local, index_ref, acc_ref, wkeep_ref, wgot_ref, far_send, near_send,
+                 far_keep, near_keep, *parts):
+    rows = parts[0].shape[0]
+    chip = index_ref[index_ref.shape[0] - 1] // 2 % 4
+    for p, ref in enumerate(parts):
         span = pl.ds(pl.multiple_of((chip ^ p) * rows, rows), rows)
         ref[...] = wkeep_ref[span, :] + wgot_ref[span, :]
-    acc[...] = jnp.zeros_like(acc)
-    add_tiles(first, tile_count, group, index_ref, tiles_ref, gt_ref, acc)
     for k in range(n):
         square, q = k // 8, k // 2 % 4
         near, far = (near_send, far_send) if k % 2 else (near_keep, far_keep)
         for b in range(block_local):
-            spot = k * block_local + b
-            total = acc[spot] + before_ref[spot]
+            total = acc_ref[k * block_local + b]
             if square:
                 far[square - 1, q, rows_of(b), :] = total
             else:
                 near[0, q, rows_of(b), :] = total
 
 
-def pair_kernel(squares, keep_ref, got_ref, *refs):
+def pair_far_kernel(squares, keep_ref, got_ref, *refs):
     for s in range(squares):
         refs[4 * s][...] = keep_ref[s, 0] + got_ref[s, 0]
         for q in range(1, 4):
             refs[4 * s + q][...] = (keep_ref[s, q] + got_ref[s, q]).astype(BF16)
 
 
-def pair_far_kernel(squares, w0, w1, w2, w3, *refs):
-    refs[-1][...] = (w0[...] + w1[...]) + (w2[...] + w3[...])
-    pair_kernel(squares, *refs[:-1])
+def pair_near_kernel(keep_ref, got_ref, weight_ref, wgot_ref, own_ref, weight_out, *pieces):
+    nodes, lanes = own_ref.shape
+    weight = weight_ref[...] + wgot_ref[...]
+    rows = weight.shape[0]
+    high, low = split_bf16(weight)
+    weight_out[...] = high.astype(F32) + low.astype(F32)
+    own_ref[...] = keep_ref[0, 0] + got_ref[0, 0]
+    for q, ref in enumerate(pieces):
+        ref[pl.ds(0, nodes), :] = (keep_ref[0, q + 1] + got_ref[0, q + 1]).astype(BF16)
+        start = nodes
+        for part in (high, low):
+            for column in range(0, weight.shape[1], lanes):
+                ref[pl.ds(start, rows), :] = part[:, column:column + lanes]
+                start += rows
+
+
+def add_four_kernel(w0, w1, w2, w3, after_ref, out_ref):
+    del after_ref
+    out_ref[...] = (w0[...] + w1[...]) + (w2[...] + w3[...])
+
+
+def add_two_kernel(own_ref, got_ref, out_ref):
+    out_ref[...] = own_ref[...] + got_ref[...]
 
 
 def add_kernel(own_ref, *refs):
@@ -227,18 +239,31 @@
     refs[-1][...] = total.astype(BF16)
 
 
-def add_both_kernel(weight_ref, wgot_ref, own_ref, *refs):
-    refs[-1][...] = weight_ref[...] + wgot_ref[...]
-    add_kernel(own_ref, *refs[:-1])
-
-
-def last_kernel(index_ref, weight_ref, other_ref, base_ref, own_ref, *refs):
+def near_kernel(base_ref, own_ref, weight_ref, g1, g2, g3, out_ref, weights_out):
+    nodes, lanes = own_ref.shape
+    for b in range(nodes // BLOCK):
+        total = own_ref[rows_of(b), :]
+        for got_ref in (g1, g2, g3):
+            total = total + got_ref[rows_of(b), :].astype(F32)
+        out_ref[rows_of(b), :] = base_ref[rows_of(b), :] + jnp.transpose(total)
+    rows, columns = weight_ref.shape
+    cuts = columns // lanes
+    weights_out[0] = weight_ref[...]
+    for q, ref in enumerate((g1, g2, g3)):
+        for cut in range(cuts):
+            high = ref[pl.ds(nodes + cut * rows, rows), :]
+            low = ref[pl.ds(nodes + (cuts + cut) * rows, rows), :]
+            weights_out[q + 1, :, pl.ds(cut * lanes, lanes)] = (
+                high.astype(F32) + low.astype(F32))
+
+
+def last_kernel(index_ref, weight_ref, other_ref, near_ref, *refs):
     got_refs, (out_ref, self_ref, neigh_ref) = refs[:-3], refs[-3:]
-    for b in range(base_ref.shape[0] // BLOCK):
-        total = own_ref[rows_of(b), :]
-        for got_ref in got_refs:
+    for b in range(near_ref.shape[0] // BLOCK):
+        total = got_refs[0][rows_of(b), :].astype(F32)
+        for got_ref in got_refs[1:]:
             total = total + got_ref[rows_of(b), :].astype(F32)
-        out_ref[rows_of(b), :] = (base_ref[rows_of(b), :] + jnp.transpose(total)).astype(BF16)
+        out_ref[rows_of(b), :] = (near_ref[rows_of(b), :] + jnp.transpose(total)).astype(BF16)
     me = index_ref[index_ref.shape[0] - 1]
     first = me % 2 == 0
     chip = me // 2 % 4
@@ -258,8 +283,7 @@
     hidden = w_self.shape[1]
     block_local = nodes // BLOCK
     tile_count = tiles.shape[0]
-    half = tile_count // 2
-    group = max(g for g in range(1, 7) if half % g == 0)
+    group = max(g for g in range(1, 7) if tile_count % g == 0)
     small = n * nodes * feat_in * 4 <= 4 * MIB
     limit = (24 if small else 56) * MIB
 
@@ -281,7 +305,7 @@
             out_specs=out_specs or jax.tree.map(lambda _: VMEM, out_shape),
             compiler_params=pltpu.CompilerParams(vmem_limit_bytes=limit),
             cost_estimate=pl.CostEstimate(
-                flops=0, bytes_accessed=int(cost_us * 3.6e6), transcendentals=0),
+                flops=int(cost_us * 1.1e9), bytes_accessed=int(cost_us * 3.6e6), transcendentals=0),
             name=name,
             **more,
         )(*[placed(x, spec) for x, spec in zip(operands, specs)])
@@ -297,7 +321,7 @@
     )
     if small:
         own_arguments = [pltpu.with_memory_space_constraint(x, pltpu.HBM) for x in own_arguments]
-    tiles_near, ws, wn, degree_wide, upstream, pre_self, feat_t, index = pl.pallas_call(
+    tiles_near, ws, wn, degree_wide, upstream, pre_self, feat_t, own, index = pl.pallas_call(
         stage_kernel,
         out_shape=(
             result(tiles.shape, BF16),
@@ -307,17 +331,18 @@
             result((nodes, hidden), F32),
             result((nodes, hidden), F32),
             result(by_block, BF16),
+            piece,
             jax.ShapeDtypeStruct((2 * tile_count + 1,), jnp.int32),
         ),
         in_specs=[SMEM] * 3 + [VMEM] * 6 + [ANY],
-        out_specs=(VMEM,) * 7 + (SMEM,),
+        out_specs=(VMEM,) * 8 + (SMEM,),
         scratch_shapes=[pltpu.SemaphoreType.DMA],
         compiler_params=pltpu.CompilerParams(vmem_limit_bytes=limit),
-        cost_estimate=pl.CostEstimate(flops=0, bytes_accessed=int(3 * 3.6e6), transcendentals=0),
+        cost_estimate=pl.CostEstimate(flops=int(3 * 1.1e9), bytes_accessed=int(3 * 3.6e6), transcendentals=0),
         name="stage_arguments",
     )(me, tile_row, tile_col, *own_arguments, placed(tiles, ANY))
 
-    same, other = gather_by_xor(features, n, call, result((4, nodes, feat_in), BF16))
+    same, other = gather_by_xor(features, own, n, call, result((4, nodes, feat_in), BF16))
     operands = (index, tiles_near, ws, wn, degree_wide, upstream, pre_self, feat_t, *same, *other)
     embedded, base, wkeep, wsend, gt = call(
         functools.partial(forward_kernel, n, group),
@@ -336,61 +361,61 @@
         ],
     )
 
-    wgot = swap(wsend, n, 1)
-    acc_shape = (n * block_local + 1, feat_in, BLOCK)
+    acc_shape = result((n * block_local + 1, feat_in, BLOCK), F32)
     acc = call(
-        functools.partial(backward_first_kernel, half, group),
-        "backward_first", result(acc_shape, F32), (index, tiles_near, gt), [SMEM, VMEM, VMEM],
-        cost_us=2.5,
-    )
-    far = result((max(squares - 1, 1), 4, nodes, feat_in), F32)
+        functools.partial(backward_kernel, group), "backward_tiles", acc_shape,
+        (index, tiles_near, gt), [SMEM, VMEM, VMEM], cost_us=3.5,
+    )
+    far = result((squares - 1, 4, nodes, feat_in), F32)
     near = result((1, 4, nodes, feat_in), F32)
-    far_send, near_send, far_keep, near_keep, *w = call(
-        functools.partial(backward_second_kernel, n, half, group),
-        "backward_second", (far, near, far, near) + (chunk,) * 4,
-        (index, tiles_near, gt, wkeep, wgot, acc), [SMEM] + [VMEM] * 5, cost_us=2.5,
-        scratch_shapes=[pltpu.VMEM(acc_shape, F32)],
-    )
-
-    count = squares - 1
-    *far_sums, wsum = call(
-        functools.partial(pair_far_kernel, count), "pair_sum_far",
-        (wide, piece, piece, piece) * count + (chunk,),
-        (w[0], *[swap(w[p], n, 2 * p) for p in (1, 2, 3)], far_keep, swap(far_send, n, 1)),
-    )
-    near_sums = call(
-        functools.partial(pair_kernel, 1), "pair_sum_near", (wide, piece, piece, piece),
-        (near_keep, swap(near_send, n, 1)),
-    )
-    sums = [*near_sums, *far_sums]
-    terms = [
-        [sums[4 * s], *[swap(sums[4 * s + q], n, 2 * q) for q in (1, 2, 3)]]
-        for s in range(squares)
+    far_send, near_send, far_keep, near_keep, *parts = call(
+        functools.partial(split_kernel, n, block_local), "split_sums",
+        (far, near, far, near) + (chunk,) * 4,
+        (index, acc, wkeep, swap(wsend, n, 1)), [SMEM] + [VMEM] * 3, cost_us=0.8,
+    )
+
+    far_sums = call(
+        functools.partial(pair_far_kernel, squares - 1), "pair_sum_far",
+        (wide, piece, piece, piece) * (squares - 1), (far_keep, swap(far_send, n, 1)),
+    )
+    wsum = call(
+        add_four_kernel, "weight_square_sum", chunk,
+        (parts[0], *[swap(parts[p], n, 2 * p) for p in (1, 2, 3)], far_sums[0]),
+        cost_us=WEIGHT_COST,
+    )
+    bit = 8
+    while 2 * bit < n:
+        wsum = call(add_two_kernel, "weight_sum", chunk, (wsum, swap(wsum, n, bit)))
+        bit *= 2
+    extra = result((nodes + 2 * chunk.shape[0] * (hidden // feat_in), feat_in), BF16)
+    near_own, wsum, *near_pieces = call(
+        pair_near_kernel, "pair_sum_near", (wide, chunk, extra, extra, extra),
+        (near_keep, swap(near_send, n, 1), wsum, swap(wsum, n, bit)),
+    )
+    near_sum, mine = call(
+        near_kernel, "near_sum", (wide, result((4,) + chunk.shape, F32)),
+        (base, near_own, wsum, *[swap(x, n, 2 * q + 2) for q, x in enumerate(near_pieces)]),
+        cost_us=NEAR_COST,
+    )
+    terms = [[near_sum]] + [
+        [far_sums[4 * s], *[swap(far_sums[4 * s + q], n, 2 * q) for q in (1, 2, 3)]]
+        for s in range(squares - 1)
     ]
     distance = 1
     while distance < squares:
-        wgot = swap(wsum, n, 8 * distance)
         for s in range(squares - distance, 0, -2 * distance):
-            if s == squares - distance:
-                total, wsum = call(
-                    add_both_kernel, "square_sum", (piece, chunk), (wsum, wgot, *terms[s]))
-            else:
-                total = call(add_kernel, "square_sum", piece, terms[s])
+            total = call(add_kernel, "square_sum", piece, terms[s], cost_us=SQUARE_COST)
             terms[s - distance].append(swap(total, n, 8 * distance))
         distance *= 2
 
-    mine = call(
-        pack_kernel, "pack_weights", result((4, feat_in // 4, hidden), F32),
-        (wsum, *[swap(wsum, n, 2 * p) for p in (1, 2, 3)]),
-    )
     grad_input, grad_self, grad_neigh = call(
         last_kernel, "grad_input_sum",
         (
             result((nodes, feat_in), BF16, False), result((feat_in, hidden), F32, False),
             result((feat_in, hidden), F32, False),
         ),
-        (index, mine, swap(mine, n, 1), base, *terms[0]),
-        [SMEM] + [VMEM] * (3 + len(terms[0])),
+        (index, mine, swap(mine, n, 1), *terms[0]),
+        [SMEM] + [VMEM] * (2 + len(terms[0])),
     )
     return (embedded, grad_input, grad_self, grad_neigh)
 

time: 68.6 us -> 62.2 us (0.907)
  starting transfers between devices: 32 us -> 28.6 us
  waiting for transfers between devices: 19.9 us -> 17 us
    ppermute x27 -> x24, starting transfers between devices: 32 us -> 28.6 us  [swap(): return lax.ppermute(x, 'row', [(i, i ^ offset) for i in range(n)])]
    ppermute x27 -> x24, waiting for transfers between devices: 19.9 us -> 17 us  [swap(): return lax.ppermute(x, 'row', [(i, i ^ offset) for i in range(n)])]
    pallas_call x10 -> x11, Pallas kernels: 11.6 us -> 11.1 us  [call(): pl.pallas_call(kernel, out_shape=out_shape, in_specs=specs, out_specs=out...]
  transfers between devices with their start and end apart: 27 -> 24, of which waited for: 12 -> 9; matrix products, arithmetic and copies ran while one was open for 0% -> 0% of each run, Pallas kernels for 8% -> 12%
where the time goes in v4:
time: 62.2 us; the launch traced here: 62 us
  starting transfers between devices  28.6 us (46%)
  waiting for transfers between devices  17 us (27%)
  Pallas kernels  14.4 us (23%)
  local copies, waits for them, and re-layouts  1.31 us (2%)
  between operations  0.77 us (1%)
    ppermute x24, starting transfers between devices, swap(): return lax.ppermute(x, 'row', [(i, i ^ offset) for i in range(n)])  28.6 us
    ppermute x24, waiting for transfers between devices, swap(): return lax.ppermute(x, 'row', [(i, i ^ offset) for i in range(n)])  17 us
    pallas_call x11, Pallas kernels, call(): pl.pallas_call(kernel, out_shape=out_shape, in_specs=specs, out_specs=out...  11.1 us
    pallas_call x1, Pallas kernels, body(): pl.pallas_call(stage_kernel, out_shape=(result(tiles.shape, BF16), result...  3.27 us
    unnamed x4, local copies, waits for them, and re-layouts  1.31 us
  transfers between devices with their start and end apart: 24, of which 9 were waited for; matrix products, arithmetic and copies ran while one was open for 0% of the time, Pallas kernels for 12%

profile of v4, /device:TPU:0, one launch (start us, length us, event | category | flops | bytes accessed | tf_op | source)
XLA Modules:
  0.0 62.0 jit_solution(7159096886940908569)
XLA Ops:
  0.6 4.1 %collective-permute-start.3 = (bf16[512,128]{1,0:T(8,128)(2,1)}, bf16[512,128]{1,0:T(8,128)(2,1)S(1)}, u32[]{:S(2)}, u32[]{:S(2)}) collective-permute-start(bf16[512,128]{1,0:T(8,128)(2,1)} %feat_ref.1), channel_id=1, source_target_pairs={{0,8},{1,9},{2,10},{3,11},{4,12},{5,13},{6,14},{7,15},{8,0},{9,1},... | collective-permute-start | bytes 393224 | tf_op jit(solution)/shard_map/ppermute | solution.py:21
  4.7 1.6 %collective-permute-start.1 = (bf16[512,128]{1,0:T(8,128)(2,1)}, bf16[512,128]{1,0:T(8,128)(2,1)S(1)}, u32[]{:S(2)}, u32[]{:S(2)}) collective-permute-start(bf16[512,128]{1,0:T(8,128)(2,1)} %feat_ref.1), channel_id=1, source_target_pairs={{0,4},{1,5},{2,6},{3,7},{4,0},{5,1},{6,2},{7,3},{8,12},{9,13},{10,... | collective-permute-start | bytes 393224 | tf_op jit(solution)/shard_map/ppermute | solution.py:21
  6.3 1.5 %collective-permute-start = (bf16[512,128]{1,0:T(8,128)(2,1)}, bf16[512,128]{1,0:T(8,128)(2,1)S(1)}, u32[]{:S(2)}, u32[]{:S(2)}) collective-permute-start(bf16[512,128]{1,0:T(8,128)(2,1)} %feat_ref.1), channel_id=1, source_target_pairs={{0,2},{1,3},{2,0},{3,1},{4,6},{5,7},{6,4},{7,5},{8,10},{9,11},{10,... | collective-permute-start | bytes 393224 | tf_op jit(solution)/shard_map/ppermute | solution.py:21
  7.8 0.4 collective-permute-start.2
  8.2 3.1 %collective-permute-done.3.refs_0_ = bf16[512,128]{1,0:T(8,128)(2,1)S(1)} collective-permute-done((bf16[512,128]{1,0:T(8,128)(2,1)}, bf16[512,128]{1,0:T(8,128)(2,1)S(1)}, u32[]{:S(2)}, u32[]{:S(2)}) %collective-permute-start.3) | collective-permute-done | bytes 131104 | tf_op jit(solution)/shard_map/ppermute | solution.py:21
  11.4 1.7 %collective-permute-start.6 = (bf16[512,128]{1,0:T(8,128)(2,1)S(1)}, bf16[512,128]{1,0:T(8,128)(2,1)S(1)}, u32[]{:S(2)}, u32[]{:S(2)}) collective-permute-start(bf16[512,128]{1,0:T(8,128)(2,1)S(1)} %collective-permute-done.3.refs_0_), channel_id=1, source_target_pairs={{0,6},{1,7},{2,4},{3,5},{4,2},{5,3},{6,0},{7,1},{8,14},{9,15},{10,... | collective-permute-start | bytes 393224 | tf_op jit(solution)/shard_map/ppermute | solution.py:21
  13.1 1.3 %collective-permute-start.5 = (bf16[512,128]{1,0:T(8,128)(2,1)S(1)}, bf16[512,128]{1,0:T(8,128)(2,1)S(1)}, u32[]{:S(2)}, u32[]{:S(2)}) collective-permute-start(bf16[512,128]{1,0:T(8,128)(2,1)S(1)} %collective-permute-done.3.refs_0_), channel_id=1, source_target_pairs={{0,4},{1,5},{2,6},{3,7},{4,0},{5,1},{6,2},{7,3},{8,12},{9,13},{10,... | collective-permute-start | bytes 393224 | tf_op jit(solution)/shard_map/ppermute | solution.py:21
  14.4 0.5 collective-permute-start.4
  14.8 0.7 %copy-done = s32[60]{0:T(128)S(1)} copy-done((s32[60]{0:T(128)S(1)}, s32[60]{0:T(128)}, u32[]{:S(2)}) %copy-start) | copy-done | bytes 264
  15.5 0.7 %copy-done.1 = s32[60]{0:T(128)S(1)} copy-done((s32[60]{0:T(128)S(1)}, s32[60]{0:T(128)}, u32[]{:S(2)}) %copy-start.1) | copy-done | bytes 264
  16.2 3.3 %stage_arguments.1 = (bf16[60,128,128]{2,1,0:T(8,128)(2,1)S(1)}, bf16[128,256]{1,0:T(8,128)(2,1)S(1)}, bf16[128,256]{1,0:T(8,128)(2,1)S(1)}, f32[4,128,128]{2,1,...) custom-call(s32[1]{0:T(128)} %bitcast.me_ref, ...), custom_call_target="tpu_custom_call" | custom-call | flops 3300000000 | bytes 10800000 | tf_op jit(solution)/shard_map/stage_arguments/pallas_call | solution.py:324
  19.4 0.0 collective-permute-done.2.refs_3_
  19.5 0.1 collective-permute-start.7
  19.6 0.4 collective-permute-done.5.refs_2_
  20.0 1.0 %collective-permute-done.4.refs_1_ = bf16[512,128]{1,0:T(8,128)(2,1)S(1)} collective-permute-done((bf16[512,128]{1,0:T(8,128)(2,1)S(1)}, bf16[512,128]{1,0:T(8,128)(2,1)S(1)}, u32[]{:S(2)}, u32[]{:S(2)}) %collective-permute-start.4) | collective-permute-done | bytes 131104 | tf_op jit(solution)/shard_map/ppermute | solution.py:21
  21.0 0.1 collective-permute-start.8
  21.1 0.4 collective-permute-done.7.refs_2_
  21.5 1.5 %collective-permute-done.8.refs_3_ = bf16[4,512,128]{2,1,0:T(8,128)(2,1)S(1)} collective-permute-done((bf16[4,512,128]{2,1,0:T(8,128)(2,1)S(1)}, bf16[4,512,128]{2,1,0:T(8,128)(2,1)S(1)}, u32[]{:S(2)}, u32[]{:S(2)}) %collective-permute-start.8) | collective-permute-done | bytes 524320 | tf_op jit(solution)/shard_map/ppermute | solution.py:21
  23.0 5.0 %forward_layer.1 = (bf16[512,256]{1,0:T(8,128)(2,1)}, f32[512,128]{1,0:T(8,128)S(1)}, f32[128,256]{1,0:T(8,128)S(1)}, f32[128,256]{1,0:T(8,128)S(1)}, bf16[4,256,128]{2,1,0:T(8,128)(2,1)S(1)}) custom-call(s32[121]{0:T(128)S(1)} %get-tuple-element.40.index_ref, bf16[60,128,128]{2,1,0:T(8,128)(2,1)S(1)} %get-tuple-element.41.tiles_ref, ...), custom_call_target="tpu_custom_call" | custom-call | flops 5500000256 | bytes 18000000 | tf_op jit(solution)/shard_map/forward_layer/pallas_call | solution.py:301
  28.0 0.1 collective-permute-start.9
  28.2 3.4 %backward_tiles.1.acc_ref = f32[65,128,128]{2,1,0:T(8,128)S(1)} custom-call(s32[121]{0:T(128)S(1)} %get-tuple-element.40.index_ref, bf16[60,128,128]{2,1,0:T(8,128)(2,1)S(1)} %get-tuple-element.41.tiles_ref, bf16[4,256,128]{2,1,0:T(8,128)(2,1)S(1)} %get-tuple-element.51.gt_ref), custom_call_target="tpu_custom_call" | custom-call | flops 3849999872 | bytes 12600000 | tf_op jit(solution)/shard_map/backward_tiles/pallas_call | solution.py:301
  31.6 0.0 collective-permute-done.9.wgot_ref
  31.6 0.8 %split_sums.1 = (f32[1,4,512,128]{3,2,1,0:T(8,128)S(1)}, f32[1,4,512,128]{3,2,1,0:T(8,128)S(1)}, f32[1,4,512,128]{3,2,1,0:T(8,128)S(1)}, f32[1,4,512,128]{3,2,1,...) custom-call(s32[121]{0:T(128)S(1)} %get-tuple-element.40.index_ref, ...), custom_call_target="tpu_custom_call" | custom-call | flops 880000000 | bytes 2880000 | tf_op jit(solution)/shard_map/split_sums/pallas_call | solution.py:301
  32.4 0.4 collective-permute-start.14
  32.9 0.1 collective-permute-start.10
  33.0 0.8 %collective-permute-start.11 = (f32[32,256]{1,0:T(8,128)S(1)}, f32[32,256]{1,0:T(8,128)S(1)}, u32[]{:S(2)}, u32[]{:S(2)}) collective-permute-start(f32[32,256]{1,0:T(8,128)S(1)} %get-tuple-element.57), channel_id=1, source_target_pairs={{0,2},{1,3},{2,0},{3,1},{4,6},{5,7},{6,4},{7,5},{8,10},{9,11},{10,... | collective-permute-start | bytes 98312 | tf_op jit(solution)/shard_map/ppermute | solution.py:21
  33.8 1.2 %collective-permute-start.12 = (f32[32,256]{1,0:T(8,128)S(1)}, f32[32,256]{1,0:T(8,128)S(1)}, u32[]{:S(2)}, u32[]{:S(2)}) collective-permute-start(f32[32,256]{1,0:T(8,128)S(1)} %get-tuple-element.58), channel_id=1, source_target_pairs={{0,4},{1,5},{2,6},{3,7},{4,0},{5,1},{6,2},{7,3},{8,12},{9,13},{10,... | collective-permute-start | bytes 98312 | tf_op jit(solution)/shard_map/ppermute | solution.py:21
  35.0 1.5 %collective-permute-start.13 = (f32[32,256]{1,0:T(8,128)S(1)}, f32[32,256]{1,0:T(8,128)S(1)}, u32[]{:S(2)}, u32[]{:S(2)}) collective-permute-start(f32[32,256]{1,0:T(8,128)S(1)} %get-tuple-element.59), channel_id=1, source_target_pairs={{0,6},{1,7},{2,4},{3,5},{4,2},{5,3},{6,0},{7,1},{8,14},{9,15},{10,... | collective-permute-start | bytes 98312 | tf_op jit(solution)/shard_map/ppermute | solution.py:21
  36.5 0.0 collective-permute-done.14.got_ref
  36.5 0.1 pair_sum_far.1
  36.6 0.9 %collective-permute-start.20 = (bf16[512,128]{1,0:T(8,128)(2,1)S(1)}, bf16[512,128]{1,0:T(8,128)(2,1)S(1)}, u32[]{:S(2)}, u32[]{:S(2)}) collective-permute-start(bf16[512,128]{1,0:T(8,128)(2,1)S(1)} %get-tuple-element.70), channel_id=1, source_target_pairs={{0,2},{1,3},{2,0},{3,1},{4,6},{5,7},{6,4},{7,5},{8,10},{9,11},{10,... | collective-permute-start | bytes 393224 | tf_op jit(solution)/shard_map/ppermute | solution.py:21
  37.5 1.2 %collective-permute-start.21 = (bf16[512,128]{1,0:T(8,128)(2,1)S(1)}, bf16[512,128]{1,0:T(8,128)(2,1)S(1)}, u32[]{:S(2)}, u32[]{:S(2)}) collective-permute-start(bf16[512,128]{1,0:T(8,128)(2,1)S(1)} %get-tuple-element.71), channel_id=1, source_target_pairs={{0,4},{1,5},{2,6},{3,7},{4,0},{5,1},{6,2},{7,3},{8,12},{9,13},{10,... | collective-permute-start | bytes 393224 | tf_op jit(solution)/shard_map/ppermute | solution.py:21
  38.7 0.0 collective-permute-done.12.w2
  38.7 1.5 %collective-permute-start.22 = (bf16[512,128]{1,0:T(8,128)(2,1)S(1)}, bf16[512,128]{1,0:T(8,128)(2,1)S(1)}, u32[]{:S(2)}, u32[]{:S(2)}) collective-permute-start(bf16[512,128]{1,0:T(8,128)(2,1)S(1)} %get-tuple-element.72), channel_id=1, source_target_pairs={{0,6},{1,7},{2,4},{3,5},{4,2},{5,3},{6,0},{7,1},{8,14},{9,15},{10,... | collective-permute-start | bytes 393224 | tf_op jit(solution)/shard_map/ppermute | solution.py:21
  40.2 3.1 %collective-permute-start.15 = (f32[32,256]{1,0:T(8,128)S(1)}, f32[32,256]{1,0:T(8,128)S(1)}, u32[]{:S(2)}, u32[]{:S(2)}) collective-permute-start(f32[32,256]{1,0:T(8,128)S(1)} %weight_square_sum.1.weight_ref), channel_id=1, source_target_pairs={{0,8},{1,9},{2,10},{3,11},{4,12},{5,13},{6,14},{7,15},{8,0},{9,1},... | collective-permute-start | bytes 98312 | tf_op jit(solution)/shard_map/ppermute | solution.py:21
  43.3 2.0 %collective-permute-done.15.wgot_ref = f32[32,256]{1,0:T(8,128)S(1)} collective-permute-done((f32[32,256]{1,0:T(8,128)S(1)}, f32[32,256]{1,0:T(8,128)S(1)}, u32[]{:S(2)}, u32[]{:S(2)}) %collective-permute-start.15) | collective-permute-done | bytes 32800 | tf_op jit(solution)/shard_map/ppermute | solution.py:21
  45.3 0.1 pair_sum_near.1
  45.4 1.4 %collective-permute-start.16 = (bf16[640,128]{1,0:T(8,128)(2,1)S(1)}, bf16[640,128]{1,0:T(8,128)(2,1)S(1)}, u32[]{:S(2)}, u32[]{:S(2)}) collective-permute-start(bf16[640,128]{1,0:T(8,128)(2,1)S(1)} %get-tuple-element.65), channel_id=1, source_target_pairs={{0,2},{1,3},{2,0},{3,1},{4,6},{5,7},{6,4},{7,5},{8,10},{9,11},{10,... | collective-permute-start | bytes 491528 | tf_op jit(solution)/shard_map/ppermute | solution.py:21
  46.8 2.5 %collective-permute-start.17 = (bf16[640,128]{1,0:T(8,128)(2,1)S(1)}, bf16[640,128]{1,0:T(8,128)(2,1)S(1)}, u32[]{:S(2)}, u32[]{:S(2)}) collective-permute-start(bf16[640,128]{1,0:T(8,128)(2,1)S(1)} %get-tuple-element.66), channel_id=1, source_target_pairs={{0,4},{1,5},{2,6},{3,7},{4,0},{5,1},{6,2},{7,3},{8,12},{9,13},{10,... | collective-permute-start | bytes 491528 | tf_op jit(solution)/shard_map/ppermute | solution.py:21
  49.3 0.7 %collective-permute-start.18 = (bf16[640,128]{1,0:T(8,128)(2,1)S(1)}, bf16[640,128]{1,0:T(8,128)(2,1)S(1)}, u32[]{:S(2)}, u32[]{:S(2)}) collective-permute-start(bf16[640,128]{1,0:T(8,128)(2,1)S(1)} %get-tuple-element.67), channel_id=1, source_target_pairs={{0,6},{1,7},{2,4},{3,5},{4,2},{5,3},{6,0},{7,1},{8,14},{9,15},{10,... | collective-permute-start | bytes 491528 | tf_op jit(solution)/shard_map/ppermute | solution.py:21
  50.0 0.1 square_sum.1
  50.0 1.9 %collective-permute-start.23 = (bf16[512,128]{1,0:T(8,128)(2,1)S(1)}, bf16[512,128]{1,0:T(8,128)(2,1)S(1)}, u32[]{:S(2)}, u32[]{:S(2)}) collective-permute-start(bf16[512,128]{1,0:T(8,128)(2,1)S(1)} %square_sum.1), channel_id=1, source_target_pairs={{0,8},{1,9},{2,10},{3,11},{4,12},{5,13},{6,14},{7,15},{8,0},{9,1},... | collective-permute-start | bytes 393224 | tf_op jit(solution)/shard_map/ppermute | solution.py:21
  51.9 5.2 %collective-permute-done.17.g2 = bf16[640,128]{1,0:T(8,128)(2,1)S(1)} collective-permute-done((bf16[640,128]{1,0:T(8,128)(2,1)S(1)}, bf16[640,128]{1,0:T(8,128)(2,1)S(1)}, u32[]{:S(2)}, u32[]{:S(2)}) %collective-permute-start.17) | collective-permute-done | bytes 163872 | tf_op jit(solution)/shard_map/ppermute | solution.py:21
  57.1 2.0 %collective-permute-done.18.g3 = bf16[640,128]{1,0:T(8,128)(2,1)S(1)} collective-permute-done((bf16[640,128]{1,0:T(8,128)(2,1)S(1)}, bf16[640,128]{1,0:T(8,128)(2,1)S(1)}, u32[]{:S(2)}, u32[]{:S(2)}) %collective-permute-start.18) | collective-permute-done | bytes 163872 | tf_op jit(solution)/shard_map/ppermute | solution.py:21
  59.1 0.1 near_sum.1
  59.3 0.1 collective-permute-start.19
  59.4 1.3 %collective-permute-done.19.other_ref = f32[4,32,256]{2,1,0:T(8,128)S(1)} collective-permute-done((f32[4,32,256]{2,1,0:T(8,128)S(1)}, f32[4,32,256]{2,1,0:T(8,128)S(1)}, u32[]{:S(2)}, u32[]{:S(2)}) %collective-permute-start.19) | collective-permute-done | bytes 131104 | tf_op jit(solution)/shard_map/ppermute | solution.py:21
  60.7 1.3 %grad_input_sum.1 = (bf16[512,128]{1,0:T(8,128)(2,1)}, f32[128,256]{1,0:T(8,128)}, f32[128,256]{1,0:T(8,128)}) custom-call(s32[121]{0:T(128)S(1)} %get-tuple-element.40.index_ref, f32[4,32,256]{2,1,0:T(8,128)S(1)} %get-tuple-element.68.weight_ref, f32[4,32,256]{2,1,0:T(8,128)S(1)} %collective-permute-done.19.other_ref, ...), custom_call_target="tpu_custom_call" | custom-call | flops 220000000 | bytes 720000 | tf_op jit(solution)/shard_map/grad_input_sum/pallas_call | solution.py:301
  (16 shorter events, 0.1 us)
Async XLA Ops:
  0.6 10.7 %collective-permute-start.3 = (bf16[512,128]{1,0:T(8,128)(2,1)}, bf16[512,128]{1,0:T(8,128)(2,1)S(1)}, u32[]{:S(2)}, u32[]{:S(2)}) collective-permute-start(bf16[512,128]{1,0:T(8,128)(2,1)} %feat_ref.1), channel_id=1, source_target_pairs={{0,8},{1,9},{2,10},{3,11},{4,12},{5,13},{6,14},{7,15},{8,0},{9,1},... | collective-permute-start | bytes 393224 | tf_op jit(solution)/shard_map/ppermute | solution.py:21
  4.7 9.7 %collective-permute-start.1 = (bf16[512,128]{1,0:T(8,128)(2,1)}, bf16[512,128]{1,0:T(8,128)(2,1)S(1)}, u32[]{:S(2)}, u32[]{:S(2)}) collective-permute-start(bf16[512,128]{1,0:T(8,128)(2,1)} %feat_ref.1), channel_id=1, source_target_pairs={{0,4},{1,5},{2,6},{3,7},{4,0},{5,1},{6,2},{7,3},{8,12},{9,13},{10,... | collective-permute-start | bytes 393224 | tf_op jit(solution)/shard_map/ppermute | solution.py:21
  6.3 13.1 %collective-permute-start = (bf16[512,128]{1,0:T(8,128)(2,1)}, bf16[512,128]{1,0:T(8,128)(2,1)S(1)}, u32[]{:S(2)}, u32[]{:S(2)}) collective-permute-start(bf16[512,128]{1,0:T(8,128)(2,1)} %feat_ref.1), channel_id=1, source_target_pairs={{0,2},{1,3},{2,0},{3,1},{4,6},{5,7},{6,4},{7,5},{8,10},{9,11},{10,... | collective-permute-start | bytes 393224 | tf_op jit(solution)/shard_map/ppermute | solution.py:21
  7.8 11.6 %collective-permute-start.2 = (bf16[512,128]{1,0:T(8,128)(2,1)}, bf16[512,128]{1,0:T(8,128)(2,1)S(1)}, u32[]{:S(2)}, u32[]{:S(2)}) collective-permute-start(bf16[512,128]{1,0:T(8,128)(2,1)} %feat_ref.1), channel_id=1, source_target_pairs={{0,6},{1,7},{2,4},{3,5},{4,2},{5,3},{6,0},{7,1},{8,14},{9,15},{10,... | collective-permute-start | bytes 393224 | tf_op jit(solution)/shard_map/ppermute | solution.py:21
  11.4 8.2 %collective-permute-start.6 = (bf16[512,128]{1,0:T(8,128)(2,1)S(1)}, bf16[512,128]{1,0:T(8,128)(2,1)S(1)}, u32[]{:S(2)}, u32[]{:S(2)}) collective-permute-start(bf16[512,128]{1,0:T(8,128)(2,1)S(1)} %collective-permute-done.3.refs_0_), channel_id=1, source_target_pairs={{0,6},{1,7},{2,4},{3,5},{4,2},{5,3},{6,0},{7,1},{8,14},{9,15},{10,... | collective-permute-start | bytes 393224 | tf_op jit(solution)/shard_map/ppermute | solution.py:21
  13.1 6.9 %collective-permute-start.5 = (bf16[512,128]{1,0:T(8,128)(2,1)S(1)}, bf16[512,128]{1,0:T(8,128)(2,1)S(1)}, u32[]{:S(2)}, u32[]{:S(2)}) collective-permute-start(bf16[512,128]{1,0:T(8,128)(2,1)S(1)} %collective-permute-done.3.refs_0_), channel_id=1, source_target_pairs={{0,4},{1,5},{2,6},{3,7},{4,0},{5,1},{6,2},{7,3},{8,12},{9,13},{10,... | collective-permute-start | bytes 393224 | tf_op jit(solution)/shard_map/ppermute | solution.py:21
  14.4 6.6 %collective-permute-start.4 = (bf16[512,128]{1,0:T(8,128)(2,1)S(1)}, bf16[512,128]{1,0:T(8,128)(2,1)S(1)}, u32[]{:S(2)}, u32[]{:S(2)}) collective-permute-start(bf16[512,128]{1,0:T(8,128)(2,1)S(1)} %collective-permute-done.3.refs_0_), channel_id=1, source_target_pairs={{0,2},{1,3},{2,0},{3,1},{4,6},{5,7},{6,4},{7,5},{8,10},{9,11},{10,... | collective-permute-start | bytes 393224 | tf_op jit(solution)/shard_map/ppermute | solution.py:21
  14.8 0.7 %copy-start = (s32[60]{0:T(128)S(1)}, s32[60]{0:T(128)}, u32[]{:S(2)}) copy-start(s32[60]{0:T(128)} %trow_ref.1) | copy-start | bytes 724
  15.5 0.7 %copy-start.1 = (s32[60]{0:T(128)S(1)}, s32[60]{0:T(128)}, u32[]{:S(2)}) copy-start(s32[60]{0:T(128)} %tcol_ref.1) | copy-start | bytes 724
  19.5 2.0 %collective-permute-start.7 = (bf16[4,512,128]{2,1,0:T(8,128)(2,1)S(1)}, bf16[4,512,128]{2,1,0:T(8,128)(2,1)S(1)}, u32[]{:S(2)}, u32[]{:S(2)}) collective-permute-start(bf16[4,512,128]{2,1,0:T(8,128)(2,1)S(1)} %pack_square.2.refs_0_), channel_id=1, source_target_pairs={{0,1},{1,0},{2,3},{3,2},{4,5},{5,4},{6,7},{7,6},{8,9},{9,8},{10,11... | collective-permute-start | bytes 1572872 | tf_op jit(solution)/shard_map/ppermute | solution.py:21
  21.0 2.0 %collective-permute-start.8 = (bf16[4,512,128]{2,1,0:T(8,128)(2,1)S(1)}, bf16[4,512,128]{2,1,0:T(8,128)(2,1)S(1)}, u32[]{:S(2)}, u32[]{:S(2)}) collective-permute-start(bf16[4,512,128]{2,1,0:T(8,128)(2,1)S(1)} %pack_square.3.refs_1_), channel_id=1, source_target_pairs={{0,1},{1,0},{2,3},{3,2},{4,5},{5,4},{6,7},{7,6},{8,9},{9,8},{10,11... | collective-permute-start | bytes 1572872 | tf_op jit(solution)/shard_map/ppermute | solution.py:21
  28.0 3.6 %collective-permute-start.9 = (f32[128,256]{1,0:T(8,128)S(1)}, f32[128,256]{1,0:T(8,128)S(1)}, u32[]{:S(2)}, u32[]{:S(2)}) collective-permute-start(f32[128,256]{1,0:T(8,128)S(1)} %get-tuple-element.53), channel_id=1, source_target_pairs={{0,1},{1,0},{2,3},{3,2},{4,5},{5,4},{6,7},{7,6},{8,9},{9,8},{10,11... | collective-permute-start | bytes 393224 | tf_op jit(solution)/shard_map/ppermute | solution.py:21
  32.4 4.1 %collective-permute-start.14 = (f32[1,4,512,128]{3,2,1,0:T(8,128)S(1)}, f32[1,4,512,128]{3,2,1,0:T(8,128)S(1)}, u32[]{:S(2)}, u32[]{:S(2)}) collective-permute-start(f32[1,4,512,128]{3,2,1,0:T(8,128)S(1)} %get-tuple-element.61), channel_id=1, source_target_pairs={{0,1},{1,0},{2,3},{3,2},{4,5},{5,4},{6,7},{7,6},{8,9},{9,8},{10,11... | collective-permute-start | bytes 3145736 | tf_op jit(solution)/shard_map/ppermute | solution.py:21
  32.9 10.4 %collective-permute-start.10 = (f32[1,4,512,128]{3,2,1,0:T(8,128)S(1)}, f32[1,4,512,128]{3,2,1,0:T(8,128)S(1)}, u32[]{:S(2)}, u32[]{:S(2)}) collective-permute-start(f32[1,4,512,128]{3,2,1,0:T(8,128)S(1)} %get-tuple-element.55), channel_id=1, source_target_pairs={{0,1},{1,0},{2,3},{3,2},{4,5},{5,4},{6,7},{7,6},{8,9},{9,8},{10,11... | collective-permute-start | bytes 3145736 | tf_op jit(solution)/shard_map/ppermute | solution.py:21
  33.0 4.5 %collective-permute-start.11 = (f32[32,256]{1,0:T(8,128)S(1)}, f32[32,256]{1,0:T(8,128)S(1)}, u32[]{:S(2)}, u32[]{:S(2)}) collective-permute-start(f32[32,256]{1,0:T(8,128)S(1)} %get-tuple-element.57), channel_id=1, source_target_pairs={{0,2},{1,3},{2,0},{3,1},{4,6},{5,7},{6,4},{7,5},{8,10},{9,11},{10,... | collective-permute-start | bytes 98312 | tf_op jit(solution)/shard_map/ppermute | solution.py:21
  33.8 4.8 %collective-permute-start.12 = (f32[32,256]{1,0:T(8,128)S(1)}, f32[32,256]{1,0:T(8,128)S(1)}, u32[]{:S(2)}, u32[]{:S(2)}) collective-permute-start(f32[32,256]{1,0:T(8,128)S(1)} %get-tuple-element.58), channel_id=1, source_target_pairs={{0,4},{1,5},{2,6},{3,7},{4,0},{5,1},{6,2},{7,3},{8,12},{9,13},{10,... | collective-permute-start | bytes 98312 | tf_op jit(solution)/shard_map/ppermute | solution.py:21
  35.0 5.2 %collective-permute-start.13 = (f32[32,256]{1,0:T(8,128)S(1)}, f32[32,256]{1,0:T(8,128)S(1)}, u32[]{:S(2)}, u32[]{:S(2)}) collective-permute-start(f32[32,256]{1,0:T(8,128)S(1)} %get-tuple-element.59), channel_id=1, source_target_pairs={{0,6},{1,7},{2,4},{3,5},{4,2},{5,3},{6,0},{7,1},{8,14},{9,15},{10,... | collective-permute-start | bytes 98312 | tf_op jit(solution)/shard_map/ppermute | solution.py:21
  36.6 12.6 %collective-permute-start.20 = (bf16[512,128]{1,0:T(8,128)(2,1)S(1)}, bf16[512,128]{1,0:T(8,128)(2,1)S(1)}, u32[]{:S(2)}, u32[]{:S(2)}) collective-permute-start(bf16[512,128]{1,0:T(8,128)(2,1)S(1)} %get-tuple-element.70), channel_id=1, source_target_pairs={{0,2},{1,3},{2,0},{3,1},{4,6},{5,7},{6,4},{7,5},{8,10},{9,11},{10,... | collective-permute-start | bytes 393224 | tf_op jit(solution)/shard_map/ppermute | solution.py:21
  37.5 12.5 %collective-permute-start.21 = (bf16[512,128]{1,0:T(8,128)(2,1)S(1)}, bf16[512,128]{1,0:T(8,128)(2,1)S(1)}, u32[]{:S(2)}, u32[]{:S(2)}) collective-permute-start(bf16[512,128]{1,0:T(8,128)(2,1)S(1)} %get-tuple-element.71), channel_id=1, source_target_pairs={{0,4},{1,5},{2,6},{3,7},{4,0},{5,1},{6,2},{7,3},{8,12},{9,13},{10,... | collective-permute-start | bytes 393224 | tf_op jit(solution)/shard_map/ppermute | solution.py:21
  38.7 11.3 %collective-permute-start.22 = (bf16[512,128]{1,0:T(8,128)(2,1)S(1)}, bf16[512,128]{1,0:T(8,128)(2,1)S(1)}, u32[]{:S(2)}, u32[]{:S(2)}) collective-permute-start(bf16[512,128]{1,0:T(8,128)(2,1)S(1)} %get-tuple-element.72), channel_id=1, source_target_pairs={{0,6},{1,7},{2,4},{3,5},{4,2},{5,3},{6,0},{7,1},{8,14},{9,15},{10,... | collective-permute-start | bytes 393224 | tf_op jit(solution)/shard_map/ppermute | solution.py:21
  40.2 5.1 %collective-permute-start.15 = (f32[32,256]{1,0:T(8,128)S(1)}, f32[32,256]{1,0:T(8,128)S(1)}, u32[]{:S(2)}, u32[]{:S(2)}) collective-permute-start(f32[32,256]{1,0:T(8,128)S(1)} %weight_square_sum.1.weight_ref), channel_id=1, source_target_pairs={{0,8},{1,9},{2,10},{3,11},{4,12},{5,13},{6,14},{7,15},{8,0},{9,1},... | collective-permute-start | bytes 98312 | tf_op jit(solution)/shard_map/ppermute | solution.py:21
  45.4 6.5 %collective-permute-start.16 = (bf16[640,128]{1,0:T(8,128)(2,1)S(1)}, bf16[640,128]{1,0:T(8,128)(2,1)S(1)}, u32[]{:S(2)}, u32[]{:S(2)}) collective-permute-start(bf16[640,128]{1,0:T(8,128)(2,1)S(1)} %get-tuple-element.65), channel_id=1, source_target_pairs={{0,2},{1,3},{2,0},{3,1},{4,6},{5,7},{6,4},{7,5},{8,10},{9,11},{10,... | collective-permute-start | bytes 491528 | tf_op jit(solution)/shard_map/ppermute | solution.py:21
  46.8 10.3 %collective-permute-start.17 = (bf16[640,128]{1,0:T(8,128)(2,1)S(1)}, bf16[640,128]{1,0:T(8,128)(2,1)S(1)}, u32[]{:S(2)}, u32[]{:S(2)}) collective-permute-start(bf16[640,128]{1,0:T(8,128)(2,1)S(1)} %get-tuple-element.66), channel_id=1, source_target_pairs={{0,4},{1,5},{2,6},{3,7},{4,0},{5,1},{6,2},{7,3},{8,12},{9,13},{10,... | collective-permute-start | bytes 491528 | tf_op jit(solution)/shard_map/ppermute | solution.py:21
  49.3 9.9 %collective-permute-start.18 = (bf16[640,128]{1,0:T(8,128)(2,1)S(1)}, bf16[640,128]{1,0:T(8,128)(2,1)S(1)}, u32[]{:S(2)}, u32[]{:S(2)}) collective-permute-start(bf16[640,128]{1,0:T(8,128)(2,1)S(1)} %get-tuple-element.67), channel_id=1, source_target_pairs={{0,6},{1,7},{2,4},{3,5},{4,2},{5,3},{6,0},{7,1},{8,14},{9,15},{10,... | collective-permute-start | bytes 491528 | tf_op jit(solution)/shard_map/ppermute | solution.py:21
  50.0 9.3 %collective-permute-start.23 = (bf16[512,128]{1,0:T(8,128)(2,1)S(1)}, bf16[512,128]{1,0:T(8,128)(2,1)S(1)}, u32[]{:S(2)}, u32[]{:S(2)}) collective-permute-start(bf16[512,128]{1,0:T(8,128)(2,1)S(1)} %square_sum.1), channel_id=1, source_target_pairs={{0,8},{1,9},{2,10},{3,11},{4,12},{5,13},{6,14},{7,15},{8,0},{9,1},... | collective-permute-start | bytes 393224 | tf_op jit(solution)/shard_map/ppermute | solution.py:21
  59.3 1.4 %collective-permute-start.19 = (f32[4,32,256]{2,1,0:T(8,128)S(1)}, f32[4,32,256]{2,1,0:T(8,128)S(1)}, u32[]{:S(2)}, u32[]{:S(2)}) collective-permute-start(f32[4,32,256]{2,1,0:T(8,128)S(1)} %get-tuple-element.68.weight_ref), channel_id=1, source_target_pairs={{0,1},{1,0},{2,3},{3,2},{4,5},{5,4},{6,7},{7,6},{8,9},{9,8},{10,11... | collective-permute-start | bytes 393224 | tf_op jit(solution)/shard_map/ppermute | solution.py:21

commit v5 on v4

--- a/solution.py
+++ b/solution.py
@@ -14,7 +14,7 @@
 ANY = pl.BlockSpec(memory_space=pl.ANY)
 MIB = 1024 * 1024
 LAST = ((1,), (1,))
-NEAR_COST, SQUARE_COST, WEIGHT_COST = 1, 4, 8
+NEAR_COST, SQUARE_COST, MAIN_COST = 8, 4, 10
 
 
 def swap(x, n, offset):
@@ -35,8 +35,10 @@
     blocks = [v for _, v in sorted(zip(offsets, blocks), key=lambda pair: pair[0])]
     same = []
     for v in blocks:
-        square = (own if v is x else v, *[swap(v, n, offset) for offset in (2, 4, 6)])
-        same.append(call(pack_kernel, "pack_square", pack, square))
+        order = (2, 6, 4) if v is x else (6, 2, 4)
+        square = (own if v is x else v, *[swap(v, n, offset) for offset in order])
+        slots = (0, *[offset // 2 for offset in order])
+        same.append(call(functools.partial(pack_kernel, slots), "pack_square", pack, square))
     return same, [swap(v, n, 1) for v in same]
 
 
@@ -62,9 +64,9 @@
     return pl.ds(b * BLOCK, BLOCK)
 
 
-def pack_kernel(*refs):
-    for i, ref in enumerate(refs[:-1]):
-        refs[-1][i] = ref[...]
+def pack_kernel(slots, *refs):
+    for slot, ref in zip(slots, refs[:-1]):
+        refs[-1][slot] = ref[...]
 
 
 def stage_kernel(me_ref, trow_ref, tcol_ref, deg_ref, mask_ref, ws_ref, wn_ref, feat_ref, cot_ref,
@@ -182,50 +184,40 @@
     lax.fori_loop(0, tile_count // group, backward, 0)
 
 
-def split_kernel(n, block_local, index_ref, acc_ref, wkeep_ref, wgot_ref, far_send, near_send,
-                 far_keep, near_keep, *parts):
+def send_kernel(square, block_local, acc_ref, send_ref):
+    for q in range(4):
+        for b in range(block_local):
+            send_ref[q, rows_of(b), :] = acc_ref[(8 * square + 2 * q + 1) * block_local + b]
+
+
+def send_weights_kernel(square, block_local, index_ref, acc_ref, wkeep_ref, wgot_ref, send_ref,
+                        *parts):
+    send_kernel(square, block_local, acc_ref, send_ref)
     rows = parts[0].shape[0]
     chip = index_ref[index_ref.shape[0] - 1] // 2 % 4
     for p, ref in enumerate(parts):
         span = pl.ds(pl.multiple_of((chip ^ p) * rows, rows), rows)
         ref[...] = wkeep_ref[span, :] + wgot_ref[span, :]
-    for k in range(n):
-        square, q = k // 8, k // 2 % 4
-        near, far = (near_send, far_send) if k % 2 else (near_keep, far_keep)
+
+
+def pair_kernel(square, acc_ref, got_ref, own_ref, *pieces):
+    block_local = own_ref.shape[0] // BLOCK
+    for q, ref in enumerate((own_ref, *pieces)):
         for b in range(block_local):
-            total = acc_ref[k * block_local + b]
-            if square:
-                far[square - 1, q, rows_of(b), :] = total
-            else:
-                near[0, q, rows_of(b), :] = total
-
-
-def pair_far_kernel(squares, keep_ref, got_ref, *refs):
-    for s in range(squares):
-        refs[4 * s][...] = keep_ref[s, 0] + got_ref[s, 0]
-        for q in range(1, 4):
-            refs[4 * s + q][...] = (keep_ref[s, q] + got_ref[s, q]).astype(BF16)
-
-
-def pair_near_kernel(keep_ref, got_ref, weight_ref, wgot_ref, own_ref, weight_out, *pieces):
+            kept = acc_ref[(8 * square + 2 * q) * block_local + b]
+            ref[rows_of(b), :] = (kept + got_ref[q, rows_of(b), :]).astype(ref.dtype)
+
+
+def pair_weights_kernel(square, acc_ref, got_ref, w1, w2, w3, own_ref, *pieces):
+    pair_kernel(square, acc_ref, got_ref, own_ref, *pieces)
     nodes, lanes = own_ref.shape
-    weight = weight_ref[...] + wgot_ref[...]
-    rows = weight.shape[0]
-    high, low = split_bf16(weight)
-    weight_out[...] = high.astype(F32) + low.astype(F32)
-    own_ref[...] = keep_ref[0, 0] + got_ref[0, 0]
-    for q, ref in enumerate(pieces):
-        ref[pl.ds(0, nodes), :] = (keep_ref[0, q + 1] + got_ref[0, q + 1]).astype(BF16)
+    for weight_ref, ref in zip((w1, w2, w3), pieces):
+        rows, columns = weight_ref.shape
         start = nodes
-        for part in (high, low):
-            for column in range(0, weight.shape[1], lanes):
+        for part in split_bf16(weight_ref[...]):
+            for column in range(0, columns, lanes):
                 ref[pl.ds(start, rows), :] = part[:, column:column + lanes]
                 start += rows
-
-
-def add_four_kernel(w0, w1, w2, w3, after_ref, out_ref):
-    del after_ref
-    out_ref[...] = (w0[...] + w1[...]) + (w2[...] + w3[...])
 
 
 def add_two_kernel(own_ref, got_ref, out_ref):
@@ -239,38 +231,47 @@
     refs[-1][...] = total.astype(BF16)
 
 
-def near_kernel(base_ref, own_ref, weight_ref, g1, g2, g3, out_ref, weights_out):
+def add_weights_kernel(weight_ref, own_ref, *refs):
+    got_refs, (out_ref, weight_out) = refs[:-2], refs[-2:]
     nodes, lanes = own_ref.shape
-    for b in range(nodes // BLOCK):
-        total = own_ref[rows_of(b), :]
-        for got_ref in (g1, g2, g3):
-            total = total + got_ref[rows_of(b), :].astype(F32)
-        out_ref[rows_of(b), :] = base_ref[rows_of(b), :] + jnp.transpose(total)
+    add_kernel(own_ref, *[ref.at[pl.ds(0, nodes), :] for ref in got_refs], out_ref)
     rows, columns = weight_ref.shape
     cuts = columns // lanes
-    weights_out[0] = weight_ref[...]
-    for q, ref in enumerate((g1, g2, g3)):
-        for cut in range(cuts):
+    for cut in range(cuts):
+        span = pl.ds(cut * lanes, lanes)
+        total = weight_ref[:, span]
+        for ref in got_refs[:3]:
             high = ref[pl.ds(nodes + cut * rows, rows), :]
             low = ref[pl.ds(nodes + (cuts + cut) * rows, rows), :]
-            weights_out[q + 1, :, pl.ds(cut * lanes, lanes)] = (
-                high.astype(F32) + low.astype(F32))
-
-
-def last_kernel(index_ref, weight_ref, other_ref, near_ref, *refs):
-    got_refs, (out_ref, self_ref, neigh_ref) = refs[:-3], refs[-3:]
+            total = total + (high.astype(F32) + low.astype(F32))
+        weight_out[:, span] = total
+
+
+def near_kernel(base_ref, own_ref, *refs):
+    for b in range(own_ref.shape[0] // BLOCK):
+        total = own_ref[rows_of(b), :]
+        for got_ref in refs[:-1]:
+            total = total + got_ref[rows_of(b), :].astype(F32)
+        refs[-1][rows_of(b), :] = base_ref[rows_of(b), :] + jnp.transpose(total)
+
+
+def main_kernel(near_ref, *refs):
     for b in range(near_ref.shape[0] // BLOCK):
-        total = got_refs[0][rows_of(b), :].astype(F32)
-        for got_ref in got_refs[1:]:
+        total = refs[0][rows_of(b), :].astype(F32)
+        for got_ref in refs[1:-1]:
             total = total + got_ref[rows_of(b), :].astype(F32)
-        out_ref[rows_of(b), :] = (near_ref[rows_of(b), :] + jnp.transpose(total)).astype(BF16)
+        refs[-1][rows_of(b), :] = (near_ref[rows_of(b), :] + jnp.transpose(total)).astype(BF16)
+
+
+def last_kernel(index_ref, weight_ref, other_ref, main_ref, out_ref, self_ref, neigh_ref):
+    out_ref[...] = main_ref[...]
     me = index_ref[index_ref.shape[0] - 1]
     first = me % 2 == 0
     chip = me // 2 % 4
-    rows = weight_ref.shape[1]
+    rows = weight_ref.shape[2]
     for p in range(4):
         span = pl.ds(pl.multiple_of((chip ^ p) * rows, rows), rows)
-        mine, other = weight_ref[p], other_ref[p]
+        mine, other = weight_ref[p // 2, p % 2], other_ref[p // 2, p % 2]
         self_ref[span, :] = jnp.where(first, mine, other)
         neigh_ref[span, :] = jnp.where(first, other, mine)
 
@@ -332,7 +333,7 @@
             result((nodes, hidden), F32),
             result(by_block, BF16),
             piece,
-            jax.ShapeDtypeStruct((2 * tile_count + 1,), jnp.int32),
+            pltpu.SMEM((2 * tile_count + 1,), jnp.int32),
         ),
         in_specs=[SMEM] * 3 + [VMEM] * 6 + [ANY],
         out_specs=(VMEM,) * 8 + (SMEM,),
@@ -366,56 +367,59 @@
         functools.partial(backward_kernel, group), "backward_tiles", acc_shape,
         (index, tiles_near, gt), [SMEM, VMEM, VMEM], cost_us=3.5,
     )
-    far = result((squares - 1, 4, nodes, feat_in), F32)
-    near = result((1, 4, nodes, feat_in), F32)
-    far_send, near_send, far_keep, near_keep, *parts = call(
-        functools.partial(split_kernel, n, block_local), "split_sums",
-        (far, near, far, near) + (chunk,) * 4,
-        (index, acc, wkeep, swap(wsend, n, 1)), [SMEM] + [VMEM] * 3, cost_us=0.8,
-    )
-
-    far_sums = call(
-        functools.partial(pair_far_kernel, squares - 1), "pair_sum_far",
-        (wide, piece, piece, piece) * (squares - 1), (far_keep, swap(far_send, n, 1)),
-    )
-    wsum = call(
-        add_four_kernel, "weight_square_sum", chunk,
-        (parts[0], *[swap(parts[p], n, 2 * p) for p in (1, 2, 3)], far_sums[0]),
-        cost_us=WEIGHT_COST,
-    )
-    bit = 8
-    while 2 * bit < n:
-        wsum = call(add_two_kernel, "weight_sum", chunk, (wsum, swap(wsum, n, bit)))
-        bit *= 2
+    send_shape = result((4, nodes, feat_in), F32)
+    send = [None] * squares
+    for s in range(squares - 1, -1, -1):
+        if s == squares - 1:
+            send[s], w0, w1, w2, w3 = call(
+                functools.partial(send_weights_kernel, s, block_local), "send_weights",
+                (send_shape,) + (chunk,) * 4, (index, acc, wkeep, swap(wsend, n, 1)),
+                [SMEM] + [VMEM] * 3)
+        else:
+            send[s] = call(
+                functools.partial(send_kernel, s, block_local), "send", send_shape, (acc,))
+
     extra = result((nodes + 2 * chunk.shape[0] * (hidden // feat_in), feat_in), BF16)
-    near_own, wsum, *near_pieces = call(
-        pair_near_kernel, "pair_sum_near", (wide, chunk, extra, extra, extra),
-        (near_keep, swap(near_send, n, 1), wsum, swap(wsum, n, bit)),
-    )
-    near_sum, mine = call(
-        near_kernel, "near_sum", (wide, result((4,) + chunk.shape, F32)),
-        (base, near_own, wsum, *[swap(x, n, 2 * q + 2) for q, x in enumerate(near_pieces)]),
-        cost_us=NEAR_COST,
-    )
-    terms = [[near_sum]] + [
-        [far_sums[4 * s], *[swap(far_sums[4 * s + q], n, 2 * q) for q in (1, 2, 3)]]
-        for s in range(squares - 1)
-    ]
+    terms = [None] * squares
+    for s in range(squares - 1, -1, -1):
+        operands = (acc, swap(send[s], n, 1))
+        if s == squares - 1:
+            own, *pieces = call(
+                functools.partial(pair_weights_kernel, s), "pair_sum_weights", (wide, extra, extra, extra),
+                operands + (w1, w2, w3))
+        else:
+            own, *pieces = call(
+                functools.partial(pair_kernel, s), "pair_sum", (wide, piece, piece, piece), operands)
+        terms[s] = [own, *[swap(x, n, 2 * q + 2) for q, x in enumerate(pieces)]]
+    near_total = call(near_kernel, "near_sum", wide, (base, *terms[0]), cost_us=NEAR_COST)
+    terms[0] = [near_total]
     distance = 1
     while distance < squares:
         for s in range(squares - distance, 0, -2 * distance):
-            total = call(add_kernel, "square_sum", piece, terms[s], cost_us=SQUARE_COST)
+            if s == squares - 1:
+                total, wsum = call(
+                    add_weights_kernel, "square_sum_weights", (piece, chunk), (w0, *terms[s]),
+                    cost_us=SQUARE_COST)
+            else:
+                total = call(add_kernel, "square_sum", piece, terms[s], cost_us=SQUARE_COST)
             terms[s - distance].append(swap(total, n, 8 * distance))
         distance *= 2
-
+    bit = 8
+    while bit < n:
+        wsum = call(add_two_kernel, "weight_sum", chunk, (wsum, swap(wsum, n, bit)))
+        bit *= 2
+    rows = chunk.shape[0]
+    two = call(functools.partial(pack_kernel, (0, 1)), "pack_weights", result((2, rows, hidden), F32), (wsum, swap(wsum, n, 2)))
+    mine = call(
+        functools.partial(pack_kernel, (0, 1)), "pack_weights", result((2, 2, rows, hidden), F32), (two, swap(two, n, 4), near_total))
+    main = call(main_kernel, "main_sum", piece, terms[0], cost_us=MAIN_COST)
     grad_input, grad_self, grad_neigh = call(
-        last_kernel, "grad_input_sum",
+        last_kernel, "write_gradients",
         (
             result((nodes, feat_in), BF16, False), result((feat_in, hidden), F32, False),
             result((feat_in, hidden), F32, False),
         ),
-        (index, mine, swap(mine, n, 1), *terms[0]),
-        [SMEM] + [VMEM] * (2 + len(terms[0])),
+        (index, mine, swap(mine, n, 1), main), [SMEM] + [VMEM] * 3,
     )
     return (embedded, grad_input, grad_self, grad_neigh)
 

time: 62.2 us -> 61.4 us (0.987)
  waiting for transfers between devices: 17 us -> 22.6 us
  starting transfers between devices: 28.6 us -> 24.9 us
  Pallas kernels: 14.4 us -> 11.5 us
    ppermute x24 -> x23, waiting for transfers between devices: 17 us -> 22.6 us  [swap(): return lax.ppermute(x, 'row', [(i, i ^ offset) for i in range(n)])]
    ppermute x24 -> x23, starting transfers between devices: 28.6 us -> 24.9 us  [swap(): return lax.ppermute(x, 'row', [(i, i ^ offset) for i in range(n)])]
    pallas_call x11 -> x15, Pallas kernels: 11.1 us -> 8.87 us  [call(): pl.pallas_call(kernel, out_shape=out_shape, in_specs=specs, out_specs=out...]
  transfers between devices with their start and end apart: 24 -> 23, of which waited for: 9 -> 14; matrix products, arithmetic and copies ran while one was open for 0% -> 0% of each run, Pallas kernels for 12% -> 10%
where the time goes in v5:
time: 61.4 us; the launch traced here: 61.2 us
  starting transfers between devices  24.9 us (41%)
  waiting for transfers between devices  22.6 us (37%)
  Pallas kernels  11.5 us (19%)
  local copies, waits for them, and re-layouts  1.31 us (2%)
  between operations  0.78 us (1%)
    ppermute x23, starting transfers between devices, swap(): return lax.ppermute(x, 'row', [(i, i ^ offset) for i in range(n)])  24.9 us
    ppermute x23, waiting for transfers between devices, swap(): return lax.ppermute(x, 'row', [(i, i ^ offset) for i in range(n)])  22.6 us
    pallas_call x15, Pallas kernels, call(): pl.pallas_call(kernel, out_shape=out_shape, in_specs=specs, out_specs=out...  8.87 us
    pallas_call x1, Pallas kernels, body(): pl.pallas_call(stage_kernel, out_shape=(result(tiles.shape, BF16), result...  2.68 us
    unnamed x4, local copies, waits for them, and re-layouts  1.31 us
  transfers between devices with their start and end apart: 23, of which 14 were waited for; matrix products, arithmetic and copies ran while one was open for 0% of the time, Pallas kernels for 10%

profile of v5, /device:TPU:0, one launch (start us, length us, event | category | flops | bytes accessed | tf_op | source)
XLA Modules:
  0.0 61.2 jit_solution(9402984340830293623)
XLA Ops:
  0.6 4.1 %collective-permute-start.3 = (bf16[512,128]{1,0:T(8,128)(2,1)}, bf16[512,128]{1,0:T(8,128)(2,1)S(1)}, u32[]{:S(2)}, u32[]{:S(2)}) collective-permute-start(bf16[512,128]{1,0:T(8,128)(2,1)} %feat_ref.1), channel_id=1, source_target_pairs={{0,8},{1,9},{2,10},{3,11},{4,12},{5,13},{6,14},{7,15},{8,0},{9,1},... | collective-permute-start | bytes 393224 | tf_op jit(solution)/shard_map/ppermute | solution.py:21
  4.7 1.5 %collective-permute-start = (bf16[512,128]{1,0:T(8,128)(2,1)}, bf16[512,128]{1,0:T(8,128)(2,1)S(1)}, u32[]{:S(2)}, u32[]{:S(2)}) collective-permute-start(bf16[512,128]{1,0:T(8,128)(2,1)} %feat_ref.1), channel_id=1, source_target_pairs={{0,2},{1,3},{2,0},{3,1},{4,6},{5,7},{6,4},{7,5},{8,10},{9,11},{10,... | collective-permute-start | bytes 393224 | tf_op jit(solution)/shard_map/ppermute | solution.py:21
  6.3 1.5 %collective-permute-start.1 = (bf16[512,128]{1,0:T(8,128)(2,1)}, bf16[512,128]{1,0:T(8,128)(2,1)S(1)}, u32[]{:S(2)}, u32[]{:S(2)}) collective-permute-start(bf16[512,128]{1,0:T(8,128)(2,1)} %feat_ref.1), channel_id=1, source_target_pairs={{0,6},{1,7},{2,4},{3,5},{4,2},{5,3},{6,0},{7,1},{8,14},{9,15},{10,... | collective-permute-start | bytes 393224 | tf_op jit(solution)/shard_map/ppermute | solution.py:21
  7.8 0.4 collective-permute-start.2
  8.2 3.1 %collective-permute-done.3.refs_0_ = bf16[512,128]{1,0:T(8,128)(2,1)S(1)} collective-permute-done((bf16[512,128]{1,0:T(8,128)(2,1)}, bf16[512,128]{1,0:T(8,128)(2,1)S(1)}, u32[]{:S(2)}, u32[]{:S(2)}) %collective-permute-start.3) | collective-permute-done | bytes 131104 | tf_op jit(solution)/shard_map/ppermute | solution.py:21
  11.4 1.7 %collective-permute-start.4 = (bf16[512,128]{1,0:T(8,128)(2,1)S(1)}, bf16[512,128]{1,0:T(8,128)(2,1)S(1)}, u32[]{:S(2)}, u32[]{:S(2)}) collective-permute-start(bf16[512,128]{1,0:T(8,128)(2,1)S(1)} %collective-permute-done.3.refs_0_), channel_id=1, source_target_pairs={{0,6},{1,7},{2,4},{3,5},{4,2},{5,3},{6,0},{7,1},{8,14},{9,15},{10,... | collective-permute-start | bytes 393224 | tf_op jit(solution)/shard_map/ppermute | solution.py:21
  13.1 0.5 collective-permute-start.5
  13.6 1.3 %collective-permute-start.6 = (bf16[512,128]{1,0:T(8,128)(2,1)S(1)}, bf16[512,128]{1,0:T(8,128)(2,1)S(1)}, u32[]{:S(2)}, u32[]{:S(2)}) collective-permute-start(bf16[512,128]{1,0:T(8,128)(2,1)S(1)} %collective-permute-done.3.refs_0_), channel_id=1, source_target_pairs={{0,4},{1,5},{2,6},{3,7},{4,0},{5,1},{6,2},{7,3},{8,12},{9,13},{10,... | collective-permute-start | bytes 393224 | tf_op jit(solution)/shard_map/ppermute | solution.py:21
  14.9 0.7 %copy-done = s32[60]{0:T(128)S(1)} copy-done((s32[60]{0:T(128)S(1)}, s32[60]{0:T(128)}, u32[]{:S(2)}) %copy-start) | copy-done | bytes 264
  15.5 0.7 %copy-done.1 = s32[60]{0:T(128)S(1)} copy-done((s32[60]{0:T(128)S(1)}, s32[60]{0:T(128)}, u32[]{:S(2)}) %copy-start.1) | copy-done | bytes 264
  16.2 2.7 %stage_arguments.1 = (bf16[60,128,128]{2,1,0:T(8,128)(2,1)S(1)}, bf16[128,256]{1,0:T(8,128)(2,1)S(1)}, bf16[128,256]{1,0:T(8,128)(2,1)S(1)}, f32[4,128,128]{2,1,...) custom-call(s32[1]{0:T(128)} %bitcast.me_ref, ...), custom_call_target="tpu_custom_call" | custom-call | flops 3300000000 | bytes 10800000 | tf_op jit(solution)/shard_map/stage_arguments/pallas_call | solution.py:325
  18.9 0.1 collective-permute-start.7
  19.0 1.4 %collective-permute-done.4.refs_1_ = bf16[512,128]{1,0:T(8,128)(2,1)S(1)} collective-permute-done((bf16[512,128]{1,0:T(8,128)(2,1)S(1)}, bf16[512,128]{1,0:T(8,128)(2,1)S(1)}, u32[]{:S(2)}, u32[]{:S(2)}) %collective-permute-start.4) | collective-permute-done | bytes 131104 | tf_op jit(solution)/shard_map/ppermute | solution.py:21
  20.4 0.6 %collective-permute-done.5.refs_2_ = bf16[512,128]{1,0:T(8,128)(2,1)S(1)} collective-permute-done((bf16[512,128]{1,0:T(8,128)(2,1)S(1)}, bf16[512,128]{1,0:T(8,128)(2,1)S(1)}, u32[]{:S(2)}, u32[]{:S(2)}) %collective-permute-start.5) | collective-permute-done | bytes 131104 | tf_op jit(solution)/shard_map/ppermute | solution.py:21
  21.0 0.1 collective-permute-done.6.refs_3_
  21.2 0.1 collective-permute-start.8
  21.3 1.9 %collective-permute-done.8.refs_3_ = bf16[4,512,128]{2,1,0:T(8,128)(2,1)S(1)} collective-permute-done((bf16[4,512,128]{2,1,0:T(8,128)(2,1)S(1)}, bf16[4,512,128]{2,1,0:T(8,128)(2,1)S(1)}, u32[]{:S(2)}, u32[]{:S(2)}) %collective-permute-start.8) | collective-permute-done | bytes 524320 | tf_op jit(solution)/shard_map/ppermute | solution.py:21
  23.2 4.5 %forward_layer.1 = (bf16[512,256]{1,0:T(8,128)(2,1)}, f32[512,128]{1,0:T(8,128)S(1)}, f32[128,256]{1,0:T(8,128)S(1)}, f32[128,256]{1,0:T(8,128)S(1)}, bf16[4,256,128]{2,1,0:T(8,128)(2,1)S(1)}) custom-call(s32[121]{0:T(128)S(4)} %get-tuple-element.36.index_ref, bf16[60,128,128]{2,1,0:T(8,128)(2,1)S(1)} %get-tuple-element.37.tiles_ref, ...), custom_call_target="tpu_custom_call" | custom-call | flops 5500000256 | bytes 18000000 | tf_op jit(solution)/shard_map/forward_layer/pallas_call | solution.py:302
  27.7 0.1 collective-permute-start.9
  27.8 2.9 %backward_tiles.1.acc_ref = f32[65,128,128]{2,1,0:T(8,128)S(1)} custom-call(s32[121]{0:T(128)S(4)} %get-tuple-element.36.index_ref, bf16[60,128,128]{2,1,0:T(8,128)(2,1)S(1)} %get-tuple-element.37.tiles_ref, bf16[4,256,128]{2,1,0:T(8,128)(2,1)S(1)} %get-tuple-element.46.gt_ref), custom_call_target="tpu_custom_call" | custom-call | flops 3849999872 | bytes 12600000 | tf_op jit(solution)/shard_map/backward_tiles/pallas_call | solution.py:302
  30.7 0.1 send_weights.1
  30.8 0.4 collective-permute-start.10
  31.3 0.2 collective-permute-start.17
  31.5 2.0 %collective-permute-done.10.got_ref = f32[4,512,128]{2,1,0:T(8,128)S(1)} collective-permute-done((f32[4,512,128]{2,1,0:T(8,128)S(1)}, f32[4,512,128]{2,1,0:T(8,128)S(1)}, u32[]{:S(2)}, u32[]{:S(2)}) %collective-permute-start.10) | collective-permute-done | bytes 1048608 | tf_op jit(solution)/shard_map/ppermute | solution.py:21
  33.5 0.1 pair_sum_weights.1
  33.6 1.6 %collective-permute-start.11 = (bf16[640,128]{1,0:T(8,128)(2,1)S(1)}, bf16[640,128]{1,0:T(8,128)(2,1)S(1)}, u32[]{:S(2)}, u32[]{:S(2)}) collective-permute-start(bf16[640,128]{1,0:T(8,128)(2,1)S(1)} %get-tuple-element.55), channel_id=1, source_target_pairs={{0,2},{1,3},{2,0},{3,1},{4,6},{5,7},{6,4},{7,5},{8,10},{9,11},{10,... | collective-permute-start | bytes 491528 | tf_op jit(solution)/shard_map/ppermute | solution.py:21
  35.3 0.3 collective-permute-start.12
  35.6 1.6 %collective-permute-start.13 = (bf16[640,128]{1,0:T(8,128)(2,1)S(1)}, bf16[640,128]{1,0:T(8,128)(2,1)S(1)}, u32[]{:S(2)}, u32[]{:S(2)}) collective-permute-start(bf16[640,128]{1,0:T(8,128)(2,1)S(1)} %get-tuple-element.57), channel_id=1, source_target_pairs={{0,6},{1,7},{2,4},{3,5},{4,2},{5,3},{6,0},{7,1},{8,14},{9,15},{10,... | collective-permute-start | bytes 491528 | tf_op jit(solution)/shard_map/ppermute | solution.py:21
  37.2 0.1 pair_sum.1
  37.3 1.6 %collective-permute-start.18 = (bf16[512,128]{1,0:T(8,128)(2,1)S(1)}, bf16[512,128]{1,0:T(8,128)(2,1)S(1)}, u32[]{:S(2)}, u32[]{:S(2)}) collective-permute-start(bf16[512,128]{1,0:T(8,128)(2,1)S(1)} %get-tuple-element.61), channel_id=1, source_target_pairs={{0,2},{1,3},{2,0},{3,1},{4,6},{5,7},{6,4},{7,5},{8,10},{9,11},{10,... | collective-permute-start | bytes 393224 | tf_op jit(solution)/shard_map/ppermute | solution.py:21
  38.9 0.3 collective-permute-start.19
  39.2 1.7 %collective-permute-done.11.refs_0_ = bf16[640,128]{1,0:T(8,128)(2,1)S(1)} collective-permute-done((bf16[640,128]{1,0:T(8,128)(2,1)S(1)}, bf16[640,128]{1,0:T(8,128)(2,1)S(1)}, u32[]{:S(2)}, u32[]{:S(2)}) %collective-permute-start.11) | collective-permute-done | bytes 163872 | tf_op jit(solution)/shard_map/ppermute | solution.py:21
  40.9 1.3 %collective-permute-start.20 = (bf16[512,128]{1,0:T(8,128)(2,1)S(1)}, bf16[512,128]{1,0:T(8,128)(2,1)S(1)}, u32[]{:S(2)}, u32[]{:S(2)}) collective-permute-start(bf16[512,128]{1,0:T(8,128)(2,1)S(1)} %get-tuple-element.63), channel_id=1, source_target_pairs={{0,6},{1,7},{2,4},{3,5},{4,2},{5,3},{6,0},{7,1},{8,14},{9,15},{10,... | collective-permute-start | bytes 393224 | tf_op jit(solution)/shard_map/ppermute | solution.py:21
  42.3 3.4 %collective-permute-done.13.refs_2_ = bf16[640,128]{1,0:T(8,128)(2,1)S(1)} collective-permute-done((bf16[640,128]{1,0:T(8,128)(2,1)S(1)}, bf16[640,128]{1,0:T(8,128)(2,1)S(1)}, u32[]{:S(2)}, u32[]{:S(2)}) %collective-permute-start.13) | collective-permute-done | bytes 163872 | tf_op jit(solution)/shard_map/ppermute | solution.py:21
  45.8 0.1 square_sum_weights.1
  45.8 1.7 %collective-permute-start.14 = (f32[32,256]{1,0:T(8,128)S(1)}, f32[32,256]{1,0:T(8,128)S(1)}, u32[]{:S(2)}, u32[]{:S(2)}) collective-permute-start(f32[32,256]{1,0:T(8,128)S(1)} %get-tuple-element.58.own_ref), channel_id=1, source_target_pairs={{0,8},{1,9},{2,10},{3,11},{4,12},{5,13},{6,14},{7,15},{8,0},{9,1},... | collective-permute-start | bytes 98312 | tf_op jit(solution)/shard_map/ppermute | solution.py:21
  47.6 3.2 %collective-permute-done.14.got_ref = f32[32,256]{1,0:T(8,128)S(1)} collective-permute-done((f32[32,256]{1,0:T(8,128)S(1)}, f32[32,256]{1,0:T(8,128)S(1)}, u32[]{:S(2)}, u32[]{:S(2)}) %collective-permute-start.14) | collective-permute-done | bytes 32800 | tf_op jit(solution)/shard_map/ppermute | solution.py:21
  50.8 1.6 %collective-permute-start.15 = (f32[32,256]{1,0:T(8,128)S(1)}, f32[32,256]{1,0:T(8,128)S(1)}, u32[]{:S(2)}, u32[]{:S(2)}) collective-permute-start(f32[32,256]{1,0:T(8,128)S(1)} %weight_sum.1.refs_0_), channel_id=1, source_target_pairs={{0,2},{1,3},{2,0},{3,1},{4,6},{5,7},{6,4},{7,5},{8,10},{9,11},{10,... | collective-permute-start | bytes 98312 | tf_op jit(solution)/shard_map/ppermute | solution.py:21
  52.4 0.9 %collective-permute-start.22 = (bf16[512,128]{1,0:T(8,128)(2,1)S(1)}, bf16[512,128]{1,0:T(8,128)(2,1)S(1)}, u32[]{:S(2)}, u32[]{:S(2)}) collective-permute-start(bf16[512,128]{1,0:T(8,128)(2,1)S(1)} %get-tuple-element.64), channel_id=1, source_target_pairs={{0,8},{1,9},{2,10},{3,11},{4,12},{5,13},{6,14},{7,15},{8,0},{9,1},... | collective-permute-start | bytes 393224 | tf_op jit(solution)/shard_map/ppermute | solution.py:21
  53.3 1.4 %collective-permute-done.15.refs_1_ = f32[32,256]{1,0:T(8,128)S(1)} collective-permute-done((f32[32,256]{1,0:T(8,128)S(1)}, f32[32,256]{1,0:T(8,128)S(1)}, u32[]{:S(2)}, u32[]{:S(2)}) %collective-permute-start.15) | collective-permute-done | bytes 32800 | tf_op jit(solution)/shard_map/ppermute | solution.py:21
  54.7 1.8 %collective-permute-start.16 = (f32[2,32,256]{2,1,0:T(8,128)S(1)}, f32[2,32,256]{2,1,0:T(8,128)S(1)}, u32[]{:S(2)}, u32[]{:S(2)}) collective-permute-start(f32[2,32,256]{2,1,0:T(8,128)S(1)} %pack_weights.2.refs_0_), channel_id=1, source_target_pairs={{0,4},{1,5},{2,6},{3,7},{4,0},{5,1},{6,2},{7,3},{8,12},{9,13},{10,... | collective-permute-start | bytes 196616 | tf_op jit(solution)/shard_map/ppermute | solution.py:21
  56.6 0.1 near_sum.1.refs_2_.near_ref
  56.7 2.3 %collective-permute-done.16.refs_1_ = f32[2,32,256]{2,1,0:T(8,128)S(1)} collective-permute-done((f32[2,32,256]{2,1,0:T(8,128)S(1)}, f32[2,32,256]{2,1,0:T(8,128)S(1)}, u32[]{:S(2)}, u32[]{:S(2)}) %collective-permute-start.16) | collective-permute-done | bytes 65568 | tf_op jit(solution)/shard_map/ppermute | solution.py:21
  59.0 0.1 collective-permute-start.21
  59.1 0.5 collective-permute-done.22.refs_0_
  59.6 0.1 main_sum.1.main_ref
  59.8 0.7 %collective-permute-done.21.other_ref = f32[2,2,32,256]{3,2,1,0:T(8,128)S(1)} collective-permute-done((f32[2,2,32,256]{3,2,1,0:T(8,128)S(1)}, f32[2,2,32,256]{3,2,1,0:T(8,128)S(1)}, u32[]{:S(2)}, u32[]{:S(2)}) %collective-permute-start.21) | collective-permute-done | bytes 131104 | tf_op jit(solution)/shard_map/ppermute | solution.py:21
  60.4 0.8 %write_gradients.1 = (bf16[512,128]{1,0:T(8,128)(2,1)}, f32[128,256]{1,0:T(8,128)}, f32[128,256]{1,0:T(8,128)}) custom-call(s32[121]{0:T(128)S(4)} %get-tuple-element.36.index_ref, f32[2,2,32,256]{3,2,1,0:T(8,128)S(1)} %pack_weights.3.weight_ref, f32[2,2,32,256]{3,2,1,0:T(8,128)S(1)} %collective-permute-done.21.other_ref, bf16[512,128]{1,0:T(8,128)(2,1)S(1)} %main_sum.1.main_ref), custom_call_target="tpu_custom_call" | custom-call | flops 220000000 | bytes 720000 | tf_op jit(solution)/shard_map/write_gradients/pallas_call | solution.py:302
  (18 shorter events, 0.2 us)
Async XLA Ops:
  0.6 10.7 %collective-permute-start.3 = (bf16[512,128]{1,0:T(8,128)(2,1)}, bf16[512,128]{1,0:T(8,128)(2,1)S(1)}, u32[]{:S(2)}, u32[]{:S(2)}) collective-permute-start(bf16[512,128]{1,0:T(8,128)(2,1)} %feat_ref.1), channel_id=1, source_target_pairs={{0,8},{1,9},{2,10},{3,11},{4,12},{5,13},{6,14},{7,15},{8,0},{9,1},... | collective-permute-start | bytes 393224 | tf_op jit(solution)/shard_map/ppermute | solution.py:21
  4.7 8.9 %collective-permute-start = (bf16[512,128]{1,0:T(8,128)(2,1)}, bf16[512,128]{1,0:T(8,128)(2,1)S(1)}, u32[]{:S(2)}, u32[]{:S(2)}) collective-permute-start(bf16[512,128]{1,0:T(8,128)(2,1)} %feat_ref.1), channel_id=1, source_target_pairs={{0,2},{1,3},{2,0},{3,1},{4,6},{5,7},{6,4},{7,5},{8,10},{9,11},{10,... | collective-permute-start | bytes 393224 | tf_op jit(solution)/shard_map/ppermute | solution.py:21
  6.3 12.6 %collective-permute-start.1 = (bf16[512,128]{1,0:T(8,128)(2,1)}, bf16[512,128]{1,0:T(8,128)(2,1)S(1)}, u32[]{:S(2)}, u32[]{:S(2)}) collective-permute-start(bf16[512,128]{1,0:T(8,128)(2,1)} %feat_ref.1), channel_id=1, source_target_pairs={{0,6},{1,7},{2,4},{3,5},{4,2},{5,3},{6,0},{7,1},{8,14},{9,15},{10,... | collective-permute-start | bytes 393224 | tf_op jit(solution)/shard_map/ppermute | solution.py:21
  7.8 11.1 %collective-permute-start.2 = (bf16[512,128]{1,0:T(8,128)(2,1)}, bf16[512,128]{1,0:T(8,128)(2,1)S(1)}, u32[]{:S(2)}, u32[]{:S(2)}) collective-permute-start(bf16[512,128]{1,0:T(8,128)(2,1)} %feat_ref.1), channel_id=1, source_target_pairs={{0,4},{1,5},{2,6},{3,7},{4,0},{5,1},{6,2},{7,3},{8,12},{9,13},{10,... | collective-permute-start | bytes 393224 | tf_op jit(solution)/shard_map/ppermute | solution.py:21
  11.4 9.1 %collective-permute-start.4 = (bf16[512,128]{1,0:T(8,128)(2,1)S(1)}, bf16[512,128]{1,0:T(8,128)(2,1)S(1)}, u32[]{:S(2)}, u32[]{:S(2)}) collective-permute-start(bf16[512,128]{1,0:T(8,128)(2,1)S(1)} %collective-permute-done.3.refs_0_), channel_id=1, source_target_pairs={{0,6},{1,7},{2,4},{3,5},{4,2},{5,3},{6,0},{7,1},{8,14},{9,15},{10,... | collective-permute-start | bytes 393224 | tf_op jit(solution)/shard_map/ppermute | solution.py:21
  13.1 7.9 %collective-permute-start.5 = (bf16[512,128]{1,0:T(8,128)(2,1)S(1)}, bf16[512,128]{1,0:T(8,128)(2,1)S(1)}, u32[]{:S(2)}, u32[]{:S(2)}) collective-permute-start(bf16[512,128]{1,0:T(8,128)(2,1)S(1)} %collective-permute-done.3.refs_0_), channel_id=1, source_target_pairs={{0,2},{1,3},{2,0},{3,1},{4,6},{5,7},{6,4},{7,5},{8,10},{9,11},{10,... | collective-permute-start | bytes 393224 | tf_op jit(solution)/shard_map/ppermute | solution.py:21
  13.6 7.6 %collective-permute-start.6 = (bf16[512,128]{1,0:T(8,128)(2,1)S(1)}, bf16[512,128]{1,0:T(8,128)(2,1)S(1)}, u32[]{:S(2)}, u32[]{:S(2)}) collective-permute-start(bf16[512,128]{1,0:T(8,128)(2,1)S(1)} %collective-permute-done.3.refs_0_), channel_id=1, source_target_pairs={{0,4},{1,5},{2,6},{3,7},{4,0},{5,1},{6,2},{7,3},{8,12},{9,13},{10,... | collective-permute-start | bytes 393224 | tf_op jit(solution)/shard_map/ppermute | solution.py:21
  14.8 0.7 %copy-start = (s32[60]{0:T(128)S(1)}, s32[60]{0:T(128)}, u32[]{:S(2)}) copy-start(s32[60]{0:T(128)} %trow_ref.1) | copy-start | bytes 724
  15.5 0.7 %copy-start.1 = (s32[60]{0:T(128)S(1)}, s32[60]{0:T(128)}, u32[]{:S(2)}) copy-start(s32[60]{0:T(128)} %tcol_ref.1) | copy-start | bytes 724
  18.9 2.4 %collective-permute-start.7 = (bf16[4,512,128]{2,1,0:T(8,128)(2,1)S(1)}, bf16[4,512,128]{2,1,0:T(8,128)(2,1)S(1)}, u32[]{:S(2)}, u32[]{:S(2)}) collective-permute-start(bf16[4,512,128]{2,1,0:T(8,128)(2,1)S(1)} %pack_square.2.refs_0_), channel_id=1, source_target_pairs={{0,1},{1,0},{2,3},{3,2},{4,5},{5,4},{6,7},{7,6},{8,9},{9,8},{10,11... | collective-permute-start | bytes 1572872 | tf_op jit(solution)/shard_map/ppermute | solution.py:21
  21.2 2.0 %collective-permute-start.8 = (bf16[4,512,128]{2,1,0:T(8,128)(2,1)S(1)}, bf16[4,512,128]{2,1,0:T(8,128)(2,1)S(1)}, u32[]{:S(2)}, u32[]{:S(2)}) collective-permute-start(bf16[4,512,128]{2,1,0:T(8,128)(2,1)S(1)} %pack_square.3.refs_1_), channel_id=1, source_target_pairs={{0,1},{1,0},{2,3},{3,2},{4,5},{5,4},{6,7},{7,6},{8,9},{9,8},{10,11... | collective-permute-start | bytes 1572872 | tf_op jit(solution)/shard_map/ppermute | solution.py:21
  27.7 3.0 %collective-permute-start.9 = (f32[128,256]{1,0:T(8,128)S(1)}, f32[128,256]{1,0:T(8,128)S(1)}, u32[]{:S(2)}, u32[]{:S(2)}) collective-permute-start(f32[128,256]{1,0:T(8,128)S(1)} %get-tuple-element.48), channel_id=1, source_target_pairs={{0,1},{1,0},{2,3},{3,2},{4,5},{5,4},{6,7},{7,6},{8,9},{9,8},{10,11... | collective-permute-start | bytes 393224 | tf_op jit(solution)/shard_map/ppermute | solution.py:21
  30.8 2.7 %collective-permute-start.10 = (f32[4,512,128]{2,1,0:T(8,128)S(1)}, f32[4,512,128]{2,1,0:T(8,128)S(1)}, u32[]{:S(2)}, u32[]{:S(2)}) collective-permute-start(f32[4,512,128]{2,1,0:T(8,128)S(1)} %get-tuple-element.50), channel_id=1, source_target_pairs={{0,1},{1,0},{2,3},{3,2},{4,5},{5,4},{6,7},{7,6},{8,9},{9,8},{10,11... | collective-permute-start | bytes 3145736 | tf_op jit(solution)/shard_map/ppermute | solution.py:21
  31.3 5.9 %collective-permute-start.17 = (f32[4,512,128]{2,1,0:T(8,128)S(1)}, f32[4,512,128]{2,1,0:T(8,128)S(1)}, u32[]{:S(2)}, u32[]{:S(2)}) collective-permute-start(f32[4,512,128]{2,1,0:T(8,128)S(1)} %send.1), channel_id=1, source_target_pairs={{0,1},{1,0},{2,3},{3,2},{4,5},{5,4},{6,7},{7,6},{8,9},{9,8},{10,11... | collective-permute-start | bytes 3145736 | tf_op jit(solution)/shard_map/ppermute | solution.py:21
  33.6 7.3 %collective-permute-start.11 = (bf16[640,128]{1,0:T(8,128)(2,1)S(1)}, bf16[640,128]{1,0:T(8,128)(2,1)S(1)}, u32[]{:S(2)}, u32[]{:S(2)}) collective-permute-start(bf16[640,128]{1,0:T(8,128)(2,1)S(1)} %get-tuple-element.55), channel_id=1, source_target_pairs={{0,2},{1,3},{2,0},{3,1},{4,6},{5,7},{6,4},{7,5},{8,10},{9,11},{10,... | collective-permute-start | bytes 491528 | tf_op jit(solution)/shard_map/ppermute | solution.py:21
  35.3 7.1 %collective-permute-start.12 = (bf16[640,128]{1,0:T(8,128)(2,1)S(1)}, bf16[640,128]{1,0:T(8,128)(2,1)S(1)}, u32[]{:S(2)}, u32[]{:S(2)}) collective-permute-start(bf16[640,128]{1,0:T(8,128)(2,1)S(1)} %get-tuple-element.56), channel_id=1, source_target_pairs={{0,4},{1,5},{2,6},{3,7},{4,0},{5,1},{6,2},{7,3},{8,12},{9,13},{10,... | collective-permute-start | bytes 491528 | tf_op jit(solution)/shard_map/ppermute | solution.py:21
  35.6 10.2 %collective-permute-start.13 = (bf16[640,128]{1,0:T(8,128)(2,1)S(1)}, bf16[640,128]{1,0:T(8,128)(2,1)S(1)}, u32[]{:S(2)}, u32[]{:S(2)}) collective-permute-start(bf16[640,128]{1,0:T(8,128)(2,1)S(1)} %get-tuple-element.57), channel_id=1, source_target_pairs={{0,6},{1,7},{2,4},{3,5},{4,2},{5,3},{6,0},{7,1},{8,14},{9,15},{10,... | collective-permute-start | bytes 491528 | tf_op jit(solution)/shard_map/ppermute | solution.py:21
  37.3 19.3 %collective-permute-start.18 = (bf16[512,128]{1,0:T(8,128)(2,1)S(1)}, bf16[512,128]{1,0:T(8,128)(2,1)S(1)}, u32[]{:S(2)}, u32[]{:S(2)}) collective-permute-start(bf16[512,128]{1,0:T(8,128)(2,1)S(1)} %get-tuple-element.61), channel_id=1, source_target_pairs={{0,2},{1,3},{2,0},{3,1},{4,6},{5,7},{6,4},{7,5},{8,10},{9,11},{10,... | collective-permute-start | bytes 393224 | tf_op jit(solution)/shard_map/ppermute | solution.py:21
  38.9 17.6 %collective-permute-start.19 = (bf16[512,128]{1,0:T(8,128)(2,1)S(1)}, bf16[512,128]{1,0:T(8,128)(2,1)S(1)}, u32[]{:S(2)}, u32[]{:S(2)}) collective-permute-start(bf16[512,128]{1,0:T(8,128)(2,1)S(1)} %get-tuple-element.62), channel_id=1, source_target_pairs={{0,4},{1,5},{2,6},{3,7},{4,0},{5,1},{6,2},{7,3},{8,12},{9,13},{10,... | collective-permute-start | bytes 393224 | tf_op jit(solution)/shard_map/ppermute | solution.py:21
  40.9 15.6 %collective-permute-start.20 = (bf16[512,128]{1,0:T(8,128)(2,1)S(1)}, bf16[512,128]{1,0:T(8,128)(2,1)S(1)}, u32[]{:S(2)}, u32[]{:S(2)}) collective-permute-start(bf16[512,128]{1,0:T(8,128)(2,1)S(1)} %get-tuple-element.63), channel_id=1, source_target_pairs={{0,6},{1,7},{2,4},{3,5},{4,2},{5,3},{6,0},{7,1},{8,14},{9,15},{10,... | collective-permute-start | bytes 393224 | tf_op jit(solution)/shard_map/ppermute | solution.py:21
  45.8 5.0 %collective-permute-start.14 = (f32[32,256]{1,0:T(8,128)S(1)}, f32[32,256]{1,0:T(8,128)S(1)}, u32[]{:S(2)}, u32[]{:S(2)}) collective-permute-start(f32[32,256]{1,0:T(8,128)S(1)} %get-tuple-element.58.own_ref), channel_id=1, source_target_pairs={{0,8},{1,9},{2,10},{3,11},{4,12},{5,13},{6,14},{7,15},{8,0},{9,1},... | collective-permute-start | bytes 98312 | tf_op jit(solution)/shard_map/ppermute | solution.py:21
  50.8 3.9 %collective-permute-start.15 = (f32[32,256]{1,0:T(8,128)S(1)}, f32[32,256]{1,0:T(8,128)S(1)}, u32[]{:S(2)}, u32[]{:S(2)}) collective-permute-start(f32[32,256]{1,0:T(8,128)S(1)} %weight_sum.1.refs_0_), channel_id=1, source_target_pairs={{0,2},{1,3},{2,0},{3,1},{4,6},{5,7},{6,4},{7,5},{8,10},{9,11},{10,... | collective-permute-start | bytes 98312 | tf_op jit(solution)/shard_map/ppermute | solution.py:21
  52.4 7.3 %collective-permute-start.22 = (bf16[512,128]{1,0:T(8,128)(2,1)S(1)}, bf16[512,128]{1,0:T(8,128)(2,1)S(1)}, u32[]{:S(2)}, u32[]{:S(2)}) collective-permute-start(bf16[512,128]{1,0:T(8,128)(2,1)S(1)} %get-tuple-element.64), channel_id=1, source_target_pairs={{0,8},{1,9},{2,10},{3,11},{4,12},{5,13},{6,14},{7,15},{8,0},{9,1},... | collective-permute-start | bytes 393224 | tf_op jit(solution)/shard_map/ppermute | solution.py:21
  54.7 4.3 %collective-permute-start.16 = (f32[2,32,256]{2,1,0:T(8,128)S(1)}, f32[2,32,256]{2,1,0:T(8,128)S(1)}, u32[]{:S(2)}, u32[]{:S(2)}) collective-permute-start(f32[2,32,256]{2,1,0:T(8,128)S(1)} %pack_weights.2.refs_0_), channel_id=1, source_target_pairs={{0,4},{1,5},{2,6},{3,7},{4,0},{5,1},{6,2},{7,3},{8,12},{9,13},{10,... | collective-permute-start | bytes 196616 | tf_op jit(solution)/shard_map/ppermute | solution.py:21
  59.0 1.4 %collective-permute-start.21 = (f32[2,2,32,256]{3,2,1,0:T(8,128)S(1)}, f32[2,2,32,256]{3,2,1,0:T(8,128)S(1)}, u32[]{:S(2)}, u32[]{:S(2)}) collective-permute-start(f32[2,2,32,256]{3,2,1,0:T(8,128)S(1)} %pack_weights.3.weight_ref), channel_id=1, source_target_pairs={{0,1},{1,0},{2,3},{3,2},{4,5},{5,4},{6,7},{7,6},{8,9},{9,8},{10,11... | collective-permute-start | bytes 393224 | tf_op jit(solution)/shard_map/ppermute | solution.py:21

commit v6 on v5

--- a/solution.py
+++ b/solution.py
@@ -14,7 +14,7 @@
 ANY = pl.BlockSpec(memory_space=pl.ANY)
 MIB = 1024 * 1024
 LAST = ((1,), (1,))
-NEAR_COST, SQUARE_COST, MAIN_COST = 8, 4, 10
+NEAR_COST, SQUARE_COST, MAIN_COST = 0.2, 0.2, 4
 
 
 def swap(x, n, offset):
@@ -200,7 +200,8 @@
         ref[...] = wkeep_ref[span, :] + wgot_ref[span, :]
 
 
-def pair_kernel(square, acc_ref, got_ref, own_ref, *pieces):
+def pair_kernel(square, acc_ref, got_ref, *refs):
+    own_ref, *pieces = refs[-4:]
     block_local = own_ref.shape[0] // BLOCK
     for q, ref in enumerate((own_ref, *pieces)):
         for b in range(block_local):
@@ -225,10 +226,10 @@
 
 
 def add_kernel(own_ref, *refs):
-    total = own_ref[...]
+    total = own_ref[...].astype(F32)
     for got_ref in refs[:-1]:
         total = total + got_ref[...].astype(F32)
-    refs[-1][...] = total.astype(BF16)
+    refs[-1][...] = total.astype(refs[-1].dtype)
 
 
 def add_weights_kernel(weight_ref, own_ref, *refs):
@@ -381,18 +382,17 @@
 
     extra = result((nodes + 2 * chunk.shape[0] * (hidden // feat_in), feat_in), BF16)
     terms = [None] * squares
-    for s in range(squares - 1, -1, -1):
+    for s in range(squares - 1, 0, -1):
         operands = (acc, swap(send[s], n, 1))
         if s == squares - 1:
             own, *pieces = call(
-                functools.partial(pair_weights_kernel, s), "pair_sum_weights", (wide, extra, extra, extra),
-                operands + (w1, w2, w3))
+                functools.partial(pair_weights_kernel, s), "pair_sum_weights",
+                (wide, extra, extra, extra), operands + (w1, w2, w3))
         else:
             own, *pieces = call(
                 functools.partial(pair_kernel, s), "pair_sum", (wide, piece, piece, piece), operands)
         terms[s] = [own, *[swap(x, n, 2 * q + 2) for q, x in enumerate(pieces)]]
-    near_total = call(near_kernel, "near_sum", wide, (base, *terms[0]), cost_us=NEAR_COST)
-    terms[0] = [near_total]
+    from_squares = []
     distance = 1
     while distance < squares:
         for s in range(squares - distance, 0, -2 * distance):
@@ -402,17 +402,23 @@
                     cost_us=SQUARE_COST)
             else:
                 total = call(add_kernel, "square_sum", piece, terms[s], cost_us=SQUARE_COST)
-            terms[s - distance].append(swap(total, n, 8 * distance))
+            target = from_squares if s == distance else terms[s - distance]
+            target.append(swap(total, n, 8 * distance))
         distance *= 2
     bit = 8
     while bit < n:
         wsum = call(add_two_kernel, "weight_sum", chunk, (wsum, swap(wsum, n, bit)))
         bit *= 2
+    own, *pieces = call(
+        functools.partial(pair_kernel, 0), "pair_sum", (wide, piece, piece, piece),
+        (acc, swap(send[0], n, 1), wsum))
+    near = [swap(x, n, 2 * q + 2) for q, x in enumerate(pieces)]
+    near_total = call(near_kernel, "near_sum", wide, (base, own, *near), cost_us=NEAR_COST)
     rows = chunk.shape[0]
     two = call(functools.partial(pack_kernel, (0, 1)), "pack_weights", result((2, rows, hidden), F32), (wsum, swap(wsum, n, 2)))
     mine = call(
         functools.partial(pack_kernel, (0, 1)), "pack_weights", result((2, 2, rows, hidden), F32), (two, swap(two, n, 4), near_total))
-    main = call(main_kernel, "main_sum", piece, terms[0], cost_us=MAIN_COST)
+    main = call(main_kernel, "main_sum", piece, (near_total, *[call(add_kernel, "far_sum", wide, (x,), cost_us=10) for x in from_squares]), cost_us=MAIN_COST)
     grad_input, grad_self, grad_neigh = call(
         last_kernel, "write_gradients",
         (

time: 61.4 us -> 68.6 us (1.12)
  waiting for transfers between devices: 22.6 us -> 31 us
  starting transfers between devices: 24.9 us -> 23.7 us
    ppermute x23, waiting for transfers between devices: 22.6 us -> 31 us  [swap(): return lax.ppermute(x, 'row', [(i, i ^ offset) for i in range(n)])]
    ppermute x23, starting transfers between devices: 24.9 us -> 23.7 us  [swap(): return lax.ppermute(x, 'row', [(i, i ^ offset) for i in range(n)])]
    pallas_call x15 -> x16, Pallas kernels: 8.87 us -> 8.94 us  [call(): pl.pallas_call(kernel, out_shape=out_shape, in_specs=specs, out_specs=out...]
  transfers between devices with their start and end apart: 23 -> 23, of which waited for: 14 -> 14; matrix products, arithmetic and copies ran while one was open for 0% -> 0% of each run, Pallas kernels for 10% -> 9%
where the time goes in v6:
time: 68.6 us; the launch traced here: 68.4 us
  waiting for transfers between devices  31 us (45%)
  starting transfers between devices  23.7 us (35%)
  Pallas kernels  11.6 us (17%)
  local copies, waits for them, and re-layouts  1.31 us (2%)
  between operations  0.82 us (1%)
    ppermute x23, waiting for transfers between devices, swap(): return lax.ppermute(x, 'row', [(i, i ^ offset) for i in range(n)])  31 us
    ppermute x23, starting transfers between devices, swap(): return lax.ppermute(x, 'row', [(i, i ^ offset) for i in range(n)])  23.7 us
    pallas_call x16, Pallas kernels, call(): pl.pallas_call(kernel, out_shape=out_shape, in_specs=specs, out_specs=out...  8.94 us
    pallas_call x1, Pallas kernels, body(): pl.pallas_call(stage_kernel, out_shape=(result(tiles.shape, BF16), result...  2.68 us
  transfers between devices with their start and end apart: 23, of which 14 were waited for; matrix products, arithmetic and copies ran while one was open for 0% of the time, Pallas kernels for 9%

profile of v6, /device:TPU:0, one launch (start us, length us, event | category | flops | bytes accessed | tf_op | source)
XLA Modules:
  0.0 68.4 jit_solution(16299398436264841912)
XLA Ops:
  0.6 4.1 %collective-permute-start.3 = (bf16[512,128]{1,0:T(8,128)(2,1)}, bf16[512,128]{1,0:T(8,128)(2,1)S(1)}, u32[]{:S(2)}, u32[]{:S(2)}) collective-permute-start(bf16[512,128]{1,0:T(8,128)(2,1)} %feat_ref.1), channel_id=1, source_target_pairs={{0,8},{1,9},{2,10},{3,11},{4,12},{5,13},{6,14},{7,15},{8,0},{9,1},... | collective-permute-start | bytes 393224 | tf_op jit(solution)/shard_map/ppermute | solution.py:21
  4.7 1.5 %collective-permute-start = (bf16[512,128]{1,0:T(8,128)(2,1)}, bf16[512,128]{1,0:T(8,128)(2,1)S(1)}, u32[]{:S(2)}, u32[]{:S(2)}) collective-permute-start(bf16[512,128]{1,0:T(8,128)(2,1)} %feat_ref.1), channel_id=1, source_target_pairs={{0,2},{1,3},{2,0},{3,1},{4,6},{5,7},{6,4},{7,5},{8,10},{9,11},{10,... | collective-permute-start | bytes 393224 | tf_op jit(solution)/shard_map/ppermute | solution.py:21
  6.3 1.5 %collective-permute-start.1 = (bf16[512,128]{1,0:T(8,128)(2,1)}, bf16[512,128]{1,0:T(8,128)(2,1)S(1)}, u32[]{:S(2)}, u32[]{:S(2)}) collective-permute-start(bf16[512,128]{1,0:T(8,128)(2,1)} %feat_ref.1), channel_id=1, source_target_pairs={{0,6},{1,7},{2,4},{3,5},{4,2},{5,3},{6,0},{7,1},{8,14},{9,15},{10,... | collective-permute-start | bytes 393224 | tf_op jit(solution)/shard_map/ppermute | solution.py:21
  7.8 0.4 collective-permute-start.2
  8.2 3.1 %collective-permute-done.3.refs_0_ = bf16[512,128]{1,0:T(8,128)(2,1)S(1)} collective-permute-done((bf16[512,128]{1,0:T(8,128)(2,1)}, bf16[512,128]{1,0:T(8,128)(2,1)S(1)}, u32[]{:S(2)}, u32[]{:S(2)}) %collective-permute-start.3) | collective-permute-done | bytes 131104 | tf_op jit(solution)/shard_map/ppermute | solution.py:21
  11.4 1.7 %collective-permute-start.4 = (bf16[512,128]{1,0:T(8,128)(2,1)S(1)}, bf16[512,128]{1,0:T(8,128)(2,1)S(1)}, u32[]{:S(2)}, u32[]{:S(2)}) collective-permute-start(bf16[512,128]{1,0:T(8,128)(2,1)S(1)} %collective-permute-done.3.refs_0_), channel_id=1, source_target_pairs={{0,6},{1,7},{2,4},{3,5},{4,2},{5,3},{6,0},{7,1},{8,14},{9,15},{10,... | collective-permute-start | bytes 393224 | tf_op jit(solution)/shard_map/ppermute | solution.py:21
  13.1 0.5 collective-permute-start.5
  13.6 1.3 %collective-permute-start.6 = (bf16[512,128]{1,0:T(8,128)(2,1)S(1)}, bf16[512,128]{1,0:T(8,128)(2,1)S(1)}, u32[]{:S(2)}, u32[]{:S(2)}) collective-permute-start(bf16[512,128]{1,0:T(8,128)(2,1)S(1)} %collective-permute-done.3.refs_0_), channel_id=1, source_target_pairs={{0,4},{1,5},{2,6},{3,7},{4,0},{5,1},{6,2},{7,3},{8,12},{9,13},{10,... | collective-permute-start | bytes 393224 | tf_op jit(solution)/shard_map/ppermute | solution.py:21
  14.9 0.7 copy-done
  15.5 0.7 copy-done.1
  16.2 2.7 %stage_arguments.1 = (bf16[60,128,128]{2,1,0:T(8,128)(2,1)S(1)}, bf16[128,256]{1,0:T(8,128)(2,1)S(1)}, bf16[128,256]{1,0:T(8,128)(2,1)S(1)}, f32[4,128,128]{2,1,...) custom-call(s32[1]{0:T(128)} %bitcast.me_ref, ...), custom_call_target="tpu_custom_call" | custom-call | flops 3300000000 | bytes 10800000 | tf_op jit(solution)/shard_map/stage_arguments/pallas_call | solution.py:326
  18.9 0.1 collective-permute-start.7
  19.0 1.4 %collective-permute-done.4.refs_1_ = bf16[512,128]{1,0:T(8,128)(2,1)S(1)} collective-permute-done((bf16[512,128]{1,0:T(8,128)(2,1)S(1)}, bf16[512,128]{1,0:T(8,128)(2,1)S(1)}, u32[]{:S(2)}, u32[]{:S(2)}) %collective-permute-start.4) | collective-permute-done | bytes 131104 | tf_op jit(solution)/shard_map/ppermute | solution.py:21
  20.4 0.6 collective-permute-done.5.refs_2_
  21.0 0.1 collective-permute-done.6.refs_3_
  21.2 0.1 collective-permute-start.8
  21.3 1.9 %collective-permute-done.8.refs_3_ = bf16[4,512,128]{2,1,0:T(8,128)(2,1)S(1)} collective-permute-done((bf16[4,512,128]{2,1,0:T(8,128)(2,1)S(1)}, bf16[4,512,128]{2,1,0:T(8,128)(2,1)S(1)}, u32[]{:S(2)}, u32[]{:S(2)}) %collective-permute-start.8) | collective-permute-done | bytes 524320 | tf_op jit(solution)/shard_map/ppermute | solution.py:21
  23.2 4.5 %forward_layer.1 = (bf16[512,256]{1,0:T(8,128)(2,1)}, f32[512,128]{1,0:T(8,128)S(1)}, f32[128,256]{1,0:T(8,128)S(1)}, f32[128,256]{1,0:T(8,128)S(1)}, bf16[4,256,128]{2,1,0:T(8,128)(2,1)S(1)}) custom-call(s32[121]{0:T(128)S(4)} %get-tuple-element.36.index_ref, bf16[60,128,128]{2,1,0:T(8,128)(2,1)S(1)} %get-tuple-element.37.tiles_ref, ...), custom_call_target="tpu_custom_call" | custom-call | flops 5500000256 | bytes 18000000 | tf_op jit(solution)/shard_map/forward_layer/pallas_call | solution.py:303
  27.7 0.1 collective-permute-start.9
  27.8 2.9 %backward_tiles.1.acc_ref = f32[65,128,128]{2,1,0:T(8,128)S(1)} custom-call(s32[121]{0:T(128)S(4)} %get-tuple-element.36.index_ref, bf16[60,128,128]{2,1,0:T(8,128)(2,1)S(1)} %get-tuple-element.37.tiles_ref, bf16[4,256,128]{2,1,0:T(8,128)(2,1)S(1)} %get-tuple-element.46.gt_ref), custom_call_target="tpu_custom_call" | custom-call | flops 3849999872 | bytes 12600000 | tf_op jit(solution)/shard_map/backward_tiles/pallas_call | solution.py:303
  30.7 0.1 send_weights.1
  30.8 0.4 collective-permute-start.10
  31.3 0.2 collective-permute-start.17
  31.5 2.0 %collective-permute-done.10.got_ref = f32[4,512,128]{2,1,0:T(8,128)S(1)} collective-permute-done((f32[4,512,128]{2,1,0:T(8,128)S(1)}, f32[4,512,128]{2,1,0:T(8,128)S(1)}, u32[]{:S(2)}, u32[]{:S(2)}) %collective-permute-start.10) | collective-permute-done | bytes 1048608 | tf_op jit(solution)/shard_map/ppermute | solution.py:21
  33.5 0.1 pair_sum_weights.1
  33.6 1.6 %collective-permute-start.11 = (bf16[640,128]{1,0:T(8,128)(2,1)S(1)}, bf16[640,128]{1,0:T(8,128)(2,1)S(1)}, u32[]{:S(2)}, u32[]{:S(2)}) collective-permute-start(bf16[640,128]{1,0:T(8,128)(2,1)S(1)} %get-tuple-element.55), channel_id=1, source_target_pairs={{0,2},{1,3},{2,0},{3,1},{4,6},{5,7},{6,4},{7,5},{8,10},{9,11},{10,... | collective-permute-start | bytes 491528 | tf_op jit(solution)/shard_map/ppermute | solution.py:21
  35.2 0.3 collective-permute-start.12
  35.6 1.6 %collective-permute-start.13 = (bf16[640,128]{1,0:T(8,128)(2,1)S(1)}, bf16[640,128]{1,0:T(8,128)(2,1)S(1)}, u32[]{:S(2)}, u32[]{:S(2)}) collective-permute-start(bf16[640,128]{1,0:T(8,128)(2,1)S(1)} %get-tuple-element.57), channel_id=1, source_target_pairs={{0,6},{1,7},{2,4},{3,5},{4,2},{5,3},{6,0},{7,1},{8,14},{9,15},{10,... | collective-permute-start | bytes 491528 | tf_op jit(solution)/shard_map/ppermute | solution.py:21
  37.2 3.0 %collective-permute-done.11.refs_0_ = bf16[640,128]{1,0:T(8,128)(2,1)S(1)} collective-permute-done((bf16[640,128]{1,0:T(8,128)(2,1)S(1)}, bf16[640,128]{1,0:T(8,128)(2,1)S(1)}, u32[]{:S(2)}, u32[]{:S(2)}) %collective-permute-start.11) | collective-permute-done | bytes 163872 | tf_op jit(solution)/shard_map/ppermute | solution.py:21
  40.2 2.2 %collective-permute-done.12.refs_1_ = bf16[640,128]{1,0:T(8,128)(2,1)S(1)} collective-permute-done((bf16[640,128]{1,0:T(8,128)(2,1)S(1)}, bf16[640,128]{1,0:T(8,128)(2,1)S(1)}, u32[]{:S(2)}, u32[]{:S(2)}) %collective-permute-start.12) | collective-permute-done | bytes 163872 | tf_op jit(solution)/shard_map/ppermute | solution.py:21
  42.3 2.5 %collective-permute-done.13.refs_2_ = bf16[640,128]{1,0:T(8,128)(2,1)S(1)} collective-permute-done((bf16[640,128]{1,0:T(8,128)(2,1)S(1)}, bf16[640,128]{1,0:T(8,128)(2,1)S(1)}, u32[]{:S(2)}, u32[]{:S(2)}) %collective-permute-start.13) | collective-permute-done | bytes 163872 | tf_op jit(solution)/shard_map/ppermute | solution.py:21
  44.8 0.1 square_sum_weights.1
  44.9 1.8 %collective-permute-start.22 = (bf16[512,128]{1,0:T(8,128)(2,1)S(1)}, bf16[512,128]{1,0:T(8,128)(2,1)S(1)}, u32[]{:S(2)}, u32[]{:S(2)}) collective-permute-start(bf16[512,128]{1,0:T(8,128)(2,1)S(1)} %get-tuple-element.64), channel_id=1, source_target_pairs={{0,8},{1,9},{2,10},{3,11},{4,12},{5,13},{6,14},{7,15},{8,0},{9,1},... | collective-permute-start | bytes 393224 | tf_op jit(solution)/shard_map/ppermute | solution.py:21
  46.7 1.2 %collective-permute-start.14 = (f32[32,256]{1,0:T(8,128)S(1)}, f32[32,256]{1,0:T(8,128)S(1)}, u32[]{:S(2)}, u32[]{:S(2)}) collective-permute-start(f32[32,256]{1,0:T(8,128)S(1)} %get-tuple-element.58.own_ref), channel_id=1, source_target_pairs={{0,8},{1,9},{2,10},{3,11},{4,12},{5,13},{6,14},{7,15},{8,0},{9,1},... | collective-permute-start | bytes 98312 | tf_op jit(solution)/shard_map/ppermute | solution.py:21
  47.9 6.8 %collective-permute-done.14.got_ref = f32[32,256]{1,0:T(8,128)S(1)} collective-permute-done((f32[32,256]{1,0:T(8,128)S(1)}, f32[32,256]{1,0:T(8,128)S(1)}, u32[]{:S(2)}, u32[]{:S(2)}) %collective-permute-start.14) | collective-permute-done | bytes 32800 | tf_op jit(solution)/shard_map/ppermute | solution.py:21
  54.7 1.4 %collective-permute-start.15 = (f32[32,256]{1,0:T(8,128)S(1)}, f32[32,256]{1,0:T(8,128)S(1)}, u32[]{:S(2)}, u32[]{:S(2)}) collective-permute-start(f32[32,256]{1,0:T(8,128)S(1)} %weight_sum.1.refs_0_), channel_id=1, source_target_pairs={{0,2},{1,3},{2,0},{3,1},{4,6},{5,7},{6,4},{7,5},{8,10},{9,11},{10,... | collective-permute-start | bytes 98312 | tf_op jit(solution)/shard_map/ppermute | solution.py:21
  56.2 0.1 pair_sum.1
  56.3 0.7 collective-permute-start.18
  56.9 2.9 %collective-permute-start.20 = (bf16[512,128]{1,0:T(8,128)(2,1)S(1)}, bf16[512,128]{1,0:T(8,128)(2,1)S(1)}, u32[]{:S(2)}, u32[]{:S(2)}) collective-permute-start(bf16[512,128]{1,0:T(8,128)(2,1)S(1)} %get-tuple-element.63), channel_id=1, source_target_pairs={{0,6},{1,7},{2,4},{3,5},{4,2},{5,3},{6,0},{7,1},{8,14},{9,15},{10,... | collective-permute-start | bytes 393224 | tf_op jit(solution)/shard_map/ppermute | solution.py:21
  59.8 0.1 collective-permute-start.16
  60.0 2.1 %collective-permute-done.18.refs_0_ = bf16[512,128]{1,0:T(8,128)(2,1)S(1)} collective-permute-done((bf16[512,128]{1,0:T(8,128)(2,1)S(1)}, bf16[512,128]{1,0:T(8,128)(2,1)S(1)}, u32[]{:S(2)}, u32[]{:S(2)}) %collective-permute-start.18) | collective-permute-done | bytes 131104 | tf_op jit(solution)/shard_map/ppermute | solution.py:21
  62.1 1.3 %collective-permute-done.19.refs_1_ = bf16[512,128]{1,0:T(8,128)(2,1)S(1)} collective-permute-done((bf16[512,128]{1,0:T(8,128)(2,1)S(1)}, bf16[512,128]{1,0:T(8,128)(2,1)S(1)}, u32[]{:S(2)}, u32[]{:S(2)}) %collective-permute-start.19) | collective-permute-done | bytes 131104 | tf_op jit(solution)/shard_map/ppermute | solution.py:21
  63.4 2.7 %collective-permute-done.20.refs_2_ = bf16[512,128]{1,0:T(8,128)(2,1)S(1)} collective-permute-done((bf16[512,128]{1,0:T(8,128)(2,1)S(1)}, bf16[512,128]{1,0:T(8,128)(2,1)S(1)}, u32[]{:S(2)}, u32[]{:S(2)}) %collective-permute-start.20) | collective-permute-done | bytes 131104 | tf_op jit(solution)/shard_map/ppermute | solution.py:21
  66.1 0.1 near_sum.1.refs_2_.near_ref
  66.2 0.1 collective-permute-start.21
  66.3 0.1 main_sum.1.main_ref
  66.5 1.2 %collective-permute-done.21.other_ref = f32[2,2,32,256]{3,2,1,0:T(8,128)S(1)} collective-permute-done((f32[2,2,32,256]{3,2,1,0:T(8,128)S(1)}, f32[2,2,32,256]{3,2,1,0:T(8,128)S(1)}, u32[]{:S(2)}, u32[]{:S(2)}) %collective-permute-start.21) | collective-permute-done | bytes 131104 | tf_op jit(solution)/shard_map/ppermute | solution.py:21
  67.6 0.8 %write_gradients.1 = (bf16[512,128]{1,0:T(8,128)(2,1)}, f32[128,256]{1,0:T(8,128)}, f32[128,256]{1,0:T(8,128)}) custom-call(s32[121]{0:T(128)S(4)} %get-tuple-element.36.index_ref, f32[2,2,32,256]{3,2,1,0:T(8,128)S(1)} %pack_weights.3.weight_ref, f32[2,2,32,256]{3,2,1,0:T(8,128)S(1)} %collective-permute-done.21.other_ref, bf16[512,128]{1,0:T(8,128)(2,1)S(1)} %main_sum.1.main_ref), custom_call_target="tpu_custom_call" | custom-call | flops 220000000 | bytes 720000 | tf_op jit(solution)/shard_map/write_gradients/pallas_call | solution.py:303
  (19 shorter events, 0.2 us)
Async XLA Ops:
  0.6 10.7 %collective-permute-start.3 = (bf16[512,128]{1,0:T(8,128)(2,1)}, bf16[512,128]{1,0:T(8,128)(2,1)S(1)}, u32[]{:S(2)}, u32[]{:S(2)}) collective-permute-start(bf16[512,128]{1,0:T(8,128)(2,1)} %feat_ref.1), channel_id=1, source_target_pairs={{0,8},{1,9},{2,10},{3,11},{4,12},{5,13},{6,14},{7,15},{8,0},{9,1},... | collective-permute-start | bytes 393224 | tf_op jit(solution)/shard_map/ppermute | solution.py:21
  4.7 8.9 %collective-permute-start = (bf16[512,128]{1,0:T(8,128)(2,1)}, bf16[512,128]{1,0:T(8,128)(2,1)S(1)}, u32[]{:S(2)}, u32[]{:S(2)}) collective-permute-start(bf16[512,128]{1,0:T(8,128)(2,1)} %feat_ref.1), channel_id=1, source_target_pairs={{0,2},{1,3},{2,0},{3,1},{4,6},{5,7},{6,4},{7,5},{8,10},{9,11},{10,... | collective-permute-start | bytes 393224 | tf_op jit(solution)/shard_map/ppermute | solution.py:21
  6.3 12.6 %collective-permute-start.1 = (bf16[512,128]{1,0:T(8,128)(2,1)}, bf16[512,128]{1,0:T(8,128)(2,1)S(1)}, u32[]{:S(2)}, u32[]{:S(2)}) collective-permute-start(bf16[512,128]{1,0:T(8,128)(2,1)} %feat_ref.1), channel_id=1, source_target_pairs={{0,6},{1,7},{2,4},{3,5},{4,2},{5,3},{6,0},{7,1},{8,14},{9,15},{10,... | collective-permute-start | bytes 393224 | tf_op jit(solution)/shard_map/ppermute | solution.py:21
  7.8 11.1 %collective-permute-start.2 = (bf16[512,128]{1,0:T(8,128)(2,1)}, bf16[512,128]{1,0:T(8,128)(2,1)S(1)}, u32[]{:S(2)}, u32[]{:S(2)}) collective-permute-start(bf16[512,128]{1,0:T(8,128)(2,1)} %feat_ref.1), channel_id=1, source_target_pairs={{0,4},{1,5},{2,6},{3,7},{4,0},{5,1},{6,2},{7,3},{8,12},{9,13},{10,... | collective-permute-start | bytes 393224 | tf_op jit(solution)/shard_map/ppermute | solution.py:21
  11.4 9.1 %collective-permute-start.4 = (bf16[512,128]{1,0:T(8,128)(2,1)S(1)}, bf16[512,128]{1,0:T(8,128)(2,1)S(1)}, u32[]{:S(2)}, u32[]{:S(2)}) collective-permute-start(bf16[512,128]{1,0:T(8,128)(2,1)S(1)} %collective-permute-done.3.refs_0_), channel_id=1, source_target_pairs={{0,6},{1,7},{2,4},{3,5},{4,2},{5,3},{6,0},{7,1},{8,14},{9,15},{10,... | collective-permute-start | bytes 393224 | tf_op jit(solution)/shard_map/ppermute | solution.py:21
  13.1 7.9 %collective-permute-start.5 = (bf16[512,128]{1,0:T(8,128)(2,1)S(1)}, bf16[512,128]{1,0:T(8,128)(2,1)S(1)}, u32[]{:S(2)}, u32[]{:S(2)}) collective-permute-start(bf16[512,128]{1,0:T(8,128)(2,1)S(1)} %collective-permute-done.3.refs_0_), channel_id=1, source_target_pairs={{0,2},{1,3},{2,0},{3,1},{4,6},{5,7},{6,4},{7,5},{8,10},{9,11},{10,... | collective-permute-start | bytes 393224 | tf_op jit(solution)/shard_map/ppermute | solution.py:21
  13.6 7.6 %collective-permute-start.6 = (bf16[512,128]{1,0:T(8,128)(2,1)S(1)}, bf16[512,128]{1,0:T(8,128)(2,1)S(1)}, u32[]{:S(2)}, u32[]{:S(2)}) collective-permute-start(bf16[512,128]{1,0:T(8,128)(2,1)S(1)} %collective-permute-done.3.refs_0_), channel_id=1, source_target_pairs={{0,4},{1,5},{2,6},{3,7},{4,0},{5,1},{6,2},{7,3},{8,12},{9,13},{10,... | collective-permute-start | bytes 393224 | tf_op jit(solution)/shard_map/ppermute | solution.py:21
  14.8 0.7 copy-start
  15.5 0.7 copy-start.1
  18.9 2.4 %collective-permute-start.7 = (bf16[4,512,128]{2,1,0:T(8,128)(2,1)S(1)}, bf16[4,512,128]{2,1,0:T(8,128)(2,1)S(1)}, u32[]{:S(2)}, u32[]{:S(2)}) collective-permute-start(bf16[4,512,128]{2,1,0:T(8,128)(2,1)S(1)} %pack_square.2.refs_0_), channel_id=1, source_target_pairs={{0,1},{1,0},{2,3},{3,2},{4,5},{5,4},{6,7},{7,6},{8,9},{9,8},{10,11... | collective-permute-start | bytes 1572872 | tf_op jit(solution)/shard_map/ppermute | solution.py:21
  21.2 2.0 %collective-permute-start.8 = (bf16[4,512,128]{2,1,0:T(8,128)(2,1)S(1)}, bf16[4,512,128]{2,1,0:T(8,128)(2,1)S(1)}, u32[]{:S(2)}, u32[]{:S(2)}) collective-permute-start(bf16[4,512,128]{2,1,0:T(8,128)(2,1)S(1)} %pack_square.3.refs_1_), channel_id=1, source_target_pairs={{0,1},{1,0},{2,3},{3,2},{4,5},{5,4},{6,7},{7,6},{8,9},{9,8},{10,11... | collective-permute-start | bytes 1572872 | tf_op jit(solution)/shard_map/ppermute | solution.py:21
  27.7 3.0 %collective-permute-start.9 = (f32[128,256]{1,0:T(8,128)S(1)}, f32[128,256]{1,0:T(8,128)S(1)}, u32[]{:S(2)}, u32[]{:S(2)}) collective-permute-start(f32[128,256]{1,0:T(8,128)S(1)} %get-tuple-element.48), channel_id=1, source_target_pairs={{0,1},{1,0},{2,3},{3,2},{4,5},{5,4},{6,7},{7,6},{8,9},{9,8},{10,11... | collective-permute-start | bytes 393224 | tf_op jit(solution)/shard_map/ppermute | solution.py:21
  30.8 2.7 %collective-permute-start.10 = (f32[4,512,128]{2,1,0:T(8,128)S(1)}, f32[4,512,128]{2,1,0:T(8,128)S(1)}, u32[]{:S(2)}, u32[]{:S(2)}) collective-permute-start(f32[4,512,128]{2,1,0:T(8,128)S(1)} %get-tuple-element.50), channel_id=1, source_target_pairs={{0,1},{1,0},{2,3},{3,2},{4,5},{5,4},{6,7},{7,6},{8,9},{9,8},{10,11... | collective-permute-start | bytes 3145736 | tf_op jit(solution)/shard_map/ppermute | solution.py:21
  31.3 24.9 %collective-permute-start.17 = (f32[4,512,128]{2,1,0:T(8,128)S(1)}, f32[4,512,128]{2,1,0:T(8,128)S(1)}, u32[]{:S(2)}, u32[]{:S(2)}) collective-permute-start(f32[4,512,128]{2,1,0:T(8,128)S(1)} %send.1), channel_id=1, source_target_pairs={{0,1},{1,0},{2,3},{3,2},{4,5},{5,4},{6,7},{7,6},{8,9},{9,8},{10,11... | collective-permute-start | bytes 3145736 | tf_op jit(solution)/shard_map/ppermute | solution.py:21
  33.6 6.5 %collective-permute-start.11 = (bf16[640,128]{1,0:T(8,128)(2,1)S(1)}, bf16[640,128]{1,0:T(8,128)(2,1)S(1)}, u32[]{:S(2)}, u32[]{:S(2)}) collective-permute-start(bf16[640,128]{1,0:T(8,128)(2,1)S(1)} %get-tuple-element.55), channel_id=1, source_target_pairs={{0,2},{1,3},{2,0},{3,1},{4,6},{5,7},{6,4},{7,5},{8,10},{9,11},{10,... | collective-permute-start | bytes 491528 | tf_op jit(solution)/shard_map/ppermute | solution.py:21
  35.2 7.1 %collective-permute-start.12 = (bf16[640,128]{1,0:T(8,128)(2,1)S(1)}, bf16[640,128]{1,0:T(8,128)(2,1)S(1)}, u32[]{:S(2)}, u32[]{:S(2)}) collective-permute-start(bf16[640,128]{1,0:T(8,128)(2,1)S(1)} %get-tuple-element.56), channel_id=1, source_target_pairs={{0,4},{1,5},{2,6},{3,7},{4,0},{5,1},{6,2},{7,3},{8,12},{9,13},{10,... | collective-permute-start | bytes 491528 | tf_op jit(solution)/shard_map/ppermute | solution.py:21
  35.6 9.3 %collective-permute-start.13 = (bf16[640,128]{1,0:T(8,128)(2,1)S(1)}, bf16[640,128]{1,0:T(8,128)(2,1)S(1)}, u32[]{:S(2)}, u32[]{:S(2)}) collective-permute-start(bf16[640,128]{1,0:T(8,128)(2,1)S(1)} %get-tuple-element.57), channel_id=1, source_target_pairs={{0,6},{1,7},{2,4},{3,5},{4,2},{5,3},{6,0},{7,1},{8,14},{9,15},{10,... | collective-permute-start | bytes 491528 | tf_op jit(solution)/shard_map/ppermute | solution.py:21
  44.9 15.0 %collective-permute-start.22 = (bf16[512,128]{1,0:T(8,128)(2,1)S(1)}, bf16[512,128]{1,0:T(8,128)(2,1)S(1)}, u32[]{:S(2)}, u32[]{:S(2)}) collective-permute-start(bf16[512,128]{1,0:T(8,128)(2,1)S(1)} %get-tuple-element.64), channel_id=1, source_target_pairs={{0,8},{1,9},{2,10},{3,11},{4,12},{5,13},{6,14},{7,15},{8,0},{9,1},... | collective-permute-start | bytes 393224 | tf_op jit(solution)/shard_map/ppermute | solution.py:21
  46.7 8.0 %collective-permute-start.14 = (f32[32,256]{1,0:T(8,128)S(1)}, f32[32,256]{1,0:T(8,128)S(1)}, u32[]{:S(2)}, u32[]{:S(2)}) collective-permute-start(f32[32,256]{1,0:T(8,128)S(1)} %get-tuple-element.58.own_ref), channel_id=1, source_target_pairs={{0,8},{1,9},{2,10},{3,11},{4,12},{5,13},{6,14},{7,15},{8,0},{9,1},... | collective-permute-start | bytes 98312 | tf_op jit(solution)/shard_map/ppermute | solution.py:21
  54.7 5.1 %collective-permute-start.15 = (f32[32,256]{1,0:T(8,128)S(1)}, f32[32,256]{1,0:T(8,128)S(1)}, u32[]{:S(2)}, u32[]{:S(2)}) collective-permute-start(f32[32,256]{1,0:T(8,128)S(1)} %weight_sum.1.refs_0_), channel_id=1, source_target_pairs={{0,2},{1,3},{2,0},{3,1},{4,6},{5,7},{6,4},{7,5},{8,10},{9,11},{10,... | collective-permute-start | bytes 98312 | tf_op jit(solution)/shard_map/ppermute | solution.py:21
  56.3 5.8 %collective-permute-start.18 = (bf16[512,128]{1,0:T(8,128)(2,1)S(1)}, bf16[512,128]{1,0:T(8,128)(2,1)S(1)}, u32[]{:S(2)}, u32[]{:S(2)}) collective-permute-start(bf16[512,128]{1,0:T(8,128)(2,1)S(1)} %get-tuple-element.61), channel_id=1, source_target_pairs={{0,2},{1,3},{2,0},{3,1},{4,6},{5,7},{6,4},{7,5},{8,10},{9,11},{10,... | collective-permute-start | bytes 393224 | tf_op jit(solution)/shard_map/ppermute | solution.py:21
  56.9 6.4 %collective-permute-start.19 = (bf16[512,128]{1,0:T(8,128)(2,1)S(1)}, bf16[512,128]{1,0:T(8,128)(2,1)S(1)}, u32[]{:S(2)}, u32[]{:S(2)}) collective-permute-start(bf16[512,128]{1,0:T(8,128)(2,1)S(1)} %get-tuple-element.62), channel_id=1, source_target_pairs={{0,4},{1,5},{2,6},{3,7},{4,0},{5,1},{6,2},{7,3},{8,12},{9,13},{10,... | collective-permute-start | bytes 393224 | tf_op jit(solution)/shard_map/ppermute | solution.py:21
  56.9 9.1 %collective-permute-start.20 = (bf16[512,128]{1,0:T(8,128)(2,1)S(1)}, bf16[512,128]{1,0:T(8,128)(2,1)S(1)}, u32[]{:S(2)}, u32[]{:S(2)}) collective-permute-start(bf16[512,128]{1,0:T(8,128)(2,1)S(1)} %get-tuple-element.63), channel_id=1, source_target_pairs={{0,6},{1,7},{2,4},{3,5},{4,2},{5,3},{6,0},{7,1},{8,14},{9,15},{10,... | collective-permute-start | bytes 393224 | tf_op jit(solution)/shard_map/ppermute | solution.py:21
  59.8 6.4 %collective-permute-start.16 = (f32[2,32,256]{2,1,0:T(8,128)S(1)}, f32[2,32,256]{2,1,0:T(8,128)S(1)}, u32[]{:S(2)}, u32[]{:S(2)}) collective-permute-start(f32[2,32,256]{2,1,0:T(8,128)S(1)} %pack_weights.2.refs_0_), channel_id=1, source_target_pairs={{0,4},{1,5},{2,6},{3,7},{4,0},{5,1},{6,2},{7,3},{8,12},{9,13},{10,... | collective-permute-start | bytes 196616 | tf_op jit(solution)/shard_map/ppermute | solution.py:21
  66.2 1.4 %collective-permute-start.21 = (f32[2,2,32,256]{3,2,1,0:T(8,128)S(1)}, f32[2,2,32,256]{3,2,1,0:T(8,128)S(1)}, u32[]{:S(2)}, u32[]{:S(2)}) collective-permute-start(f32[2,2,32,256]{3,2,1,0:T(8,128)S(1)} %pack_weights.3.weight_ref), channel_id=1, source_target_pairs={{0,1},{1,0},{2,3},{3,2},{4,5},{5,4},{6,7},{7,6},{8,9},{9,8},{10,11... | collective-permute-start | bytes 393224 | tf_op jit(solution)/shard_map/ppermute | solution.py:21

commit v7 on v5

--- a/solution.py
+++ b/solution.py
@@ -14,7 +14,7 @@
 ANY = pl.BlockSpec(memory_space=pl.ANY)
 MIB = 1024 * 1024
 LAST = ((1,), (1,))
-NEAR_COST, SQUARE_COST, MAIN_COST = 8, 4, 10
+NEAR_COST, SQUARE_COST, MAIN_COST, FAR_COST = 4, 0.2, 0.2, 10
 
 
 def swap(x, n, offset):
@@ -200,51 +200,69 @@
         ref[...] = wkeep_ref[span, :] + wgot_ref[span, :]
 
 
-def pair_kernel(square, acc_ref, got_ref, own_ref, *pieces):
-    block_local = own_ref.shape[0] // BLOCK
-    for q, ref in enumerate((own_ref, *pieces)):
-        for b in range(block_local):
-            kept = acc_ref[(8 * square + 2 * q) * block_local + b]
-            ref[rows_of(b), :] = (kept + got_ref[q, rows_of(b), :]).astype(ref.dtype)
-
-
-def pair_weights_kernel(square, acc_ref, got_ref, w1, w2, w3, own_ref, *pieces):
-    pair_kernel(square, acc_ref, got_ref, own_ref, *pieces)
-    nodes, lanes = own_ref.shape
-    for weight_ref, ref in zip((w1, w2, w3), pieces):
-        rows, columns = weight_ref.shape
-        start = nodes
-        for part in split_bf16(weight_ref[...]):
+def put_weights(refs, ref, start):
+    lanes = ref.shape[1]
+    for weight in refs:
+        rows, columns = weight.shape
+        for part in split_bf16(weight):
             for column in range(0, columns, lanes):
                 ref[pl.ds(start, rows), :] = part[:, column:column + lanes]
                 start += rows
 
 
+def add_weights(weight_ref, ref, start, out_ref):
+    lanes = ref.shape[1]
+    rows, columns = weight_ref.shape
+    for column in range(0, columns, lanes):
+        high = ref[pl.ds(start + column // lanes * rows, rows), :]
+        low = ref[pl.ds(start + (columns + column) // lanes * rows, rows), :]
+        span = pl.ds(column, lanes)
+        out_ref[:, span] = weight_ref[:, span] + (high.astype(F32) + low.astype(F32))
+
+
+def pair_kernel(square, kept, sent, acc_ref, got_ref, *refs):
+    weights, refs = refs[:-3], refs[-3:]
+    nodes = refs[0].shape[0]
+    block_local = nodes // BLOCK
+    places = [(refs[0], 0), (refs[1], 0), (refs[2], 0), (refs[2], nodes)]
+    for q, (ref, start) in zip((*kept, *sent), places):
+        for b in range(block_local):
+            total = acc_ref[(8 * square + 2 * q) * block_local + b] + got_ref[q, rows_of(b), :]
+            ref[pl.ds(start + b * BLOCK, BLOCK), :] = total.astype(ref.dtype)
+    put_weights([ref[...] for ref in weights], refs[2], 2 * nodes)
+
+
+def middle_kernel(first_ref, second_ref, got_ref, *refs):
+    nodes = first_ref.shape[0]
+    if len(refs) == 2:
+        first_out, second_out = refs
+    else:
+        weight_ref, weight_send_ref, first_out, second_out, weight_out, scratch = refs
+        rows = 2 * weight_ref.shape[0] * weight_ref.shape[1] // first_ref.shape[1]
+        add_weights(weight_ref, got_ref, 2 * nodes, weight_out)
+        add_weights(weight_send_ref, got_ref, 2 * nodes + rows, scratch)
+        put_weights([scratch[...]], second_out, nodes)
+    for ref, start, out in ((first_ref, 0, first_out), (second_ref, nodes, second_out)):
+        total = ref[...] + got_ref[pl.ds(start, nodes), :].astype(F32)
+        out[pl.ds(0, nodes), :] = total.astype(out.dtype)
+
+
 def add_two_kernel(own_ref, got_ref, out_ref):
     out_ref[...] = own_ref[...] + got_ref[...]
 
 
 def add_kernel(own_ref, *refs):
-    total = own_ref[...]
+    total = own_ref[...].astype(F32)
     for got_ref in refs[:-1]:
         total = total + got_ref[...].astype(F32)
-    refs[-1][...] = total.astype(BF16)
+    refs[-1][...] = total.astype(refs[-1].dtype)
 
 
 def add_weights_kernel(weight_ref, own_ref, *refs):
     got_refs, (out_ref, weight_out) = refs[:-2], refs[-2:]
-    nodes, lanes = own_ref.shape
+    nodes = own_ref.shape[0]
     add_kernel(own_ref, *[ref.at[pl.ds(0, nodes), :] for ref in got_refs], out_ref)
-    rows, columns = weight_ref.shape
-    cuts = columns // lanes
-    for cut in range(cuts):
-        span = pl.ds(cut * lanes, lanes)
-        total = weight_ref[:, span]
-        for ref in got_refs[:3]:
-            high = ref[pl.ds(nodes + cut * rows, rows), :]
-            low = ref[pl.ds(nodes + (cuts + cut) * rows, rows), :]
-            total = total + (high.astype(F32) + low.astype(F32))
-        weight_out[:, span] = total
+    add_weights(weight_ref, got_refs[0], nodes, weight_out)
 
 
 def near_kernel(base_ref, own_ref, *refs):
@@ -379,18 +397,26 @@
             send[s] = call(
                 functools.partial(send_kernel, s, block_local), "send", send_shape, (acc,))
 
-    extra = result((nodes + 2 * chunk.shape[0] * (hidden // feat_in), feat_in), BF16)
+    rows = chunk.shape[0]
+    more = 2 * rows * hidden // feat_in
     terms = [None] * squares
     for s in range(squares - 1, -1, -1):
-        operands = (acc, swap(send[s], n, 1))
-        if s == squares - 1:
-            own, *pieces = call(
-                functools.partial(pair_weights_kernel, s), "pair_sum_weights", (wide, extra, extra, extra),
-                operands + (w1, w2, w3))
+        heavy = s == squares - 1
+        along, across = (2, 4) if s else (4, 2)
+        kept, sent = ((0, 2), (1, 3)) if s else ((0, 1), (2, 3))
+        first, second, piece_out = call(
+            functools.partial(pair_kernel, s, kept, sent), "pair_sum",
+            (wide, wide, result((2 * nodes + 2 * more * heavy, feat_in), BF16)),
+            (acc, swap(send[s], n, 1)) + ((w1, w3) if heavy else ()))
+        out_shape = (wide, result((nodes + more * heavy, feat_in), BF16))
+        got = swap(piece_out, n, along)
+        if heavy:
+            first, piece_out, wsum = call(
+                middle_kernel, "middle_sum_weights", out_shape + (chunk,),
+                (first, second, got, w0, w2), scratch_shapes=[pltpu.VMEM((rows, hidden), F32)])
         else:
-            own, *pieces = call(
-                functools.partial(pair_kernel, s), "pair_sum", (wide, piece, piece, piece), operands)
-        terms[s] = [own, *[swap(x, n, 2 * q + 2) for q, x in enumerate(pieces)]]
+            first, piece_out = call(middle_kernel, "middle_sum", out_shape, (first, second, got))
+        terms[s] = [first, swap(piece_out, n, across)]
     near_total = call(near_kernel, "near_sum", wide, (base, *terms[0]), cost_us=NEAR_COST)
     terms[0] = [near_total]
     distance = 1
@@ -398,20 +424,26 @@
         for s in range(squares - distance, 0, -2 * distance):
             if s == squares - 1:
                 total, wsum = call(
-                    add_weights_kernel, "square_sum_weights", (piece, chunk), (w0, *terms[s]),
+                    add_weights_kernel, "square_sum_weights", (piece, chunk), (wsum, *terms[s]),
                     cost_us=SQUARE_COST)
             else:
                 total = call(add_kernel, "square_sum", piece, terms[s], cost_us=SQUARE_COST)
-            terms[s - distance].append(swap(total, n, 8 * distance))
+            if s == distance:
+                total = swap(total, n, 8 * distance)
+                terms[0].append(call(add_kernel, "far_sum", wide, (total,), cost_us=FAR_COST))
+            else:
+                terms[s - distance].append(swap(total, n, 8 * distance))
         distance *= 2
     bit = 8
     while bit < n:
         wsum = call(add_two_kernel, "weight_sum", chunk, (wsum, swap(wsum, n, bit)))
         bit *= 2
-    rows = chunk.shape[0]
-    two = call(functools.partial(pack_kernel, (0, 1)), "pack_weights", result((2, rows, hidden), F32), (wsum, swap(wsum, n, 2)))
+    two = call(
+        functools.partial(pack_kernel, (0, 1)), "pack_weights", result((2, rows, hidden), F32),
+        (wsum, swap(wsum, n, 2), near_total))
     mine = call(
-        functools.partial(pack_kernel, (0, 1)), "pack_weights", result((2, 2, rows, hidden), F32), (two, swap(two, n, 4), near_total))
+        functools.partial(pack_kernel, (0, 1)), "pack_weights", result((2, 2, rows, hidden), F32),
+        (two, swap(two, n, 4)))
     main = call(main_kernel, "main_sum", piece, terms[0], cost_us=MAIN_COST)
     grad_input, grad_self, grad_neigh = call(
         last_kernel, "write_gradients",

time: 61.4 us -> 67 us (1.091)
  waiting for transfers between devices: 22.6 us -> 32.5 us
  starting transfers between devices: 24.9 us -> 20.5 us
    ppermute x23 -> x21, waiting for transfers between devices: 22.6 us -> 32.5 us  [swap(): return lax.ppermute(x, 'row', [(i, i ^ offset) for i in range(n)])]
    ppermute x23 -> x21, starting transfers between devices: 24.9 us -> 20.5 us  [swap(): return lax.ppermute(x, 'row', [(i, i ^ offset) for i in range(n)])]
    pallas_call x15 -> x18, Pallas kernels: 8.87 us -> 8.98 us  [call(): pl.pallas_call(kernel, out_shape=out_shape, in_specs=specs, out_specs=out...]
  transfers between devices with their start and end apart: 23 -> 21, of which waited for: 14 -> 12; matrix products, arithmetic and copies ran while one was open for 0% -> 0% of each run, Pallas kernels for 10% -> 9%
where the time goes in v7:
time: 67 us; the launch traced here: 66.8 us
  waiting for transfers between devices  32.5 us (49%)
  starting transfers between devices  20.5 us (31%)
  Pallas kernels  11.7 us (17%)
  local copies, waits for them, and re-layouts  1.31 us (2%)
  between operations  0.81 us (1%)
    ppermute x21, waiting for transfers between devices, swap(): return lax.ppermute(x, 'row', [(i, i ^ offset) for i in range(n)])  32.5 us
    ppermute x21, starting transfers between devices, swap(): return lax.ppermute(x, 'row', [(i, i ^ offset) for i in range(n)])  20.5 us
    pallas_call x18, Pallas kernels, call(): pl.pallas_call(kernel, out_shape=out_shape, in_specs=specs, out_specs=out...  8.98 us
    pallas_call x1, Pallas kernels, body(): pl.pallas_call(stage_kernel, out_shape=(result(tiles.shape, BF16), result...  2.68 us
  transfers between devices with their start and end apart: 21, of which 12 were waited for; matrix products, arithmetic and copies ran while one was open for 0% of the time, Pallas kernels for 9%

profile of v7, /device:TPU:0, one launch (start us, length us, event | category | flops | bytes accessed | tf_op | source)
XLA Modules:
  0.0 66.8 jit_solution(16183761949025212394)
XLA Ops:
  0.6 4.1 %collective-permute-start.3 = (bf16[512,128]{1,0:T(8,128)(2,1)}, bf16[512,128]{1,0:T(8,128)(2,1)S(1)}, u32[]{:S(2)}, u32[]{:S(2)}) collective-permute-start(bf16[512,128]{1,0:T(8,128)(2,1)} %feat_ref.1), channel_id=1, source_target_pairs={{0,8},{1,9},{2,10},{3,11},{4,12},{5,13},{6,14},{7,15},{8,0},{9,1},... | collective-permute-start | bytes 393224 | tf_op jit(solution)/shard_map/ppermute | solution.py:21
  4.7 1.5 %collective-permute-start = (bf16[512,128]{1,0:T(8,128)(2,1)}, bf16[512,128]{1,0:T(8,128)(2,1)S(1)}, u32[]{:S(2)}, u32[]{:S(2)}) collective-permute-start(bf16[512,128]{1,0:T(8,128)(2,1)} %feat_ref.1), channel_id=1, source_target_pairs={{0,2},{1,3},{2,0},{3,1},{4,6},{5,7},{6,4},{7,5},{8,10},{9,11},{10,... | collective-permute-start | bytes 393224 | tf_op jit(solution)/shard_map/ppermute | solution.py:21
  6.3 1.5 %collective-permute-start.1 = (bf16[512,128]{1,0:T(8,128)(2,1)}, bf16[512,128]{1,0:T(8,128)(2,1)S(1)}, u32[]{:S(2)}, u32[]{:S(2)}) collective-permute-start(bf16[512,128]{1,0:T(8,128)(2,1)} %feat_ref.1), channel_id=1, source_target_pairs={{0,6},{1,7},{2,4},{3,5},{4,2},{5,3},{6,0},{7,1},{8,14},{9,15},{10,... | collective-permute-start | bytes 393224 | tf_op jit(solution)/shard_map/ppermute | solution.py:21
  7.8 0.4 collective-permute-start.2
  8.2 3.1 %collective-permute-done.3.refs_0_ = bf16[512,128]{1,0:T(8,128)(2,1)S(1)} collective-permute-done((bf16[512,128]{1,0:T(8,128)(2,1)}, bf16[512,128]{1,0:T(8,128)(2,1)S(1)}, u32[]{:S(2)}, u32[]{:S(2)}) %collective-permute-start.3) | collective-permute-done | bytes 131104 | tf_op jit(solution)/shard_map/ppermute | solution.py:21
  11.4 1.7 %collective-permute-start.4 = (bf16[512,128]{1,0:T(8,128)(2,1)S(1)}, bf16[512,128]{1,0:T(8,128)(2,1)S(1)}, u32[]{:S(2)}, u32[]{:S(2)}) collective-permute-start(bf16[512,128]{1,0:T(8,128)(2,1)S(1)} %collective-permute-done.3.refs_0_), channel_id=1, source_target_pairs={{0,6},{1,7},{2,4},{3,5},{4,2},{5,3},{6,0},{7,1},{8,14},{9,15},{10,... | collective-permute-start | bytes 393224 | tf_op jit(solution)/shard_map/ppermute | solution.py:21
  13.1 0.5 collective-permute-start.5
  13.6 0.0 collective-permute-done.refs_1_
  13.6 1.3 %collective-permute-start.6 = (bf16[512,128]{1,0:T(8,128)(2,1)S(1)}, bf16[512,128]{1,0:T(8,128)(2,1)S(1)}, u32[]{:S(2)}, u32[]{:S(2)}) collective-permute-start(bf16[512,128]{1,0:T(8,128)(2,1)S(1)} %collective-permute-done.3.refs_0_), channel_id=1, source_target_pairs={{0,4},{1,5},{2,6},{3,7},{4,0},{5,1},{6,2},{7,3},{8,12},{9,13},{10,... | collective-permute-start | bytes 393224 | tf_op jit(solution)/shard_map/ppermute | solution.py:21
  14.9 0.7 copy-done
  15.5 0.7 copy-done.1
  16.2 2.7 %stage_arguments.1 = (bf16[60,128,128]{2,1,0:T(8,128)(2,1)S(1)}, bf16[128,256]{1,0:T(8,128)(2,1)S(1)}, bf16[128,256]{1,0:T(8,128)(2,1)S(1)}, f32[4,128,128]{2,1,...) custom-call(s32[1]{0:T(128)} %bitcast.me_ref, ...), custom_call_target="tpu_custom_call" | custom-call | flops 3300000000 | bytes 10800000 | tf_op jit(solution)/shard_map/stage_arguments/pallas_call | solution.py:343
  18.8 0.0 collective-permute-done.1.refs_2_
  18.9 0.1 collective-permute-start.7
  19.0 1.4 %collective-permute-done.4.refs_1_ = bf16[512,128]{1,0:T(8,128)(2,1)S(1)} collective-permute-done((bf16[512,128]{1,0:T(8,128)(2,1)S(1)}, bf16[512,128]{1,0:T(8,128)(2,1)S(1)}, u32[]{:S(2)}, u32[]{:S(2)}) %collective-permute-start.4) | collective-permute-done | bytes 131104 | tf_op jit(solution)/shard_map/ppermute | solution.py:21
  20.4 0.6 collective-permute-done.5.refs_2_
  21.0 0.1 collective-permute-done.6.refs_3_
  21.2 0.1 collective-permute-start.8
  21.3 1.9 %collective-permute-done.8.refs_3_ = bf16[4,512,128]{2,1,0:T(8,128)(2,1)S(1)} collective-permute-done((bf16[4,512,128]{2,1,0:T(8,128)(2,1)S(1)}, bf16[4,512,128]{2,1,0:T(8,128)(2,1)S(1)}, u32[]{:S(2)}, u32[]{:S(2)}) %collective-permute-start.8) | collective-permute-done | bytes 524320 | tf_op jit(solution)/shard_map/ppermute | solution.py:21
  23.2 4.5 %forward_layer.1 = (bf16[512,256]{1,0:T(8,128)(2,1)}, f32[512,128]{1,0:T(8,128)S(1)}, f32[128,256]{1,0:T(8,128)S(1)}, f32[128,256]{1,0:T(8,128)S(1)}, bf16[4,256,128]{2,1,0:T(8,128)(2,1)S(1)}) custom-call(s32[121]{0:T(128)S(4)} %get-tuple-element.39.index_ref, bf16[60,128,128]{2,1,0:T(8,128)(2,1)S(1)} %get-tuple-element.40.tiles_ref, ...), custom_call_target="tpu_custom_call" | custom-call | flops 5500000256 | bytes 18000000 | tf_op jit(solution)/shard_map/forward_layer/pallas_call | solution.py:320
  27.7 0.1 collective-permute-start.9
  27.8 2.9 %backward_tiles.1.acc_ref = f32[65,128,128]{2,1,0:T(8,128)S(1)} custom-call(s32[121]{0:T(128)S(4)} %get-tuple-element.39.index_ref, bf16[60,128,128]{2,1,0:T(8,128)(2,1)S(1)} %get-tuple-element.40.tiles_ref, bf16[4,256,128]{2,1,0:T(8,128)(2,1)S(1)} %get-tuple-element.49.gt_ref), custom_call_target="tpu_custom_call" | custom-call | flops 3849999872 | bytes 12600000 | tf_op jit(solution)/shard_map/backward_tiles/pallas_call | solution.py:320
  30.7 0.1 send_weights.1
  30.7 0.5 collective-permute-start.10
  31.2 0.1 send.1
  31.3 0.2 collective-permute-start.15
  31.5 2.0 %collective-permute-done.10.got_ref = f32[4,512,128]{2,1,0:T(8,128)S(1)} collective-permute-done((f32[4,512,128]{2,1,0:T(8,128)S(1)}, f32[4,512,128]{2,1,0:T(8,128)S(1)}, u32[]{:S(2)}, u32[]{:S(2)}) %collective-permute-start.10) | collective-permute-done | bytes 1048608 | tf_op jit(solution)/shard_map/ppermute | solution.py:21
  33.5 0.1 pair_sum.2
  33.6 1.6 %collective-permute-start.11 = (bf16[1280,128]{1,0:T(8,128)(2,1)S(1)}, bf16[1280,128]{1,0:T(8,128)(2,1)S(1)}, u32[]{:S(2)}, u32[]{:S(2)}) collective-permute-start(bf16[1280,128]{1,0:T(8,128)(2,1)S(1)} %get-tuple-element.57), channel_id=1, source_target_pairs={{0,2},{1,3},{2,0},{3,1},{4,6},{5,7},{6,4},{7,5},{8,10},{9,11},{10,... | collective-permute-start | bytes 983048 | tf_op jit(solution)/shard_map/ppermute | solution.py:21
  35.2 0.1 pair_sum.3
  35.4 0.4 collective-permute-start.16
  35.7 7.9 %collective-permute-done.11.got_ref = bf16[1280,128]{1,0:T(8,128)(2,1)S(1)} collective-permute-done((bf16[1280,128]{1,0:T(8,128)(2,1)S(1)}, bf16[1280,128]{1,0:T(8,128)(2,1)S(1)}, u32[]{:S(2)}, u32[]{:S(2)}) %collective-permute-start.11) | collective-permute-done | bytes 327712 | tf_op jit(solution)/shard_map/ppermute | solution.py:21
  43.7 0.1 middle_sum_weights.1
  43.7 0.5 collective-permute-start.12
  44.3 1.5 %collective-permute-start.17 = (bf16[512,128]{1,0:T(8,128)(2,1)S(1)}, bf16[512,128]{1,0:T(8,128)(2,1)S(1)}, u32[]{:S(2)}, u32[]{:S(2)}) collective-permute-start(bf16[512,128]{1,0:T(8,128)(2,1)S(1)} %get-tuple-element.69), channel_id=1, source_target_pairs={{0,2},{1,3},{2,0},{3,1},{4,6},{5,7},{6,4},{7,5},{8,10},{9,11},{10,... | collective-permute-start | bytes 393224 | tf_op jit(solution)/shard_map/ppermute | solution.py:21
  45.8 3.7 %collective-permute-done.12.refs_0_ = bf16[640,128]{1,0:T(8,128)(2,1)S(1)} collective-permute-done((bf16[640,128]{1,0:T(8,128)(2,1)S(1)}, bf16[640,128]{1,0:T(8,128)(2,1)S(1)}, u32[]{:S(2)}, u32[]{:S(2)}) %collective-permute-start.12) | collective-permute-done | bytes 163872 | tf_op jit(solution)/shard_map/ppermute | solution.py:21
  49.5 1.8 %collective-permute-start.13 = (f32[32,256]{1,0:T(8,128)S(1)}, f32[32,256]{1,0:T(8,128)S(1)}, u32[]{:S(2)}, u32[]{:S(2)}) collective-permute-start(f32[32,256]{1,0:T(8,128)S(1)} %get-tuple-element.63.own_ref), channel_id=1, source_target_pairs={{0,8},{1,9},{2,10},{3,11},{4,12},{5,13},{6,14},{7,15},{8,0},{9,1},... | collective-permute-start | bytes 98312 | tf_op jit(solution)/shard_map/ppermute | solution.py:21
  51.3 1.2 %collective-permute-start.20 = (bf16[512,128]{1,0:T(8,128)(2,1)S(1)}, bf16[512,128]{1,0:T(8,128)(2,1)S(1)}, u32[]{:S(2)}, u32[]{:S(2)}) collective-permute-start(bf16[512,128]{1,0:T(8,128)(2,1)S(1)} %get-tuple-element.70), channel_id=1, source_target_pairs={{0,8},{1,9},{2,10},{3,11},{4,12},{5,13},{6,14},{7,15},{8,0},{9,1},... | collective-permute-start | bytes 393224 | tf_op jit(solution)/shard_map/ppermute | solution.py:21
  52.5 4.0 %collective-permute-done.13.got_ref = f32[32,256]{1,0:T(8,128)S(1)} collective-permute-done((f32[32,256]{1,0:T(8,128)S(1)}, f32[32,256]{1,0:T(8,128)S(1)}, u32[]{:S(2)}, u32[]{:S(2)}) %collective-permute-start.13) | collective-permute-done | bytes 32800 | tf_op jit(solution)/shard_map/ppermute | solution.py:21
  56.4 1.4 %collective-permute-start.14 = (f32[32,256]{1,0:T(8,128)S(1)}, f32[32,256]{1,0:T(8,128)S(1)}, u32[]{:S(2)}, u32[]{:S(2)}) collective-permute-start(f32[32,256]{1,0:T(8,128)S(1)} %weight_sum.1.refs_0_), channel_id=1, source_target_pairs={{0,2},{1,3},{2,0},{3,1},{4,6},{5,7},{6,4},{7,5},{8,10},{9,11},{10,... | collective-permute-start | bytes 98312 | tf_op jit(solution)/shard_map/ppermute | solution.py:21
  57.9 0.0 collective-permute-done.17.refs_0_
  57.9 0.1 near_sum.1.refs_2_.near_ref
  58.0 2.3 %collective-permute-done.14.refs_1_ = f32[32,256]{1,0:T(8,128)S(1)} collective-permute-done((f32[32,256]{1,0:T(8,128)S(1)}, f32[32,256]{1,0:T(8,128)S(1)}, u32[]{:S(2)}, u32[]{:S(2)}) %collective-permute-start.14) | collective-permute-done | bytes 32800 | tf_op jit(solution)/shard_map/ppermute | solution.py:21
  60.4 4.3 %collective-permute-done.18.refs_1_ = f32[2,32,256]{2,1,0:T(8,128)S(1)} collective-permute-done((f32[2,32,256]{2,1,0:T(8,128)S(1)}, f32[2,32,256]{2,1,0:T(8,128)S(1)}, u32[]{:S(2)}, u32[]{:S(2)}) %collective-permute-start.18) | collective-permute-done | bytes 65568 | tf_op jit(solution)/shard_map/ppermute | solution.py:21
  64.6 0.1 collective-permute-start.19
  64.7 0.1 main_sum.1.main_ref
  64.9 1.2 %collective-permute-done.19.other_ref = f32[2,2,32,256]{3,2,1,0:T(8,128)S(1)} collective-permute-done((f32[2,2,32,256]{3,2,1,0:T(8,128)S(1)}, f32[2,2,32,256]{3,2,1,0:T(8,128)S(1)}, u32[]{:S(2)}, u32[]{:S(2)}) %collective-permute-start.19) | collective-permute-done | bytes 131104 | tf_op jit(solution)/shard_map/ppermute | solution.py:21
  66.0 0.8 %write_gradients.1 = (bf16[512,128]{1,0:T(8,128)(2,1)}, f32[128,256]{1,0:T(8,128)}, f32[128,256]{1,0:T(8,128)}) custom-call(s32[121]{0:T(128)S(4)} %get-tuple-element.39.index_ref, f32[2,2,32,256]{3,2,1,0:T(8,128)S(1)} %pack_weights.3.weight_ref, f32[2,2,32,256]{3,2,1,0:T(8,128)S(1)} %collective-permute-done.19.other_ref, bf16[512,128]{1,0:T(8,128)(2,1)S(1)} %main_sum.1.main_ref), custom_call_target="tpu_custom_call" | custom-call | flops 220000000 | bytes 720000 | tf_op jit(solution)/shard_map/write_gradients/pallas_call | solution.py:320
  (17 shorter events, 0.2 us)
Async XLA Ops:
  0.6 10.7 %collective-permute-start.3 = (bf16[512,128]{1,0:T(8,128)(2,1)}, bf16[512,128]{1,0:T(8,128)(2,1)S(1)}, u32[]{:S(2)}, u32[]{:S(2)}) collective-permute-start(bf16[512,128]{1,0:T(8,128)(2,1)} %feat_ref.1), channel_id=1, source_target_pairs={{0,8},{1,9},{2,10},{3,11},{4,12},{5,13},{6,14},{7,15},{8,0},{9,1},... | collective-permute-start | bytes 393224 | tf_op jit(solution)/shard_map/ppermute | solution.py:21
  4.7 8.9 %collective-permute-start = (bf16[512,128]{1,0:T(8,128)(2,1)}, bf16[512,128]{1,0:T(8,128)(2,1)S(1)}, u32[]{:S(2)}, u32[]{:S(2)}) collective-permute-start(bf16[512,128]{1,0:T(8,128)(2,1)} %feat_ref.1), channel_id=1, source_target_pairs={{0,2},{1,3},{2,0},{3,1},{4,6},{5,7},{6,4},{7,5},{8,10},{9,11},{10,... | collective-permute-start | bytes 393224 | tf_op jit(solution)/shard_map/ppermute | solution.py:21
  6.3 12.6 %collective-permute-start.1 = (bf16[512,128]{1,0:T(8,128)(2,1)}, bf16[512,128]{1,0:T(8,128)(2,1)S(1)}, u32[]{:S(2)}, u32[]{:S(2)}) collective-permute-start(bf16[512,128]{1,0:T(8,128)(2,1)} %feat_ref.1), channel_id=1, source_target_pairs={{0,6},{1,7},{2,4},{3,5},{4,2},{5,3},{6,0},{7,1},{8,14},{9,15},{10,... | collective-permute-start | bytes 393224 | tf_op jit(solution)/shard_map/ppermute | solution.py:21
  7.8 11.1 %collective-permute-start.2 = (bf16[512,128]{1,0:T(8,128)(2,1)}, bf16[512,128]{1,0:T(8,128)(2,1)S(1)}, u32[]{:S(2)}, u32[]{:S(2)}) collective-permute-start(bf16[512,128]{1,0:T(8,128)(2,1)} %feat_ref.1), channel_id=1, source_target_pairs={{0,4},{1,5},{2,6},{3,7},{4,0},{5,1},{6,2},{7,3},{8,12},{9,13},{10,... | collective-permute-start | bytes 393224 | tf_op jit(solution)/shard_map/ppermute | solution.py:21
  11.4 9.1 %collective-permute-start.4 = (bf16[512,128]{1,0:T(8,128)(2,1)S(1)}, bf16[512,128]{1,0:T(8,128)(2,1)S(1)}, u32[]{:S(2)}, u32[]{:S(2)}) collective-permute-start(bf16[512,128]{1,0:T(8,128)(2,1)S(1)} %collective-permute-done.3.refs_0_), channel_id=1, source_target_pairs={{0,6},{1,7},{2,4},{3,5},{4,2},{5,3},{6,0},{7,1},{8,14},{9,15},{10,... | collective-permute-start | bytes 393224 | tf_op jit(solution)/shard_map/ppermute | solution.py:21
  13.1 7.9 %collective-permute-start.5 = (bf16[512,128]{1,0:T(8,128)(2,1)S(1)}, bf16[512,128]{1,0:T(8,128)(2,1)S(1)}, u32[]{:S(2)}, u32[]{:S(2)}) collective-permute-start(bf16[512,128]{1,0:T(8,128)(2,1)S(1)} %collective-permute-done.3.refs_0_), channel_id=1, source_target_pairs={{0,2},{1,3},{2,0},{3,1},{4,6},{5,7},{6,4},{7,5},{8,10},{9,11},{10,... | collective-permute-start | bytes 393224 | tf_op jit(solution)/shard_map/ppermute | solution.py:21
  13.6 7.6 %collective-permute-start.6 = (bf16[512,128]{1,0:T(8,128)(2,1)S(1)}, bf16[512,128]{1,0:T(8,128)(2,1)S(1)}, u32[]{:S(2)}, u32[]{:S(2)}) collective-permute-start(bf16[512,128]{1,0:T(8,128)(2,1)S(1)} %collective-permute-done.3.refs_0_), channel_id=1, source_target_pairs={{0,4},{1,5},{2,6},{3,7},{4,0},{5,1},{6,2},{7,3},{8,12},{9,13},{10,... | collective-permute-start | bytes 393224 | tf_op jit(solution)/shard_map/ppermute | solution.py:21
  14.8 0.7 copy-start
  15.5 0.7 copy-start.1
  18.9 2.4 %collective-permute-start.7 = (bf16[4,512,128]{2,1,0:T(8,128)(2,1)S(1)}, bf16[4,512,128]{2,1,0:T(8,128)(2,1)S(1)}, u32[]{:S(2)}, u32[]{:S(2)}) collective-permute-start(bf16[4,512,128]{2,1,0:T(8,128)(2,1)S(1)} %pack_square.2.refs_0_), channel_id=1, source_target_pairs={{0,1},{1,0},{2,3},{3,2},{4,5},{5,4},{6,7},{7,6},{8,9},{9,8},{10,11... | collective-permute-start | bytes 1572872 | tf_op jit(solution)/shard_map/ppermute | solution.py:21
  21.2 2.0 %collective-permute-start.8 = (bf16[4,512,128]{2,1,0:T(8,128)(2,1)S(1)}, bf16[4,512,128]{2,1,0:T(8,128)(2,1)S(1)}, u32[]{:S(2)}, u32[]{:S(2)}) collective-permute-start(bf16[4,512,128]{2,1,0:T(8,128)(2,1)S(1)} %pack_square.3.refs_1_), channel_id=1, source_target_pairs={{0,1},{1,0},{2,3},{3,2},{4,5},{5,4},{6,7},{7,6},{8,9},{9,8},{10,11... | collective-permute-start | bytes 1572872 | tf_op jit(solution)/shard_map/ppermute | solution.py:21
  27.7 3.0 %collective-permute-start.9 = (f32[128,256]{1,0:T(8,128)S(1)}, f32[128,256]{1,0:T(8,128)S(1)}, u32[]{:S(2)}, u32[]{:S(2)}) collective-permute-start(f32[128,256]{1,0:T(8,128)S(1)} %get-tuple-element.51), channel_id=1, source_target_pairs={{0,1},{1,0},{2,3},{3,2},{4,5},{5,4},{6,7},{7,6},{8,9},{9,8},{10,11... | collective-permute-start | bytes 393224 | tf_op jit(solution)/shard_map/ppermute | solution.py:21
  30.7 2.7 %collective-permute-start.10 = (f32[4,512,128]{2,1,0:T(8,128)S(1)}, f32[4,512,128]{2,1,0:T(8,128)S(1)}, u32[]{:S(2)}, u32[]{:S(2)}) collective-permute-start(f32[4,512,128]{2,1,0:T(8,128)S(1)} %get-tuple-element.52), channel_id=1, source_target_pairs={{0,1},{1,0},{2,3},{3,2},{4,5},{5,4},{6,7},{7,6},{8,9},{9,8},{10,11... | collective-permute-start | bytes 3145736 | tf_op jit(solution)/shard_map/ppermute | solution.py:21
  31.3 4.0 %collective-permute-start.15 = (f32[4,512,128]{2,1,0:T(8,128)S(1)}, f32[4,512,128]{2,1,0:T(8,128)S(1)}, u32[]{:S(2)}, u32[]{:S(2)}) collective-permute-start(f32[4,512,128]{2,1,0:T(8,128)S(1)} %send.1), channel_id=1, source_target_pairs={{0,1},{1,0},{2,3},{3,2},{4,5},{5,4},{6,7},{7,6},{8,9},{9,8},{10,11... | collective-permute-start | bytes 3145736 | tf_op jit(solution)/shard_map/ppermute | solution.py:21
  33.6 10.1 %collective-permute-start.11 = (bf16[1280,128]{1,0:T(8,128)(2,1)S(1)}, bf16[1280,128]{1,0:T(8,128)(2,1)S(1)}, u32[]{:S(2)}, u32[]{:S(2)}) collective-permute-start(bf16[1280,128]{1,0:T(8,128)(2,1)S(1)} %get-tuple-element.57), channel_id=1, source_target_pairs={{0,2},{1,3},{2,0},{3,1},{4,6},{5,7},{6,4},{7,5},{8,10},{9,11},{10,... | collective-permute-start | bytes 983048 | tf_op jit(solution)/shard_map/ppermute | solution.py:21
  35.4 8.8 %collective-permute-start.16 = (bf16[1024,128]{1,0:T(8,128)(2,1)S(1)}, bf16[1024,128]{1,0:T(8,128)(2,1)S(1)}, u32[]{:S(2)}, u32[]{:S(2)}) collective-permute-start(bf16[1024,128]{1,0:T(8,128)(2,1)S(1)} %get-tuple-element.67), channel_id=1, source_target_pairs={{0,4},{1,5},{2,6},{3,7},{4,0},{5,1},{6,2},{7,3},{8,12},{9,13},{10,... | collective-permute-start | bytes 786440 | tf_op jit(solution)/shard_map/ppermute | solution.py:21
  43.7 5.7 %collective-permute-start.12 = (bf16[640,128]{1,0:T(8,128)(2,1)S(1)}, bf16[640,128]{1,0:T(8,128)(2,1)S(1)}, u32[]{:S(2)}, u32[]{:S(2)}) collective-permute-start(bf16[640,128]{1,0:T(8,128)(2,1)S(1)} %get-tuple-element.62), channel_id=1, source_target_pairs={{0,4},{1,5},{2,6},{3,7},{4,0},{5,1},{6,2},{7,3},{8,12},{9,13},{10,... | collective-permute-start | bytes 491528 | tf_op jit(solution)/shard_map/ppermute | solution.py:21
  44.3 13.6 %collective-permute-start.17 = (bf16[512,128]{1,0:T(8,128)(2,1)S(1)}, bf16[512,128]{1,0:T(8,128)(2,1)S(1)}, u32[]{:S(2)}, u32[]{:S(2)}) collective-permute-start(bf16[512,128]{1,0:T(8,128)(2,1)S(1)} %get-tuple-element.69), channel_id=1, source_target_pairs={{0,2},{1,3},{2,0},{3,1},{4,6},{5,7},{6,4},{7,5},{8,10},{9,11},{10,... | collective-permute-start | bytes 393224 | tf_op jit(solution)/shard_map/ppermute | solution.py:21
  49.5 6.9 %collective-permute-start.13 = (f32[32,256]{1,0:T(8,128)S(1)}, f32[32,256]{1,0:T(8,128)S(1)}, u32[]{:S(2)}, u32[]{:S(2)}) collective-permute-start(f32[32,256]{1,0:T(8,128)S(1)} %get-tuple-element.63.own_ref), channel_id=1, source_target_pairs={{0,8},{1,9},{2,10},{3,11},{4,12},{5,13},{6,14},{7,15},{8,0},{9,1},... | collective-permute-start | bytes 98312 | tf_op jit(solution)/shard_map/ppermute | solution.py:21
  51.3 13.4 %collective-permute-start.20 = (bf16[512,128]{1,0:T(8,128)(2,1)S(1)}, bf16[512,128]{1,0:T(8,128)(2,1)S(1)}, u32[]{:S(2)}, u32[]{:S(2)}) collective-permute-start(bf16[512,128]{1,0:T(8,128)(2,1)S(1)} %get-tuple-element.70), channel_id=1, source_target_pairs={{0,8},{1,9},{2,10},{3,11},{4,12},{5,13},{6,14},{7,15},{8,0},{9,1},... | collective-permute-start | bytes 393224 | tf_op jit(solution)/shard_map/ppermute | solution.py:21
  56.4 3.9 %collective-permute-start.14 = (f32[32,256]{1,0:T(8,128)S(1)}, f32[32,256]{1,0:T(8,128)S(1)}, u32[]{:S(2)}, u32[]{:S(2)}) collective-permute-start(f32[32,256]{1,0:T(8,128)S(1)} %weight_sum.1.refs_0_), channel_id=1, source_target_pairs={{0,2},{1,3},{2,0},{3,1},{4,6},{5,7},{6,4},{7,5},{8,10},{9,11},{10,... | collective-permute-start | bytes 98312 | tf_op jit(solution)/shard_map/ppermute | solution.py:21
  60.3 4.3 %collective-permute-start.18 = (f32[2,32,256]{2,1,0:T(8,128)S(1)}, f32[2,32,256]{2,1,0:T(8,128)S(1)}, u32[]{:S(2)}, u32[]{:S(2)}) collective-permute-start(f32[2,32,256]{2,1,0:T(8,128)S(1)} %pack_weights.2.refs_0_), channel_id=1, source_target_pairs={{0,4},{1,5},{2,6},{3,7},{4,0},{5,1},{6,2},{7,3},{8,12},{9,13},{10,... | collective-permute-start | bytes 196616 | tf_op jit(solution)/shard_map/ppermute | solution.py:21
  64.6 1.4 %collective-permute-start.19 = (f32[2,2,32,256]{3,2,1,0:T(8,128)S(1)}, f32[2,2,32,256]{3,2,1,0:T(8,128)S(1)}, u32[]{:S(2)}, u32[]{:S(2)}) collective-permute-start(f32[2,2,32,256]{3,2,1,0:T(8,128)S(1)} %pack_weights.3.weight_ref), channel_id=1, source_target_pairs={{0,1},{1,0},{2,3},{3,2},{4,5},{5,4},{6,7},{7,6},{8,9},{9,8},{10,11... | collective-permute-start | bytes 393224 | tf_op jit(solution)/shard_map/ppermute | solution.py:21

commit v8 on v5

--- a/solution.py
+++ b/solution.py
@@ -14,7 +14,7 @@
 ANY = pl.BlockSpec(memory_space=pl.ANY)
 MIB = 1024 * 1024
 LAST = ((1,), (1,))
-NEAR_COST, SQUARE_COST, MAIN_COST = 8, 4, 10
+NEAR_COST, SQUARE_COST, MAIN_COST, FAR_COST, WEIGHT_COST = 1, 4, 0.2, 10, 8
 
 
 def swap(x, n, offset):
@@ -190,31 +190,36 @@
             send_ref[q, rows_of(b), :] = acc_ref[(8 * square + 2 * q + 1) * block_local + b]
 
 
+def cut_kernel(index_ref, wkeep_ref, wgot_ref, keep_ref, send_ref):
+    rows = keep_ref.shape[0]
+    square = index_ref[index_ref.shape[0] - 1] // 8 % 2
+    for p, ref in enumerate((keep_ref, send_ref)):
+        span = pl.ds(pl.multiple_of((square ^ p) * rows, rows), rows)
+        ref[...] = wkeep_ref[span, :] + wgot_ref[span, :]
+
+
 def send_weights_kernel(square, block_local, index_ref, acc_ref, wkeep_ref, wgot_ref, send_ref,
-                        *parts):
+                        *halves):
+    cut_kernel(index_ref, wkeep_ref, wgot_ref, *halves)
     send_kernel(square, block_local, acc_ref, send_ref)
-    rows = parts[0].shape[0]
-    chip = index_ref[index_ref.shape[0] - 1] // 2 % 4
-    for p, ref in enumerate(parts):
-        span = pl.ds(pl.multiple_of((chip ^ p) * rows, rows), rows)
-        ref[...] = wkeep_ref[span, :] + wgot_ref[span, :]
 
 
 def pair_kernel(square, acc_ref, got_ref, own_ref, *pieces):
-    block_local = own_ref.shape[0] // BLOCK
+    nodes = own_ref.shape[0]
     for q, ref in enumerate((own_ref, *pieces)):
-        for b in range(block_local):
-            kept = acc_ref[(8 * square + 2 * q) * block_local + b]
+        for b in range(nodes // BLOCK):
+            kept = acc_ref[(8 * square + 2 * q) * (nodes // BLOCK) + b]
             ref[rows_of(b), :] = (kept + got_ref[q, rows_of(b), :]).astype(ref.dtype)
 
 
-def pair_weights_kernel(square, acc_ref, got_ref, w1, w2, w3, own_ref, *pieces):
+def pair_weights_kernel(square, acc_ref, got_ref, weight_ref, own_ref, *pieces):
     pair_kernel(square, acc_ref, got_ref, own_ref, *pieces)
     nodes, lanes = own_ref.shape
-    for weight_ref, ref in zip((w1, w2, w3), pieces):
-        rows, columns = weight_ref.shape
+    rows, columns = weight_ref.shape
+    parts = split_bf16(weight_ref[...])
+    for ref in pieces:
         start = nodes
-        for part in split_bf16(weight_ref[...]):
+        for part in parts:
             for column in range(0, columns, lanes):
                 ref[pl.ds(start, rows), :] = part[:, column:column + lanes]
                 start += rows
@@ -225,34 +230,29 @@
 
 
 def add_kernel(own_ref, *refs):
-    total = own_ref[...]
+    total = own_ref[...].astype(F32)
     for got_ref in refs[:-1]:
         total = total + got_ref[...].astype(F32)
-    refs[-1][...] = total.astype(BF16)
-
-
-def add_weights_kernel(weight_ref, own_ref, *refs):
-    got_refs, (out_ref, weight_out) = refs[:-2], refs[-2:]
+    refs[-1][...] = total.astype(refs[-1].dtype)
+
+
+def near_kernel(base_ref, own_ref, weight_ref, g1, g2, g3, out_ref, weight_out):
     nodes, lanes = own_ref.shape
-    add_kernel(own_ref, *[ref.at[pl.ds(0, nodes), :] for ref in got_refs], out_ref)
+    for b in range(nodes // BLOCK):
+        total = own_ref[rows_of(b), :]
+        for got_ref in (g1, g2, g3):
+            total = total + got_ref[rows_of(b), :].astype(F32)
+        out_ref[rows_of(b), :] = base_ref[rows_of(b), :] + jnp.transpose(total)
     rows, columns = weight_ref.shape
-    cuts = columns // lanes
-    for cut in range(cuts):
+    for cut in range(columns // lanes):
         span = pl.ds(cut * lanes, lanes)
-        total = weight_ref[:, span]
-        for ref in got_refs[:3]:
+        high, low = split_bf16(weight_ref[:, span])
+        terms = [high.astype(F32) + low.astype(F32)]
+        for ref in (g1, g2, g3):
             high = ref[pl.ds(nodes + cut * rows, rows), :]
-            low = ref[pl.ds(nodes + (cuts + cut) * rows, rows), :]
-            total = total + (high.astype(F32) + low.astype(F32))
-        weight_out[:, span] = total
-
-
-def near_kernel(base_ref, own_ref, *refs):
-    for b in range(own_ref.shape[0] // BLOCK):
-        total = own_ref[rows_of(b), :]
-        for got_ref in refs[:-1]:
-            total = total + got_ref[rows_of(b), :].astype(F32)
-        refs[-1][rows_of(b), :] = base_ref[rows_of(b), :] + jnp.transpose(total)
+            low = ref[pl.ds(nodes + (columns // lanes + cut) * rows, rows), :]
+            terms.append(high.astype(F32) + low.astype(F32))
+        weight_out[:, span] = (terms[0] + terms[1]) + (terms[2] + terms[3])
 
 
 def main_kernel(near_ref, *refs):
@@ -267,11 +267,11 @@
     out_ref[...] = main_ref[...]
     me = index_ref[index_ref.shape[0] - 1]
     first = me % 2 == 0
-    chip = me // 2 % 4
-    rows = weight_ref.shape[2]
-    for p in range(4):
-        span = pl.ds(pl.multiple_of((chip ^ p) * rows, rows), rows)
-        mine, other = weight_ref[p // 2, p % 2], other_ref[p // 2, p % 2]
+    square = me // 8 % 2
+    rows = weight_ref.shape[1]
+    for p in range(2):
+        span = pl.ds(pl.multiple_of((square ^ p) * rows, rows), rows)
+        mine, other = weight_ref[p], other_ref[p]
         self_ref[span, :] = jnp.where(first, mine, other)
         neigh_ref[span, :] = jnp.where(first, other, mine)
 
@@ -313,7 +313,7 @@
 
     wide, piece = result((nodes, feat_in), F32), result((nodes, feat_in), BF16)
     weight = result((feat_in, hidden), F32)
-    chunk = result((feat_in // 4, hidden), F32)
+    chunk = result((feat_in // 2, hidden), F32)
     by_block = (block_local, BLOCK, feat_in)
 
     own_arguments = (
@@ -371,47 +371,48 @@
     send = [None] * squares
     for s in range(squares - 1, -1, -1):
         if s == squares - 1:
-            send[s], w0, w1, w2, w3 = call(
+            send[s], wsum, wsend = call(
                 functools.partial(send_weights_kernel, s, block_local), "send_weights",
-                (send_shape,) + (chunk,) * 4, (index, acc, wkeep, swap(wsend, n, 1)),
+                (send_shape, chunk, chunk), (index, acc, wkeep, swap(wsend, n, 1)),
                 [SMEM] + [VMEM] * 3)
         else:
             send[s] = call(
                 functools.partial(send_kernel, s, block_local), "send", send_shape, (acc,))
 
-    extra = result((nodes + 2 * chunk.shape[0] * (hidden // feat_in), feat_in), BF16)
     terms = [None] * squares
-    for s in range(squares - 1, -1, -1):
-        operands = (acc, swap(send[s], n, 1))
-        if s == squares - 1:
-            own, *pieces = call(
-                functools.partial(pair_weights_kernel, s), "pair_sum_weights", (wide, extra, extra, extra),
-                operands + (w1, w2, w3))
-        else:
-            own, *pieces = call(
-                functools.partial(pair_kernel, s), "pair_sum", (wide, piece, piece, piece), operands)
+    for s in range(squares - 1, 0, -1):
+        own, *pieces = call(
+            functools.partial(pair_kernel, s), "pair_sum", (wide, piece, piece, piece),
+            (acc, swap(send[s], n, 1)))
         terms[s] = [own, *[swap(x, n, 2 * q + 2) for q, x in enumerate(pieces)]]
-    near_total = call(near_kernel, "near_sum", wide, (base, *terms[0]), cost_us=NEAR_COST)
+    wsum = call(add_two_kernel, "weight_sum", chunk, (wsum, swap(wsend, n, 8)), cost_us=WEIGHT_COST)
+    bit = 16
+    while bit < n:
+        wsum = call(add_two_kernel, "weight_sum", chunk, (wsum, swap(wsum, n, bit)))
+        bit *= 2
+    rows = chunk.shape[0]
+    extra = result((nodes + 2 * rows * (hidden // feat_in), feat_in), BF16)
+    own, *pieces = call(
+        functools.partial(pair_weights_kernel, 0), "pair_sum_weights", (wide, extra, extra, extra),
+        (acc, swap(send[0], n, 1), wsum))
+    near_total, wsum = call(
+        near_kernel, "near_sum", (wide, chunk),
+        (base, own, wsum, *[swap(x, n, 2 * q + 2) for q, x in enumerate(pieces)]),
+        cost_us=NEAR_COST)
     terms[0] = [near_total]
     distance = 1
     while distance < squares:
         for s in range(squares - distance, 0, -2 * distance):
-            if s == squares - 1:
-                total, wsum = call(
-                    add_weights_kernel, "square_sum_weights", (piece, chunk), (w0, *terms[s]),
-                    cost_us=SQUARE_COST)
+            total = call(add_kernel, "square_sum", piece, terms[s], cost_us=SQUARE_COST)
+            if s == distance:
+                total = swap(total, n, 8 * distance)
+                terms[0].append(call(add_kernel, "far_sum", wide, (total,), cost_us=FAR_COST))
             else:
-                total = call(add_kernel, "square_sum", piece, terms[s], cost_us=SQUARE_COST)
-            terms[s - distance].append(swap(total, n, 8 * distance))
+                terms[s - distance].append(swap(total, n, 8 * distance))
         distance *= 2
-    bit = 8
-    while bit < n:
-        wsum = call(add_two_kernel, "weight_sum", chunk, (wsum, swap(wsum, n, bit)))
-        bit *= 2
-    rows = chunk.shape[0]
-    two = call(functools.partial(pack_kernel, (0, 1)), "pack_weights", result((2, rows, hidden), F32), (wsum, swap(wsum, n, 2)))
     mine = call(
-        functools.partial(pack_kernel, (0, 1)), "pack_weights", result((2, 2, rows, hidden), F32), (two, swap(two, n, 4), near_total))
+        functools.partial(pack_kernel, (0, 1)), "pack_weights", result((2, rows, hidden), F32),
+        (wsum, swap(wsum, n, 8)))
     main = call(main_kernel, "main_sum", piece, terms[0], cost_us=MAIN_COST)
     grad_input, grad_self, grad_neigh = call(
         last_kernel, "write_gradients",

time: 61.4 us -> 63.9 us (1.041)
  waiting for transfers between devices: 22.6 us -> 27.8 us
  starting transfers between devices: 24.9 us -> 22.2 us
    ppermute x23 -> x22, waiting for transfers between devices: 22.6 us -> 27.8 us  [swap(): return lax.ppermute(x, 'row', [(i, i ^ offset) for i in range(n)])]
    ppermute x23 -> x22, starting transfers between devices: 24.9 us -> 22.2 us  [swap(): return lax.ppermute(x, 'row', [(i, i ^ offset) for i in range(n)])]
  transfers between devices with their start and end apart: 23 -> 22, of which waited for: 14 -> 13; matrix products, arithmetic and copies ran while one was open for 0% -> 0% of each run, Pallas kernels for 10% -> 10%
where the time goes in v8:
time: 63.9 us; the launch traced here: 63.7 us
  waiting for transfers between devices  27.8 us (44%)
  starting transfers between devices  22.2 us (35%)
  Pallas kernels  11.6 us (18%)
  local copies, waits for them, and re-layouts  1.31 us (2%)
  between operations  0.81 us (1%)
    ppermute x22, waiting for transfers between devices, swap(): return lax.ppermute(x, 'row', [(i, i ^ offset) for i in range(n)])  27.8 us
    ppermute x22, starting transfers between devices, swap(): return lax.ppermute(x, 'row', [(i, i ^ offset) for i in range(n)])  22.2 us
    pallas_call x15, Pallas kernels, call(): pl.pallas_call(kernel, out_shape=out_shape, in_specs=specs, out_specs=out...  8.93 us
    pallas_call x1, Pallas kernels, body(): pl.pallas_call(stage_kernel, out_shape=(result(tiles.shape, BF16), result...  2.68 us
    unnamed x4, local copies, waits for them, and re-layouts  1.31 us
  transfers between devices with their start and end apart: 22, of which 13 were waited for; matrix products, arithmetic and copies ran while one was open for 0% of the time, Pallas kernels for 10%

profile of v8, /device:TPU:0, one launch (start us, length us, event | category | flops | bytes accessed | tf_op | source)
XLA Modules:
  0.0 63.7 jit_solution(8594257622931787789)
XLA Ops:
  0.6 4.1 %collective-permute-start.3 = (bf16[512,128]{1,0:T(8,128)(2,1)}, bf16[512,128]{1,0:T(8,128)(2,1)S(1)}, u32[]{:S(2)}, u32[]{:S(2)}) collective-permute-start(bf16[512,128]{1,0:T(8,128)(2,1)} %feat_ref.1), channel_id=1, source_target_pairs={{0,8},{1,9},{2,10},{3,11},{4,12},{5,13},{6,14},{7,15},{8,0},{9,1},... | collective-permute-start | bytes 393224 | tf_op jit(solution)/shard_map/ppermute | solution.py:21
  4.7 1.5 %collective-permute-start = (bf16[512,128]{1,0:T(8,128)(2,1)}, bf16[512,128]{1,0:T(8,128)(2,1)S(1)}, u32[]{:S(2)}, u32[]{:S(2)}) collective-permute-start(bf16[512,128]{1,0:T(8,128)(2,1)} %feat_ref.1), channel_id=1, source_target_pairs={{0,2},{1,3},{2,0},{3,1},{4,6},{5,7},{6,4},{7,5},{8,10},{9,11},{10,... | collective-permute-start | bytes 393224 | tf_op jit(solution)/shard_map/ppermute | solution.py:21
  6.3 1.5 %collective-permute-start.1 = (bf16[512,128]{1,0:T(8,128)(2,1)}, bf16[512,128]{1,0:T(8,128)(2,1)S(1)}, u32[]{:S(2)}, u32[]{:S(2)}) collective-permute-start(bf16[512,128]{1,0:T(8,128)(2,1)} %feat_ref.1), channel_id=1, source_target_pairs={{0,6},{1,7},{2,4},{3,5},{4,2},{5,3},{6,0},{7,1},{8,14},{9,15},{10,... | collective-permute-start | bytes 393224 | tf_op jit(solution)/shard_map/ppermute | solution.py:21
  7.8 0.4 collective-permute-start.2
  8.2 3.1 %collective-permute-done.3.refs_0_ = bf16[512,128]{1,0:T(8,128)(2,1)S(1)} collective-permute-done((bf16[512,128]{1,0:T(8,128)(2,1)}, bf16[512,128]{1,0:T(8,128)(2,1)S(1)}, u32[]{:S(2)}, u32[]{:S(2)}) %collective-permute-start.3) | collective-permute-done | bytes 131104 | tf_op jit(solution)/shard_map/ppermute | solution.py:21
  11.4 1.7 %collective-permute-start.4 = (bf16[512,128]{1,0:T(8,128)(2,1)S(1)}, bf16[512,128]{1,0:T(8,128)(2,1)S(1)}, u32[]{:S(2)}, u32[]{:S(2)}) collective-permute-start(bf16[512,128]{1,0:T(8,128)(2,1)S(1)} %collective-permute-done.3.refs_0_), channel_id=1, source_target_pairs={{0,6},{1,7},{2,4},{3,5},{4,2},{5,3},{6,0},{7,1},{8,14},{9,15},{10,... | collective-permute-start | bytes 393224 | tf_op jit(solution)/shard_map/ppermute | solution.py:21
  13.1 0.5 collective-permute-start.5
  13.6 1.3 %collective-permute-start.6 = (bf16[512,128]{1,0:T(8,128)(2,1)S(1)}, bf16[512,128]{1,0:T(8,128)(2,1)S(1)}, u32[]{:S(2)}, u32[]{:S(2)}) collective-permute-start(bf16[512,128]{1,0:T(8,128)(2,1)S(1)} %collective-permute-done.3.refs_0_), channel_id=1, source_target_pairs={{0,4},{1,5},{2,6},{3,7},{4,0},{5,1},{6,2},{7,3},{8,12},{9,13},{10,... | collective-permute-start | bytes 393224 | tf_op jit(solution)/shard_map/ppermute | solution.py:21
  14.9 0.7 %copy-done = s32[60]{0:T(128)S(1)} copy-done((s32[60]{0:T(128)S(1)}, s32[60]{0:T(128)}, u32[]{:S(2)}) %copy-start) | copy-done | bytes 264
  15.5 0.7 %copy-done.1 = s32[60]{0:T(128)S(1)} copy-done((s32[60]{0:T(128)S(1)}, s32[60]{0:T(128)}, u32[]{:S(2)}) %copy-start.1) | copy-done | bytes 264
  16.2 2.7 %stage_arguments.1 = (bf16[60,128,128]{2,1,0:T(8,128)(2,1)S(1)}, bf16[128,256]{1,0:T(8,128)(2,1)S(1)}, bf16[128,256]{1,0:T(8,128)(2,1)S(1)}, f32[4,128,128]{2,1,...) custom-call(s32[1]{0:T(128)} %bitcast.me_ref, ...), custom_call_target="tpu_custom_call" | custom-call | flops 3300000000 | bytes 10800000 | tf_op jit(solution)/shard_map/stage_arguments/pallas_call | solution.py:325
  18.9 0.1 collective-permute-start.7
  19.0 1.4 %collective-permute-done.4.refs_1_ = bf16[512,128]{1,0:T(8,128)(2,1)S(1)} collective-permute-done((bf16[512,128]{1,0:T(8,128)(2,1)S(1)}, bf16[512,128]{1,0:T(8,128)(2,1)S(1)}, u32[]{:S(2)}, u32[]{:S(2)}) %collective-permute-start.4) | collective-permute-done | bytes 131104 | tf_op jit(solution)/shard_map/ppermute | solution.py:21
  20.4 0.6 collective-permute-done.5.refs_2_
  21.0 0.1 collective-permute-done.6.refs_3_
  21.2 0.1 collective-permute-start.8
  21.3 1.9 %collective-permute-done.8.refs_3_ = bf16[4,512,128]{2,1,0:T(8,128)(2,1)S(1)} collective-permute-done((bf16[4,512,128]{2,1,0:T(8,128)(2,1)S(1)}, bf16[4,512,128]{2,1,0:T(8,128)(2,1)S(1)}, u32[]{:S(2)}, u32[]{:S(2)}) %collective-permute-start.8) | collective-permute-done | bytes 524320 | tf_op jit(solution)/shard_map/ppermute | solution.py:21
  23.2 4.5 %forward_layer.1 = (bf16[512,256]{1,0:T(8,128)(2,1)}, f32[512,128]{1,0:T(8,128)S(1)}, f32[128,256]{1,0:T(8,128)S(1)}, f32[128,256]{1,0:T(8,128)S(1)}, bf16[4,256,128]{2,1,0:T(8,128)(2,1)S(1)}) custom-call(s32[121]{0:T(128)S(4)} %get-tuple-element.34.index_ref, bf16[60,128,128]{2,1,0:T(8,128)(2,1)S(1)} %get-tuple-element.35.tiles_ref, ...), custom_call_target="tpu_custom_call" | custom-call | flops 5500000256 | bytes 18000000 | tf_op jit(solution)/shard_map/forward_layer/pallas_call | solution.py:302
  27.7 0.1 collective-permute-start.10
  27.8 2.9 %backward_tiles.1.acc_ref = f32[65,128,128]{2,1,0:T(8,128)S(1)} custom-call(s32[121]{0:T(128)S(4)} %get-tuple-element.34.index_ref, bf16[60,128,128]{2,1,0:T(8,128)(2,1)S(1)} %get-tuple-element.35.tiles_ref, bf16[4,256,128]{2,1,0:T(8,128)(2,1)S(1)} %get-tuple-element.45.gt_ref), custom_call_target="tpu_custom_call" | custom-call | flops 3849999872 | bytes 12600000 | tf_op jit(solution)/shard_map/backward_tiles/pallas_call | solution.py:302
  30.7 0.1 send_weights.1
  30.8 0.5 collective-permute-start.17
  31.2 0.1 send.1
  31.3 0.2 collective-permute-start.9
  31.5 1.7 %collective-permute-start.11 = (f32[64,256]{1,0:T(8,128)S(1)}, f32[64,256]{1,0:T(8,128)S(1)}, u32[]{:S(2)}, u32[]{:S(2)}) collective-permute-start(f32[64,256]{1,0:T(8,128)S(1)} %get-tuple-element.49), channel_id=1, source_target_pairs={{0,8},{1,9},{2,10},{3,11},{4,12},{5,13},{6,14},{7,15},{8,0},{9,1},... | collective-permute-start | bytes 196616 | tf_op jit(solution)/shard_map/ppermute | solution.py:21
  33.2 0.3 collective-permute-done.17.got_ref
  33.5 0.1 pair_sum.1
  33.6 1.7 %collective-permute-start.18 = (bf16[512,128]{1,0:T(8,128)(2,1)S(1)}, bf16[512,128]{1,0:T(8,128)(2,1)S(1)}, u32[]{:S(2)}, u32[]{:S(2)}) collective-permute-start(bf16[512,128]{1,0:T(8,128)(2,1)S(1)} %get-tuple-element.58), channel_id=1, source_target_pairs={{0,2},{1,3},{2,0},{3,1},{4,6},{5,7},{6,4},{7,5},{8,10},{9,11},{10,... | collective-permute-start | bytes 393224 | tf_op jit(solution)/shard_map/ppermute | solution.py:21
  35.2 1.0 %collective-permute-start.19 = (bf16[512,128]{1,0:T(8,128)(2,1)S(1)}, bf16[512,128]{1,0:T(8,128)(2,1)S(1)}, u32[]{:S(2)}, u32[]{:S(2)}) collective-permute-start(bf16[512,128]{1,0:T(8,128)(2,1)S(1)} %get-tuple-element.59), channel_id=1, source_target_pairs={{0,4},{1,5},{2,6},{3,7},{4,0},{5,1},{6,2},{7,3},{8,12},{9,13},{10,... | collective-permute-start | bytes 393224 | tf_op jit(solution)/shard_map/ppermute | solution.py:21
  36.3 0.9 %collective-permute-start.20 = (bf16[512,128]{1,0:T(8,128)(2,1)S(1)}, bf16[512,128]{1,0:T(8,128)(2,1)S(1)}, u32[]{:S(2)}, u32[]{:S(2)}) collective-permute-start(bf16[512,128]{1,0:T(8,128)(2,1)S(1)} %get-tuple-element.60), channel_id=1, source_target_pairs={{0,6},{1,7},{2,4},{3,5},{4,2},{5,3},{6,0},{7,1},{8,14},{9,15},{10,... | collective-permute-start | bytes 393224 | tf_op jit(solution)/shard_map/ppermute | solution.py:21
  37.2 1.0 %collective-permute-done.11.got_ref = f32[64,256]{1,0:T(8,128)S(1)} collective-permute-done((f32[64,256]{1,0:T(8,128)S(1)}, f32[64,256]{1,0:T(8,128)S(1)}, u32[]{:S(2)}, u32[]{:S(2)}) %collective-permute-start.11) | collective-permute-done | bytes 65568 | tf_op jit(solution)/shard_map/ppermute | solution.py:21
  38.2 0.1 pair_sum_weights.1
  38.3 1.6 %collective-permute-start.12 = (bf16[768,128]{1,0:T(8,128)(2,1)S(1)}, bf16[768,128]{1,0:T(8,128)(2,1)S(1)}, u32[]{:S(2)}, u32[]{:S(2)}) collective-permute-start(bf16[768,128]{1,0:T(8,128)(2,1)S(1)} %get-tuple-element.51), channel_id=1, source_target_pairs={{0,2},{1,3},{2,0},{3,1},{4,6},{5,7},{6,4},{7,5},{8,10},{9,11},{10,... | collective-permute-start | bytes 589832 | tf_op jit(solution)/shard_map/ppermute | solution.py:21
  39.9 0.1 collective-permute-start.13
  40.0 1.9 %collective-permute-start.14 = (bf16[768,128]{1,0:T(8,128)(2,1)S(1)}, bf16[768,128]{1,0:T(8,128)(2,1)S(1)}, u32[]{:S(2)}, u32[]{:S(2)}) collective-permute-start(bf16[768,128]{1,0:T(8,128)(2,1)S(1)} %get-tuple-element.53), channel_id=1, source_target_pairs={{0,6},{1,7},{2,4},{3,5},{4,2},{5,3},{6,0},{7,1},{8,14},{9,15},{10,... | collective-permute-start | bytes 589832 | tf_op jit(solution)/shard_map/ppermute | solution.py:21
  41.9 2.9 %collective-permute-done.20.refs_2_ = bf16[512,128]{1,0:T(8,128)(2,1)S(1)} collective-permute-done((bf16[512,128]{1,0:T(8,128)(2,1)S(1)}, bf16[512,128]{1,0:T(8,128)(2,1)S(1)}, u32[]{:S(2)}, u32[]{:S(2)}) %collective-permute-start.20) | collective-permute-done | bytes 131104 | tf_op jit(solution)/shard_map/ppermute | solution.py:21
  44.7 0.1 square_sum.1
  44.8 1.2 %collective-permute-start.21 = (bf16[512,128]{1,0:T(8,128)(2,1)S(1)}, bf16[512,128]{1,0:T(8,128)(2,1)S(1)}, u32[]{:S(2)}, u32[]{:S(2)}) collective-permute-start(bf16[512,128]{1,0:T(8,128)(2,1)S(1)} %square_sum.1), channel_id=1, source_target_pairs={{0,8},{1,9},{2,10},{3,11},{4,12},{5,13},{6,14},{7,15},{8,0},{9,1},... | collective-permute-start | bytes 393224 | tf_op jit(solution)/shard_map/ppermute | solution.py:21
  46.1 1.7 %collective-permute-done.12.g1 = bf16[768,128]{1,0:T(8,128)(2,1)S(1)} collective-permute-done((bf16[768,128]{1,0:T(8,128)(2,1)S(1)}, bf16[768,128]{1,0:T(8,128)(2,1)S(1)}, u32[]{:S(2)}, u32[]{:S(2)}) %collective-permute-start.12) | collective-permute-done | bytes 196640 | tf_op jit(solution)/shard_map/ppermute | solution.py:21
  47.8 3.7 %collective-permute-done.13.g2 = bf16[768,128]{1,0:T(8,128)(2,1)S(1)} collective-permute-done((bf16[768,128]{1,0:T(8,128)(2,1)S(1)}, bf16[768,128]{1,0:T(8,128)(2,1)S(1)}, u32[]{:S(2)}, u32[]{:S(2)}) %collective-permute-start.13) | collective-permute-done | bytes 196640 | tf_op jit(solution)/shard_map/ppermute | solution.py:21
  51.5 4.4 %collective-permute-done.14.g3 = bf16[768,128]{1,0:T(8,128)(2,1)S(1)} collective-permute-done((bf16[768,128]{1,0:T(8,128)(2,1)S(1)}, bf16[768,128]{1,0:T(8,128)(2,1)S(1)}, u32[]{:S(2)}, u32[]{:S(2)}) %collective-permute-start.14) | collective-permute-done | bytes 196640 | tf_op jit(solution)/shard_map/ppermute | solution.py:21
  55.9 0.1 near_sum.1
  56.0 0.1 collective-permute-start.15
  56.1 5.4 %collective-permute-done.15.refs_1_ = f32[64,256]{1,0:T(8,128)S(1)} collective-permute-done((f32[64,256]{1,0:T(8,128)S(1)}, f32[64,256]{1,0:T(8,128)S(1)}, u32[]{:S(2)}, u32[]{:S(2)}) %collective-permute-start.15) | collective-permute-done | bytes 65568 | tf_op jit(solution)/shard_map/ppermute | solution.py:21
  61.5 0.1 collective-permute-start.16
  61.6 0.1 main_sum.1.main_ref
  61.8 1.2 %collective-permute-done.16.other_ref = f32[2,64,256]{2,1,0:T(8,128)S(1)} collective-permute-done((f32[2,64,256]{2,1,0:T(8,128)S(1)}, f32[2,64,256]{2,1,0:T(8,128)S(1)}, u32[]{:S(2)}, u32[]{:S(2)}) %collective-permute-start.16) | collective-permute-done | bytes 131104 | tf_op jit(solution)/shard_map/ppermute | solution.py:21
  62.9 0.8 %write_gradients.1 = (bf16[512,128]{1,0:T(8,128)(2,1)}, f32[128,256]{1,0:T(8,128)}, f32[128,256]{1,0:T(8,128)}) custom-call(s32[121]{0:T(128)S(4)} %get-tuple-element.34.index_ref, f32[2,64,256]{2,1,0:T(8,128)S(1)} %pack_weights.1.weight_ref, f32[2,64,256]{2,1,0:T(8,128)S(1)} %collective-permute-done.16.other_ref, bf16[512,128]{1,0:T(8,128)(2,1)S(1)} %main_sum.1.main_ref), custom_call_target="tpu_custom_call" | custom-call | flops 220000000 | bytes 720000 | tf_op jit(solution)/shard_map/write_gradients/pallas_call | solution.py:302
  (16 shorter events, 0.1 us)
Async XLA Ops:
  0.6 10.7 %collective-permute-start.3 = (bf16[512,128]{1,0:T(8,128)(2,1)}, bf16[512,128]{1,0:T(8,128)(2,1)S(1)}, u32[]{:S(2)}, u32[]{:S(2)}) collective-permute-start(bf16[512,128]{1,0:T(8,128)(2,1)} %feat_ref.1), channel_id=1, source_target_pairs={{0,8},{1,9},{2,10},{3,11},{4,12},{5,13},{6,14},{7,15},{8,0},{9,1},... | collective-permute-start | bytes 393224 | tf_op jit(solution)/shard_map/ppermute | solution.py:21
  4.7 8.9 %collective-permute-start = (bf16[512,128]{1,0:T(8,128)(2,1)}, bf16[512,128]{1,0:T(8,128)(2,1)S(1)}, u32[]{:S(2)}, u32[]{:S(2)}) collective-permute-start(bf16[512,128]{1,0:T(8,128)(2,1)} %feat_ref.1), channel_id=1, source_target_pairs={{0,2},{1,3},{2,0},{3,1},{4,6},{5,7},{6,4},{7,5},{8,10},{9,11},{10,... | collective-permute-start | bytes 393224 | tf_op jit(solution)/shard_map/ppermute | solution.py:21
  6.3 12.6 %collective-permute-start.1 = (bf16[512,128]{1,0:T(8,128)(2,1)}, bf16[512,128]{1,0:T(8,128)(2,1)S(1)}, u32[]{:S(2)}, u32[]{:S(2)}) collective-permute-start(bf16[512,128]{1,0:T(8,128)(2,1)} %feat_ref.1), channel_id=1, source_target_pairs={{0,6},{1,7},{2,4},{3,5},{4,2},{5,3},{6,0},{7,1},{8,14},{9,15},{10,... | collective-permute-start | bytes 393224 | tf_op jit(solution)/shard_map/ppermute | solution.py:21
  7.8 11.1 %collective-permute-start.2 = (bf16[512,128]{1,0:T(8,128)(2,1)}, bf16[512,128]{1,0:T(8,128)(2,1)S(1)}, u32[]{:S(2)}, u32[]{:S(2)}) collective-permute-start(bf16[512,128]{1,0:T(8,128)(2,1)} %feat_ref.1), channel_id=1, source_target_pairs={{0,4},{1,5},{2,6},{3,7},{4,0},{5,1},{6,2},{7,3},{8,12},{9,13},{10,... | collective-permute-start | bytes 393224 | tf_op jit(solution)/shard_map/ppermute | solution.py:21
  11.4 9.1 %collective-permute-start.4 = (bf16[512,128]{1,0:T(8,128)(2,1)S(1)}, bf16[512,128]{1,0:T(8,128)(2,1)S(1)}, u32[]{:S(2)}, u32[]{:S(2)}) collective-permute-start(bf16[512,128]{1,0:T(8,128)(2,1)S(1)} %collective-permute-done.3.refs_0_), channel_id=1, source_target_pairs={{0,6},{1,7},{2,4},{3,5},{4,2},{5,3},{6,0},{7,1},{8,14},{9,15},{10,... | collective-permute-start | bytes 393224 | tf_op jit(solution)/shard_map/ppermute | solution.py:21
  13.1 7.9 %collective-permute-start.5 = (bf16[512,128]{1,0:T(8,128)(2,1)S(1)}, bf16[512,128]{1,0:T(8,128)(2,1)S(1)}, u32[]{:S(2)}, u32[]{:S(2)}) collective-permute-start(bf16[512,128]{1,0:T(8,128)(2,1)S(1)} %collective-permute-done.3.refs_0_), channel_id=1, source_target_pairs={{0,2},{1,3},{2,0},{3,1},{4,6},{5,7},{6,4},{7,5},{8,10},{9,11},{10,... | collective-permute-start | bytes 393224 | tf_op jit(solution)/shard_map/ppermute | solution.py:21
  13.6 7.6 %collective-permute-start.6 = (bf16[512,128]{1,0:T(8,128)(2,1)S(1)}, bf16[512,128]{1,0:T(8,128)(2,1)S(1)}, u32[]{:S(2)}, u32[]{:S(2)}) collective-permute-start(bf16[512,128]{1,0:T(8,128)(2,1)S(1)} %collective-permute-done.3.refs_0_), channel_id=1, source_target_pairs={{0,4},{1,5},{2,6},{3,7},{4,0},{5,1},{6,2},{7,3},{8,12},{9,13},{10,... | collective-permute-start | bytes 393224 | tf_op jit(solution)/shard_map/ppermute | solution.py:21
  14.8 0.7 %copy-start = (s32[60]{0:T(128)S(1)}, s32[60]{0:T(128)}, u32[]{:S(2)}) copy-start(s32[60]{0:T(128)} %trow_ref.1) | copy-start | bytes 724
  15.5 0.7 %copy-start.1 = (s32[60]{0:T(128)S(1)}, s32[60]{0:T(128)}, u32[]{:S(2)}) copy-start(s32[60]{0:T(128)} %tcol_ref.1) | copy-start | bytes 724
  18.9 2.4 %collective-permute-start.7 = (bf16[4,512,128]{2,1,0:T(8,128)(2,1)S(1)}, bf16[4,512,128]{2,1,0:T(8,128)(2,1)S(1)}, u32[]{:S(2)}, u32[]{:S(2)}) collective-permute-start(bf16[4,512,128]{2,1,0:T(8,128)(2,1)S(1)} %pack_square.2.refs_0_), channel_id=1, source_target_pairs={{0,1},{1,0},{2,3},{3,2},{4,5},{5,4},{6,7},{7,6},{8,9},{9,8},{10,11... | collective-permute-start | bytes 1572872 | tf_op jit(solution)/shard_map/ppermute | solution.py:21
  21.2 2.0 %collective-permute-start.8 = (bf16[4,512,128]{2,1,0:T(8,128)(2,1)S(1)}, bf16[4,512,128]{2,1,0:T(8,128)(2,1)S(1)}, u32[]{:S(2)}, u32[]{:S(2)}) collective-permute-start(bf16[4,512,128]{2,1,0:T(8,128)(2,1)S(1)} %pack_square.3.refs_1_), channel_id=1, source_target_pairs={{0,1},{1,0},{2,3},{3,2},{4,5},{5,4},{6,7},{7,6},{8,9},{9,8},{10,11... | collective-permute-start | bytes 1572872 | tf_op jit(solution)/shard_map/ppermute | solution.py:21
  27.7 3.0 %collective-permute-start.10 = (f32[128,256]{1,0:T(8,128)S(1)}, f32[128,256]{1,0:T(8,128)S(1)}, u32[]{:S(2)}, u32[]{:S(2)}) collective-permute-start(f32[128,256]{1,0:T(8,128)S(1)} %get-tuple-element.47), channel_id=1, source_target_pairs={{0,1},{1,0},{2,3},{3,2},{4,5},{5,4},{6,7},{7,6},{8,9},{9,8},{10,11... | collective-permute-start | bytes 393224 | tf_op jit(solution)/shard_map/ppermute | solution.py:21
  30.8 2.7 %collective-permute-start.17 = (f32[4,512,128]{2,1,0:T(8,128)S(1)}, f32[4,512,128]{2,1,0:T(8,128)S(1)}, u32[]{:S(2)}, u32[]{:S(2)}) collective-permute-start(f32[4,512,128]{2,1,0:T(8,128)S(1)} %get-tuple-element.56), channel_id=1, source_target_pairs={{0,1},{1,0},{2,3},{3,2},{4,5},{5,4},{6,7},{7,6},{8,9},{9,8},{10,11... | collective-permute-start | bytes 3145736 | tf_op jit(solution)/shard_map/ppermute | solution.py:21
  31.3 6.9 %collective-permute-start.9 = (f32[4,512,128]{2,1,0:T(8,128)S(1)}, f32[4,512,128]{2,1,0:T(8,128)S(1)}, u32[]{:S(2)}, u32[]{:S(2)}) collective-permute-start(f32[4,512,128]{2,1,0:T(8,128)S(1)} %send.1), channel_id=1, source_target_pairs={{0,1},{1,0},{2,3},{3,2},{4,5},{5,4},{6,7},{7,6},{8,9},{9,8},{10,11... | collective-permute-start | bytes 3145736 | tf_op jit(solution)/shard_map/ppermute | solution.py:21
  31.5 6.7 %collective-permute-start.11 = (f32[64,256]{1,0:T(8,128)S(1)}, f32[64,256]{1,0:T(8,128)S(1)}, u32[]{:S(2)}, u32[]{:S(2)}) collective-permute-start(f32[64,256]{1,0:T(8,128)S(1)} %get-tuple-element.49), channel_id=1, source_target_pairs={{0,8},{1,9},{2,10},{3,11},{4,12},{5,13},{6,14},{7,15},{8,0},{9,1},... | collective-permute-start | bytes 196616 | tf_op jit(solution)/shard_map/ppermute | solution.py:21
  33.6 6.4 %collective-permute-start.18 = (bf16[512,128]{1,0:T(8,128)(2,1)S(1)}, bf16[512,128]{1,0:T(8,128)(2,1)S(1)}, u32[]{:S(2)}, u32[]{:S(2)}) collective-permute-start(bf16[512,128]{1,0:T(8,128)(2,1)S(1)} %get-tuple-element.58), channel_id=1, source_target_pairs={{0,2},{1,3},{2,0},{3,1},{4,6},{5,7},{6,4},{7,5},{8,10},{9,11},{10,... | collective-permute-start | bytes 393224 | tf_op jit(solution)/shard_map/ppermute | solution.py:21
  35.2 6.6 %collective-permute-start.19 = (bf16[512,128]{1,0:T(8,128)(2,1)S(1)}, bf16[512,128]{1,0:T(8,128)(2,1)S(1)}, u32[]{:S(2)}, u32[]{:S(2)}) collective-permute-start(bf16[512,128]{1,0:T(8,128)(2,1)S(1)} %get-tuple-element.59), channel_id=1, source_target_pairs={{0,4},{1,5},{2,6},{3,7},{4,0},{5,1},{6,2},{7,3},{8,12},{9,13},{10,... | collective-permute-start | bytes 393224 | tf_op jit(solution)/shard_map/ppermute | solution.py:21
  36.3 8.5 %collective-permute-start.20 = (bf16[512,128]{1,0:T(8,128)(2,1)S(1)}, bf16[512,128]{1,0:T(8,128)(2,1)S(1)}, u32[]{:S(2)}, u32[]{:S(2)}) collective-permute-start(bf16[512,128]{1,0:T(8,128)(2,1)S(1)} %get-tuple-element.60), channel_id=1, source_target_pairs={{0,6},{1,7},{2,4},{3,5},{4,2},{5,3},{6,0},{7,1},{8,14},{9,15},{10,... | collective-permute-start | bytes 393224 | tf_op jit(solution)/shard_map/ppermute | solution.py:21
  38.3 9.5 %collective-permute-start.12 = (bf16[768,128]{1,0:T(8,128)(2,1)S(1)}, bf16[768,128]{1,0:T(8,128)(2,1)S(1)}, u32[]{:S(2)}, u32[]{:S(2)}) collective-permute-start(bf16[768,128]{1,0:T(8,128)(2,1)S(1)} %get-tuple-element.51), channel_id=1, source_target_pairs={{0,2},{1,3},{2,0},{3,1},{4,6},{5,7},{6,4},{7,5},{8,10},{9,11},{10,... | collective-permute-start | bytes 589832 | tf_op jit(solution)/shard_map/ppermute | solution.py:21
  39.9 11.6 %collective-permute-start.13 = (bf16[768,128]{1,0:T(8,128)(2,1)S(1)}, bf16[768,128]{1,0:T(8,128)(2,1)S(1)}, u32[]{:S(2)}, u32[]{:S(2)}) collective-permute-start(bf16[768,128]{1,0:T(8,128)(2,1)S(1)} %get-tuple-element.52), channel_id=1, source_target_pairs={{0,4},{1,5},{2,6},{3,7},{4,0},{5,1},{6,2},{7,3},{8,12},{9,13},{10,... | collective-permute-start | bytes 589832 | tf_op jit(solution)/shard_map/ppermute | solution.py:21
  40.0 15.9 %collective-permute-start.14 = (bf16[768,128]{1,0:T(8,128)(2,1)S(1)}, bf16[768,128]{1,0:T(8,128)(2,1)S(1)}, u32[]{:S(2)}, u32[]{:S(2)}) collective-permute-start(bf16[768,128]{1,0:T(8,128)(2,1)S(1)} %get-tuple-element.53), channel_id=1, source_target_pairs={{0,6},{1,7},{2,4},{3,5},{4,2},{5,3},{6,0},{7,1},{8,14},{9,15},{10,... | collective-permute-start | bytes 589832 | tf_op jit(solution)/shard_map/ppermute | solution.py:21
  44.8 16.8 %collective-permute-start.21 = (bf16[512,128]{1,0:T(8,128)(2,1)S(1)}, bf16[512,128]{1,0:T(8,128)(2,1)S(1)}, u32[]{:S(2)}, u32[]{:S(2)}) collective-permute-start(bf16[512,128]{1,0:T(8,128)(2,1)S(1)} %square_sum.1), channel_id=1, source_target_pairs={{0,8},{1,9},{2,10},{3,11},{4,12},{5,13},{6,14},{7,15},{8,0},{9,1},... | collective-permute-start | bytes 393224 | tf_op jit(solution)/shard_map/ppermute | solution.py:21
  56.0 5.5 %collective-permute-start.15 = (f32[64,256]{1,0:T(8,128)S(1)}, f32[64,256]{1,0:T(8,128)S(1)}, u32[]{:S(2)}, u32[]{:S(2)}) collective-permute-start(f32[64,256]{1,0:T(8,128)S(1)} %get-tuple-element.54.refs_0_), channel_id=1, source_target_pairs={{0,8},{1,9},{2,10},{3,11},{4,12},{5,13},{6,14},{7,15},{8,0},{9,1},... | collective-permute-start | bytes 196616 | tf_op jit(solution)/shard_map/ppermute | solution.py:21
  61.5 1.4 %collective-permute-start.16 = (f32[2,64,256]{2,1,0:T(8,128)S(1)}, f32[2,64,256]{2,1,0:T(8,128)S(1)}, u32[]{:S(2)}, u32[]{:S(2)}) collective-permute-start(f32[2,64,256]{2,1,0:T(8,128)S(1)} %pack_weights.1.weight_ref), channel_id=1, source_target_pairs={{0,1},{1,0},{2,3},{3,2},{4,5},{5,4},{6,7},{7,6},{8,9},{9,8},{10,11... | collective-permute-start | bytes 393224 | tf_op jit(solution)/shard_map/ppermute | solution.py:21

commit v9 on v5

--- a/solution.py
+++ b/solution.py
@@ -14,7 +14,7 @@
 ANY = pl.BlockSpec(memory_space=pl.ANY)
 MIB = 1024 * 1024
 LAST = ((1,), (1,))
-NEAR_COST, SQUARE_COST, MAIN_COST = 8, 4, 10
+NEAR_COST, SQUARE_COST, MAIN_COST, FAR_COST = 4, 0.2, 0.2, 10
 
 
 def swap(x, n, offset):
@@ -70,7 +70,7 @@
 
 
 def stage_kernel(me_ref, trow_ref, tcol_ref, deg_ref, mask_ref, ws_ref, wn_ref, feat_ref, cot_ref,
-                 tiles_ref, tiles_out, ws_out, wn_out, deg_out, up_out, pre_out, featt_out,
+                 tiles_ref, tiles_out, ws_out, wn_out, inverse_out, up_out, pre_out, featt_out,
                  own_out, index_out, sem):
     copy = pltpu.make_async_copy(tiles_ref, tiles_out, sem)
     copy.start()
@@ -97,7 +97,7 @@
     for b in range(block_local):
         degree = rows_to_lanes(deg_ref[pl.ds(b, 1), :].astype(F32))
         mask = rows_to_lanes(mask_ref[pl.ds(b, 1), :].astype(F32))
-        deg_out[b] = degree
+        inverse_out[b] = 1.0 / degree
         feat = feat_ref[rows_of(b), :]
         featt_out[b] = jnp.transpose(feat.astype(F32)).astype(BF16)
         pre_out[rows_of(b), :] = dot(feat, ws)
@@ -106,12 +106,12 @@
     copy.wait()
 
 
-def forward_kernel(n, group, index_ref, tiles_ref, ws_ref, wn_ref, deg_ref, up_ref, pre_ref,
+def forward_kernel(n, group, index_ref, tiles_ref, ws_ref, wn_ref, inverse_ref, up_ref, pre_ref,
                    featt_ref, *refs):
     squares = n // 8
     feat_refs, refs = refs[:2 * squares], refs[2 * squares:]
     emb_ref, base_ref, wkeep_ref, wsend_ref, gt_ref, feats, raw, wsum = refs
-    block_local = deg_ref.shape[0]
+    block_local = inverse_ref.shape[0]
     tile_count = tiles_ref.shape[0]
 
     raw[...] = jnp.zeros_like(raw)
@@ -137,13 +137,13 @@
     wn = wn_ref[...]
     ws = ws_ref[...]
     for b in range(block_local):
-        degree = deg_ref[b]
+        inverse = inverse_ref[b]
         raw_b = raw[b]
-        pre = pre_ref[rows_of(b), :] + dot_wide(raw_b / degree, wn)
+        pre = pre_ref[rows_of(b), :] + dot_wide(raw_b * inverse, wn)
         sig = jax.nn.sigmoid(pre)
         emb_ref[rows_of(b), :] = (pre * sig).astype(BF16)
         grad_pre = up_ref[rows_of(b), :] * sig * (1.0 + pre * (1.0 - sig))
-        scaled = (grad_pre / jnp.concatenate([degree, degree], axis=1)).astype(BF16)
+        scaled = (grad_pre * jnp.concatenate([inverse, inverse], axis=1)).astype(BF16)
         gp_high, gp_low = split_bf16(grad_pre)
         feat_t = featt_ref[b]
         grad_self = dot(feat_t, gp_high) + dot(feat_t, gp_low)
@@ -225,10 +225,10 @@
 
 
 def add_kernel(own_ref, *refs):
-    total = own_ref[...]
+    total = own_ref[...].astype(F32)
     for got_ref in refs[:-1]:
         total = total + got_ref[...].astype(F32)
-    refs[-1][...] = total.astype(BF16)
+    refs[-1][...] = total.astype(refs[-1].dtype)
 
 
 def add_weights_kernel(weight_ref, own_ref, *refs):
@@ -263,15 +263,14 @@
         refs[-1][rows_of(b), :] = (near_ref[rows_of(b), :] + jnp.transpose(total)).astype(BF16)
 
 
-def last_kernel(index_ref, weight_ref, other_ref, main_ref, out_ref, self_ref, neigh_ref):
-    out_ref[...] = main_ref[...]
+def last_kernel(index_ref, weight_ref, other_ref, self_ref, neigh_ref):
     me = index_ref[index_ref.shape[0] - 1]
     first = me % 2 == 0
     chip = me // 2 % 4
-    rows = weight_ref.shape[2]
+    rows = weight_ref.shape[1]
     for p in range(4):
         span = pl.ds(pl.multiple_of((chip ^ p) * rows, rows), rows)
-        mine, other = weight_ref[p // 2, p % 2], other_ref[p // 2, p % 2]
+        mine, other = weight_ref[p], other_ref[p]
         self_ref[span, :] = jnp.where(first, mine, other)
         neigh_ref[span, :] = jnp.where(first, other, mine)
 
@@ -322,7 +321,7 @@
     )
     if small:
         own_arguments = [pltpu.with_memory_space_constraint(x, pltpu.HBM) for x in own_arguments]
-    tiles_near, ws, wn, degree_wide, upstream, pre_self, feat_t, own, index = pl.pallas_call(
+    tiles_near, ws, wn, inverse, upstream, pre_self, feat_t, own, index = pl.pallas_call(
         stage_kernel,
         out_shape=(
             result(tiles.shape, BF16),
@@ -344,7 +343,7 @@
     )(me, tile_row, tile_col, *own_arguments, placed(tiles, ANY))
 
     same, other = gather_by_xor(features, own, n, call, result((4, nodes, feat_in), BF16))
-    operands = (index, tiles_near, ws, wn, degree_wide, upstream, pre_self, feat_t, *same, *other)
+    operands = (index, tiles_near, ws, wn, inverse, upstream, pre_self, feat_t, *same, *other)
     embedded, base, wkeep, wsend, gt = call(
         functools.partial(forward_kernel, n, group),
         "forward_layer",
@@ -402,25 +401,28 @@
                     cost_us=SQUARE_COST)
             else:
                 total = call(add_kernel, "square_sum", piece, terms[s], cost_us=SQUARE_COST)
-            terms[s - distance].append(swap(total, n, 8 * distance))
+            if s == distance:
+                total = swap(total, n, 8 * distance)
+                terms[0].append(call(add_kernel, "far_sum", wide, (total,), cost_us=FAR_COST))
+            else:
+                terms[s - distance].append(swap(total, n, 8 * distance))
         distance *= 2
     bit = 8
     while bit < n:
         wsum = call(add_two_kernel, "weight_sum", chunk, (wsum, swap(wsum, n, bit)))
         bit *= 2
     rows = chunk.shape[0]
-    two = call(functools.partial(pack_kernel, (0, 1)), "pack_weights", result((2, rows, hidden), F32), (wsum, swap(wsum, n, 2)))
     mine = call(
-        functools.partial(pack_kernel, (0, 1)), "pack_weights", result((2, 2, rows, hidden), F32), (two, swap(two, n, 4), near_total))
-    main = call(main_kernel, "main_sum", piece, terms[0], cost_us=MAIN_COST)
-    grad_input, grad_self, grad_neigh = call(
-        last_kernel, "write_gradients",
-        (
-            result((nodes, feat_in), BF16, False), result((feat_in, hidden), F32, False),
-            result((feat_in, hidden), F32, False),
-        ),
-        (index, mine, swap(mine, n, 1), main), [SMEM] + [VMEM] * 3,
-    )
+        functools.partial(pack_kernel, (0, 1, 2, 3)), "pack_weights",
+        result((4, rows, hidden), F32),
+        (wsum, *[swap(wsum, n, offset) for offset in (2, 4, 6)], near_total))
+    grad_input = call(
+        main_kernel, "grad_input_sum", result((nodes, feat_in), BF16, False), terms[0],
+        cost_us=MAIN_COST)
+    full = result((feat_in, hidden), F32, False)
+    grad_self, grad_neigh = call(
+        last_kernel, "write_weights", (full, full), (index, mine, swap(mine, n, 1)),
+        [SMEM] + [VMEM] * 2)
     return (embedded, grad_input, grad_self, grad_neigh)
 
 

time: 61.4 us -> 62.9 us (1.024)
  starting transfers between devices: 24.9 us -> 27.8 us
  waiting for transfers between devices: 22.6 us -> 20.6 us
  Pallas kernels: 11.5 us -> 12.2 us
    ppermute x23 -> x24, starting transfers between devices: 24.9 us -> 27.8 us  [swap(): return lax.ppermute(x, 'row', [(i, i ^ offset) for i in range(n)])]
    ppermute x23 -> x24, waiting for transfers between devices: 22.6 us -> 20.6 us  [swap(): return lax.ppermute(x, 'row', [(i, i ^ offset) for i in range(n)])]
    pallas_call x15, Pallas kernels: 8.87 us -> 9.54 us  [call(): pl.pallas_call(kernel, out_shape=out_shape, in_specs=specs, out_specs=out...]
  transfers between devices with their start and end apart: 23 -> 24, of which waited for: 14 -> 14; matrix products, arithmetic and copies ran while one was open for 0% -> 0% of each run, Pallas kernels for 10% -> 11%
where the time goes in v9:
time: 62.9 us; the launch traced here: 62.7 us
  starting transfers between devices  27.8 us (44%)
  waiting for transfers between devices  20.6 us (33%)
  Pallas kernels  12.2 us (19%)
  local copies, waits for them, and re-layouts  1.31 us (2%)
  between operations  0.79 us (1%)
    ppermute x24, starting transfers between devices, swap(): return lax.ppermute(x, 'row', [(i, i ^ offset) for i in range(n)])  27.8 us
    ppermute x24, waiting for transfers between devices, swap(): return lax.ppermute(x, 'row', [(i, i ^ offset) for i in range(n)])  20.6 us
    pallas_call x15, Pallas kernels, call(): pl.pallas_call(kernel, out_shape=out_shape, in_specs=specs, out_specs=out...  9.54 us
    pallas_call x1, Pallas kernels, body(): pl.pallas_call(stage_kernel, out_shape=(result(tiles.shape, BF16), result...  2.68 us
    unnamed x4, local copies, waits for them, and re-layouts  1.31 us
  transfers between devices with their start and end apart: 24, of which 14 were waited for; matrix products, arithmetic and copies ran while one was open for 0% of the time, Pallas kernels for 11%

profile of v9, /device:TPU:0, one launch (start us, length us, event | category | flops | bytes accessed | tf_op | source)
XLA Modules:
  0.0 62.7 jit_solution(10261766535839431297)
XLA Ops:
  0.6 4.1 %collective-permute-start.3 = (bf16[512,128]{1,0:T(8,128)(2,1)}, bf16[512,128]{1,0:T(8,128)(2,1)S(1)}, u32[]{:S(2)}, u32[]{:S(2)}) collective-permute-start(bf16[512,128]{1,0:T(8,128)(2,1)} %feat_ref.1), channel_id=1, source_target_pairs={{0,8},{1,9},{2,10},{3,11},{4,12},{5,13},{6,14},{7,15},{8,0},{9,1},... | collective-permute-start | bytes 393224 | tf_op jit(solution)/shard_map/ppermute | solution.py:21
  4.7 1.5 %collective-permute-start = (bf16[512,128]{1,0:T(8,128)(2,1)}, bf16[512,128]{1,0:T(8,128)(2,1)S(1)}, u32[]{:S(2)}, u32[]{:S(2)}) collective-permute-start(bf16[512,128]{1,0:T(8,128)(2,1)} %feat_ref.1), channel_id=1, source_target_pairs={{0,2},{1,3},{2,0},{3,1},{4,6},{5,7},{6,4},{7,5},{8,10},{9,11},{10,... | collective-permute-start | bytes 393224 | tf_op jit(solution)/shard_map/ppermute | solution.py:21
  6.3 1.5 %collective-permute-start.1 = (bf16[512,128]{1,0:T(8,128)(2,1)}, bf16[512,128]{1,0:T(8,128)(2,1)S(1)}, u32[]{:S(2)}, u32[]{:S(2)}) collective-permute-start(bf16[512,128]{1,0:T(8,128)(2,1)} %feat_ref.1), channel_id=1, source_target_pairs={{0,6},{1,7},{2,4},{3,5},{4,2},{5,3},{6,0},{7,1},{8,14},{9,15},{10,... | collective-permute-start | bytes 393224 | tf_op jit(solution)/shard_map/ppermute | solution.py:21
  7.8 0.4 collective-permute-start.2
  8.2 3.1 %collective-permute-done.3.refs_0_ = bf16[512,128]{1,0:T(8,128)(2,1)S(1)} collective-permute-done((bf16[512,128]{1,0:T(8,128)(2,1)}, bf16[512,128]{1,0:T(8,128)(2,1)S(1)}, u32[]{:S(2)}, u32[]{:S(2)}) %collective-permute-start.3) | collective-permute-done | bytes 131104 | tf_op jit(solution)/shard_map/ppermute | solution.py:21
  11.4 1.7 %collective-permute-start.4 = (bf16[512,128]{1,0:T(8,128)(2,1)S(1)}, bf16[512,128]{1,0:T(8,128)(2,1)S(1)}, u32[]{:S(2)}, u32[]{:S(2)}) collective-permute-start(bf16[512,128]{1,0:T(8,128)(2,1)S(1)} %collective-permute-done.3.refs_0_), channel_id=1, source_target_pairs={{0,6},{1,7},{2,4},{3,5},{4,2},{5,3},{6,0},{7,1},{8,14},{9,15},{10,... | collective-permute-start | bytes 393224 | tf_op jit(solution)/shard_map/ppermute | solution.py:21
  13.1 0.5 collective-permute-start.5
  13.6 1.3 %collective-permute-start.6 = (bf16[512,128]{1,0:T(8,128)(2,1)S(1)}, bf16[512,128]{1,0:T(8,128)(2,1)S(1)}, u32[]{:S(2)}, u32[]{:S(2)}) collective-permute-start(bf16[512,128]{1,0:T(8,128)(2,1)S(1)} %collective-permute-done.3.refs_0_), channel_id=1, source_target_pairs={{0,4},{1,5},{2,6},{3,7},{4,0},{5,1},{6,2},{7,3},{8,12},{9,13},{10,... | collective-permute-start | bytes 393224 | tf_op jit(solution)/shard_map/ppermute | solution.py:21
  14.9 0.7 %copy-done = s32[60]{0:T(128)S(1)} copy-done((s32[60]{0:T(128)S(1)}, s32[60]{0:T(128)}, u32[]{:S(2)}) %copy-start) | copy-done | bytes 264
  15.5 0.7 %copy-done.1 = s32[60]{0:T(128)S(1)} copy-done((s32[60]{0:T(128)S(1)}, s32[60]{0:T(128)}, u32[]{:S(2)}) %copy-start.1) | copy-done | bytes 264
  16.2 2.7 %stage_arguments.1 = (bf16[60,128,128]{2,1,0:T(8,128)(2,1)S(1)}, bf16[128,256]{1,0:T(8,128)(2,1)S(1)}, bf16[128,256]{1,0:T(8,128)(2,1)S(1)}, f32[4,128,128]{2,1,...) custom-call(s32[1]{0:T(128)} %bitcast.me_ref, ...), custom_call_target="tpu_custom_call" | custom-call | flops 3300000000 | bytes 10800000 | tf_op jit(solution)/shard_map/stage_arguments/pallas_call | solution.py:324
  18.9 0.1 collective-permute-start.7
  19.0 1.4 %collective-permute-done.4.refs_1_ = bf16[512,128]{1,0:T(8,128)(2,1)S(1)} collective-permute-done((bf16[512,128]{1,0:T(8,128)(2,1)S(1)}, bf16[512,128]{1,0:T(8,128)(2,1)S(1)}, u32[]{:S(2)}, u32[]{:S(2)}) %collective-permute-start.4) | collective-permute-done | bytes 131104 | tf_op jit(solution)/shard_map/ppermute | solution.py:21
  20.4 0.6 collective-permute-done.5.refs_2_
  21.0 0.1 collective-permute-done.6.refs_3_
  21.2 0.1 collective-permute-start.8
  21.3 1.9 %collective-permute-done.8.refs_3_ = bf16[4,512,128]{2,1,0:T(8,128)(2,1)S(1)} collective-permute-done((bf16[4,512,128]{2,1,0:T(8,128)(2,1)S(1)}, bf16[4,512,128]{2,1,0:T(8,128)(2,1)S(1)}, u32[]{:S(2)}, u32[]{:S(2)}) %collective-permute-start.8) | collective-permute-done | bytes 524320 | tf_op jit(solution)/shard_map/ppermute | solution.py:21
  23.2 4.5 %forward_layer.1 = (bf16[512,256]{1,0:T(8,128)(2,1)}, f32[512,128]{1,0:T(8,128)S(1)}, f32[128,256]{1,0:T(8,128)S(1)}, f32[128,256]{1,0:T(8,128)S(1)}, bf16[4,256,128]{2,1,0:T(8,128)(2,1)S(1)}) custom-call(s32[121]{0:T(128)S(4)} %get-tuple-element.35.index_ref, bf16[60,128,128]{2,1,0:T(8,128)(2,1)S(1)} %get-tuple-element.36.tiles_ref, ...), custom_call_target="tpu_custom_call" | custom-call | flops 5500000256 | bytes 18000000 | tf_op jit(solution)/shard_map/forward_layer/pallas_call | solution.py:301
  27.7 0.1 collective-permute-start.13
  27.8 2.9 %backward_tiles.1.acc_ref = f32[65,128,128]{2,1,0:T(8,128)S(1)} custom-call(s32[121]{0:T(128)S(4)} %get-tuple-element.35.index_ref, bf16[60,128,128]{2,1,0:T(8,128)(2,1)S(1)} %get-tuple-element.36.tiles_ref, bf16[4,256,128]{2,1,0:T(8,128)(2,1)S(1)} %get-tuple-element.46.gt_ref), custom_call_target="tpu_custom_call" | custom-call | flops 3849999872 | bytes 12600000 | tf_op jit(solution)/shard_map/backward_tiles/pallas_call | solution.py:301
  30.7 0.1 send_weights.1
  30.8 0.4 collective-permute-start.14
  31.3 0.2 collective-permute-start.9
  31.5 2.0 %collective-permute-done.14.got_ref = f32[4,512,128]{2,1,0:T(8,128)S(1)} collective-permute-done((f32[4,512,128]{2,1,0:T(8,128)S(1)}, f32[4,512,128]{2,1,0:T(8,128)S(1)}, u32[]{:S(2)}, u32[]{:S(2)}) %collective-permute-start.14) | collective-permute-done | bytes 1048608 | tf_op jit(solution)/shard_map/ppermute | solution.py:21
  33.5 0.1 pair_sum_weights.1
  33.6 1.7 %collective-permute-start.15 = (bf16[640,128]{1,0:T(8,128)(2,1)S(1)}, bf16[640,128]{1,0:T(8,128)(2,1)S(1)}, u32[]{:S(2)}, u32[]{:S(2)}) collective-permute-start(bf16[640,128]{1,0:T(8,128)(2,1)S(1)} %get-tuple-element.59), channel_id=1, source_target_pairs={{0,2},{1,3},{2,0},{3,1},{4,6},{5,7},{6,4},{7,5},{8,10},{9,11},{10,... | collective-permute-start | bytes 491528 | tf_op jit(solution)/shard_map/ppermute | solution.py:21
  35.3 0.3 collective-permute-start.16
  35.6 1.6 %collective-permute-start.17 = (bf16[640,128]{1,0:T(8,128)(2,1)S(1)}, bf16[640,128]{1,0:T(8,128)(2,1)S(1)}, u32[]{:S(2)}, u32[]{:S(2)}) collective-permute-start(bf16[640,128]{1,0:T(8,128)(2,1)S(1)} %get-tuple-element.61), channel_id=1, source_target_pairs={{0,6},{1,7},{2,4},{3,5},{4,2},{5,3},{6,0},{7,1},{8,14},{9,15},{10,... | collective-permute-start | bytes 491528 | tf_op jit(solution)/shard_map/ppermute | solution.py:21
  37.2 0.1 pair_sum.1
  37.3 1.6 %collective-permute-start.10 = (bf16[512,128]{1,0:T(8,128)(2,1)S(1)}, bf16[512,128]{1,0:T(8,128)(2,1)S(1)}, u32[]{:S(2)}, u32[]{:S(2)}) collective-permute-start(bf16[512,128]{1,0:T(8,128)(2,1)S(1)} %get-tuple-element.48), channel_id=1, source_target_pairs={{0,2},{1,3},{2,0},{3,1},{4,6},{5,7},{6,4},{7,5},{8,10},{9,11},{10,... | collective-permute-start | bytes 393224 | tf_op jit(solution)/shard_map/ppermute | solution.py:21
  38.9 0.3 collective-permute-start.11
  39.2 1.7 %collective-permute-done.15.refs_0_ = bf16[640,128]{1,0:T(8,128)(2,1)S(1)} collective-permute-done((bf16[640,128]{1,0:T(8,128)(2,1)S(1)}, bf16[640,128]{1,0:T(8,128)(2,1)S(1)}, u32[]{:S(2)}, u32[]{:S(2)}) %collective-permute-start.15) | collective-permute-done | bytes 163872 | tf_op jit(solution)/shard_map/ppermute | solution.py:21
  40.9 1.3 %collective-permute-start.12 = (bf16[512,128]{1,0:T(8,128)(2,1)S(1)}, bf16[512,128]{1,0:T(8,128)(2,1)S(1)}, u32[]{:S(2)}, u32[]{:S(2)}) collective-permute-start(bf16[512,128]{1,0:T(8,128)(2,1)S(1)} %get-tuple-element.50), channel_id=1, source_target_pairs={{0,6},{1,7},{2,4},{3,5},{4,2},{5,3},{6,0},{7,1},{8,14},{9,15},{10,... | collective-permute-start | bytes 393224 | tf_op jit(solution)/shard_map/ppermute | solution.py:21
  42.3 3.4 %collective-permute-done.17.refs_2_ = bf16[640,128]{1,0:T(8,128)(2,1)S(1)} collective-permute-done((bf16[640,128]{1,0:T(8,128)(2,1)S(1)}, bf16[640,128]{1,0:T(8,128)(2,1)S(1)}, u32[]{:S(2)}, u32[]{:S(2)}) %collective-permute-start.17) | collective-permute-done | bytes 163872 | tf_op jit(solution)/shard_map/ppermute | solution.py:21
  45.8 0.1 square_sum_weights.1
  45.8 1.8 %collective-permute-start.19 = (f32[32,256]{1,0:T(8,128)S(1)}, f32[32,256]{1,0:T(8,128)S(1)}, u32[]{:S(2)}, u32[]{:S(2)}) collective-permute-start(f32[32,256]{1,0:T(8,128)S(1)} %get-tuple-element.63.own_ref), channel_id=1, source_target_pairs={{0,8},{1,9},{2,10},{3,11},{4,12},{5,13},{6,14},{7,15},{8,0},{9,1},... | collective-permute-start | bytes 98312 | tf_op jit(solution)/shard_map/ppermute | solution.py:21
  47.6 1.2 %collective-permute-start.18 = (bf16[512,128]{1,0:T(8,128)(2,1)S(1)}, bf16[512,128]{1,0:T(8,128)(2,1)S(1)}, u32[]{:S(2)}, u32[]{:S(2)}) collective-permute-start(bf16[512,128]{1,0:T(8,128)(2,1)S(1)} %get-tuple-element.62), channel_id=1, source_target_pairs={{0,8},{1,9},{2,10},{3,11},{4,12},{5,13},{6,14},{7,15},{8,0},{9,1},... | collective-permute-start | bytes 393224 | tf_op jit(solution)/shard_map/ppermute | solution.py:21
  48.8 2.4 %collective-permute-done.19.got_ref = f32[32,256]{1,0:T(8,128)S(1)} collective-permute-done((f32[32,256]{1,0:T(8,128)S(1)}, f32[32,256]{1,0:T(8,128)S(1)}, u32[]{:S(2)}, u32[]{:S(2)}) %collective-permute-start.19) | collective-permute-done | bytes 32800 | tf_op jit(solution)/shard_map/ppermute | solution.py:21
  51.3 4.4 %collective-permute-start.20 = (f32[32,256]{1,0:T(8,128)S(1)}, f32[32,256]{1,0:T(8,128)S(1)}, u32[]{:S(2)}, u32[]{:S(2)}) collective-permute-start(f32[32,256]{1,0:T(8,128)S(1)} %weight_sum.1.refs_0_), channel_id=1, source_target_pairs={{0,2},{1,3},{2,0},{3,1},{4,6},{5,7},{6,4},{7,5},{8,10},{9,11},{10,... | collective-permute-start | bytes 98312 | tf_op jit(solution)/shard_map/ppermute | solution.py:21
  55.7 1.5 %collective-permute-start.22 = (f32[32,256]{1,0:T(8,128)S(1)}, f32[32,256]{1,0:T(8,128)S(1)}, u32[]{:S(2)}, u32[]{:S(2)}) collective-permute-start(f32[32,256]{1,0:T(8,128)S(1)} %weight_sum.1.refs_0_), channel_id=1, source_target_pairs={{0,6},{1,7},{2,4},{3,5},{4,2},{5,3},{6,0},{7,1},{8,14},{9,15},{10,... | collective-permute-start | bytes 98312 | tf_op jit(solution)/shard_map/ppermute | solution.py:21
  57.3 0.1 near_sum.1.near_ref.refs_4_
  57.4 0.2 collective-permute-done.20.refs_1_
  57.6 2.0 %collective-permute-done.21.refs_2_ = f32[32,256]{1,0:T(8,128)S(1)} collective-permute-done((f32[32,256]{1,0:T(8,128)S(1)}, f32[32,256]{1,0:T(8,128)S(1)}, u32[]{:S(2)}, u32[]{:S(2)}) %collective-permute-start.21) | collective-permute-done | bytes 32800 | tf_op jit(solution)/shard_map/ppermute | solution.py:21
  59.6 1.0 %collective-permute-done.22.refs_3_ = f32[32,256]{1,0:T(8,128)S(1)} collective-permute-done((f32[32,256]{1,0:T(8,128)S(1)}, f32[32,256]{1,0:T(8,128)S(1)}, u32[]{:S(2)}, u32[]{:S(2)}) %collective-permute-start.22) | collective-permute-done | bytes 32800 | tf_op jit(solution)/shard_map/ppermute | solution.py:21
  60.6 0.1 collective-permute-start.23
  60.7 0.8 %grad_input_sum.1 = bf16[512,128]{1,0:T(8,128)(2,1)} custom-call(f32[512,128]{1,0:T(8,128)S(1)} %near_sum.1.near_ref.refs_4_, f32[512,128]{1,0:T(8,128)S(1)} %far_sum.1.refs_0_), custom_call_target="tpu_custom_call" | custom-call | flops 220000000 | bytes 720000 | tf_op jit(solution)/shard_map/grad_input_sum/pallas_call | solution.py:301
  61.5 0.5 collective-permute-done.23.other_ref
  62.0 0.7 %write_weights.1 = (f32[128,256]{1,0:T(8,128)}, f32[128,256]{1,0:T(8,128)}) custom-call(s32[121]{0:T(128)S(4)} %get-tuple-element.35.index_ref, f32[4,32,256]{2,1,0:T(8,128)S(1)} %pack_weights.1.weight_ref, f32[4,32,256]{2,1,0:T(8,128)S(1)} %collective-permute-done.23.other_ref), custom_call_target="tpu_custom_call" | custom-call | flops 220000000 | bytes 720000 | tf_op jit(solution)/shard_map/write_weights/pallas_call | solution.py:301
  (20 shorter events, 0.3 us)
Async XLA Ops:
  0.6 10.7 %collective-permute-start.3 = (bf16[512,128]{1,0:T(8,128)(2,1)}, bf16[512,128]{1,0:T(8,128)(2,1)S(1)}, u32[]{:S(2)}, u32[]{:S(2)}) collective-permute-start(bf16[512,128]{1,0:T(8,128)(2,1)} %feat_ref.1), channel_id=1, source_target_pairs={{0,8},{1,9},{2,10},{3,11},{4,12},{5,13},{6,14},{7,15},{8,0},{9,1},... | collective-permute-start | bytes 393224 | tf_op jit(solution)/shard_map/ppermute | solution.py:21
  4.7 8.9 %collective-permute-start = (bf16[512,128]{1,0:T(8,128)(2,1)}, bf16[512,128]{1,0:T(8,128)(2,1)S(1)}, u32[]{:S(2)}, u32[]{:S(2)}) collective-permute-start(bf16[512,128]{1,0:T(8,128)(2,1)} %feat_ref.1), channel_id=1, source_target_pairs={{0,2},{1,3},{2,0},{3,1},{4,6},{5,7},{6,4},{7,5},{8,10},{9,11},{10,... | collective-permute-start | bytes 393224 | tf_op jit(solution)/shard_map/ppermute | solution.py:21
  6.3 12.6 %collective-permute-start.1 = (bf16[512,128]{1,0:T(8,128)(2,1)}, bf16[512,128]{1,0:T(8,128)(2,1)S(1)}, u32[]{:S(2)}, u32[]{:S(2)}) collective-permute-start(bf16[512,128]{1,0:T(8,128)(2,1)} %feat_ref.1), channel_id=1, source_target_pairs={{0,6},{1,7},{2,4},{3,5},{4,2},{5,3},{6,0},{7,1},{8,14},{9,15},{10,... | collective-permute-start | bytes 393224 | tf_op jit(solution)/shard_map/ppermute | solution.py:21
  7.8 11.1 %collective-permute-start.2 = (bf16[512,128]{1,0:T(8,128)(2,1)}, bf16[512,128]{1,0:T(8,128)(2,1)S(1)}, u32[]{:S(2)}, u32[]{:S(2)}) collective-permute-start(bf16[512,128]{1,0:T(8,128)(2,1)} %feat_ref.1), channel_id=1, source_target_pairs={{0,4},{1,5},{2,6},{3,7},{4,0},{5,1},{6,2},{7,3},{8,12},{9,13},{10,... | collective-permute-start | bytes 393224 | tf_op jit(solution)/shard_map/ppermute | solution.py:21
  11.4 9.1 %collective-permute-start.4 = (bf16[512,128]{1,0:T(8,128)(2,1)S(1)}, bf16[512,128]{1,0:T(8,128)(2,1)S(1)}, u32[]{:S(2)}, u32[]{:S(2)}) collective-permute-start(bf16[512,128]{1,0:T(8,128)(2,1)S(1)} %collective-permute-done.3.refs_0_), channel_id=1, source_target_pairs={{0,6},{1,7},{2,4},{3,5},{4,2},{5,3},{6,0},{7,1},{8,14},{9,15},{10,... | collective-permute-start | bytes 393224 | tf_op jit(solution)/shard_map/ppermute | solution.py:21
  13.1 7.9 %collective-permute-start.5 = (bf16[512,128]{1,0:T(8,128)(2,1)S(1)}, bf16[512,128]{1,0:T(8,128)(2,1)S(1)}, u32[]{:S(2)}, u32[]{:S(2)}) collective-permute-start(bf16[512,128]{1,0:T(8,128)(2,1)S(1)} %collective-permute-done.3.refs_0_), channel_id=1, source_target_pairs={{0,2},{1,3},{2,0},{3,1},{4,6},{5,7},{6,4},{7,5},{8,10},{9,11},{10,... | collective-permute-start | bytes 393224 | tf_op jit(solution)/shard_map/ppermute | solution.py:21
  13.6 7.6 %collective-permute-start.6 = (bf16[512,128]{1,0:T(8,128)(2,1)S(1)}, bf16[512,128]{1,0:T(8,128)(2,1)S(1)}, u32[]{:S(2)}, u32[]{:S(2)}) collective-permute-start(bf16[512,128]{1,0:T(8,128)(2,1)S(1)} %collective-permute-done.3.refs_0_), channel_id=1, source_target_pairs={{0,4},{1,5},{2,6},{3,7},{4,0},{5,1},{6,2},{7,3},{8,12},{9,13},{10,... | collective-permute-start | bytes 393224 | tf_op jit(solution)/shard_map/ppermute | solution.py:21
  14.8 0.7 %copy-start = (s32[60]{0:T(128)S(1)}, s32[60]{0:T(128)}, u32[]{:S(2)}) copy-start(s32[60]{0:T(128)} %trow_ref.1) | copy-start | bytes 724
  15.5 0.7 %copy-start.1 = (s32[60]{0:T(128)S(1)}, s32[60]{0:T(128)}, u32[]{:S(2)}) copy-start(s32[60]{0:T(128)} %tcol_ref.1) | copy-start | bytes 724
  18.9 2.4 %collective-permute-start.7 = (bf16[4,512,128]{2,1,0:T(8,128)(2,1)S(1)}, bf16[4,512,128]{2,1,0:T(8,128)(2,1)S(1)}, u32[]{:S(2)}, u32[]{:S(2)}) collective-permute-start(bf16[4,512,128]{2,1,0:T(8,128)(2,1)S(1)} %pack_square.2.refs_0_), channel_id=1, source_target_pairs={{0,1},{1,0},{2,3},{3,2},{4,5},{5,4},{6,7},{7,6},{8,9},{9,8},{10,11... | collective-permute-start | bytes 1572872 | tf_op jit(solution)/shard_map/ppermute | solution.py:21
  21.2 2.0 %collective-permute-start.8 = (bf16[4,512,128]{2,1,0:T(8,128)(2,1)S(1)}, bf16[4,512,128]{2,1,0:T(8,128)(2,1)S(1)}, u32[]{:S(2)}, u32[]{:S(2)}) collective-permute-start(bf16[4,512,128]{2,1,0:T(8,128)(2,1)S(1)} %pack_square.3.refs_1_), channel_id=1, source_target_pairs={{0,1},{1,0},{2,3},{3,2},{4,5},{5,4},{6,7},{7,6},{8,9},{9,8},{10,11... | collective-permute-start | bytes 1572872 | tf_op jit(solution)/shard_map/ppermute | solution.py:21
  27.7 3.0 %collective-permute-start.13 = (f32[128,256]{1,0:T(8,128)S(1)}, f32[128,256]{1,0:T(8,128)S(1)}, u32[]{:S(2)}, u32[]{:S(2)}) collective-permute-start(f32[128,256]{1,0:T(8,128)S(1)} %get-tuple-element.52), channel_id=1, source_target_pairs={{0,1},{1,0},{2,3},{3,2},{4,5},{5,4},{6,7},{7,6},{8,9},{9,8},{10,11... | collective-permute-start | bytes 393224 | tf_op jit(solution)/shard_map/ppermute | solution.py:21
  30.8 2.7 %collective-permute-start.14 = (f32[4,512,128]{2,1,0:T(8,128)S(1)}, f32[4,512,128]{2,1,0:T(8,128)S(1)}, u32[]{:S(2)}, u32[]{:S(2)}) collective-permute-start(f32[4,512,128]{2,1,0:T(8,128)S(1)} %get-tuple-element.54), channel_id=1, source_target_pairs={{0,1},{1,0},{2,3},{3,2},{4,5},{5,4},{6,7},{7,6},{8,9},{9,8},{10,11... | collective-permute-start | bytes 3145736 | tf_op jit(solution)/shard_map/ppermute | solution.py:21
  31.3 5.9 %collective-permute-start.9 = (f32[4,512,128]{2,1,0:T(8,128)S(1)}, f32[4,512,128]{2,1,0:T(8,128)S(1)}, u32[]{:S(2)}, u32[]{:S(2)}) collective-permute-start(f32[4,512,128]{2,1,0:T(8,128)S(1)} %send.1), channel_id=1, source_target_pairs={{0,1},{1,0},{2,3},{3,2},{4,5},{5,4},{6,7},{7,6},{8,9},{9,8},{10,11... | collective-permute-start | bytes 3145736 | tf_op jit(solution)/shard_map/ppermute | solution.py:21
  33.6 7.3 %collective-permute-start.15 = (bf16[640,128]{1,0:T(8,128)(2,1)S(1)}, bf16[640,128]{1,0:T(8,128)(2,1)S(1)}, u32[]{:S(2)}, u32[]{:S(2)}) collective-permute-start(bf16[640,128]{1,0:T(8,128)(2,1)S(1)} %get-tuple-element.59), channel_id=1, source_target_pairs={{0,2},{1,3},{2,0},{3,1},{4,6},{5,7},{6,4},{7,5},{8,10},{9,11},{10,... | collective-permute-start | bytes 491528 | tf_op jit(solution)/shard_map/ppermute | solution.py:21
  35.3 7.1 %collective-permute-start.16 = (bf16[640,128]{1,0:T(8,128)(2,1)S(1)}, bf16[640,128]{1,0:T(8,128)(2,1)S(1)}, u32[]{:S(2)}, u32[]{:S(2)}) collective-permute-start(bf16[640,128]{1,0:T(8,128)(2,1)S(1)} %get-tuple-element.60), channel_id=1, source_target_pairs={{0,4},{1,5},{2,6},{3,7},{4,0},{5,1},{6,2},{7,3},{8,12},{9,13},{10,... | collective-permute-start | bytes 491528 | tf_op jit(solution)/shard_map/ppermute | solution.py:21
  35.6 10.2 %collective-permute-start.17 = (bf16[640,128]{1,0:T(8,128)(2,1)S(1)}, bf16[640,128]{1,0:T(8,128)(2,1)S(1)}, u32[]{:S(2)}, u32[]{:S(2)}) collective-permute-start(bf16[640,128]{1,0:T(8,128)(2,1)S(1)} %get-tuple-element.61), channel_id=1, source_target_pairs={{0,6},{1,7},{2,4},{3,5},{4,2},{5,3},{6,0},{7,1},{8,14},{9,15},{10,... | collective-permute-start | bytes 491528 | tf_op jit(solution)/shard_map/ppermute | solution.py:21
  37.3 18.4 %collective-permute-start.10 = (bf16[512,128]{1,0:T(8,128)(2,1)S(1)}, bf16[512,128]{1,0:T(8,128)(2,1)S(1)}, u32[]{:S(2)}, u32[]{:S(2)}) collective-permute-start(bf16[512,128]{1,0:T(8,128)(2,1)S(1)} %get-tuple-element.48), channel_id=1, source_target_pairs={{0,2},{1,3},{2,0},{3,1},{4,6},{5,7},{6,4},{7,5},{8,10},{9,11},{10,... | collective-permute-start | bytes 393224 | tf_op jit(solution)/shard_map/ppermute | solution.py:21
  38.9 16.8 %collective-permute-start.11 = (bf16[512,128]{1,0:T(8,128)(2,1)S(1)}, bf16[512,128]{1,0:T(8,128)(2,1)S(1)}, u32[]{:S(2)}, u32[]{:S(2)}) collective-permute-start(bf16[512,128]{1,0:T(8,128)(2,1)S(1)} %get-tuple-element.49), channel_id=1, source_target_pairs={{0,4},{1,5},{2,6},{3,7},{4,0},{5,1},{6,2},{7,3},{8,12},{9,13},{10,... | collective-permute-start | bytes 393224 | tf_op jit(solution)/shard_map/ppermute | solution.py:21
  40.9 16.3 %collective-permute-start.12 = (bf16[512,128]{1,0:T(8,128)(2,1)S(1)}, bf16[512,128]{1,0:T(8,128)(2,1)S(1)}, u32[]{:S(2)}, u32[]{:S(2)}) collective-permute-start(bf16[512,128]{1,0:T(8,128)(2,1)S(1)} %get-tuple-element.50), channel_id=1, source_target_pairs={{0,6},{1,7},{2,4},{3,5},{4,2},{5,3},{6,0},{7,1},{8,14},{9,15},{10,... | collective-permute-start | bytes 393224 | tf_op jit(solution)/shard_map/ppermute | solution.py:21
  45.8 5.4 %collective-permute-start.19 = (f32[32,256]{1,0:T(8,128)S(1)}, f32[32,256]{1,0:T(8,128)S(1)}, u32[]{:S(2)}, u32[]{:S(2)}) collective-permute-start(f32[32,256]{1,0:T(8,128)S(1)} %get-tuple-element.63.own_ref), channel_id=1, source_target_pairs={{0,8},{1,9},{2,10},{3,11},{4,12},{5,13},{6,14},{7,15},{8,0},{9,1},... | collective-permute-start | bytes 98312 | tf_op jit(solution)/shard_map/ppermute | solution.py:21
  47.6 13.1 %collective-permute-start.18 = (bf16[512,128]{1,0:T(8,128)(2,1)S(1)}, bf16[512,128]{1,0:T(8,128)(2,1)S(1)}, u32[]{:S(2)}, u32[]{:S(2)}) collective-permute-start(bf16[512,128]{1,0:T(8,128)(2,1)S(1)} %get-tuple-element.62), channel_id=1, source_target_pairs={{0,8},{1,9},{2,10},{3,11},{4,12},{5,13},{6,14},{7,15},{8,0},{9,1},... | collective-permute-start | bytes 393224 | tf_op jit(solution)/shard_map/ppermute | solution.py:21
  51.3 6.3 %collective-permute-start.20 = (f32[32,256]{1,0:T(8,128)S(1)}, f32[32,256]{1,0:T(8,128)S(1)}, u32[]{:S(2)}, u32[]{:S(2)}) collective-permute-start(f32[32,256]{1,0:T(8,128)S(1)} %weight_sum.1.refs_0_), channel_id=1, source_target_pairs={{0,2},{1,3},{2,0},{3,1},{4,6},{5,7},{6,4},{7,5},{8,10},{9,11},{10,... | collective-permute-start | bytes 98312 | tf_op jit(solution)/shard_map/ppermute | solution.py:21
  55.7 3.9 %collective-permute-start.21 = (f32[32,256]{1,0:T(8,128)S(1)}, f32[32,256]{1,0:T(8,128)S(1)}, u32[]{:S(2)}, u32[]{:S(2)}) collective-permute-start(f32[32,256]{1,0:T(8,128)S(1)} %weight_sum.1.refs_0_), channel_id=1, source_target_pairs={{0,4},{1,5},{2,6},{3,7},{4,0},{5,1},{6,2},{7,3},{8,12},{9,13},{10,... | collective-permute-start | bytes 98312 | tf_op jit(solution)/shard_map/ppermute | solution.py:21
  55.7 4.9 %collective-permute-start.22 = (f32[32,256]{1,0:T(8,128)S(1)}, f32[32,256]{1,0:T(8,128)S(1)}, u32[]{:S(2)}, u32[]{:S(2)}) collective-permute-start(f32[32,256]{1,0:T(8,128)S(1)} %weight_sum.1.refs_0_), channel_id=1, source_target_pairs={{0,6},{1,7},{2,4},{3,5},{4,2},{5,3},{6,0},{7,1},{8,14},{9,15},{10,... | collective-permute-start | bytes 98312 | tf_op jit(solution)/shard_map/ppermute | solution.py:21
  60.6 1.4 %collective-permute-start.23 = (f32[4,32,256]{2,1,0:T(8,128)S(1)}, f32[4,32,256]{2,1,0:T(8,128)S(1)}, u32[]{:S(2)}, u32[]{:S(2)}) collective-permute-start(f32[4,32,256]{2,1,0:T(8,128)S(1)} %pack_weights.1.weight_ref), channel_id=1, source_target_pairs={{0,1},{1,0},{2,3},{3,2},{4,5},{5,4},{6,7},{7,6},{8,9},{9,8},{10,11... | collective-permute-start | bytes 393224 | tf_op jit(solution)/shard_map/ppermute | solution.py:21

commit v10 on v9

--- a/solution.py
+++ b/solution.py
@@ -14,7 +14,7 @@
 ANY = pl.BlockSpec(memory_space=pl.ANY)
 MIB = 1024 * 1024
 LAST = ((1,), (1,))
-NEAR_COST, SQUARE_COST, MAIN_COST, FAR_COST = 4, 0.2, 0.2, 10
+NEAR_COST, SQUARE_COST, MAIN_COST = 8, 4, 10
 
 
 def swap(x, n, offset):
@@ -69,7 +69,7 @@
         refs[-1][slot] = ref[...]
 
 
-def stage_kernel(me_ref, trow_ref, tcol_ref, deg_ref, mask_ref, ws_ref, wn_ref, feat_ref, cot_ref,
+def stage_kernel(dumps, me_ref, trow_ref, tcol_ref, deg_ref, mask_ref, ws_ref, wn_ref, feat_ref, cot_ref,
                  tiles_ref, tiles_out, ws_out, wn_out, inverse_out, up_out, pre_out, featt_out,
                  own_out, index_out, sem):
     copy = pltpu.make_async_copy(tiles_ref, tiles_out, sem)
@@ -77,19 +77,40 @@
     block_local = feat_ref.shape[0] // BLOCK
     tile_count = trow_ref.shape[0]
     me = me_ref[0]
-    index_out[2 * tile_count] = me
-
-    def place(t, carry):
+    index_out[index_out.shape[0] - 1] = me
+
+    def clear(i, carry):
+        for section in range(2):
+            index_out[3 * section * tile_count + i] = 0
+            index_out[(3 * section + 1) * tile_count + i] = block_local
+            index_out[(3 * section + 2) * tile_count + i] = dumps[section]
+        return carry
+
+    def place(t, counts):
         col = tcol_ref[t]
         live = col >= 0
         col = jnp.maximum(col, 0)
-        position = ((col // block_local) ^ me) * block_local + col % block_local
+        chip_core = (col // block_local) ^ me
+        far = chip_core >= 8
+        position = jnp.where(far, chip_core - 8, chip_core) * block_local + col % block_local
         row = jnp.clip(trow_ref[t] - me * block_local, 0, block_local - 1)
-        index_out[t] = jnp.where(live, row, block_local)
-        index_out[tile_count + t] = position
-        return carry
-
-    lax.fori_loop(0, tile_count, place, 0)
+        near_count, far_count = counts
+        spot = jnp.where(far, 3 * tile_count + far_count, near_count)
+
+        @pl.when(live)
+        def _():
+            index_out[spot] = t
+            index_out[spot + tile_count] = row
+            index_out[spot + 2 * tile_count] = position
+
+        add = live.astype(jnp.int32)
+        add_far = far.astype(jnp.int32) * add
+        return near_count + add - add_far, far_count + add_far
+
+    lax.fori_loop(0, tile_count, clear, 0)
+    near_count, far_count = lax.fori_loop(0, tile_count, place, (jnp.int32(0), jnp.int32(0)))
+    index_out[6 * tile_count] = near_count
+    index_out[6 * tile_count + 1] = far_count
     own_out[...] = feat_ref[...]
     ws_out[...] = ws_ref[...]
     wn_out[...] = wn_ref[...]
@@ -106,15 +127,28 @@
     copy.wait()
 
 
-def forward_kernel(n, group, index_ref, tiles_ref, ws_ref, wn_ref, inverse_ref, up_ref, pre_ref,
-                   featt_ref, *refs):
-    squares = n // 8
-    feat_refs, refs = refs[:2 * squares], refs[2 * squares:]
-    emb_ref, base_ref, wkeep_ref, wsend_ref, gt_ref, feats, raw, wsum = refs
-    block_local = inverse_ref.shape[0]
-    tile_count = tiles_ref.shape[0]
-
-    raw[...] = jnp.zeros_like(raw)
+def over_tiles(section, group, index_ref, product, add):
+    tile_count = (index_ref.shape[0] - 3) // 6
+    start = 3 * section * tile_count
+
+    def step(i, carry):
+        spots = [start + i * group + u for u in range(group)]
+        entries = [
+            (index_ref[spot], index_ref[spot + tile_count], index_ref[spot + 2 * tile_count])
+            for spot in spots
+        ]
+        products = [product(*entry) for entry in entries]
+        for entry, value in zip(entries, products):
+            add(*entry, value)
+        return carry
+
+    count = index_ref[6 * tile_count + section]
+    lax.fori_loop(0, (count + group - 1) // group, step, 0)
+
+
+def gathered_products(section, group, index_ref, tiles_ref, feat_refs, feats, raw):
+    squares = len(feat_refs) // 2
+    block_local = raw.shape[0] - 1
     for s in range(squares):
         for q in range(4):
             for core in range(2):
@@ -122,17 +156,27 @@
                     spot = (8 * s + 2 * q + core) * block_local + b
                     feats[spot] = feat_refs[core * squares + s][q, rows_of(b), :]
 
-    def forward(step, carry):
-        rows, products = [], []
-        for u in range(group):
-            t = step * group + u
-            rows.append(index_ref[t])
-            products.append(dot(tiles_ref[t], feats[index_ref[tile_count + t]]))
-        for row, product in zip(rows, products):
-            raw[row] += product
-        return carry
-
-    lax.fori_loop(0, tile_count // group, forward, 0)
+    def add(t, row, position, value):
+        raw[row] += value
+
+    over_tiles(
+        section, group, index_ref,
+        lambda t, row, position: dot(tiles_ref[t], feats[jnp.minimum(position, feats.shape[0] - 1)]),
+        add)
+
+
+def forward_near_kernel(group, index_ref, tiles_ref, same_ref, other_ref, raw, feats):
+    raw[...] = jnp.zeros_like(raw)
+    gathered_products(0, group, index_ref, tiles_ref, (same_ref, other_ref), feats, raw)
+
+
+def forward_kernel(group, far, index_ref, tiles_ref, ws_ref, wn_ref, inverse_ref, up_ref, pre_ref,
+                   featt_ref, near_ref, *refs):
+    feat_refs, refs = refs[:2 * far], refs[2 * far:]
+    emb_ref, base_ref, wkeep_ref, wsend_ref, gt_ref, feats, raw, wsum = refs
+    block_local = inverse_ref.shape[0]
+    raw[...] = near_ref[...]
+    gathered_products(1, group, index_ref, tiles_ref, feat_refs, feats, raw)
 
     wn = wn_ref[...]
     ws = ws_ref[...]
@@ -158,41 +202,34 @@
         gt_ref[b, :BLOCK, :] = high
         gt_ref[b, BLOCK:, :] = low
 
-    core = index_ref[2 * tile_count] % 2
+    core = index_ref[index_ref.shape[0] - 1] % 2
     wkeep_ref[...] = wsum[core]
     wsend_ref[...] = wsum[1 - core]
 
 
-def backward_kernel(group, index_ref, tiles_ref, gt_ref, acc_ref):
+def backward_kernel(section, group, index_ref, tiles_ref, gt_ref, acc_ref):
     block_local = gt_ref.shape[0]
-    tile_count = tiles_ref.shape[0]
-    dump = acc_ref.shape[0] - 1
     acc_ref[...] = jnp.zeros_like(acc_ref)
 
-    def backward(step, carry):
-        places, products = [], []
-        for u in range(group):
-            t = step * group + u
-            row = index_ref[t]
-            places.append(jnp.where(row < block_local, index_ref[tile_count + t], dump))
-            both = dot(gt_ref[jnp.minimum(row, block_local - 1)], tiles_ref[t])
-            products.append(both[:BLOCK] + both[BLOCK:])
-        for position, product in zip(places, products):
-            acc_ref[position] += product
-        return carry
-
-    lax.fori_loop(0, tile_count // group, backward, 0)
-
-
-def send_kernel(square, block_local, acc_ref, send_ref):
+    def product(t, row, position):
+        both = dot(gt_ref[jnp.minimum(row, block_local - 1)], tiles_ref[t])
+        return both[:BLOCK] + both[BLOCK:]
+
+    def add(t, row, position, value):
+        acc_ref[position] += value
+
+    over_tiles(section, group, index_ref, product, add)
+
+
+def send_kernel(square, acc_ref, *refs):
+    send_ref = refs[-1]
+    block_local = send_ref.shape[1] // BLOCK
     for q in range(4):
         for b in range(block_local):
             send_ref[q, rows_of(b), :] = acc_ref[(8 * square + 2 * q + 1) * block_local + b]
 
 
-def send_weights_kernel(square, block_local, index_ref, acc_ref, wkeep_ref, wgot_ref, send_ref,
-                        *parts):
-    send_kernel(square, block_local, acc_ref, send_ref)
+def cut_kernel(index_ref, wkeep_ref, wgot_ref, *parts):
     rows = parts[0].shape[0]
     chip = index_ref[index_ref.shape[0] - 1] // 2 % 4
     for p, ref in enumerate(parts):
@@ -225,10 +262,10 @@
 
 
 def add_kernel(own_ref, *refs):
-    total = own_ref[...].astype(F32)
+    total = own_ref[...]
     for got_ref in refs[:-1]:
         total = total + got_ref[...].astype(F32)
-    refs[-1][...] = total.astype(refs[-1].dtype)
+    refs[-1][...] = total.astype(BF16)
 
 
 def add_weights_kernel(weight_ref, own_ref, *refs):
@@ -267,10 +304,10 @@
     me = index_ref[index_ref.shape[0] - 1]
     first = me % 2 == 0
     chip = me // 2 % 4
-    rows = weight_ref.shape[1]
+    rows = weight_ref.shape[2]
     for p in range(4):
         span = pl.ds(pl.multiple_of((chip ^ p) * rows, rows), rows)
-        mine, other = weight_ref[p], other_ref[p]
+        mine, other = weight_ref[p // 2, p % 2], other_ref[p // 2, p % 2]
         self_ref[span, :] = jnp.where(first, mine, other)
         neigh_ref[span, :] = jnp.where(first, other, mine)
 
@@ -322,7 +359,7 @@
     if small:
         own_arguments = [pltpu.with_memory_space_constraint(x, pltpu.HBM) for x in own_arguments]
     tiles_near, ws, wn, inverse, upstream, pre_self, feat_t, own, index = pl.pallas_call(
-        stage_kernel,
+        functools.partial(stage_kernel, (8 * block_local, (n - 8) * block_local)),
         out_shape=(
             result(tiles.shape, BF16),
             result(w_self.shape, BF16),
@@ -332,7 +369,7 @@
             result((nodes, hidden), F32),
             result(by_block, BF16),
             piece,
-            pltpu.SMEM((2 * tile_count + 1,), jnp.int32),
+            pltpu.SMEM((6 * tile_count + 3,), jnp.int32),
         ),
         in_specs=[SMEM] * 3 + [VMEM] * 6 + [ANY],
         out_specs=(VMEM,) * 8 + (SMEM,),
@@ -343,9 +380,18 @@
     )(me, tile_row, tile_col, *own_arguments, placed(tiles, ANY))
 
     same, other = gather_by_xor(features, own, n, call, result((4, nodes, feat_in), BF16))
-    operands = (index, tiles_near, ws, wn, inverse, upstream, pre_self, feat_t, *same, *other)
+    near_square = (8 * block_local, BLOCK, feat_in)
+    far_squares = ((n - 8) * block_local, BLOCK, feat_in)
+    raw_shape = (block_local + 1, BLOCK, feat_in)
+    raw = call(
+        functools.partial(forward_near_kernel, group), "forward_near", result(raw_shape, F32),
+        (index, tiles_near, same[0], other[0]), [SMEM] + [VMEM] * 3, cost_us=0.1,
+        scratch_shapes=[pltpu.VMEM(near_square, BF16)],
+    )
+    operands = (
+        index, tiles_near, ws, wn, inverse, upstream, pre_self, feat_t, raw, *same[1:], *other[1:])
     embedded, base, wkeep, wsend, gt = call(
-        functools.partial(forward_kernel, n, group),
+        functools.partial(forward_kernel, group, squares - 1),
         "forward_layer",
         (
             result((nodes, hidden), BF16, False), wide, weight, weight,
@@ -353,42 +399,41 @@
         ),
         operands,
         [SMEM] + [VMEM] * (len(operands) - 1),
-        cost_us=5,
+        cost_us=4,
         scratch_shapes=[
-            pltpu.VMEM((n * block_local, BLOCK, feat_in), BF16),
-            pltpu.VMEM((block_local + 1, BLOCK, feat_in), F32),
+            pltpu.VMEM(far_squares, BF16),
+            pltpu.VMEM(raw_shape, F32),
             pltpu.VMEM((2, feat_in, hidden), F32),
         ],
     )
 
-    acc_shape = result((n * block_local + 1, feat_in, BLOCK), F32)
-    acc = call(
-        functools.partial(backward_kernel, group), "backward_tiles", acc_shape,
-        (index, tiles_near, gt), [SMEM, VMEM, VMEM], cost_us=3.5,
-    )
+    w0, w1, w2, w3 = call(
+        cut_kernel, "cut_weights", (chunk,) * 4, (index, wkeep, swap(wsend, n, 1)),
+        [SMEM, VMEM, VMEM])
+
     send_shape = result((4, nodes, feat_in), F32)
-    send = [None] * squares
-    for s in range(squares - 1, -1, -1):
-        if s == squares - 1:
-            send[s], w0, w1, w2, w3 = call(
-                functools.partial(send_weights_kernel, s, block_local), "send_weights",
-                (send_shape,) + (chunk,) * 4, (index, acc, wkeep, swap(wsend, n, 1)),
-                [SMEM] + [VMEM] * 3)
-        else:
-            send[s] = call(
-                functools.partial(send_kernel, s, block_local), "send", send_shape, (acc,))
-
+    sums, got = [], [None] * squares
+    for section, shape in ((1, far_squares), (0, near_square)):
+        acc = call(
+            functools.partial(backward_kernel, section, group), "backward_tiles",
+            result((shape[0] + 1,) + shape[1:], F32), (index, tiles_near, gt), [SMEM, VMEM, VMEM],
+            cost_us=1.5)
+        sums.insert(0, acc)
+        for s in range(squares - 1, 0, -1) if section else (0,):
+            operands = (acc,) if section else (acc, w0)
+            got[s] = swap(
+                call(functools.partial(send_kernel, s - section), "send", send_shape, operands), n, 1)
     extra = result((nodes + 2 * chunk.shape[0] * (hidden // feat_in), feat_in), BF16)
     terms = [None] * squares
     for s in range(squares - 1, -1, -1):
-        operands = (acc, swap(send[s], n, 1))
+        operands = (sums[min(s, 1)], got[s])
         if s == squares - 1:
             own, *pieces = call(
-                functools.partial(pair_weights_kernel, s), "pair_sum_weights", (wide, extra, extra, extra),
+                functools.partial(pair_weights_kernel, max(s - 1, 0)), "pair_sum_weights", (wide, extra, extra, extra),
                 operands + (w1, w2, w3))
         else:
             own, *pieces = call(
-                functools.partial(pair_kernel, s), "pair_sum", (wide, piece, piece, piece), operands)
+                functools.partial(pair_kernel, max(s - 1, 0)), "pair_sum", (wide, piece, piece, piece), operands)
         terms[s] = [own, *[swap(x, n, 2 * q + 2) for q, x in enumerate(pieces)]]
     near_total = call(near_kernel, "near_sum", wide, (base, *terms[0]), cost_us=NEAR_COST)
     terms[0] = [near_total]
@@ -401,21 +446,16 @@
                     cost_us=SQUARE_COST)
             else:
                 total = call(add_kernel, "square_sum", piece, terms[s], cost_us=SQUARE_COST)
-            if s == distance:
-                total = swap(total, n, 8 * distance)
-                terms[0].append(call(add_kernel, "far_sum", wide, (total,), cost_us=FAR_COST))
-            else:
-                terms[s - distance].append(swap(total, n, 8 * distance))
+            terms[s - distance].append(swap(total, n, 8 * distance))
         distance *= 2
     bit = 8
     while bit < n:
         wsum = call(add_two_kernel, "weight_sum", chunk, (wsum, swap(wsum, n, bit)))
         bit *= 2
     rows = chunk.shape[0]
+    two = call(functools.partial(pack_kernel, (0, 1)), "pack_weights", result((2, rows, hidden), F32), (wsum, swap(wsum, n, 2)))
     mine = call(
-        functools.partial(pack_kernel, (0, 1, 2, 3)), "pack_weights",
-        result((4, rows, hidden), F32),
-        (wsum, *[swap(wsum, n, offset) for offset in (2, 4, 6)], near_total))
+        functools.partial(pack_kernel, (0, 1)), "pack_weights", result((2, 2, rows, hidden), F32), (two, swap(two, n, 4), near_total))
     grad_input = call(
         main_kernel, "grad_input_sum", result((nodes, feat_in), BF16, False), terms[0],
         cost_us=MAIN_COST)

time: 62.9 us -> 59.4 us (0.944)
  starting transfers between devices: 27.8 us -> 24.1 us
    ppermute x24 -> x23, starting transfers between devices: 27.8 us -> 24.1 us  [swap(): return lax.ppermute(x, 'row', [(i, i ^ offset) for i in range(n)])]
    ppermute x24 -> x23, waiting for transfers between devices: 20.6 us -> 20.4 us  [swap(): return lax.ppermute(x, 'row', [(i, i ^ offset) for i in range(n)])]
    pallas_call x15 -> x18, Pallas kernels: 9.54 us -> 9.54 us  [call(): pl.pallas_call(kernel, out_shape=out_shape, in_specs=specs, out_specs=out...]
  transfers between devices with their start and end apart: 24 -> 23, of which waited for: 14 -> 13; matrix products, arithmetic and copies ran while one was open for 0% -> 0% of each run, Pallas kernels for 11% -> 14%
where the time goes in v10:
time: 59.4 us; the launch traced here: 59.3 us
  starting transfers between devices  24.1 us (41%)
  waiting for transfers between devices  20.4 us (34%)
  Pallas kernels  12.6 us (21%)
  local copies, waits for them, and re-layouts  1.31 us (2%)
  between operations  0.81 us (1%)
    ppermute x23, starting transfers between devices, swap(): return lax.ppermute(x, 'row', [(i, i ^ offset) for i in range(n)])  24.1 us
    ppermute x23, waiting for transfers between devices, swap(): return lax.ppermute(x, 'row', [(i, i ^ offset) for i in range(n)])  20.4 us
    pallas_call x18, Pallas kernels, call(): pl.pallas_call(kernel, out_shape=out_shape, in_specs=specs, out_specs=out...  9.54 us
    pallas_call x1, Pallas kernels, body(): pl.pallas_call(functools.partial(stage_kernel, (8 * block_local, (n - 8)...  3.09 us
    unnamed x4, local copies, waits for them, and re-layouts  1.31 us
  transfers between devices with their start and end apart: 23, of which 13 were waited for; matrix products, arithmetic and copies ran while one was open for 0% of the time, Pallas kernels for 14%

profile of v10, /device:TPU:0, one launch (start us, length us, event | category | flops | bytes accessed | tf_op | source)
XLA Modules:
  0.0 59.3 jit_solution(47091798339959389)
XLA Ops:
  0.6 4.1 %collective-permute-start.4 = (bf16[512,128]{1,0:T(8,128)(2,1)}, bf16[512,128]{1,0:T(8,128)(2,1)S(1)}, u32[]{:S(2)}, u32[]{:S(2)}) collective-permute-start(bf16[512,128]{1,0:T(8,128)(2,1)} %feat_ref.1), channel_id=1, source_target_pairs={{0,8},{1,9},{2,10},{3,11},{4,12},{5,13},{6,14},{7,15},{8,0},{9,1},... | collective-permute-start | bytes 393224 | tf_op jit(solution)/shard_map/ppermute | solution.py:21
  4.7 1.5 %collective-permute-start = (bf16[512,128]{1,0:T(8,128)(2,1)}, bf16[512,128]{1,0:T(8,128)(2,1)S(1)}, u32[]{:S(2)}, u32[]{:S(2)}) collective-permute-start(bf16[512,128]{1,0:T(8,128)(2,1)} %feat_ref.1), channel_id=1, source_target_pairs={{0,2},{1,3},{2,0},{3,1},{4,6},{5,7},{6,4},{7,5},{8,10},{9,11},{10,... | collective-permute-start | bytes 393224 | tf_op jit(solution)/shard_map/ppermute | solution.py:21
  6.3 1.5 %collective-permute-start.1 = (bf16[512,128]{1,0:T(8,128)(2,1)}, bf16[512,128]{1,0:T(8,128)(2,1)S(1)}, u32[]{:S(2)}, u32[]{:S(2)}) collective-permute-start(bf16[512,128]{1,0:T(8,128)(2,1)} %feat_ref.1), channel_id=1, source_target_pairs={{0,6},{1,7},{2,4},{3,5},{4,2},{5,3},{6,0},{7,1},{8,14},{9,15},{10,... | collective-permute-start | bytes 393224 | tf_op jit(solution)/shard_map/ppermute | solution.py:21
  7.8 0.4 collective-permute-start.2
  8.2 3.1 %collective-permute-done.4.refs_0_ = bf16[512,128]{1,0:T(8,128)(2,1)S(1)} collective-permute-done((bf16[512,128]{1,0:T(8,128)(2,1)}, bf16[512,128]{1,0:T(8,128)(2,1)S(1)}, u32[]{:S(2)}, u32[]{:S(2)}) %collective-permute-start.4) | collective-permute-done | bytes 131104 | tf_op jit(solution)/shard_map/ppermute | solution.py:21
  11.4 1.7 %collective-permute-start.5 = (bf16[512,128]{1,0:T(8,128)(2,1)S(1)}, bf16[512,128]{1,0:T(8,128)(2,1)S(1)}, u32[]{:S(2)}, u32[]{:S(2)}) collective-permute-start(bf16[512,128]{1,0:T(8,128)(2,1)S(1)} %collective-permute-done.4.refs_0_), channel_id=1, source_target_pairs={{0,6},{1,7},{2,4},{3,5},{4,2},{5,3},{6,0},{7,1},{8,14},{9,15},{10,... | collective-permute-start | bytes 393224 | tf_op jit(solution)/shard_map/ppermute | solution.py:21
  13.1 0.5 collective-permute-start.6
  13.6 1.3 %collective-permute-start.7 = (bf16[512,128]{1,0:T(8,128)(2,1)S(1)}, bf16[512,128]{1,0:T(8,128)(2,1)S(1)}, u32[]{:S(2)}, u32[]{:S(2)}) collective-permute-start(bf16[512,128]{1,0:T(8,128)(2,1)S(1)} %collective-permute-done.4.refs_0_), channel_id=1, source_target_pairs={{0,4},{1,5},{2,6},{3,7},{4,0},{5,1},{6,2},{7,3},{8,12},{9,13},{10,... | collective-permute-start | bytes 393224 | tf_op jit(solution)/shard_map/ppermute | solution.py:21
  14.9 0.7 %copy-done = s32[60]{0:T(128)S(1)} copy-done((s32[60]{0:T(128)S(1)}, s32[60]{0:T(128)}, u32[]{:S(2)}) %copy-start) | copy-done | bytes 264
  15.5 0.7 %copy-done.1 = s32[60]{0:T(128)S(1)} copy-done((s32[60]{0:T(128)S(1)}, s32[60]{0:T(128)}, u32[]{:S(2)}) %copy-start.1) | copy-done | bytes 264
  16.2 3.1 %stage_arguments.1 = (bf16[60,128,128]{2,1,0:T(8,128)(2,1)S(1)}, bf16[128,256]{1,0:T(8,128)(2,1)S(1)}, bf16[128,256]{1,0:T(8,128)(2,1)S(1)}, f32[4,128,128]{2,1,...) custom-call(s32[1]{0:T(128)} %bitcast.me_ref, ...), custom_call_target="tpu_custom_call" | custom-call | flops 3300000000 | bytes 10800000 | tf_op jit(solution)/shard_map/stage_arguments/pallas_call | solution.py:361
  19.3 0.1 collective-permute-start.3
  19.4 1.0 %collective-permute-done.5.refs_1_ = bf16[512,128]{1,0:T(8,128)(2,1)S(1)} collective-permute-done((bf16[512,128]{1,0:T(8,128)(2,1)S(1)}, bf16[512,128]{1,0:T(8,128)(2,1)S(1)}, u32[]{:S(2)}, u32[]{:S(2)}) %collective-permute-start.5) | collective-permute-done | bytes 131104 | tf_op jit(solution)/shard_map/ppermute | solution.py:21
  20.4 0.6 %collective-permute-done.6.refs_2_ = bf16[512,128]{1,0:T(8,128)(2,1)S(1)} collective-permute-done((bf16[512,128]{1,0:T(8,128)(2,1)S(1)}, bf16[512,128]{1,0:T(8,128)(2,1)S(1)}, u32[]{:S(2)}, u32[]{:S(2)}) %collective-permute-start.6) | collective-permute-done | bytes 131104 | tf_op jit(solution)/shard_map/ppermute | solution.py:21
  21.0 0.1 collective-permute-done.7.refs_3_
  21.2 0.1 collective-permute-start.8
  21.3 1.1 %forward_near.1.near_ref = f32[5,128,128]{2,1,0:T(8,128)S(1)} custom-call(s32[363]{0:T(512)S(4)} %get-tuple-element.34.index_ref, bf16[60,128,128]{2,1,0:T(8,128)(2,1)S(1)} %get-tuple-element.35.tiles_ref, bf16[4,512,128]{2,1,0:T(8,128)(2,1)S(1)} %pack_square.2.same_ref, bf16[4,512,128]{2,1,0:T(8,128)(2,1)S(1)} %collective-permute-done.3.other_ref), custom_call_target="tpu_custom_call" | custom-call | flops 110000000 | bytes 360000 | tf_op jit(solution)/shard_map/forward_near/pallas_call | solution.py:338
  22.4 0.7 %collective-permute-done.8.refs_1_ = bf16[4,512,128]{2,1,0:T(8,128)(2,1)S(1)} collective-permute-done((bf16[4,512,128]{2,1,0:T(8,128)(2,1)S(1)}, bf16[4,512,128]{2,1,0:T(8,128)(2,1)S(1)}, u32[]{:S(2)}, u32[]{:S(2)}) %collective-permute-start.8) | collective-permute-done | bytes 524320 | tf_op jit(solution)/shard_map/ppermute | solution.py:21
  23.2 3.4 %forward_layer.1 = (bf16[512,256]{1,0:T(8,128)(2,1)}, f32[512,128]{1,0:T(8,128)S(1)}, f32[128,256]{1,0:T(8,128)S(1)}, f32[128,256]{1,0:T(8,128)S(1)}, bf16[4,256,128]{2,1,0:T(8,128)(2,1)S(1)}) custom-call(s32[363]{0:T(512)S(4)} %get-tuple-element.34.index_ref, bf16[60,128,128]{2,1,0:T(8,128)(2,1)S(1)} %get-tuple-element.35.tiles_ref, ...), custom_call_target="tpu_custom_call" | custom-call | flops 4400000000 | bytes 14400000 | tf_op jit(solution)/shard_map/forward_layer/pallas_call | solution.py:338
  26.5 1.4 %backward_tiles.3.acc_ref = f32[33,128,128]{2,1,0:T(8,128)S(1)} custom-call(s32[363]{0:T(512)S(4)} %get-tuple-element.34.index_ref, bf16[60,128,128]{2,1,0:T(8,128)(2,1)S(1)} %get-tuple-element.35.tiles_ref, bf16[4,256,128]{2,1,0:T(8,128)(2,1)S(1)} %get-tuple-element.45.gt_ref), custom_call_target="tpu_custom_call" | custom-call | flops 1650000000 | bytes 5400000 | tf_op jit(solution)/shard_map/backward_tiles/pallas_call | solution.py:338
  28.0 0.1 send.3
  28.1 0.1 collective-permute-start.14
  28.1 1.4 %backward_tiles.2.acc_ref = f32[33,128,128]{2,1,0:T(8,128)S(1)} custom-call(s32[363]{0:T(512)S(4)} %get-tuple-element.34.index_ref, bf16[60,128,128]{2,1,0:T(8,128)(2,1)S(1)} %get-tuple-element.35.tiles_ref, bf16[4,256,128]{2,1,0:T(8,128)(2,1)S(1)} %get-tuple-element.45.gt_ref), custom_call_target="tpu_custom_call" | custom-call | flops 1650000000 | bytes 5400000 | tf_op jit(solution)/shard_map/backward_tiles/pallas_call | solution.py:338
  29.6 0.1 send.2
  29.7 0.3 collective-permute-start.10
  30.0 0.8 %collective-permute-done.14.got_ref = f32[4,512,128]{2,1,0:T(8,128)S(1)} collective-permute-done((f32[4,512,128]{2,1,0:T(8,128)S(1)}, f32[4,512,128]{2,1,0:T(8,128)S(1)}, u32[]{:S(2)}, u32[]{:S(2)}) %collective-permute-start.14) | collective-permute-done | bytes 1048608 | tf_op jit(solution)/shard_map/ppermute | solution.py:21
  30.8 0.1 pair_sum_weights.1
  30.9 1.6 %collective-permute-start.15 = (bf16[640,128]{1,0:T(8,128)(2,1)S(1)}, bf16[640,128]{1,0:T(8,128)(2,1)S(1)}, u32[]{:S(2)}, u32[]{:S(2)}) collective-permute-start(bf16[640,128]{1,0:T(8,128)(2,1)S(1)} %get-tuple-element.57), channel_id=1, source_target_pairs={{0,2},{1,3},{2,0},{3,1},{4,6},{5,7},{6,4},{7,5},{8,10},{9,11},{10,... | collective-permute-start | bytes 491528 | tf_op jit(solution)/shard_map/ppermute | solution.py:21
  32.5 1.9 %collective-permute-start.17 = (bf16[640,128]{1,0:T(8,128)(2,1)S(1)}, bf16[640,128]{1,0:T(8,128)(2,1)S(1)}, u32[]{:S(2)}, u32[]{:S(2)}) collective-permute-start(bf16[640,128]{1,0:T(8,128)(2,1)S(1)} %get-tuple-element.59), channel_id=1, source_target_pairs={{0,6},{1,7},{2,4},{3,5},{4,2},{5,3},{6,0},{7,1},{8,14},{9,15},{10,... | collective-permute-start | bytes 491528 | tf_op jit(solution)/shard_map/ppermute | solution.py:21
  34.5 0.1 pair_sum.1
  34.6 1.6 %collective-permute-start.11 = (bf16[512,128]{1,0:T(8,128)(2,1)S(1)}, bf16[512,128]{1,0:T(8,128)(2,1)S(1)}, u32[]{:S(2)}, u32[]{:S(2)}) collective-permute-start(bf16[512,128]{1,0:T(8,128)(2,1)S(1)} %get-tuple-element.50), channel_id=1, source_target_pairs={{0,2},{1,3},{2,0},{3,1},{4,6},{5,7},{6,4},{7,5},{8,10},{9,11},{10,... | collective-permute-start | bytes 393224 | tf_op jit(solution)/shard_map/ppermute | solution.py:21
  36.2 2.1 %collective-permute-done.15.refs_0_ = bf16[640,128]{1,0:T(8,128)(2,1)S(1)} collective-permute-done((bf16[640,128]{1,0:T(8,128)(2,1)S(1)}, bf16[640,128]{1,0:T(8,128)(2,1)S(1)}, u32[]{:S(2)}, u32[]{:S(2)}) %collective-permute-start.15) | collective-permute-done | bytes 163872 | tf_op jit(solution)/shard_map/ppermute | solution.py:21
  38.3 0.5 collective-permute-start.13
  38.8 0.8 %collective-permute-done.16.refs_1_ = bf16[640,128]{1,0:T(8,128)(2,1)S(1)} collective-permute-done((bf16[640,128]{1,0:T(8,128)(2,1)S(1)}, bf16[640,128]{1,0:T(8,128)(2,1)S(1)}, u32[]{:S(2)}, u32[]{:S(2)}) %collective-permute-start.16) | collective-permute-done | bytes 163872 | tf_op jit(solution)/shard_map/ppermute | solution.py:21
  39.6 3.5 %collective-permute-done.17.refs_2_ = bf16[640,128]{1,0:T(8,128)(2,1)S(1)} collective-permute-done((bf16[640,128]{1,0:T(8,128)(2,1)S(1)}, bf16[640,128]{1,0:T(8,128)(2,1)S(1)}, u32[]{:S(2)}, u32[]{:S(2)}) %collective-permute-start.17) | collective-permute-done | bytes 163872 | tf_op jit(solution)/shard_map/ppermute | solution.py:21
  43.1 0.1 square_sum_weights.1
  43.1 1.6 %collective-permute-start.19 = (f32[32,256]{1,0:T(8,128)S(1)}, f32[32,256]{1,0:T(8,128)S(1)}, u32[]{:S(2)}, u32[]{:S(2)}) collective-permute-start(f32[32,256]{1,0:T(8,128)S(1)} %get-tuple-element.61.own_ref), channel_id=1, source_target_pairs={{0,8},{1,9},{2,10},{3,11},{4,12},{5,13},{6,14},{7,15},{8,0},{9,1},... | collective-permute-start | bytes 98312 | tf_op jit(solution)/shard_map/ppermute | solution.py:21
  44.8 3.3 %collective-permute-done.19.got_ref = f32[32,256]{1,0:T(8,128)S(1)} collective-permute-done((f32[32,256]{1,0:T(8,128)S(1)}, f32[32,256]{1,0:T(8,128)S(1)}, u32[]{:S(2)}, u32[]{:S(2)}) %collective-permute-start.19) | collective-permute-done | bytes 32800 | tf_op jit(solution)/shard_map/ppermute | solution.py:21
  48.1 1.5 %collective-permute-start.20 = (f32[32,256]{1,0:T(8,128)S(1)}, f32[32,256]{1,0:T(8,128)S(1)}, u32[]{:S(2)}, u32[]{:S(2)}) collective-permute-start(f32[32,256]{1,0:T(8,128)S(1)} %weight_sum.1.refs_0_), channel_id=1, source_target_pairs={{0,2},{1,3},{2,0},{3,1},{4,6},{5,7},{6,4},{7,5},{8,10},{9,11},{10,... | collective-permute-start | bytes 98312 | tf_op jit(solution)/shard_map/ppermute | solution.py:21
  49.6 1.5 %collective-permute-start.18 = (bf16[512,128]{1,0:T(8,128)(2,1)S(1)}, bf16[512,128]{1,0:T(8,128)(2,1)S(1)}, u32[]{:S(2)}, u32[]{:S(2)}) collective-permute-start(bf16[512,128]{1,0:T(8,128)(2,1)S(1)} %get-tuple-element.60), channel_id=1, source_target_pairs={{0,8},{1,9},{2,10},{3,11},{4,12},{5,13},{6,14},{7,15},{8,0},{9,1},... | collective-permute-start | bytes 393224 | tf_op jit(solution)/shard_map/ppermute | solution.py:21
  51.1 1.0 %collective-permute-done.20.refs_1_ = f32[32,256]{1,0:T(8,128)S(1)} collective-permute-done((f32[32,256]{1,0:T(8,128)S(1)}, f32[32,256]{1,0:T(8,128)S(1)}, u32[]{:S(2)}, u32[]{:S(2)}) %collective-permute-start.20) | collective-permute-done | bytes 32800 | tf_op jit(solution)/shard_map/ppermute | solution.py:21
  52.0 2.2 %collective-permute-start.21 = (f32[2,32,256]{2,1,0:T(8,128)S(1)}, f32[2,32,256]{2,1,0:T(8,128)S(1)}, u32[]{:S(2)}, u32[]{:S(2)}) collective-permute-start(f32[2,32,256]{2,1,0:T(8,128)S(1)} %pack_weights.2.refs_0_), channel_id=1, source_target_pairs={{0,4},{1,5},{2,6},{3,7},{4,0},{5,1},{6,2},{7,3},{8,12},{9,13},{10,... | collective-permute-start | bytes 196616 | tf_op jit(solution)/shard_map/ppermute | solution.py:21
  54.2 0.1 near_sum.1.near_ref.refs_2_
  54.4 2.8 %collective-permute-done.21.refs_1_ = f32[2,32,256]{2,1,0:T(8,128)S(1)} collective-permute-done((f32[2,32,256]{2,1,0:T(8,128)S(1)}, f32[2,32,256]{2,1,0:T(8,128)S(1)}, u32[]{:S(2)}, u32[]{:S(2)}) %collective-permute-start.21) | collective-permute-done | bytes 65568 | tf_op jit(solution)/shard_map/ppermute | solution.py:21
  57.2 0.1 collective-permute-start.22
  57.3 0.8 %grad_input_sum.1 = bf16[512,128]{1,0:T(8,128)(2,1)} custom-call(f32[512,128]{1,0:T(8,128)S(1)} %near_sum.1.near_ref.refs_2_, bf16[512,128]{1,0:T(8,128)(2,1)S(1)} %collective-permute-done.18.refs_0_), custom_call_target="tpu_custom_call" | custom-call | flops 11000000512 | bytes 36000000 | tf_op jit(solution)/shard_map/grad_input_sum/pallas_call | solution.py:338
  58.0 0.6 collective-permute-done.22.other_ref
  58.6 0.7 %write_weights.1 = (f32[128,256]{1,0:T(8,128)}, f32[128,256]{1,0:T(8,128)}) custom-call(s32[363]{0:T(512)S(4)} %get-tuple-element.34.index_ref, f32[2,2,32,256]{3,2,1,0:T(8,128)S(1)} %pack_weights.3.weight_ref, f32[2,2,32,256]{3,2,1,0:T(8,128)S(1)} %collective-permute-done.22.other_ref), custom_call_target="tpu_custom_call" | custom-call | flops 220000000 | bytes 720000 | tf_op jit(solution)/shard_map/write_weights/pallas_call | solution.py:338
  (21 shorter events, 0.2 us)
Async XLA Ops:
  0.6 10.7 %collective-permute-start.4 = (bf16[512,128]{1,0:T(8,128)(2,1)}, bf16[512,128]{1,0:T(8,128)(2,1)S(1)}, u32[]{:S(2)}, u32[]{:S(2)}) collective-permute-start(bf16[512,128]{1,0:T(8,128)(2,1)} %feat_ref.1), channel_id=1, source_target_pairs={{0,8},{1,9},{2,10},{3,11},{4,12},{5,13},{6,14},{7,15},{8,0},{9,1},... | collective-permute-start | bytes 393224 | tf_op jit(solution)/shard_map/ppermute | solution.py:21
  4.7 8.9 %collective-permute-start = (bf16[512,128]{1,0:T(8,128)(2,1)}, bf16[512,128]{1,0:T(8,128)(2,1)S(1)}, u32[]{:S(2)}, u32[]{:S(2)}) collective-permute-start(bf16[512,128]{1,0:T(8,128)(2,1)} %feat_ref.1), channel_id=1, source_target_pairs={{0,2},{1,3},{2,0},{3,1},{4,6},{5,7},{6,4},{7,5},{8,10},{9,11},{10,... | collective-permute-start | bytes 393224 | tf_op jit(solution)/shard_map/ppermute | solution.py:21
  6.3 13.0 %collective-permute-start.1 = (bf16[512,128]{1,0:T(8,128)(2,1)}, bf16[512,128]{1,0:T(8,128)(2,1)S(1)}, u32[]{:S(2)}, u32[]{:S(2)}) collective-permute-start(bf16[512,128]{1,0:T(8,128)(2,1)} %feat_ref.1), channel_id=1, source_target_pairs={{0,6},{1,7},{2,4},{3,5},{4,2},{5,3},{6,0},{7,1},{8,14},{9,15},{10,... | collective-permute-start | bytes 393224 | tf_op jit(solution)/shard_map/ppermute | solution.py:21
  7.8 11.5 %collective-permute-start.2 = (bf16[512,128]{1,0:T(8,128)(2,1)}, bf16[512,128]{1,0:T(8,128)(2,1)S(1)}, u32[]{:S(2)}, u32[]{:S(2)}) collective-permute-start(bf16[512,128]{1,0:T(8,128)(2,1)} %feat_ref.1), channel_id=1, source_target_pairs={{0,4},{1,5},{2,6},{3,7},{4,0},{5,1},{6,2},{7,3},{8,12},{9,13},{10,... | collective-permute-start | bytes 393224 | tf_op jit(solution)/shard_map/ppermute | solution.py:21
  11.4 9.1 %collective-permute-start.5 = (bf16[512,128]{1,0:T(8,128)(2,1)S(1)}, bf16[512,128]{1,0:T(8,128)(2,1)S(1)}, u32[]{:S(2)}, u32[]{:S(2)}) collective-permute-start(bf16[512,128]{1,0:T(8,128)(2,1)S(1)} %collective-permute-done.4.refs_0_), channel_id=1, source_target_pairs={{0,6},{1,7},{2,4},{3,5},{4,2},{5,3},{6,0},{7,1},{8,14},{9,15},{10,... | collective-permute-start | bytes 393224 | tf_op jit(solution)/shard_map/ppermute | solution.py:21
  13.1 7.9 %collective-permute-start.6 = (bf16[512,128]{1,0:T(8,128)(2,1)S(1)}, bf16[512,128]{1,0:T(8,128)(2,1)S(1)}, u32[]{:S(2)}, u32[]{:S(2)}) collective-permute-start(bf16[512,128]{1,0:T(8,128)(2,1)S(1)} %collective-permute-done.4.refs_0_), channel_id=1, source_target_pairs={{0,2},{1,3},{2,0},{3,1},{4,6},{5,7},{6,4},{7,5},{8,10},{9,11},{10,... | collective-permute-start | bytes 393224 | tf_op jit(solution)/shard_map/ppermute | solution.py:21
  13.6 7.6 %collective-permute-start.7 = (bf16[512,128]{1,0:T(8,128)(2,1)S(1)}, bf16[512,128]{1,0:T(8,128)(2,1)S(1)}, u32[]{:S(2)}, u32[]{:S(2)}) collective-permute-start(bf16[512,128]{1,0:T(8,128)(2,1)S(1)} %collective-permute-done.4.refs_0_), channel_id=1, source_target_pairs={{0,4},{1,5},{2,6},{3,7},{4,0},{5,1},{6,2},{7,3},{8,12},{9,13},{10,... | collective-permute-start | bytes 393224 | tf_op jit(solution)/shard_map/ppermute | solution.py:21
  14.8 0.7 %copy-start = (s32[60]{0:T(128)S(1)}, s32[60]{0:T(128)}, u32[]{:S(2)}) copy-start(s32[60]{0:T(128)} %trow_ref.1) | copy-start | bytes 724
  15.5 0.7 %copy-start.1 = (s32[60]{0:T(128)S(1)}, s32[60]{0:T(128)}, u32[]{:S(2)}) copy-start(s32[60]{0:T(128)} %tcol_ref.1) | copy-start | bytes 724
  19.3 2.0 %collective-permute-start.3 = (bf16[4,512,128]{2,1,0:T(8,128)(2,1)S(1)}, bf16[4,512,128]{2,1,0:T(8,128)(2,1)S(1)}, u32[]{:S(2)}, u32[]{:S(2)}) collective-permute-start(bf16[4,512,128]{2,1,0:T(8,128)(2,1)S(1)} %pack_square.2.same_ref), channel_id=1, source_target_pairs={{0,1},{1,0},{2,3},{3,2},{4,5},{5,4},{6,7},{7,6},{8,9},{9,8},{10,11... | collective-permute-start | bytes 1572872 | tf_op jit(solution)/shard_map/ppermute | solution.py:21
  21.2 2.0 %collective-permute-start.8 = (bf16[4,512,128]{2,1,0:T(8,128)(2,1)S(1)}, bf16[4,512,128]{2,1,0:T(8,128)(2,1)S(1)}, u32[]{:S(2)}, u32[]{:S(2)}) collective-permute-start(bf16[4,512,128]{2,1,0:T(8,128)(2,1)S(1)} %pack_square.3.refs_0_), channel_id=1, source_target_pairs={{0,1},{1,0},{2,3},{3,2},{4,5},{5,4},{6,7},{7,6},{8,9},{9,8},{10,11... | collective-permute-start | bytes 1572872 | tf_op jit(solution)/shard_map/ppermute | solution.py:21
  26.5 3.0 %collective-permute-start.9 = (f32[128,256]{1,0:T(8,128)S(1)}, f32[128,256]{1,0:T(8,128)S(1)}, u32[]{:S(2)}, u32[]{:S(2)}) collective-permute-start(f32[128,256]{1,0:T(8,128)S(1)} %get-tuple-element.47), channel_id=1, source_target_pairs={{0,1},{1,0},{2,3},{3,2},{4,5},{5,4},{6,7},{7,6},{8,9},{9,8},{10,11... | collective-permute-start | bytes 393224 | tf_op jit(solution)/shard_map/ppermute | solution.py:21
  28.1 2.7 %collective-permute-start.14 = (f32[4,512,128]{2,1,0:T(8,128)S(1)}, f32[4,512,128]{2,1,0:T(8,128)S(1)}, u32[]{:S(2)}, u32[]{:S(2)}) collective-permute-start(f32[4,512,128]{2,1,0:T(8,128)S(1)} %send.3), channel_id=1, source_target_pairs={{0,1},{1,0},{2,3},{3,2},{4,5},{5,4},{6,7},{7,6},{8,9},{9,8},{10,11... | collective-permute-start | bytes 3145736 | tf_op jit(solution)/shard_map/ppermute | solution.py:21
  29.7 4.7 %collective-permute-start.10 = (f32[4,512,128]{2,1,0:T(8,128)S(1)}, f32[4,512,128]{2,1,0:T(8,128)S(1)}, u32[]{:S(2)}, u32[]{:S(2)}) collective-permute-start(f32[4,512,128]{2,1,0:T(8,128)S(1)} %send.2), channel_id=1, source_target_pairs={{0,1},{1,0},{2,3},{3,2},{4,5},{5,4},{6,7},{7,6},{8,9},{9,8},{10,11... | collective-permute-start | bytes 3145736 | tf_op jit(solution)/shard_map/ppermute | solution.py:21
  30.9 7.4 %collective-permute-start.15 = (bf16[640,128]{1,0:T(8,128)(2,1)S(1)}, bf16[640,128]{1,0:T(8,128)(2,1)S(1)}, u32[]{:S(2)}, u32[]{:S(2)}) collective-permute-start(bf16[640,128]{1,0:T(8,128)(2,1)S(1)} %get-tuple-element.57), channel_id=1, source_target_pairs={{0,2},{1,3},{2,0},{3,1},{4,6},{5,7},{6,4},{7,5},{8,10},{9,11},{10,... | collective-permute-start | bytes 491528 | tf_op jit(solution)/shard_map/ppermute | solution.py:21
  32.5 7.1 %collective-permute-start.16 = (bf16[640,128]{1,0:T(8,128)(2,1)S(1)}, bf16[640,128]{1,0:T(8,128)(2,1)S(1)}, u32[]{:S(2)}, u32[]{:S(2)}) collective-permute-start(bf16[640,128]{1,0:T(8,128)(2,1)S(1)} %get-tuple-element.58), channel_id=1, source_target_pairs={{0,4},{1,5},{2,6},{3,7},{4,0},{5,1},{6,2},{7,3},{8,12},{9,13},{10,... | collective-permute-start | bytes 491528 | tf_op jit(solution)/shard_map/ppermute | solution.py:21
  32.5 10.5 %collective-permute-start.17 = (bf16[640,128]{1,0:T(8,128)(2,1)S(1)}, bf16[640,128]{1,0:T(8,128)(2,1)S(1)}, u32[]{:S(2)}, u32[]{:S(2)}) collective-permute-start(bf16[640,128]{1,0:T(8,128)(2,1)S(1)} %get-tuple-element.59), channel_id=1, source_target_pairs={{0,6},{1,7},{2,4},{3,5},{4,2},{5,3},{6,0},{7,1},{8,14},{9,15},{10,... | collective-permute-start | bytes 491528 | tf_op jit(solution)/shard_map/ppermute | solution.py:21
  34.6 19.7 %collective-permute-start.11 = (bf16[512,128]{1,0:T(8,128)(2,1)S(1)}, bf16[512,128]{1,0:T(8,128)(2,1)S(1)}, u32[]{:S(2)}, u32[]{:S(2)}) collective-permute-start(bf16[512,128]{1,0:T(8,128)(2,1)S(1)} %get-tuple-element.50), channel_id=1, source_target_pairs={{0,2},{1,3},{2,0},{3,1},{4,6},{5,7},{6,4},{7,5},{8,10},{9,11},{10,... | collective-permute-start | bytes 393224 | tf_op jit(solution)/shard_map/ppermute | solution.py:21
  36.2 18.0 %collective-permute-start.12 = (bf16[512,128]{1,0:T(8,128)(2,1)S(1)}, bf16[512,128]{1,0:T(8,128)(2,1)S(1)}, u32[]{:S(2)}, u32[]{:S(2)}) collective-permute-start(bf16[512,128]{1,0:T(8,128)(2,1)S(1)} %get-tuple-element.51), channel_id=1, source_target_pairs={{0,4},{1,5},{2,6},{3,7},{4,0},{5,1},{6,2},{7,3},{8,12},{9,13},{10,... | collective-permute-start | bytes 393224 | tf_op jit(solution)/shard_map/ppermute | solution.py:21
  38.3 15.9 %collective-permute-start.13 = (bf16[512,128]{1,0:T(8,128)(2,1)S(1)}, bf16[512,128]{1,0:T(8,128)(2,1)S(1)}, u32[]{:S(2)}, u32[]{:S(2)}) collective-permute-start(bf16[512,128]{1,0:T(8,128)(2,1)S(1)} %get-tuple-element.52), channel_id=1, source_target_pairs={{0,6},{1,7},{2,4},{3,5},{4,2},{5,3},{6,0},{7,1},{8,14},{9,15},{10,... | collective-permute-start | bytes 393224 | tf_op jit(solution)/shard_map/ppermute | solution.py:21
  43.1 5.0 %collective-permute-start.19 = (f32[32,256]{1,0:T(8,128)S(1)}, f32[32,256]{1,0:T(8,128)S(1)}, u32[]{:S(2)}, u32[]{:S(2)}) collective-permute-start(f32[32,256]{1,0:T(8,128)S(1)} %get-tuple-element.61.own_ref), channel_id=1, source_target_pairs={{0,8},{1,9},{2,10},{3,11},{4,12},{5,13},{6,14},{7,15},{8,0},{9,1},... | collective-permute-start | bytes 98312 | tf_op jit(solution)/shard_map/ppermute | solution.py:21
  48.1 3.9 %collective-permute-start.20 = (f32[32,256]{1,0:T(8,128)S(1)}, f32[32,256]{1,0:T(8,128)S(1)}, u32[]{:S(2)}, u32[]{:S(2)}) collective-permute-start(f32[32,256]{1,0:T(8,128)S(1)} %weight_sum.1.refs_0_), channel_id=1, source_target_pairs={{0,2},{1,3},{2,0},{3,1},{4,6},{5,7},{6,4},{7,5},{8,10},{9,11},{10,... | collective-permute-start | bytes 98312 | tf_op jit(solution)/shard_map/ppermute | solution.py:21
  49.6 7.7 %collective-permute-start.18 = (bf16[512,128]{1,0:T(8,128)(2,1)S(1)}, bf16[512,128]{1,0:T(8,128)(2,1)S(1)}, u32[]{:S(2)}, u32[]{:S(2)}) collective-permute-start(bf16[512,128]{1,0:T(8,128)(2,1)S(1)} %get-tuple-element.60), channel_id=1, source_target_pairs={{0,8},{1,9},{2,10},{3,11},{4,12},{5,13},{6,14},{7,15},{8,0},{9,1},... | collective-permute-start | bytes 393224 | tf_op jit(solution)/shard_map/ppermute | solution.py:21
  52.0 5.1 %collective-permute-start.21 = (f32[2,32,256]{2,1,0:T(8,128)S(1)}, f32[2,32,256]{2,1,0:T(8,128)S(1)}, u32[]{:S(2)}, u32[]{:S(2)}) collective-permute-start(f32[2,32,256]{2,1,0:T(8,128)S(1)} %pack_weights.2.refs_0_), channel_id=1, source_target_pairs={{0,4},{1,5},{2,6},{3,7},{4,0},{5,1},{6,2},{7,3},{8,12},{9,13},{10,... | collective-permute-start | bytes 196616 | tf_op jit(solution)/shard_map/ppermute | solution.py:21
  57.2 1.4 %collective-permute-start.22 = (f32[2,2,32,256]{3,2,1,0:T(8,128)S(1)}, f32[2,2,32,256]{3,2,1,0:T(8,128)S(1)}, u32[]{:S(2)}, u32[]{:S(2)}) collective-permute-start(f32[2,2,32,256]{3,2,1,0:T(8,128)S(1)} %pack_weights.3.weight_ref), channel_id=1, source_target_pairs={{0,1},{1,0},{2,3},{3,2},{4,5},{5,4},{6,7},{7,6},{8,9},{9,8},{10,11... | collective-permute-start | bytes 393224 | tf_op jit(solution)/shard_map/ppermute | solution.py:21

commit v11 on v10

--- a/solution.py
+++ b/solution.py
@@ -434,7 +434,7 @@
         else:
             own, *pieces = call(
                 functools.partial(pair_kernel, max(s - 1, 0)), "pair_sum", (wide, piece, piece, piece), operands)
-        terms[s] = [own, *[swap(x, n, 2 * q + 2) for q, x in enumerate(pieces)]]
+        terms[s] = [own, *[swap(pieces[q - 1], n, 2 * q) for q in (3, 1, 2)]]
     near_total = call(near_kernel, "near_sum", wide, (base, *terms[0]), cost_us=NEAR_COST)
     terms[0] = [near_total]
     distance = 1

time: 59.4 us -> 59 us (level)
  Pallas kernels: 12.6 us -> 11.2 us
  waiting for transfers between devices: 20.4 us -> 21.5 us
    pallas_call x18, Pallas kernels: 9.54 us -> 8.12 us  [call(): pl.pallas_call(kernel, out_shape=out_shape, in_specs=specs, out_specs=out...]
    ppermute x23, waiting for transfers between devices: 20.4 us -> 21.5 us  [swap(): return lax.ppermute(x, 'row', [(i, i ^ offset) for i in range(n)])]
  transfers between devices with their start and end apart: 23 -> 23, of which waited for: 13 -> 13; matrix products, arithmetic and copies ran while one was open for 0% -> 0% of each run, Pallas kernels for 14% -> 13%
where the time goes in v11:
time: 59 us; the launch traced here: 58.9 us
  starting transfers between devices  24.1 us (41%)
  waiting for transfers between devices  21.5 us (36%)
  Pallas kernels  11.2 us (19%)
  local copies, waits for them, and re-layouts  1.31 us (2%)
  between operations  0.8 us (1%)
    ppermute x23, starting transfers between devices, swap(): return lax.ppermute(x, 'row', [(i, i ^ offset) for i in range(n)])  24.1 us
    ppermute x23, waiting for transfers between devices, swap(): return lax.ppermute(x, 'row', [(i, i ^ offset) for i in range(n)])  21.5 us
    pallas_call x18, Pallas kernels, call(): pl.pallas_call(kernel, out_shape=out_shape, in_specs=specs, out_specs=out...  8.12 us
    pallas_call x1, Pallas kernels, body(): pl.pallas_call(functools.partial(stage_kernel, (8 * block_local, (n - 8)...  3.09 us
    unnamed x4, local copies, waits for them, and re-layouts  1.31 us
  transfers between devices with their start and end apart: 23, of which 13 were waited for; matrix products, arithmetic and copies ran while one was open for 0% of the time, Pallas kernels for 13%

profile of v11, /device:TPU:0, one launch (start us, length us, event | category | flops | bytes accessed | tf_op | source)
XLA Modules:
  0.0 58.9 jit_solution(6137483515219680531)
XLA Ops:
  0.6 4.1 %collective-permute-start.4 = (bf16[512,128]{1,0:T(8,128)(2,1)}, bf16[512,128]{1,0:T(8,128)(2,1)S(1)}, u32[]{:S(2)}, u32[]{:S(2)}) collective-permute-start(bf16[512,128]{1,0:T(8,128)(2,1)} %feat_ref.1), channel_id=1, source_target_pairs={{0,8},{1,9},{2,10},{3,11},{4,12},{5,13},{6,14},{7,15},{8,0},{9,1},... | collective-permute-start | bytes 393224 | tf_op jit(solution)/shard_map/ppermute | solution.py:21
  4.7 1.5 %collective-permute-start = (bf16[512,128]{1,0:T(8,128)(2,1)}, bf16[512,128]{1,0:T(8,128)(2,1)S(1)}, u32[]{:S(2)}, u32[]{:S(2)}) collective-permute-start(bf16[512,128]{1,0:T(8,128)(2,1)} %feat_ref.1), channel_id=1, source_target_pairs={{0,2},{1,3},{2,0},{3,1},{4,6},{5,7},{6,4},{7,5},{8,10},{9,11},{10,... | collective-permute-start | bytes 393224 | tf_op jit(solution)/shard_map/ppermute | solution.py:21
  6.3 1.5 %collective-permute-start.1 = (bf16[512,128]{1,0:T(8,128)(2,1)}, bf16[512,128]{1,0:T(8,128)(2,1)S(1)}, u32[]{:S(2)}, u32[]{:S(2)}) collective-permute-start(bf16[512,128]{1,0:T(8,128)(2,1)} %feat_ref.1), channel_id=1, source_target_pairs={{0,6},{1,7},{2,4},{3,5},{4,2},{5,3},{6,0},{7,1},{8,14},{9,15},{10,... | collective-permute-start | bytes 393224 | tf_op jit(solution)/shard_map/ppermute | solution.py:21
  7.8 0.4 collective-permute-start.2
  8.2 3.1 %collective-permute-done.4.refs_0_ = bf16[512,128]{1,0:T(8,128)(2,1)S(1)} collective-permute-done((bf16[512,128]{1,0:T(8,128)(2,1)}, bf16[512,128]{1,0:T(8,128)(2,1)S(1)}, u32[]{:S(2)}, u32[]{:S(2)}) %collective-permute-start.4) | collective-permute-done | bytes 131104 | tf_op jit(solution)/shard_map/ppermute | solution.py:21
  11.4 1.7 %collective-permute-start.5 = (bf16[512,128]{1,0:T(8,128)(2,1)S(1)}, bf16[512,128]{1,0:T(8,128)(2,1)S(1)}, u32[]{:S(2)}, u32[]{:S(2)}) collective-permute-start(bf16[512,128]{1,0:T(8,128)(2,1)S(1)} %collective-permute-done.4.refs_0_), channel_id=1, source_target_pairs={{0,6},{1,7},{2,4},{3,5},{4,2},{5,3},{6,0},{7,1},{8,14},{9,15},{10,... | collective-permute-start | bytes 393224 | tf_op jit(solution)/shard_map/ppermute | solution.py:21
  13.1 0.5 collective-permute-start.6
  13.6 1.3 %collective-permute-start.7 = (bf16[512,128]{1,0:T(8,128)(2,1)S(1)}, bf16[512,128]{1,0:T(8,128)(2,1)S(1)}, u32[]{:S(2)}, u32[]{:S(2)}) collective-permute-start(bf16[512,128]{1,0:T(8,128)(2,1)S(1)} %collective-permute-done.4.refs_0_), channel_id=1, source_target_pairs={{0,4},{1,5},{2,6},{3,7},{4,0},{5,1},{6,2},{7,3},{8,12},{9,13},{10,... | collective-permute-start | bytes 393224 | tf_op jit(solution)/shard_map/ppermute | solution.py:21
  14.9 0.7 %copy-done = s32[60]{0:T(128)S(1)} copy-done((s32[60]{0:T(128)S(1)}, s32[60]{0:T(128)}, u32[]{:S(2)}) %copy-start) | copy-done | bytes 264
  15.5 0.7 %copy-done.1 = s32[60]{0:T(128)S(1)} copy-done((s32[60]{0:T(128)S(1)}, s32[60]{0:T(128)}, u32[]{:S(2)}) %copy-start.1) | copy-done | bytes 264
  16.2 3.1 %stage_arguments.1 = (bf16[60,128,128]{2,1,0:T(8,128)(2,1)S(1)}, bf16[128,256]{1,0:T(8,128)(2,1)S(1)}, bf16[128,256]{1,0:T(8,128)(2,1)S(1)}, f32[4,128,128]{2,1,...) custom-call(s32[1]{0:T(128)} %bitcast.me_ref, ...), custom_call_target="tpu_custom_call" | custom-call | flops 3300000000 | bytes 10800000 | tf_op jit(solution)/shard_map/stage_arguments/pallas_call | solution.py:361
  19.3 0.1 collective-permute-start.3
  19.4 1.0 %collective-permute-done.5.refs_1_ = bf16[512,128]{1,0:T(8,128)(2,1)S(1)} collective-permute-done((bf16[512,128]{1,0:T(8,128)(2,1)S(1)}, bf16[512,128]{1,0:T(8,128)(2,1)S(1)}, u32[]{:S(2)}, u32[]{:S(2)}) %collective-permute-start.5) | collective-permute-done | bytes 131104 | tf_op jit(solution)/shard_map/ppermute | solution.py:21
  20.4 0.6 %collective-permute-done.6.refs_2_ = bf16[512,128]{1,0:T(8,128)(2,1)S(1)} collective-permute-done((bf16[512,128]{1,0:T(8,128)(2,1)S(1)}, bf16[512,128]{1,0:T(8,128)(2,1)S(1)}, u32[]{:S(2)}, u32[]{:S(2)}) %collective-permute-start.6) | collective-permute-done | bytes 131104 | tf_op jit(solution)/shard_map/ppermute | solution.py:21
  21.0 0.1 collective-permute-done.7.refs_3_
  21.3 0.9 %forward_near.1.near_ref = f32[5,128,128]{2,1,0:T(8,128)S(1)} custom-call(s32[363]{0:T(512)S(4)} %get-tuple-element.34.index_ref, bf16[60,128,128]{2,1,0:T(8,128)(2,1)S(1)} %get-tuple-element.35.tiles_ref, bf16[4,512,128]{2,1,0:T(8,128)(2,1)S(1)} %pack_square.2.same_ref, bf16[4,512,128]{2,1,0:T(8,128)(2,1)S(1)} %collective-permute-done.3.other_ref), custom_call_target="tpu_custom_call" | custom-call | flops 110000000 | bytes 360000 | tf_op jit(solution)/shard_map/forward_near/pallas_call | solution.py:338
  22.2 0.9 %collective-permute-done.8.refs_1_ = bf16[4,512,128]{2,1,0:T(8,128)(2,1)S(1)} collective-permute-done((bf16[4,512,128]{2,1,0:T(8,128)(2,1)S(1)}, bf16[4,512,128]{2,1,0:T(8,128)(2,1)S(1)}, u32[]{:S(2)}, u32[]{:S(2)}) %collective-permute-start.8) | collective-permute-done | bytes 524320 | tf_op jit(solution)/shard_map/ppermute | solution.py:21
  23.2 2.9 %forward_layer.1 = (bf16[512,256]{1,0:T(8,128)(2,1)}, f32[512,128]{1,0:T(8,128)S(1)}, f32[128,256]{1,0:T(8,128)S(1)}, f32[128,256]{1,0:T(8,128)S(1)}, bf16[4,256,128]{2,1,0:T(8,128)(2,1)S(1)}) custom-call(s32[363]{0:T(512)S(4)} %get-tuple-element.34.index_ref, bf16[60,128,128]{2,1,0:T(8,128)(2,1)S(1)} %get-tuple-element.35.tiles_ref, ...), custom_call_target="tpu_custom_call" | custom-call | flops 4400000000 | bytes 14400000 | tf_op jit(solution)/shard_map/forward_layer/pallas_call | solution.py:338
  26.1 0.1 collective-permute-start.9
  26.2 0.9 %backward_tiles.3.acc_ref = f32[33,128,128]{2,1,0:T(8,128)S(1)} custom-call(s32[363]{0:T(512)S(4)} %get-tuple-element.34.index_ref, bf16[60,128,128]{2,1,0:T(8,128)(2,1)S(1)} %get-tuple-element.35.tiles_ref, bf16[4,256,128]{2,1,0:T(8,128)(2,1)S(1)} %get-tuple-element.45.gt_ref), custom_call_target="tpu_custom_call" | custom-call | flops 1650000000 | bytes 5400000 | tf_op jit(solution)/shard_map/backward_tiles/pallas_call | solution.py:338
  27.2 0.4 collective-permute-start.14
  27.7 1.2 %backward_tiles.2.acc_ref = f32[33,128,128]{2,1,0:T(8,128)S(1)} custom-call(s32[363]{0:T(512)S(4)} %get-tuple-element.34.index_ref, bf16[60,128,128]{2,1,0:T(8,128)(2,1)S(1)} %get-tuple-element.35.tiles_ref, bf16[4,256,128]{2,1,0:T(8,128)(2,1)S(1)} %get-tuple-element.45.gt_ref), custom_call_target="tpu_custom_call" | custom-call | flops 1650000000 | bytes 5400000 | tf_op jit(solution)/shard_map/backward_tiles/pallas_call | solution.py:338
  29.0 0.2 collective-permute-start.10
  29.2 0.8 %collective-permute-done.14.got_ref = f32[4,512,128]{2,1,0:T(8,128)S(1)} collective-permute-done((f32[4,512,128]{2,1,0:T(8,128)S(1)}, f32[4,512,128]{2,1,0:T(8,128)S(1)}, u32[]{:S(2)}, u32[]{:S(2)}) %collective-permute-start.14) | collective-permute-done | bytes 1048608 | tf_op jit(solution)/shard_map/ppermute | solution.py:21
  30.0 0.1 pair_sum_weights.1
  30.1 2.1 %collective-permute-start.15 = (bf16[640,128]{1,0:T(8,128)(2,1)S(1)}, bf16[640,128]{1,0:T(8,128)(2,1)S(1)}, u32[]{:S(2)}, u32[]{:S(2)}) collective-permute-start(bf16[640,128]{1,0:T(8,128)(2,1)S(1)} %get-tuple-element.57), channel_id=1, source_target_pairs={{0,6},{1,7},{2,4},{3,5},{4,2},{5,3},{6,0},{7,1},{8,14},{9,15},{10,... | collective-permute-start | bytes 491528 | tf_op jit(solution)/shard_map/ppermute | solution.py:21
  32.2 0.6 collective-permute-start.16
  32.8 1.4 %collective-permute-start.17 = (bf16[640,128]{1,0:T(8,128)(2,1)S(1)}, bf16[640,128]{1,0:T(8,128)(2,1)S(1)}, u32[]{:S(2)}, u32[]{:S(2)}) collective-permute-start(bf16[640,128]{1,0:T(8,128)(2,1)S(1)} %get-tuple-element.59), channel_id=1, source_target_pairs={{0,4},{1,5},{2,6},{3,7},{4,0},{5,1},{6,2},{7,3},{8,12},{9,13},{10,... | collective-permute-start | bytes 491528 | tf_op jit(solution)/shard_map/ppermute | solution.py:21
  34.1 0.1 pair_sum.1
  34.2 1.6 %collective-permute-start.11 = (bf16[512,128]{1,0:T(8,128)(2,1)S(1)}, bf16[512,128]{1,0:T(8,128)(2,1)S(1)}, u32[]{:S(2)}, u32[]{:S(2)}) collective-permute-start(bf16[512,128]{1,0:T(8,128)(2,1)S(1)} %get-tuple-element.50), channel_id=1, source_target_pairs={{0,6},{1,7},{2,4},{3,5},{4,2},{5,3},{6,0},{7,1},{8,14},{9,15},{10,... | collective-permute-start | bytes 393224 | tf_op jit(solution)/shard_map/ppermute | solution.py:21
  35.9 0.6 collective-permute-start.12
  36.4 1.7 %collective-permute-done.15.refs_0_ = bf16[640,128]{1,0:T(8,128)(2,1)S(1)} collective-permute-done((bf16[640,128]{1,0:T(8,128)(2,1)S(1)}, bf16[640,128]{1,0:T(8,128)(2,1)S(1)}, u32[]{:S(2)}, u32[]{:S(2)}) %collective-permute-start.15) | collective-permute-done | bytes 163872 | tf_op jit(solution)/shard_map/ppermute | solution.py:21
  38.1 1.1 %collective-permute-start.13 = (bf16[512,128]{1,0:T(8,128)(2,1)S(1)}, bf16[512,128]{1,0:T(8,128)(2,1)S(1)}, u32[]{:S(2)}, u32[]{:S(2)}) collective-permute-start(bf16[512,128]{1,0:T(8,128)(2,1)S(1)} %get-tuple-element.52), channel_id=1, source_target_pairs={{0,4},{1,5},{2,6},{3,7},{4,0},{5,1},{6,2},{7,3},{8,12},{9,13},{10,... | collective-permute-start | bytes 393224 | tf_op jit(solution)/shard_map/ppermute | solution.py:21
  39.2 2.5 %collective-permute-done.16.refs_1_ = bf16[640,128]{1,0:T(8,128)(2,1)S(1)} collective-permute-done((bf16[640,128]{1,0:T(8,128)(2,1)S(1)}, bf16[640,128]{1,0:T(8,128)(2,1)S(1)}, u32[]{:S(2)}, u32[]{:S(2)}) %collective-permute-start.16) | collective-permute-done | bytes 163872 | tf_op jit(solution)/shard_map/ppermute | solution.py:21
  41.7 1.0 %collective-permute-done.17.refs_2_ = bf16[640,128]{1,0:T(8,128)(2,1)S(1)} collective-permute-done((bf16[640,128]{1,0:T(8,128)(2,1)S(1)}, bf16[640,128]{1,0:T(8,128)(2,1)S(1)}, u32[]{:S(2)}, u32[]{:S(2)}) %collective-permute-start.17) | collective-permute-done | bytes 163872 | tf_op jit(solution)/shard_map/ppermute | solution.py:21
  42.7 0.1 square_sum_weights.1
  42.8 1.2 %collective-permute-start.19 = (f32[32,256]{1,0:T(8,128)S(1)}, f32[32,256]{1,0:T(8,128)S(1)}, u32[]{:S(2)}, u32[]{:S(2)}) collective-permute-start(f32[32,256]{1,0:T(8,128)S(1)} %get-tuple-element.61.own_ref), channel_id=1, source_target_pairs={{0,8},{1,9},{2,10},{3,11},{4,12},{5,13},{6,14},{7,15},{8,0},{9,1},... | collective-permute-start | bytes 98312 | tf_op jit(solution)/shard_map/ppermute | solution.py:21
  44.0 4.0 %collective-permute-done.19.got_ref = f32[32,256]{1,0:T(8,128)S(1)} collective-permute-done((f32[32,256]{1,0:T(8,128)S(1)}, f32[32,256]{1,0:T(8,128)S(1)}, u32[]{:S(2)}, u32[]{:S(2)}) %collective-permute-start.19) | collective-permute-done | bytes 32800 | tf_op jit(solution)/shard_map/ppermute | solution.py:21
  48.0 0.7 %collective-permute-start.20 = (f32[32,256]{1,0:T(8,128)S(1)}, f32[32,256]{1,0:T(8,128)S(1)}, u32[]{:S(2)}, u32[]{:S(2)}) collective-permute-start(f32[32,256]{1,0:T(8,128)S(1)} %weight_sum.1.refs_0_), channel_id=1, source_target_pairs={{0,2},{1,3},{2,0},{3,1},{4,6},{5,7},{6,4},{7,5},{8,10},{9,11},{10,... | collective-permute-start | bytes 98312 | tf_op jit(solution)/shard_map/ppermute | solution.py:21
  48.6 1.7 %collective-permute-start.18 = (bf16[512,128]{1,0:T(8,128)(2,1)S(1)}, bf16[512,128]{1,0:T(8,128)(2,1)S(1)}, u32[]{:S(2)}, u32[]{:S(2)}) collective-permute-start(bf16[512,128]{1,0:T(8,128)(2,1)S(1)} %get-tuple-element.60), channel_id=1, source_target_pairs={{0,8},{1,9},{2,10},{3,11},{4,12},{5,13},{6,14},{7,15},{8,0},{9,1},... | collective-permute-start | bytes 393224 | tf_op jit(solution)/shard_map/ppermute | solution.py:21
  50.3 1.6 %collective-permute-done.20.refs_1_ = f32[32,256]{1,0:T(8,128)S(1)} collective-permute-done((f32[32,256]{1,0:T(8,128)S(1)}, f32[32,256]{1,0:T(8,128)S(1)}, u32[]{:S(2)}, u32[]{:S(2)}) %collective-permute-start.20) | collective-permute-done | bytes 32800 | tf_op jit(solution)/shard_map/ppermute | solution.py:21
  51.9 1.1 %collective-permute-start.21 = (f32[2,32,256]{2,1,0:T(8,128)S(1)}, f32[2,32,256]{2,1,0:T(8,128)S(1)}, u32[]{:S(2)}, u32[]{:S(2)}) collective-permute-start(f32[2,32,256]{2,1,0:T(8,128)S(1)} %pack_weights.2.refs_0_), channel_id=1, source_target_pairs={{0,4},{1,5},{2,6},{3,7},{4,0},{5,1},{6,2},{7,3},{8,12},{9,13},{10,... | collective-permute-start | bytes 196616 | tf_op jit(solution)/shard_map/ppermute | solution.py:21
  53.0 0.1 near_sum.1.near_ref.refs_2_
  53.2 3.6 %collective-permute-done.21.refs_1_ = f32[2,32,256]{2,1,0:T(8,128)S(1)} collective-permute-done((f32[2,32,256]{2,1,0:T(8,128)S(1)}, f32[2,32,256]{2,1,0:T(8,128)S(1)}, u32[]{:S(2)}, u32[]{:S(2)}) %collective-permute-start.21) | collective-permute-done | bytes 65568 | tf_op jit(solution)/shard_map/ppermute | solution.py:21
  56.8 0.1 collective-permute-start.22
  56.9 0.8 %grad_input_sum.1 = bf16[512,128]{1,0:T(8,128)(2,1)} custom-call(f32[512,128]{1,0:T(8,128)S(1)} %near_sum.1.near_ref.refs_2_, bf16[512,128]{1,0:T(8,128)(2,1)S(1)} %collective-permute-done.18.refs_0_), custom_call_target="tpu_custom_call" | custom-call | flops 11000000512 | bytes 36000000 | tf_op jit(solution)/shard_map/grad_input_sum/pallas_call | solution.py:338
  57.6 0.6 collective-permute-done.22.other_ref
  58.2 0.7 %write_weights.1 = (f32[128,256]{1,0:T(8,128)}, f32[128,256]{1,0:T(8,128)}) custom-call(s32[363]{0:T(512)S(4)} %get-tuple-element.34.index_ref, f32[2,2,32,256]{3,2,1,0:T(8,128)S(1)} %pack_weights.3.weight_ref, f32[2,2,32,256]{3,2,1,0:T(8,128)S(1)} %collective-permute-done.22.other_ref), custom_call_target="tpu_custom_call" | custom-call | flops 220000000 | bytes 720000 | tf_op jit(solution)/shard_map/write_weights/pallas_call | solution.py:338
  (21 shorter events, 0.4 us)
Async XLA Ops:
  0.6 10.7 %collective-permute-start.4 = (bf16[512,128]{1,0:T(8,128)(2,1)}, bf16[512,128]{1,0:T(8,128)(2,1)S(1)}, u32[]{:S(2)}, u32[]{:S(2)}) collective-permute-start(bf16[512,128]{1,0:T(8,128)(2,1)} %feat_ref.1), channel_id=1, source_target_pairs={{0,8},{1,9},{2,10},{3,11},{4,12},{5,13},{6,14},{7,15},{8,0},{9,1},... | collective-permute-start | bytes 393224 | tf_op jit(solution)/shard_map/ppermute | solution.py:21
  4.7 8.9 %collective-permute-start = (bf16[512,128]{1,0:T(8,128)(2,1)}, bf16[512,128]{1,0:T(8,128)(2,1)S(1)}, u32[]{:S(2)}, u32[]{:S(2)}) collective-permute-start(bf16[512,128]{1,0:T(8,128)(2,1)} %feat_ref.1), channel_id=1, source_target_pairs={{0,2},{1,3},{2,0},{3,1},{4,6},{5,7},{6,4},{7,5},{8,10},{9,11},{10,... | collective-permute-start | bytes 393224 | tf_op jit(solution)/shard_map/ppermute | solution.py:21
  6.3 13.0 %collective-permute-start.1 = (bf16[512,128]{1,0:T(8,128)(2,1)}, bf16[512,128]{1,0:T(8,128)(2,1)S(1)}, u32[]{:S(2)}, u32[]{:S(2)}) collective-permute-start(bf16[512,128]{1,0:T(8,128)(2,1)} %feat_ref.1), channel_id=1, source_target_pairs={{0,6},{1,7},{2,4},{3,5},{4,2},{5,3},{6,0},{7,1},{8,14},{9,15},{10,... | collective-permute-start | bytes 393224 | tf_op jit(solution)/shard_map/ppermute | solution.py:21
  7.8 11.5 %collective-permute-start.2 = (bf16[512,128]{1,0:T(8,128)(2,1)}, bf16[512,128]{1,0:T(8,128)(2,1)S(1)}, u32[]{:S(2)}, u32[]{:S(2)}) collective-permute-start(bf16[512,128]{1,0:T(8,128)(2,1)} %feat_ref.1), channel_id=1, source_target_pairs={{0,4},{1,5},{2,6},{3,7},{4,0},{5,1},{6,2},{7,3},{8,12},{9,13},{10,... | collective-permute-start | bytes 393224 | tf_op jit(solution)/shard_map/ppermute | solution.py:21
  11.4 9.1 %collective-permute-start.5 = (bf16[512,128]{1,0:T(8,128)(2,1)S(1)}, bf16[512,128]{1,0:T(8,128)(2,1)S(1)}, u32[]{:S(2)}, u32[]{:S(2)}) collective-permute-start(bf16[512,128]{1,0:T(8,128)(2,1)S(1)} %collective-permute-done.4.refs_0_), channel_id=1, source_target_pairs={{0,6},{1,7},{2,4},{3,5},{4,2},{5,3},{6,0},{7,1},{8,14},{9,15},{10,... | collective-permute-start | bytes 393224 | tf_op jit(solution)/shard_map/ppermute | solution.py:21
  13.1 7.9 %collective-permute-start.6 = (bf16[512,128]{1,0:T(8,128)(2,1)S(1)}, bf16[512,128]{1,0:T(8,128)(2,1)S(1)}, u32[]{:S(2)}, u32[]{:S(2)}) collective-permute-start(bf16[512,128]{1,0:T(8,128)(2,1)S(1)} %collective-permute-done.4.refs_0_), channel_id=1, source_target_pairs={{0,2},{1,3},{2,0},{3,1},{4,6},{5,7},{6,4},{7,5},{8,10},{9,11},{10,... | collective-permute-start | bytes 393224 | tf_op jit(solution)/shard_map/ppermute | solution.py:21
  13.6 7.6 %collective-permute-start.7 = (bf16[512,128]{1,0:T(8,128)(2,1)S(1)}, bf16[512,128]{1,0:T(8,128)(2,1)S(1)}, u32[]{:S(2)}, u32[]{:S(2)}) collective-permute-start(bf16[512,128]{1,0:T(8,128)(2,1)S(1)} %collective-permute-done.4.refs_0_), channel_id=1, source_target_pairs={{0,4},{1,5},{2,6},{3,7},{4,0},{5,1},{6,2},{7,3},{8,12},{9,13},{10,... | collective-permute-start | bytes 393224 | tf_op jit(solution)/shard_map/ppermute | solution.py:21
  14.8 0.7 %copy-start = (s32[60]{0:T(128)S(1)}, s32[60]{0:T(128)}, u32[]{:S(2)}) copy-start(s32[60]{0:T(128)} %trow_ref.1) | copy-start | bytes 724
  15.5 0.7 %copy-start.1 = (s32[60]{0:T(128)S(1)}, s32[60]{0:T(128)}, u32[]{:S(2)}) copy-start(s32[60]{0:T(128)} %tcol_ref.1) | copy-start | bytes 724
  19.3 2.0 %collective-permute-start.3 = (bf16[4,512,128]{2,1,0:T(8,128)(2,1)S(1)}, bf16[4,512,128]{2,1,0:T(8,128)(2,1)S(1)}, u32[]{:S(2)}, u32[]{:S(2)}) collective-permute-start(bf16[4,512,128]{2,1,0:T(8,128)(2,1)S(1)} %pack_square.2.same_ref), channel_id=1, source_target_pairs={{0,1},{1,0},{2,3},{3,2},{4,5},{5,4},{6,7},{7,6},{8,9},{9,8},{10,11... | collective-permute-start | bytes 1572872 | tf_op jit(solution)/shard_map/ppermute | solution.py:21
  21.2 2.0 %collective-permute-start.8 = (bf16[4,512,128]{2,1,0:T(8,128)(2,1)S(1)}, bf16[4,512,128]{2,1,0:T(8,128)(2,1)S(1)}, u32[]{:S(2)}, u32[]{:S(2)}) collective-permute-start(bf16[4,512,128]{2,1,0:T(8,128)(2,1)S(1)} %pack_square.3.refs_0_), channel_id=1, source_target_pairs={{0,1},{1,0},{2,3},{3,2},{4,5},{5,4},{6,7},{7,6},{8,9},{9,8},{10,11... | collective-permute-start | bytes 1572872 | tf_op jit(solution)/shard_map/ppermute | solution.py:21
  26.1 2.8 %collective-permute-start.9 = (f32[128,256]{1,0:T(8,128)S(1)}, f32[128,256]{1,0:T(8,128)S(1)}, u32[]{:S(2)}, u32[]{:S(2)}) collective-permute-start(f32[128,256]{1,0:T(8,128)S(1)} %get-tuple-element.47), channel_id=1, source_target_pairs={{0,1},{1,0},{2,3},{3,2},{4,5},{5,4},{6,7},{7,6},{8,9},{9,8},{10,11... | collective-permute-start | bytes 393224 | tf_op jit(solution)/shard_map/ppermute | solution.py:21
  27.2 2.7 %collective-permute-start.14 = (f32[4,512,128]{2,1,0:T(8,128)S(1)}, f32[4,512,128]{2,1,0:T(8,128)S(1)}, u32[]{:S(2)}, u32[]{:S(2)}) collective-permute-start(f32[4,512,128]{2,1,0:T(8,128)S(1)} %send.3), channel_id=1, source_target_pairs={{0,1},{1,0},{2,3},{3,2},{4,5},{5,4},{6,7},{7,6},{8,9},{9,8},{10,11... | collective-permute-start | bytes 3145736 | tf_op jit(solution)/shard_map/ppermute | solution.py:21
  29.0 5.1 %collective-permute-start.10 = (f32[4,512,128]{2,1,0:T(8,128)S(1)}, f32[4,512,128]{2,1,0:T(8,128)S(1)}, u32[]{:S(2)}, u32[]{:S(2)}) collective-permute-start(f32[4,512,128]{2,1,0:T(8,128)S(1)} %send.2), channel_id=1, source_target_pairs={{0,1},{1,0},{2,3},{3,2},{4,5},{5,4},{6,7},{7,6},{8,9},{9,8},{10,11... | collective-permute-start | bytes 3145736 | tf_op jit(solution)/shard_map/ppermute | solution.py:21
  30.1 8.0 %collective-permute-start.15 = (bf16[640,128]{1,0:T(8,128)(2,1)S(1)}, bf16[640,128]{1,0:T(8,128)(2,1)S(1)}, u32[]{:S(2)}, u32[]{:S(2)}) collective-permute-start(bf16[640,128]{1,0:T(8,128)(2,1)S(1)} %get-tuple-element.57), channel_id=1, source_target_pairs={{0,6},{1,7},{2,4},{3,5},{4,2},{5,3},{6,0},{7,1},{8,14},{9,15},{10,... | collective-permute-start | bytes 491528 | tf_op jit(solution)/shard_map/ppermute | solution.py:21
  32.2 9.5 %collective-permute-start.16 = (bf16[640,128]{1,0:T(8,128)(2,1)S(1)}, bf16[640,128]{1,0:T(8,128)(2,1)S(1)}, u32[]{:S(2)}, u32[]{:S(2)}) collective-permute-start(bf16[640,128]{1,0:T(8,128)(2,1)S(1)} %get-tuple-element.58), channel_id=1, source_target_pairs={{0,2},{1,3},{2,0},{3,1},{4,6},{5,7},{6,4},{7,5},{8,10},{9,11},{10,... | collective-permute-start | bytes 491528 | tf_op jit(solution)/shard_map/ppermute | solution.py:21
  32.8 9.9 %collective-permute-start.17 = (bf16[640,128]{1,0:T(8,128)(2,1)S(1)}, bf16[640,128]{1,0:T(8,128)(2,1)S(1)}, u32[]{:S(2)}, u32[]{:S(2)}) collective-permute-start(bf16[640,128]{1,0:T(8,128)(2,1)S(1)} %get-tuple-element.59), channel_id=1, source_target_pairs={{0,4},{1,5},{2,6},{3,7},{4,0},{5,1},{6,2},{7,3},{8,12},{9,13},{10,... | collective-permute-start | bytes 491528 | tf_op jit(solution)/shard_map/ppermute | solution.py:21
  34.2 18.8 %collective-permute-start.11 = (bf16[512,128]{1,0:T(8,128)(2,1)S(1)}, bf16[512,128]{1,0:T(8,128)(2,1)S(1)}, u32[]{:S(2)}, u32[]{:S(2)}) collective-permute-start(bf16[512,128]{1,0:T(8,128)(2,1)S(1)} %get-tuple-element.50), channel_id=1, source_target_pairs={{0,6},{1,7},{2,4},{3,5},{4,2},{5,3},{6,0},{7,1},{8,14},{9,15},{10,... | collective-permute-start | bytes 393224 | tf_op jit(solution)/shard_map/ppermute | solution.py:21
  35.9 17.2 %collective-permute-start.12 = (bf16[512,128]{1,0:T(8,128)(2,1)S(1)}, bf16[512,128]{1,0:T(8,128)(2,1)S(1)}, u32[]{:S(2)}, u32[]{:S(2)}) collective-permute-start(bf16[512,128]{1,0:T(8,128)(2,1)S(1)} %get-tuple-element.51), channel_id=1, source_target_pairs={{0,2},{1,3},{2,0},{3,1},{4,6},{5,7},{6,4},{7,5},{8,10},{9,11},{10,... | collective-permute-start | bytes 393224 | tf_op jit(solution)/shard_map/ppermute | solution.py:21
  38.1 14.9 %collective-permute-start.13 = (bf16[512,128]{1,0:T(8,128)(2,1)S(1)}, bf16[512,128]{1,0:T(8,128)(2,1)S(1)}, u32[]{:S(2)}, u32[]{:S(2)}) collective-permute-start(bf16[512,128]{1,0:T(8,128)(2,1)S(1)} %get-tuple-element.52), channel_id=1, source_target_pairs={{0,4},{1,5},{2,6},{3,7},{4,0},{5,1},{6,2},{7,3},{8,12},{9,13},{10,... | collective-permute-start | bytes 393224 | tf_op jit(solution)/shard_map/ppermute | solution.py:21
  42.8 5.2 %collective-permute-start.19 = (f32[32,256]{1,0:T(8,128)S(1)}, f32[32,256]{1,0:T(8,128)S(1)}, u32[]{:S(2)}, u32[]{:S(2)}) collective-permute-start(f32[32,256]{1,0:T(8,128)S(1)} %get-tuple-element.61.own_ref), channel_id=1, source_target_pairs={{0,8},{1,9},{2,10},{3,11},{4,12},{5,13},{6,14},{7,15},{8,0},{9,1},... | collective-permute-start | bytes 98312 | tf_op jit(solution)/shard_map/ppermute | solution.py:21
  48.0 3.9 %collective-permute-start.20 = (f32[32,256]{1,0:T(8,128)S(1)}, f32[32,256]{1,0:T(8,128)S(1)}, u32[]{:S(2)}, u32[]{:S(2)}) collective-permute-start(f32[32,256]{1,0:T(8,128)S(1)} %weight_sum.1.refs_0_), channel_id=1, source_target_pairs={{0,2},{1,3},{2,0},{3,1},{4,6},{5,7},{6,4},{7,5},{8,10},{9,11},{10,... | collective-permute-start | bytes 98312 | tf_op jit(solution)/shard_map/ppermute | solution.py:21
  48.6 8.2 %collective-permute-start.18 = (bf16[512,128]{1,0:T(8,128)(2,1)S(1)}, bf16[512,128]{1,0:T(8,128)(2,1)S(1)}, u32[]{:S(2)}, u32[]{:S(2)}) collective-permute-start(bf16[512,128]{1,0:T(8,128)(2,1)S(1)} %get-tuple-element.60), channel_id=1, source_target_pairs={{0,8},{1,9},{2,10},{3,11},{4,12},{5,13},{6,14},{7,15},{8,0},{9,1},... | collective-permute-start | bytes 393224 | tf_op jit(solution)/shard_map/ppermute | solution.py:21
  51.9 4.9 %collective-permute-start.21 = (f32[2,32,256]{2,1,0:T(8,128)S(1)}, f32[2,32,256]{2,1,0:T(8,128)S(1)}, u32[]{:S(2)}, u32[]{:S(2)}) collective-permute-start(f32[2,32,256]{2,1,0:T(8,128)S(1)} %pack_weights.2.refs_0_), channel_id=1, source_target_pairs={{0,4},{1,5},{2,6},{3,7},{4,0},{5,1},{6,2},{7,3},{8,12},{9,13},{10,... | collective-permute-start | bytes 196616 | tf_op jit(solution)/shard_map/ppermute | solution.py:21
  56.8 1.4 %collective-permute-start.22 = (f32[2,2,32,256]{3,2,1,0:T(8,128)S(1)}, f32[2,2,32,256]{3,2,1,0:T(8,128)S(1)}, u32[]{:S(2)}, u32[]{:S(2)}) collective-permute-start(f32[2,2,32,256]{3,2,1,0:T(8,128)S(1)} %pack_weights.3.weight_ref), channel_id=1, source_target_pairs={{0,1},{1,0},{2,3},{3,2},{4,5},{5,4},{6,7},{7,6},{8,9},{9,8},{10,11... | collective-permute-start | bytes 393224 | tf_op jit(solution)/shard_map/ppermute | solution.py:21

commit v12 on v11

--- a/solution.py
+++ b/solution.py
@@ -170,38 +170,39 @@
     gathered_products(0, group, index_ref, tiles_ref, (same_ref, other_ref), feats, raw)
 
 
-def forward_kernel(group, far, index_ref, tiles_ref, ws_ref, wn_ref, inverse_ref, up_ref, pre_ref,
-                   featt_ref, near_ref, *refs):
+def forward_kernel(group, far, index_ref, tiles_ref, wn_ref, inverse_ref, up_ref, pre_ref,
+                   near_ref, *refs):
     feat_refs, refs = refs[:2 * far], refs[2 * far:]
-    emb_ref, base_ref, wkeep_ref, wsend_ref, gt_ref, feats, raw, wsum = refs
+    emb_ref, high_ref, low_ref, scaled_ref, gt_ref, raw, feats = refs
     block_local = inverse_ref.shape[0]
     raw[...] = near_ref[...]
     gathered_products(1, group, index_ref, tiles_ref, feat_refs, feats, raw)
-
     wn = wn_ref[...]
-    ws = ws_ref[...]
     for b in range(block_local):
         inverse = inverse_ref[b]
-        raw_b = raw[b]
-        pre = pre_ref[rows_of(b), :] + dot_wide(raw_b * inverse, wn)
+        pre = pre_ref[rows_of(b), :] + dot_wide(raw[b] * inverse, wn)
         sig = jax.nn.sigmoid(pre)
         emb_ref[rows_of(b), :] = (pre * sig).astype(BF16)
         grad_pre = up_ref[rows_of(b), :] * sig * (1.0 + pre * (1.0 - sig))
         scaled = (grad_pre * jnp.concatenate([inverse, inverse], axis=1)).astype(BF16)
-        gp_high, gp_low = split_bf16(grad_pre)
+        scaled_ref[rows_of(b), :] = scaled
+        high_ref[rows_of(b), :], low_ref[rows_of(b), :] = split_bf16(grad_pre)
+        high, low = split_bf16(dot(wn, scaled, LAST))
+        gt_ref[b, :BLOCK, :] = high
+        gt_ref[b, BLOCK:, :] = low
+
+
+def weights_kernel(index_ref, high_ref, low_ref, scaled_ref, raw_ref, featt_ref, *refs):
+    wkeep_ref, wsend_ref, wsum = refs[-3:]
+    for b in range(featt_ref.shape[0]):
         feat_t = featt_ref[b]
-        grad_self = dot(feat_t, gp_high) + dot(feat_t, gp_low)
-        grad_neigh = dot_wide(jnp.transpose(raw_b), scaled)
+        grad_self = dot(feat_t, high_ref[rows_of(b), :]) + dot(feat_t, low_ref[rows_of(b), :])
+        grad_neigh = dot_wide(jnp.transpose(raw_ref[b]), scaled_ref[rows_of(b), :])
         if b == 0:
             wsum[0], wsum[1] = grad_self, grad_neigh
         else:
             wsum[0] += grad_self
             wsum[1] += grad_neigh
-        base_ref[rows_of(b), :] = dot(gp_high, ws, LAST) + dot(gp_low, ws, LAST)
-        high, low = split_bf16(dot(wn, scaled, LAST))
-        gt_ref[b, :BLOCK, :] = high
-        gt_ref[b, BLOCK:, :] = low
-
     core = index_ref[index_ref.shape[0] - 1] % 2
     wkeep_ref[...] = wsum[core]
     wsend_ref[...] = wsum[1 - core]
@@ -284,12 +285,14 @@
         weight_out[:, span] = total
 
 
-def near_kernel(base_ref, own_ref, *refs):
+def near_kernel(high_ref, low_ref, ws_ref, own_ref, *refs):
+    ws = ws_ref[...]
     for b in range(own_ref.shape[0] // BLOCK):
         total = own_ref[rows_of(b), :]
         for got_ref in refs[:-1]:
             total = total + got_ref[rows_of(b), :].astype(F32)
-        refs[-1][rows_of(b), :] = base_ref[rows_of(b), :] + jnp.transpose(total)
+        base = dot(high_ref[rows_of(b), :], ws, LAST) + dot(low_ref[rows_of(b), :], ws, LAST)
+        refs[-1][rows_of(b), :] = base + jnp.transpose(total)
 
 
 def main_kernel(near_ref, *refs):
@@ -307,7 +310,7 @@
     rows = weight_ref.shape[2]
     for p in range(4):
         span = pl.ds(pl.multiple_of((chip ^ p) * rows, rows), rows)
-        mine, other = weight_ref[p // 2, p % 2], other_ref[p // 2, p % 2]
+        mine, other = weight_ref[p % 2, p // 2], other_ref[p % 2, p // 2]
         self_ref[span, :] = jnp.where(first, mine, other)
         neigh_ref[span, :] = jnp.where(first, other, mine)
 
@@ -320,7 +323,7 @@
     hidden = w_self.shape[1]
     block_local = nodes // BLOCK
     tile_count = tiles.shape[0]
-    group = max(g for g in range(1, 7) if tile_count % g == 0)
+    group = max(g for g in range(1, 11) if tile_count % g == 0)
     small = n * nodes * feat_in * 4 <= 4 * MIB
     limit = (24 if small else 56) * MIB
 
@@ -388,31 +391,24 @@
         (index, tiles_near, same[0], other[0]), [SMEM] + [VMEM] * 3, cost_us=0.1,
         scratch_shapes=[pltpu.VMEM(near_square, BF16)],
     )
-    operands = (
-        index, tiles_near, ws, wn, inverse, upstream, pre_self, feat_t, raw, *same[1:], *other[1:])
-    embedded, base, wkeep, wsend, gt = call(
+    operands = (index, tiles_near, wn, inverse, upstream, pre_self, raw, *same[1:], *other[1:])
+    wide_out = result((nodes, hidden), BF16)
+    embedded, high, low, scaled, gt, raw = call(
         functools.partial(forward_kernel, group, squares - 1),
         "forward_layer",
         (
-            result((nodes, hidden), BF16, False), wide, weight, weight,
-            result((block_local, 2 * feat_in, BLOCK), BF16),
+            result((nodes, hidden), BF16, False), wide_out, wide_out, wide_out,
+            result((block_local, 2 * feat_in, BLOCK), BF16), result(raw_shape, F32),
         ),
         operands,
         [SMEM] + [VMEM] * (len(operands) - 1),
-        cost_us=4,
-        scratch_shapes=[
-            pltpu.VMEM(far_squares, BF16),
-            pltpu.VMEM(raw_shape, F32),
-            pltpu.VMEM((2, feat_in, hidden), F32),
-        ],
+        cost_us=3,
+        scratch_shapes=[pltpu.VMEM(far_squares, BF16)],
     )
-
-    w0, w1, w2, w3 = call(
-        cut_kernel, "cut_weights", (chunk,) * 4, (index, wkeep, swap(wsend, n, 1)),
-        [SMEM, VMEM, VMEM])
 
     send_shape = result((4, nodes, feat_in), F32)
     sums, got = [], [None] * squares
+    after = None
     for section, shape in ((1, far_squares), (0, near_square)):
         acc = call(
             functools.partial(backward_kernel, section, group), "backward_tiles",
@@ -421,8 +417,18 @@
         sums.insert(0, acc)
         for s in range(squares - 1, 0, -1) if section else (0,):
             operands = (acc,) if section else (acc, w0)
-            got[s] = swap(
-                call(functools.partial(send_kernel, s - section), "send", send_shape, operands), n, 1)
+            send = call(functools.partial(send_kernel, s - section), "send", send_shape, operands)
+            got[s] = swap(send, n, 1)
+            after = send if after is None else after
+        if section:
+            wkeep, wsend = call(
+                weights_kernel, "weights", (weight, weight),
+                (index, high, low, scaled, raw, feat_t, after), [SMEM] + [VMEM] * 6, cost_us=1,
+                scratch_shapes=[pltpu.VMEM((2, feat_in, hidden), F32)])
+            w0, w1, w2, w3 = call(
+                cut_kernel, "cut_weights", (chunk,) * 4, (index, wkeep, swap(wsend, n, 1)),
+                [SMEM, VMEM, VMEM])
+
     extra = result((nodes + 2 * chunk.shape[0] * (hidden // feat_in), feat_in), BF16)
     terms = [None] * squares
     for s in range(squares - 1, -1, -1):
@@ -435,7 +441,7 @@
             own, *pieces = call(
                 functools.partial(pair_kernel, max(s - 1, 0)), "pair_sum", (wide, piece, piece, piece), operands)
         terms[s] = [own, *[swap(pieces[q - 1], n, 2 * q) for q in (3, 1, 2)]]
-    near_total = call(near_kernel, "near_sum", wide, (base, *terms[0]), cost_us=NEAR_COST)
+    near_total = call(near_kernel, "near_sum", wide, (high, low, ws, *terms[0]), cost_us=NEAR_COST)
     terms[0] = [near_total]
     distance = 1
     while distance < squares:
@@ -453,9 +459,9 @@
         wsum = call(add_two_kernel, "weight_sum", chunk, (wsum, swap(wsum, n, bit)))
         bit *= 2
     rows = chunk.shape[0]
-    two = call(functools.partial(pack_kernel, (0, 1)), "pack_weights", result((2, rows, hidden), F32), (wsum, swap(wsum, n, 2)))
+    two = call(functools.partial(pack_kernel, (0, 1)), "pack_weights", result((2, rows, hidden), F32), (wsum, swap(wsum, n, 4)))
     mine = call(
-        functools.partial(pack_kernel, (0, 1)), "pack_weights", result((2, 2, rows, hidden), F32), (two, swap(two, n, 4), near_total))
+        functools.partial(pack_kernel, (0, 1)), "pack_weights", result((2, 2, rows, hidden), F32), (two, swap(two, n, 2), near_total))
     grad_input = call(
         main_kernel, "grad_input_sum", result((nodes, feat_in), BF16, False), terms[0],
         cost_us=MAIN_COST)

time: 59 us -> 58.4 us (0.990)
  waiting for transfers between devices: 21.5 us -> 19.9 us
  starting transfers between devices: 24.1 us -> 24.9 us
    ppermute x23, waiting for transfers between devices: 21.5 us -> 19.9 us  [swap(): return lax.ppermute(x, 'row', [(i, i ^ offset) for i in range(n)])]
    ppermute x23, starting transfers between devices: 24.1 us -> 24.9 us  [swap(): return lax.ppermute(x, 'row', [(i, i ^ offset) for i in range(n)])]
    pallas_call x18 -> x19, Pallas kernels: 8.12 us -> 8.47 us  [call(): pl.pallas_call(kernel, out_shape=out_shape, in_specs=specs, out_specs=out...]
  transfers between devices with their start and end apart: 23 -> 23, of which waited for: 13 -> 13; matrix products, arithmetic and copies ran while one was open for 0% -> 0% of each run, Pallas kernels for 13% -> 12%
where the time goes in v12:
time: 58.4 us
  starting transfers between devices  24.9 us (43%)
  waiting for transfers between devices  19.9 us (34%)
  Pallas kernels  11.6 us (20%)
  local copies, waits for them, and re-layouts  1.31 us (2%)
  between operations  0.8 us (1%)
    ppermute x23, starting transfers between devices, swap(): return lax.ppermute(x, 'row', [(i, i ^ offset) for i in range(n)])  24.9 us
    ppermute x23, waiting for transfers between devices, swap(): return lax.ppermute(x, 'row', [(i, i ^ offset) for i in range(n)])  19.9 us
    pallas_call x19, Pallas kernels, call(): pl.pallas_call(kernel, out_shape=out_shape, in_specs=specs, out_specs=out...  8.47 us
    pallas_call x1, Pallas kernels, body(): pl.pallas_call(functools.partial(stage_kernel, (8 * block_local, (n - 8)...  3.09 us
    unnamed x4, local copies, waits for them, and re-layouts  1.31 us
  transfers between devices with their start and end apart: 23, of which 13 were waited for; matrix products, arithmetic and copies ran while one was open for 0% of the time, Pallas kernels for 12%

profile of v12, /device:TPU:0, one launch (start us, length us, event | category | flops | bytes accessed | tf_op | source)
XLA Modules:
  0.0 58.4 jit_solution(8678735916980191745)
XLA Ops:
  0.6 4.1 %collective-permute-start.4 = (bf16[512,128]{1,0:T(8,128)(2,1)}, bf16[512,128]{1,0:T(8,128)(2,1)S(1)}, u32[]{:S(2)}, u32[]{:S(2)}) collective-permute-start(bf16[512,128]{1,0:T(8,128)(2,1)} %feat_ref.1), channel_id=1, source_target_pairs={{0,8},{1,9},{2,10},{3,11},{4,12},{5,13},{6,14},{7,15},{8,0},{9,1},... | collective-permute-start | bytes 393224 | tf_op jit(solution)/shard_map/ppermute | solution.py:21
  4.7 1.5 %collective-permute-start = (bf16[512,128]{1,0:T(8,128)(2,1)}, bf16[512,128]{1,0:T(8,128)(2,1)S(1)}, u32[]{:S(2)}, u32[]{:S(2)}) collective-permute-start(bf16[512,128]{1,0:T(8,128)(2,1)} %feat_ref.1), channel_id=1, source_target_pairs={{0,2},{1,3},{2,0},{3,1},{4,6},{5,7},{6,4},{7,5},{8,10},{9,11},{10,... | collective-permute-start | bytes 393224 | tf_op jit(solution)/shard_map/ppermute | solution.py:21
  6.3 1.5 %collective-permute-start.1 = (bf16[512,128]{1,0:T(8,128)(2,1)}, bf16[512,128]{1,0:T(8,128)(2,1)S(1)}, u32[]{:S(2)}, u32[]{:S(2)}) collective-permute-start(bf16[512,128]{1,0:T(8,128)(2,1)} %feat_ref.1), channel_id=1, source_target_pairs={{0,6},{1,7},{2,4},{3,5},{4,2},{5,3},{6,0},{7,1},{8,14},{9,15},{10,... | collective-permute-start | bytes 393224 | tf_op jit(solution)/shard_map/ppermute | solution.py:21
  7.8 0.4 collective-permute-start.2
  8.2 3.1 %collective-permute-done.4.refs_0_ = bf16[512,128]{1,0:T(8,128)(2,1)S(1)} collective-permute-done((bf16[512,128]{1,0:T(8,128)(2,1)}, bf16[512,128]{1,0:T(8,128)(2,1)S(1)}, u32[]{:S(2)}, u32[]{:S(2)}) %collective-permute-start.4) | collective-permute-done | bytes 131104 | tf_op jit(solution)/shard_map/ppermute | solution.py:21
  11.4 1.7 %collective-permute-start.5 = (bf16[512,128]{1,0:T(8,128)(2,1)S(1)}, bf16[512,128]{1,0:T(8,128)(2,1)S(1)}, u32[]{:S(2)}, u32[]{:S(2)}) collective-permute-start(bf16[512,128]{1,0:T(8,128)(2,1)S(1)} %collective-permute-done.4.refs_0_), channel_id=1, source_target_pairs={{0,6},{1,7},{2,4},{3,5},{4,2},{5,3},{6,0},{7,1},{8,14},{9,15},{10,... | collective-permute-start | bytes 393224 | tf_op jit(solution)/shard_map/ppermute | solution.py:21
  13.1 0.5 collective-permute-start.6
  13.6 1.3 %collective-permute-start.7 = (bf16[512,128]{1,0:T(8,128)(2,1)S(1)}, bf16[512,128]{1,0:T(8,128)(2,1)S(1)}, u32[]{:S(2)}, u32[]{:S(2)}) collective-permute-start(bf16[512,128]{1,0:T(8,128)(2,1)S(1)} %collective-permute-done.4.refs_0_), channel_id=1, source_target_pairs={{0,4},{1,5},{2,6},{3,7},{4,0},{5,1},{6,2},{7,3},{8,12},{9,13},{10,... | collective-permute-start | bytes 393224 | tf_op jit(solution)/shard_map/ppermute | solution.py:21
  14.9 0.7 %copy-done = s32[60]{0:T(128)S(1)} copy-done((s32[60]{0:T(128)S(1)}, s32[60]{0:T(128)}, u32[]{:S(2)}) %copy-start) | copy-done | bytes 264
  15.5 0.7 %copy-done.1 = s32[60]{0:T(128)S(1)} copy-done((s32[60]{0:T(128)S(1)}, s32[60]{0:T(128)}, u32[]{:S(2)}) %copy-start.1) | copy-done | bytes 264
  16.2 3.1 %stage_arguments.1 = (bf16[60,128,128]{2,1,0:T(8,128)(2,1)S(1)}, bf16[128,256]{1,0:T(8,128)(2,1)S(1)}, bf16[128,256]{1,0:T(8,128)(2,1)S(1)}, f32[4,128,128]{2,1,...) custom-call(s32[1]{0:T(128)} %bitcast.me_ref, ...), custom_call_target="tpu_custom_call" | custom-call | flops 3300000000 | bytes 10800000 | tf_op jit(solution)/shard_map/stage_arguments/pallas_call | solution.py:364
  19.3 0.1 collective-permute-start.3
  19.4 1.0 %collective-permute-done.5.refs_1_ = bf16[512,128]{1,0:T(8,128)(2,1)S(1)} collective-permute-done((bf16[512,128]{1,0:T(8,128)(2,1)S(1)}, bf16[512,128]{1,0:T(8,128)(2,1)S(1)}, u32[]{:S(2)}, u32[]{:S(2)}) %collective-permute-start.5) | collective-permute-done | bytes 131104 | tf_op jit(solution)/shard_map/ppermute | solution.py:21
  20.4 0.6 %collective-permute-done.6.refs_2_ = bf16[512,128]{1,0:T(8,128)(2,1)S(1)} collective-permute-done((bf16[512,128]{1,0:T(8,128)(2,1)S(1)}, bf16[512,128]{1,0:T(8,128)(2,1)S(1)}, u32[]{:S(2)}, u32[]{:S(2)}) %collective-permute-start.6) | collective-permute-done | bytes 131104 | tf_op jit(solution)/shard_map/ppermute | solution.py:21
  21.0 0.1 collective-permute-done.7.refs_3_
  21.3 0.8 %forward_near.1.near_ref = f32[5,128,128]{2,1,0:T(8,128)S(1)} custom-call(s32[363]{0:T(512)S(4)} %get-tuple-element.37.index_ref, bf16[60,128,128]{2,1,0:T(8,128)(2,1)S(1)} %get-tuple-element.38.tiles_ref, bf16[4,512,128]{2,1,0:T(8,128)(2,1)S(1)} %pack_square.2.same_ref, bf16[4,512,128]{2,1,0:T(8,128)(2,1)S(1)} %collective-permute-done.3.other_ref), custom_call_target="tpu_custom_call" | custom-call | flops 110000000 | bytes 360000 | tf_op jit(solution)/shard_map/forward_near/pallas_call | solution.py:341
  22.2 1.0 %collective-permute-done.8.refs_1_ = bf16[4,512,128]{2,1,0:T(8,128)(2,1)S(1)} collective-permute-done((bf16[4,512,128]{2,1,0:T(8,128)(2,1)S(1)}, bf16[4,512,128]{2,1,0:T(8,128)(2,1)S(1)}, u32[]{:S(2)}, u32[]{:S(2)}) %collective-permute-start.8) | collective-permute-done | bytes 524320 | tf_op jit(solution)/shard_map/ppermute | solution.py:21
  23.2 2.6 %forward_layer.1 = (bf16[512,256]{1,0:T(8,128)(2,1)}, bf16[512,256]{1,0:T(8,128)(2,1)S(1)}, bf16[512,256]{1,0:T(8,128)(2,1)S(1)}, bf16[512,256]{1,0:T(8,128)(2,1...) custom-call(s32[363]{0:T(512)S(4)} %get-tuple-element.37.index_ref, ...), custom_call_target="tpu_custom_call" | custom-call | flops 3300000000 | bytes 10800000 | tf_op jit(solution)/shard_map/forward_layer/pallas_call | solution.py:341
  25.7 1.1 %backward_tiles.3.acc_ref = f32[33,128,128]{2,1,0:T(8,128)S(1)} custom-call(s32[363]{0:T(512)S(4)} %get-tuple-element.37.index_ref, bf16[60,128,128]{2,1,0:T(8,128)(2,1)S(1)} %get-tuple-element.38.tiles_ref, bf16[4,256,128]{2,1,0:T(8,128)(2,1)S(1)} %get-tuple-element.48.gt_ref), custom_call_target="tpu_custom_call" | custom-call | flops 1650000000 | bytes 5400000 | tf_op jit(solution)/shard_map/backward_tiles/pallas_call | solution.py:341
  26.9 0.1 collective-permute-start.14
  27.0 0.5 weights.1
  27.5 0.6 collective-permute-start.9
  28.1 1.1 %backward_tiles.2.acc_ref = f32[33,128,128]{2,1,0:T(8,128)S(1)} custom-call(s32[363]{0:T(512)S(4)} %get-tuple-element.37.index_ref, bf16[60,128,128]{2,1,0:T(8,128)(2,1)S(1)} %get-tuple-element.38.tiles_ref, bf16[4,256,128]{2,1,0:T(8,128)(2,1)S(1)} %get-tuple-element.48.gt_ref), custom_call_target="tpu_custom_call" | custom-call | flops 1650000000 | bytes 5400000 | tf_op jit(solution)/shard_map/backward_tiles/pallas_call | solution.py:341
  29.2 0.6 %collective-permute-done.9.wgot_ref = f32[128,256]{1,0:T(8,128)S(1)} collective-permute-done((f32[128,256]{1,0:T(8,128)S(1)}, f32[128,256]{1,0:T(8,128)S(1)}, u32[]{:S(2)}, u32[]{:S(2)}) %collective-permute-start.9) | collective-permute-done | bytes 131104 | tf_op jit(solution)/shard_map/ppermute | solution.py:21
  30.0 0.2 collective-permute-start.10
  30.2 0.1 pair_sum_weights.1
  30.3 1.4 %collective-permute-start.15 = (bf16[640,128]{1,0:T(8,128)(2,1)S(1)}, bf16[640,128]{1,0:T(8,128)(2,1)S(1)}, u32[]{:S(2)}, u32[]{:S(2)}) collective-permute-start(bf16[640,128]{1,0:T(8,128)(2,1)S(1)} %get-tuple-element.63), channel_id=1, source_target_pairs={{0,6},{1,7},{2,4},{3,5},{4,2},{5,3},{6,0},{7,1},{8,14},{9,15},{10,... | collective-permute-start | bytes 491528 | tf_op jit(solution)/shard_map/ppermute | solution.py:21
  31.7 0.5 collective-permute-start.16
  32.2 1.6 %collective-permute-start.17 = (bf16[640,128]{1,0:T(8,128)(2,1)S(1)}, bf16[640,128]{1,0:T(8,128)(2,1)S(1)}, u32[]{:S(2)}, u32[]{:S(2)}) collective-permute-start(bf16[640,128]{1,0:T(8,128)(2,1)S(1)} %get-tuple-element.65), channel_id=1, source_target_pairs={{0,4},{1,5},{2,6},{3,7},{4,0},{5,1},{6,2},{7,3},{8,12},{9,13},{10,... | collective-permute-start | bytes 491528 | tf_op jit(solution)/shard_map/ppermute | solution.py:21
  33.8 0.1 pair_sum.1
  33.9 1.4 %collective-permute-start.11 = (bf16[512,128]{1,0:T(8,128)(2,1)S(1)}, bf16[512,128]{1,0:T(8,128)(2,1)S(1)}, u32[]{:S(2)}, u32[]{:S(2)}) collective-permute-start(bf16[512,128]{1,0:T(8,128)(2,1)S(1)} %get-tuple-element.56), channel_id=1, source_target_pairs={{0,6},{1,7},{2,4},{3,5},{4,2},{5,3},{6,0},{7,1},{8,14},{9,15},{10,... | collective-permute-start | bytes 393224 | tf_op jit(solution)/shard_map/ppermute | solution.py:21
  35.3 0.5 collective-permute-start.12
  35.9 2.5 %collective-permute-done.15.refs_0_ = bf16[640,128]{1,0:T(8,128)(2,1)S(1)} collective-permute-done((bf16[640,128]{1,0:T(8,128)(2,1)S(1)}, bf16[640,128]{1,0:T(8,128)(2,1)S(1)}, u32[]{:S(2)}, u32[]{:S(2)}) %collective-permute-start.15) | collective-permute-done | bytes 163872 | tf_op jit(solution)/shard_map/ppermute | solution.py:21
  38.3 0.4 collective-permute-start.13
  38.7 3.2 %collective-permute-done.16.refs_1_ = bf16[640,128]{1,0:T(8,128)(2,1)S(1)} collective-permute-done((bf16[640,128]{1,0:T(8,128)(2,1)S(1)}, bf16[640,128]{1,0:T(8,128)(2,1)S(1)}, u32[]{:S(2)}, u32[]{:S(2)}) %collective-permute-start.16) | collective-permute-done | bytes 163872 | tf_op jit(solution)/shard_map/ppermute | solution.py:21
  41.9 0.1 collective-permute-done.17.refs_2_
  41.9 0.1 square_sum_weights.1
  42.0 1.7 %collective-permute-start.19 = (f32[32,256]{1,0:T(8,128)S(1)}, f32[32,256]{1,0:T(8,128)S(1)}, u32[]{:S(2)}, u32[]{:S(2)}) collective-permute-start(f32[32,256]{1,0:T(8,128)S(1)} %get-tuple-element.67.own_ref), channel_id=1, source_target_pairs={{0,8},{1,9},{2,10},{3,11},{4,12},{5,13},{6,14},{7,15},{8,0},{9,1},... | collective-permute-start | bytes 98312 | tf_op jit(solution)/shard_map/ppermute | solution.py:21
  43.7 3.3 %collective-permute-done.19.got_ref = f32[32,256]{1,0:T(8,128)S(1)} collective-permute-done((f32[32,256]{1,0:T(8,128)S(1)}, f32[32,256]{1,0:T(8,128)S(1)}, u32[]{:S(2)}, u32[]{:S(2)}) %collective-permute-start.19) | collective-permute-done | bytes 32800 | tf_op jit(solution)/shard_map/ppermute | solution.py:21
  47.0 2.0 %collective-permute-start.20 = (f32[32,256]{1,0:T(8,128)S(1)}, f32[32,256]{1,0:T(8,128)S(1)}, u32[]{:S(2)}, u32[]{:S(2)}) collective-permute-start(f32[32,256]{1,0:T(8,128)S(1)} %weight_sum.1.refs_0_), channel_id=1, source_target_pairs={{0,4},{1,5},{2,6},{3,7},{4,0},{5,1},{6,2},{7,3},{8,12},{9,13},{10,... | collective-permute-start | bytes 98312 | tf_op jit(solution)/shard_map/ppermute | solution.py:21
  49.0 1.6 %collective-permute-start.18 = (bf16[512,128]{1,0:T(8,128)(2,1)S(1)}, bf16[512,128]{1,0:T(8,128)(2,1)S(1)}, u32[]{:S(2)}, u32[]{:S(2)}) collective-permute-start(bf16[512,128]{1,0:T(8,128)(2,1)S(1)} %get-tuple-element.66), channel_id=1, source_target_pairs={{0,8},{1,9},{2,10},{3,11},{4,12},{5,13},{6,14},{7,15},{8,0},{9,1},... | collective-permute-start | bytes 393224 | tf_op jit(solution)/shard_map/ppermute | solution.py:21
  50.7 0.3 collective-permute-done.20.refs_1_
  50.9 1.5 %collective-permute-start.21 = (f32[2,32,256]{2,1,0:T(8,128)S(1)}, f32[2,32,256]{2,1,0:T(8,128)S(1)}, u32[]{:S(2)}, u32[]{:S(2)}) collective-permute-start(f32[2,32,256]{2,1,0:T(8,128)S(1)} %pack_weights.2.refs_0_), channel_id=1, source_target_pairs={{0,2},{1,3},{2,0},{3,1},{4,6},{5,7},{6,4},{7,5},{8,10},{9,11},{10,... | collective-permute-start | bytes 196616 | tf_op jit(solution)/shard_map/ppermute | solution.py:21
  52.5 0.3 near_sum.1.near_ref.refs_2_
  52.8 2.4 %collective-permute-done.21.refs_1_ = f32[2,32,256]{2,1,0:T(8,128)S(1)} collective-permute-done((f32[2,32,256]{2,1,0:T(8,128)S(1)}, f32[2,32,256]{2,1,0:T(8,128)S(1)}, u32[]{:S(2)}, u32[]{:S(2)}) %collective-permute-start.21) | collective-permute-done | bytes 65568 | tf_op jit(solution)/shard_map/ppermute | solution.py:21
  55.3 1.6 %collective-permute-done.18.refs_0_ = bf16[512,128]{1,0:T(8,128)(2,1)S(1)} collective-permute-done((bf16[512,128]{1,0:T(8,128)(2,1)S(1)}, bf16[512,128]{1,0:T(8,128)(2,1)S(1)}, u32[]{:S(2)}, u32[]{:S(2)}) %collective-permute-start.18) | collective-permute-done | bytes 131104 | tf_op jit(solution)/shard_map/ppermute | solution.py:21
  56.9 0.8 %grad_input_sum.1 = bf16[512,128]{1,0:T(8,128)(2,1)} custom-call(f32[512,128]{1,0:T(8,128)S(1)} %near_sum.1.near_ref.refs_2_, bf16[512,128]{1,0:T(8,128)(2,1)S(1)} %collective-permute-done.18.refs_0_), custom_call_target="tpu_custom_call" | custom-call | flops 11000000512 | bytes 36000000 | tf_op jit(solution)/shard_map/grad_input_sum/pallas_call | solution.py:341
  57.7 0.7 %write_weights.1 = (f32[128,256]{1,0:T(8,128)}, f32[128,256]{1,0:T(8,128)}) custom-call(s32[363]{0:T(512)S(4)} %get-tuple-element.37.index_ref, f32[2,2,32,256]{3,2,1,0:T(8,128)S(1)} %pack_weights.3.weight_ref, f32[2,2,32,256]{3,2,1,0:T(8,128)S(1)} %collective-permute-done.22.other_ref), custom_call_target="tpu_custom_call" | custom-call | flops 220000000 | bytes 720000 | tf_op jit(solution)/shard_map/write_weights/pallas_call | solution.py:341
  (22 shorter events, 0.4 us)
Async XLA Ops:
  0.6 10.7 %collective-permute-start.4 = (bf16[512,128]{1,0:T(8,128)(2,1)}, bf16[512,128]{1,0:T(8,128)(2,1)S(1)}, u32[]{:S(2)}, u32[]{:S(2)}) collective-permute-start(bf16[512,128]{1,0:T(8,128)(2,1)} %feat_ref.1), channel_id=1, source_target_pairs={{0,8},{1,9},{2,10},{3,11},{4,12},{5,13},{6,14},{7,15},{8,0},{9,1},... | collective-permute-start | bytes 393224 | tf_op jit(solution)/shard_map/ppermute | solution.py:21
  4.7 8.9 %collective-permute-start = (bf16[512,128]{1,0:T(8,128)(2,1)}, bf16[512,128]{1,0:T(8,128)(2,1)S(1)}, u32[]{:S(2)}, u32[]{:S(2)}) collective-permute-start(bf16[512,128]{1,0:T(8,128)(2,1)} %feat_ref.1), channel_id=1, source_target_pairs={{0,2},{1,3},{2,0},{3,1},{4,6},{5,7},{6,4},{7,5},{8,10},{9,11},{10,... | collective-permute-start | bytes 393224 | tf_op jit(solution)/shard_map/ppermute | solution.py:21
  6.3 13.0 %collective-permute-start.1 = (bf16[512,128]{1,0:T(8,128)(2,1)}, bf16[512,128]{1,0:T(8,128)(2,1)S(1)}, u32[]{:S(2)}, u32[]{:S(2)}) collective-permute-start(bf16[512,128]{1,0:T(8,128)(2,1)} %feat_ref.1), channel_id=1, source_target_pairs={{0,6},{1,7},{2,4},{3,5},{4,2},{5,3},{6,0},{7,1},{8,14},{9,15},{10,... | collective-permute-start | bytes 393224 | tf_op jit(solution)/shard_map/ppermute | solution.py:21
  7.8 11.5 %collective-permute-start.2 = (bf16[512,128]{1,0:T(8,128)(2,1)}, bf16[512,128]{1,0:T(8,128)(2,1)S(1)}, u32[]{:S(2)}, u32[]{:S(2)}) collective-permute-start(bf16[512,128]{1,0:T(8,128)(2,1)} %feat_ref.1), channel_id=1, source_target_pairs={{0,4},{1,5},{2,6},{3,7},{4,0},{5,1},{6,2},{7,3},{8,12},{9,13},{10,... | collective-permute-start | bytes 393224 | tf_op jit(solution)/shard_map/ppermute | solution.py:21
  11.4 9.1 %collective-permute-start.5 = (bf16[512,128]{1,0:T(8,128)(2,1)S(1)}, bf16[512,128]{1,0:T(8,128)(2,1)S(1)}, u32[]{:S(2)}, u32[]{:S(2)}) collective-permute-start(bf16[512,128]{1,0:T(8,128)(2,1)S(1)} %collective-permute-done.4.refs_0_), channel_id=1, source_target_pairs={{0,6},{1,7},{2,4},{3,5},{4,2},{5,3},{6,0},{7,1},{8,14},{9,15},{10,... | collective-permute-start | bytes 393224 | tf_op jit(solution)/shard_map/ppermute | solution.py:21
  13.1 7.9 %collective-permute-start.6 = (bf16[512,128]{1,0:T(8,128)(2,1)S(1)}, bf16[512,128]{1,0:T(8,128)(2,1)S(1)}, u32[]{:S(2)}, u32[]{:S(2)}) collective-permute-start(bf16[512,128]{1,0:T(8,128)(2,1)S(1)} %collective-permute-done.4.refs_0_), channel_id=1, source_target_pairs={{0,2},{1,3},{2,0},{3,1},{4,6},{5,7},{6,4},{7,5},{8,10},{9,11},{10,... | collective-permute-start | bytes 393224 | tf_op jit(solution)/shard_map/ppermute | solution.py:21
  13.6 7.6 %collective-permute-start.7 = (bf16[512,128]{1,0:T(8,128)(2,1)S(1)}, bf16[512,128]{1,0:T(8,128)(2,1)S(1)}, u32[]{:S(2)}, u32[]{:S(2)}) collective-permute-start(bf16[512,128]{1,0:T(8,128)(2,1)S(1)} %collective-permute-done.4.refs_0_), channel_id=1, source_target_pairs={{0,4},{1,5},{2,6},{3,7},{4,0},{5,1},{6,2},{7,3},{8,12},{9,13},{10,... | collective-permute-start | bytes 393224 | tf_op jit(solution)/shard_map/ppermute | solution.py:21
  14.8 0.7 %copy-start = (s32[60]{0:T(128)S(1)}, s32[60]{0:T(128)}, u32[]{:S(2)}) copy-start(s32[60]{0:T(128)} %trow_ref.1) | copy-start | bytes 724
  15.5 0.7 %copy-start.1 = (s32[60]{0:T(128)S(1)}, s32[60]{0:T(128)}, u32[]{:S(2)}) copy-start(s32[60]{0:T(128)} %tcol_ref.1) | copy-start | bytes 724
  19.3 2.0 %collective-permute-start.3 = (bf16[4,512,128]{2,1,0:T(8,128)(2,1)S(1)}, bf16[4,512,128]{2,1,0:T(8,128)(2,1)S(1)}, u32[]{:S(2)}, u32[]{:S(2)}) collective-permute-start(bf16[4,512,128]{2,1,0:T(8,128)(2,1)S(1)} %pack_square.2.same_ref), channel_id=1, source_target_pairs={{0,1},{1,0},{2,3},{3,2},{4,5},{5,4},{6,7},{7,6},{8,9},{9,8},{10,11... | collective-permute-start | bytes 1572872 | tf_op jit(solution)/shard_map/ppermute | solution.py:21
  21.2 2.0 %collective-permute-start.8 = (bf16[4,512,128]{2,1,0:T(8,128)(2,1)S(1)}, bf16[4,512,128]{2,1,0:T(8,128)(2,1)S(1)}, u32[]{:S(2)}, u32[]{:S(2)}) collective-permute-start(bf16[4,512,128]{2,1,0:T(8,128)(2,1)S(1)} %pack_square.3.refs_0_), channel_id=1, source_target_pairs={{0,1},{1,0},{2,3},{3,2},{4,5},{5,4},{6,7},{7,6},{8,9},{9,8},{10,11... | collective-permute-start | bytes 1572872 | tf_op jit(solution)/shard_map/ppermute | solution.py:21
  26.9 3.2 %collective-permute-start.14 = (f32[4,512,128]{2,1,0:T(8,128)S(1)}, f32[4,512,128]{2,1,0:T(8,128)S(1)}, u32[]{:S(2)}, u32[]{:S(2)}) collective-permute-start(f32[4,512,128]{2,1,0:T(8,128)S(1)} %send.2.refs_0_), channel_id=1, source_target_pairs={{0,1},{1,0},{2,3},{3,2},{4,5},{5,4},{6,7},{7,6},{8,9},{9,8},{10,11... | collective-permute-start | bytes 3145736 | tf_op jit(solution)/shard_map/ppermute | solution.py:21
  27.5 2.3 %collective-permute-start.9 = (f32[128,256]{1,0:T(8,128)S(1)}, f32[128,256]{1,0:T(8,128)S(1)}, u32[]{:S(2)}, u32[]{:S(2)}) collective-permute-start(f32[128,256]{1,0:T(8,128)S(1)} %get-tuple-element.53), channel_id=1, source_target_pairs={{0,1},{1,0},{2,3},{3,2},{4,5},{5,4},{6,7},{7,6},{8,9},{9,8},{10,11... | collective-permute-start | bytes 393224 | tf_op jit(solution)/shard_map/ppermute | solution.py:21
  30.0 3.9 %collective-permute-start.10 = (f32[4,512,128]{2,1,0:T(8,128)S(1)}, f32[4,512,128]{2,1,0:T(8,128)S(1)}, u32[]{:S(2)}, u32[]{:S(2)}) collective-permute-start(f32[4,512,128]{2,1,0:T(8,128)S(1)} %send.3), channel_id=1, source_target_pairs={{0,1},{1,0},{2,3},{3,2},{4,5},{5,4},{6,7},{7,6},{8,9},{9,8},{10,11... | collective-permute-start | bytes 3145736 | tf_op jit(solution)/shard_map/ppermute | solution.py:21
  30.3 8.0 %collective-permute-start.15 = (bf16[640,128]{1,0:T(8,128)(2,1)S(1)}, bf16[640,128]{1,0:T(8,128)(2,1)S(1)}, u32[]{:S(2)}, u32[]{:S(2)}) collective-permute-start(bf16[640,128]{1,0:T(8,128)(2,1)S(1)} %get-tuple-element.63), channel_id=1, source_target_pairs={{0,6},{1,7},{2,4},{3,5},{4,2},{5,3},{6,0},{7,1},{8,14},{9,15},{10,... | collective-permute-start | bytes 491528 | tf_op jit(solution)/shard_map/ppermute | solution.py:21
  31.7 10.2 %collective-permute-start.16 = (bf16[640,128]{1,0:T(8,128)(2,1)S(1)}, bf16[640,128]{1,0:T(8,128)(2,1)S(1)}, u32[]{:S(2)}, u32[]{:S(2)}) collective-permute-start(bf16[640,128]{1,0:T(8,128)(2,1)S(1)} %get-tuple-element.64), channel_id=1, source_target_pairs={{0,2},{1,3},{2,0},{3,1},{4,6},{5,7},{6,4},{7,5},{8,10},{9,11},{10,... | collective-permute-start | bytes 491528 | tf_op jit(solution)/shard_map/ppermute | solution.py:21
  32.2 9.7 %collective-permute-start.17 = (bf16[640,128]{1,0:T(8,128)(2,1)S(1)}, bf16[640,128]{1,0:T(8,128)(2,1)S(1)}, u32[]{:S(2)}, u32[]{:S(2)}) collective-permute-start(bf16[640,128]{1,0:T(8,128)(2,1)S(1)} %get-tuple-element.65), channel_id=1, source_target_pairs={{0,4},{1,5},{2,6},{3,7},{4,0},{5,1},{6,2},{7,3},{8,12},{9,13},{10,... | collective-permute-start | bytes 491528 | tf_op jit(solution)/shard_map/ppermute | solution.py:21
  33.9 18.5 %collective-permute-start.11 = (bf16[512,128]{1,0:T(8,128)(2,1)S(1)}, bf16[512,128]{1,0:T(8,128)(2,1)S(1)}, u32[]{:S(2)}, u32[]{:S(2)}) collective-permute-start(bf16[512,128]{1,0:T(8,128)(2,1)S(1)} %get-tuple-element.56), channel_id=1, source_target_pairs={{0,6},{1,7},{2,4},{3,5},{4,2},{5,3},{6,0},{7,1},{8,14},{9,15},{10,... | collective-permute-start | bytes 393224 | tf_op jit(solution)/shard_map/ppermute | solution.py:21
  35.3 17.2 %collective-permute-start.12 = (bf16[512,128]{1,0:T(8,128)(2,1)S(1)}, bf16[512,128]{1,0:T(8,128)(2,1)S(1)}, u32[]{:S(2)}, u32[]{:S(2)}) collective-permute-start(bf16[512,128]{1,0:T(8,128)(2,1)S(1)} %get-tuple-element.57), channel_id=1, source_target_pairs={{0,2},{1,3},{2,0},{3,1},{4,6},{5,7},{6,4},{7,5},{8,10},{9,11},{10,... | collective-permute-start | bytes 393224 | tf_op jit(solution)/shard_map/ppermute | solution.py:21
  38.3 14.2 %collective-permute-start.13 = (bf16[512,128]{1,0:T(8,128)(2,1)S(1)}, bf16[512,128]{1,0:T(8,128)(2,1)S(1)}, u32[]{:S(2)}, u32[]{:S(2)}) collective-permute-start(bf16[512,128]{1,0:T(8,128)(2,1)S(1)} %get-tuple-element.58), channel_id=1, source_target_pairs={{0,4},{1,5},{2,6},{3,7},{4,0},{5,1},{6,2},{7,3},{8,12},{9,13},{10,... | collective-permute-start | bytes 393224 | tf_op jit(solution)/shard_map/ppermute | solution.py:21
  42.0 5.0 %collective-permute-start.19 = (f32[32,256]{1,0:T(8,128)S(1)}, f32[32,256]{1,0:T(8,128)S(1)}, u32[]{:S(2)}, u32[]{:S(2)}) collective-permute-start(f32[32,256]{1,0:T(8,128)S(1)} %get-tuple-element.67.own_ref), channel_id=1, source_target_pairs={{0,8},{1,9},{2,10},{3,11},{4,12},{5,13},{6,14},{7,15},{8,0},{9,1},... | collective-permute-start | bytes 98312 | tf_op jit(solution)/shard_map/ppermute | solution.py:21
  47.0 3.9 %collective-permute-start.20 = (f32[32,256]{1,0:T(8,128)S(1)}, f32[32,256]{1,0:T(8,128)S(1)}, u32[]{:S(2)}, u32[]{:S(2)}) collective-permute-start(f32[32,256]{1,0:T(8,128)S(1)} %weight_sum.1.refs_0_), channel_id=1, source_target_pairs={{0,4},{1,5},{2,6},{3,7},{4,0},{5,1},{6,2},{7,3},{8,12},{9,13},{10,... | collective-permute-start | bytes 98312 | tf_op jit(solution)/shard_map/ppermute | solution.py:21
  49.0 7.9 %collective-permute-start.18 = (bf16[512,128]{1,0:T(8,128)(2,1)S(1)}, bf16[512,128]{1,0:T(8,128)(2,1)S(1)}, u32[]{:S(2)}, u32[]{:S(2)}) collective-permute-start(bf16[512,128]{1,0:T(8,128)(2,1)S(1)} %get-tuple-element.66), channel_id=1, source_target_pairs={{0,8},{1,9},{2,10},{3,11},{4,12},{5,13},{6,14},{7,15},{8,0},{9,1},... | collective-permute-start | bytes 393224 | tf_op jit(solution)/shard_map/ppermute | solution.py:21
  50.9 4.3 %collective-permute-start.21 = (f32[2,32,256]{2,1,0:T(8,128)S(1)}, f32[2,32,256]{2,1,0:T(8,128)S(1)}, u32[]{:S(2)}, u32[]{:S(2)}) collective-permute-start(f32[2,32,256]{2,1,0:T(8,128)S(1)} %pack_weights.2.refs_0_), channel_id=1, source_target_pairs={{0,2},{1,3},{2,0},{3,1},{4,6},{5,7},{6,4},{7,5},{8,10},{9,11},{10,... | collective-permute-start | bytes 196616 | tf_op jit(solution)/shard_map/ppermute | solution.py:21
  55.2 2.5 %collective-permute-start.22 = (f32[2,2,32,256]{3,2,1,0:T(8,128)S(1)}, f32[2,2,32,256]{3,2,1,0:T(8,128)S(1)}, u32[]{:S(2)}, u32[]{:S(2)}) collective-permute-start(f32[2,2,32,256]{3,2,1,0:T(8,128)S(1)} %pack_weights.3.weight_ref), channel_id=1, source_target_pairs={{0,1},{1,0},{2,3},{3,2},{4,5},{5,4},{6,7},{7,6},{8,9},{9,8},{10,11... | collective-permute-start | bytes 393224 | tf_op jit(solution)/shard_map/ppermute | solution.py:21

commit v13 on v12

--- a/solution.py
+++ b/solution.py
@@ -14,7 +14,7 @@
 ANY = pl.BlockSpec(memory_space=pl.ANY)
 MIB = 1024 * 1024
 LAST = ((1,), (1,))
-NEAR_COST, SQUARE_COST, MAIN_COST = 8, 4, 10
+NEAR_COST, SQUARE_COST, MAIN_COST = 0.2, 4, 10
 
 
 def swap(x, n, offset):
@@ -208,7 +208,8 @@
     wsend_ref[...] = wsum[1 - core]
 
 
-def backward_kernel(section, group, index_ref, tiles_ref, gt_ref, acc_ref):
+def backward_kernel(section, group, index_ref, tiles_ref, gt_ref, *refs):
+    acc_ref = refs[-1]
     block_local = gt_ref.shape[0]
     acc_ref[...] = jnp.zeros_like(acc_ref)
 
@@ -238,16 +239,17 @@
         ref[...] = wkeep_ref[span, :] + wgot_ref[span, :]
 
 
-def pair_kernel(square, acc_ref, got_ref, own_ref, *pieces):
-    block_local = own_ref.shape[0] // BLOCK
-    for q, ref in enumerate((own_ref, *pieces)):
+def pair_kernel(square, chips, acc_ref, got_ref, *refs):
+    refs = refs[-len(chips):]
+    block_local = got_ref.shape[1] // BLOCK
+    for q, ref in zip(chips, refs):
         for b in range(block_local):
             kept = acc_ref[(8 * square + 2 * q) * block_local + b]
             ref[rows_of(b), :] = (kept + got_ref[q, rows_of(b), :]).astype(ref.dtype)
 
 
 def pair_weights_kernel(square, acc_ref, got_ref, w1, w2, w3, own_ref, *pieces):
-    pair_kernel(square, acc_ref, got_ref, own_ref, *pieces)
+    pair_kernel(square, range(4), acc_ref, got_ref, own_ref, *pieces)
     nodes, lanes = own_ref.shape
     for weight_ref, ref in zip((w1, w2, w3), pieces):
         rows, columns = weight_ref.shape
@@ -406,43 +408,45 @@
         scratch_shapes=[pltpu.VMEM(far_squares, BF16)],
     )
 
+    wkeep, wsend = call(
+        weights_kernel, "weights", (weight, weight),
+        (index, high, low, scaled, raw, feat_t), [SMEM] + [VMEM] * 5, cost_us=1,
+        scratch_shapes=[pltpu.VMEM((2, feat_in, hidden), F32)])
+    w0, w1, w2, w3 = call(
+        cut_kernel, "cut_weights", (chunk,) * 4, (index, wkeep, swap(wsend, n, 1)),
+        [SMEM, VMEM, VMEM])
+
     send_shape = result((4, nodes, feat_in), F32)
     sums, got = [], [None] * squares
-    after = None
     for section, shape in ((1, far_squares), (0, near_square)):
         acc = call(
             functools.partial(backward_kernel, section, group), "backward_tiles",
-            result((shape[0] + 1,) + shape[1:], F32), (index, tiles_near, gt), [SMEM, VMEM, VMEM],
-            cost_us=1.5)
+            result((shape[0] + 1,) + shape[1:], F32), (index, tiles_near, gt, wkeep),
+            [SMEM] + [VMEM] * 3, cost_us=1.5 if section else 0.3)
         sums.insert(0, acc)
         for s in range(squares - 1, 0, -1) if section else (0,):
-            operands = (acc,) if section else (acc, w0)
+            operands = (acc, wkeep if section else w0)
             send = call(functools.partial(send_kernel, s - section), "send", send_shape, operands)
             got[s] = swap(send, n, 1)
-            after = send if after is None else after
-        if section:
-            wkeep, wsend = call(
-                weights_kernel, "weights", (weight, weight),
-                (index, high, low, scaled, raw, feat_t, after), [SMEM] + [VMEM] * 6, cost_us=1,
-                scratch_shapes=[pltpu.VMEM((2, feat_in, hidden), F32)])
-            w0, w1, w2, w3 = call(
-                cut_kernel, "cut_weights", (chunk,) * 4, (index, wkeep, swap(wsend, n, 1)),
-                [SMEM, VMEM, VMEM])
 
     extra = result((nodes + 2 * chunk.shape[0] * (hidden // feat_in), feat_in), BF16)
-    terms = [None] * squares
-    for s in range(squares - 1, -1, -1):
-        operands = (sums[min(s, 1)], got[s])
+    terms = [[]]
+    for s in range(1, squares):
+        operands = (sums[1], got[s])
         if s == squares - 1:
             own, *pieces = call(
-                functools.partial(pair_weights_kernel, max(s - 1, 0)), "pair_sum_weights", (wide, extra, extra, extra),
-                operands + (w1, w2, w3))
+                functools.partial(pair_weights_kernel, s - 1), "pair_sum_weights",
+                (wide, extra, extra, extra), operands + (w1, w2, w3))
         else:
             own, *pieces = call(
-                functools.partial(pair_kernel, max(s - 1, 0)), "pair_sum", (wide, piece, piece, piece), operands)
-        terms[s] = [own, *[swap(pieces[q - 1], n, 2 * q) for q in (3, 1, 2)]]
-    near_total = call(near_kernel, "near_sum", wide, (high, low, ws, *terms[0]), cost_us=NEAR_COST)
-    terms[0] = [near_total]
+                functools.partial(pair_kernel, s - 1, range(4)), "pair_sum",
+                (wide, piece, piece, piece), operands)
+        terms.append([own, *[swap(pieces[q - 1], n, 2 * q) for q in (3, 1, 2)]])
+    near_operands = (sums[0], got[0])
+    own, *pieces = call(
+        functools.partial(pair_kernel, 0, (0, 3, 1)), "pair_sum", (wide, piece, piece),
+        near_operands)
+    near = [own, swap(pieces[0], n, 6), swap(pieces[1], n, 2)]
     distance = 1
     while distance < squares:
         for s in range(squares - distance, 0, -2 * distance):
@@ -454,6 +458,11 @@
                 total = call(add_kernel, "square_sum", piece, terms[s], cost_us=SQUARE_COST)
             terms[s - distance].append(swap(total, n, 8 * distance))
         distance *= 2
+    later = call(
+        functools.partial(pair_kernel, 0, (2,)), "pair_sum_later", piece, near_operands + (total,))
+    near.append(swap(later, n, 4))
+    near_total = call(near_kernel, "near_sum", wide, (high, low, ws, *near), cost_us=NEAR_COST)
+    terms[0].insert(0, near_total)
     bit = 8
     while bit < n:
         wsum = call(add_two_kernel, "weight_sum", chunk, (wsum, swap(wsum, n, bit)))

time: 58.4 us -> 58 us (level)
  waiting for transfers between devices: 19.9 us -> 18.5 us
  starting transfers between devices: 24.9 us -> 25.7 us
    ppermute x23, waiting for transfers between devices: 19.9 us -> 18.5 us  [swap(): return lax.ppermute(x, 'row', [(i, i ^ offset) for i in range(n)])]
    ppermute x23, starting transfers between devices: 24.9 us -> 25.7 us  [swap(): return lax.ppermute(x, 'row', [(i, i ^ offset) for i in range(n)])]
    pallas_call x19 -> x20, Pallas kernels: 8.47 us -> 8.49 us  [call(): pl.pallas_call(kernel, out_shape=out_shape, in_specs=specs, out_specs=out...]
  transfers between devices with their start and end apart: 23 -> 23, of which waited for: 13 -> 12; matrix products, arithmetic and copies ran while one was open for 0% -> 0% of each run, Pallas kernels for 12% -> 13%
where the time goes in v13:
time: 58 us; the launch traced here: 57.8 us
  starting transfers between devices  25.7 us (44%)
  waiting for transfers between devices  18.5 us (32%)
  Pallas kernels  11.6 us (20%)
  local copies, waits for them, and re-layouts  1.31 us (2%)
  between operations  0.81 us (1%)
    ppermute x23, starting transfers between devices, swap(): return lax.ppermute(x, 'row', [(i, i ^ offset) for i in range(n)])  25.7 us
    ppermute x23, waiting for transfers between devices, swap(): return lax.ppermute(x, 'row', [(i, i ^ offset) for i in range(n)])  18.5 us
    pallas_call x20, Pallas kernels, call(): pl.pallas_call(kernel, out_shape=out_shape, in_specs=specs, out_specs=out...  8.49 us
    pallas_call x1, Pallas kernels, body(): pl.pallas_call(functools.partial(stage_kernel, (8 * block_local, (n - 8)...  3.09 us
    unnamed x4, local copies, waits for them, and re-layouts  1.31 us
  transfers between devices with their start and end apart: 23, of which 12 were waited for; matrix products, arithmetic and copies ran while one was open for 0% of the time, Pallas kernels for 13%

profile of v13, /device:TPU:0, one launch (start us, length us, event | category | flops | bytes accessed | tf_op | source)
XLA Modules:
  0.0 57.8 jit_solution(15713974274131350903)
XLA Ops:
  0.6 4.1 %collective-permute-start.4 = (bf16[512,128]{1,0:T(8,128)(2,1)}, bf16[512,128]{1,0:T(8,128)(2,1)S(1)}, u32[]{:S(2)}, u32[]{:S(2)}) collective-permute-start(bf16[512,128]{1,0:T(8,128)(2,1)} %feat_ref.1), channel_id=1, source_target_pairs={{0,8},{1,9},{2,10},{3,11},{4,12},{5,13},{6,14},{7,15},{8,0},{9,1},... | collective-permute-start | bytes 393224 | tf_op jit(solution)/shard_map/ppermute | solution.py:21
  4.7 1.5 %collective-permute-start = (bf16[512,128]{1,0:T(8,128)(2,1)}, bf16[512,128]{1,0:T(8,128)(2,1)S(1)}, u32[]{:S(2)}, u32[]{:S(2)}) collective-permute-start(bf16[512,128]{1,0:T(8,128)(2,1)} %feat_ref.1), channel_id=1, source_target_pairs={{0,2},{1,3},{2,0},{3,1},{4,6},{5,7},{6,4},{7,5},{8,10},{9,11},{10,... | collective-permute-start | bytes 393224 | tf_op jit(solution)/shard_map/ppermute | solution.py:21
  6.3 1.5 %collective-permute-start.1 = (bf16[512,128]{1,0:T(8,128)(2,1)}, bf16[512,128]{1,0:T(8,128)(2,1)S(1)}, u32[]{:S(2)}, u32[]{:S(2)}) collective-permute-start(bf16[512,128]{1,0:T(8,128)(2,1)} %feat_ref.1), channel_id=1, source_target_pairs={{0,6},{1,7},{2,4},{3,5},{4,2},{5,3},{6,0},{7,1},{8,14},{9,15},{10,... | collective-permute-start | bytes 393224 | tf_op jit(solution)/shard_map/ppermute | solution.py:21
  7.8 0.4 collective-permute-start.2
  8.2 3.1 %collective-permute-done.4.refs_0_ = bf16[512,128]{1,0:T(8,128)(2,1)S(1)} collective-permute-done((bf16[512,128]{1,0:T(8,128)(2,1)}, bf16[512,128]{1,0:T(8,128)(2,1)S(1)}, u32[]{:S(2)}, u32[]{:S(2)}) %collective-permute-start.4) | collective-permute-done | bytes 131104 | tf_op jit(solution)/shard_map/ppermute | solution.py:21
  11.4 1.7 %collective-permute-start.5 = (bf16[512,128]{1,0:T(8,128)(2,1)S(1)}, bf16[512,128]{1,0:T(8,128)(2,1)S(1)}, u32[]{:S(2)}, u32[]{:S(2)}) collective-permute-start(bf16[512,128]{1,0:T(8,128)(2,1)S(1)} %collective-permute-done.4.refs_0_), channel_id=1, source_target_pairs={{0,6},{1,7},{2,4},{3,5},{4,2},{5,3},{6,0},{7,1},{8,14},{9,15},{10,... | collective-permute-start | bytes 393224 | tf_op jit(solution)/shard_map/ppermute | solution.py:21
  13.1 0.5 collective-permute-start.6
  13.6 1.3 %collective-permute-start.7 = (bf16[512,128]{1,0:T(8,128)(2,1)S(1)}, bf16[512,128]{1,0:T(8,128)(2,1)S(1)}, u32[]{:S(2)}, u32[]{:S(2)}) collective-permute-start(bf16[512,128]{1,0:T(8,128)(2,1)S(1)} %collective-permute-done.4.refs_0_), channel_id=1, source_target_pairs={{0,4},{1,5},{2,6},{3,7},{4,0},{5,1},{6,2},{7,3},{8,12},{9,13},{10,... | collective-permute-start | bytes 393224 | tf_op jit(solution)/shard_map/ppermute | solution.py:21
  14.9 0.7 %copy-done = s32[60]{0:T(128)S(1)} copy-done((s32[60]{0:T(128)S(1)}, s32[60]{0:T(128)}, u32[]{:S(2)}) %copy-start) | copy-done | bytes 264
  15.5 0.7 %copy-done.1 = s32[60]{0:T(128)S(1)} copy-done((s32[60]{0:T(128)S(1)}, s32[60]{0:T(128)}, u32[]{:S(2)}) %copy-start.1) | copy-done | bytes 264
  16.2 3.1 %stage_arguments.1 = (bf16[60,128,128]{2,1,0:T(8,128)(2,1)S(1)}, bf16[128,256]{1,0:T(8,128)(2,1)S(1)}, bf16[128,256]{1,0:T(8,128)(2,1)S(1)}, f32[4,128,128]{2,1,...) custom-call(s32[1]{0:T(128)} %bitcast.me_ref, ...), custom_call_target="tpu_custom_call" | custom-call | flops 3300000000 | bytes 10800000 | tf_op jit(solution)/shard_map/stage_arguments/pallas_call | solution.py:366
  19.3 0.1 collective-permute-start.3
  19.4 1.0 %collective-permute-done.5.refs_1_ = bf16[512,128]{1,0:T(8,128)(2,1)S(1)} collective-permute-done((bf16[512,128]{1,0:T(8,128)(2,1)S(1)}, bf16[512,128]{1,0:T(8,128)(2,1)S(1)}, u32[]{:S(2)}, u32[]{:S(2)}) %collective-permute-start.5) | collective-permute-done | bytes 131104 | tf_op jit(solution)/shard_map/ppermute | solution.py:21
  20.4 0.6 %collective-permute-done.6.refs_2_ = bf16[512,128]{1,0:T(8,128)(2,1)S(1)} collective-permute-done((bf16[512,128]{1,0:T(8,128)(2,1)S(1)}, bf16[512,128]{1,0:T(8,128)(2,1)S(1)}, u32[]{:S(2)}, u32[]{:S(2)}) %collective-permute-start.6) | collective-permute-done | bytes 131104 | tf_op jit(solution)/shard_map/ppermute | solution.py:21
  21.0 0.1 collective-permute-done.7.refs_3_
  21.3 0.8 %forward_near.1.near_ref = f32[5,128,128]{2,1,0:T(8,128)S(1)} custom-call(s32[363]{0:T(512)S(4)} %get-tuple-element.36.index_ref, bf16[60,128,128]{2,1,0:T(8,128)(2,1)S(1)} %get-tuple-element.37.tiles_ref, bf16[4,512,128]{2,1,0:T(8,128)(2,1)S(1)} %pack_square.2.same_ref, bf16[4,512,128]{2,1,0:T(8,128)(2,1)S(1)} %collective-permute-done.3.other_ref), custom_call_target="tpu_custom_call" | custom-call | flops 110000000 | bytes 360000 | tf_op jit(solution)/shard_map/forward_near/pallas_call | solution.py:343
  22.2 1.0 %collective-permute-done.8.refs_1_ = bf16[4,512,128]{2,1,0:T(8,128)(2,1)S(1)} collective-permute-done((bf16[4,512,128]{2,1,0:T(8,128)(2,1)S(1)}, bf16[4,512,128]{2,1,0:T(8,128)(2,1)S(1)}, u32[]{:S(2)}, u32[]{:S(2)}) %collective-permute-start.8) | collective-permute-done | bytes 524320 | tf_op jit(solution)/shard_map/ppermute | solution.py:21
  23.2 2.6 %forward_layer.1 = (bf16[512,256]{1,0:T(8,128)(2,1)}, bf16[512,256]{1,0:T(8,128)(2,1)S(1)}, bf16[512,256]{1,0:T(8,128)(2,1)S(1)}, bf16[512,256]{1,0:T(8,128)(2,1...) custom-call(s32[363]{0:T(512)S(4)} %get-tuple-element.36.index_ref, ...), custom_call_target="tpu_custom_call" | custom-call | flops 3300000000 | bytes 10800000 | tf_op jit(solution)/shard_map/forward_layer/pallas_call | solution.py:343
  25.7 0.5 weights.1
  26.2 0.2 collective-permute-start.9
  26.5 1.1 %backward_tiles.3.acc_ref = f32[33,128,128]{2,1,0:T(8,128)S(1)} custom-call(s32[363]{0:T(512)S(4)} %get-tuple-element.36.index_ref, bf16[60,128,128]{2,1,0:T(8,128)(2,1)S(1)} %get-tuple-element.37.tiles_ref, bf16[4,256,128]{2,1,0:T(8,128)(2,1)S(1)} %get-tuple-element.47.gt_ref, f32[128,256]{1,0:T(8,128)S(1)} %get-tuple-element.51.refs_0_.wkeep_ref), custom_call_target="tpu_custom_call" | custom-call | flops 1650000000 | bytes 5400000 | tf_op jit(solution)/shard_map/backward_tiles/pallas_call | solution.py:343
  27.7 0.4 collective-permute-start.13
  28.1 1.1 %backward_tiles.2.acc_ref = f32[33,128,128]{2,1,0:T(8,128)S(1)} custom-call(s32[363]{0:T(512)S(4)} %get-tuple-element.36.index_ref, bf16[60,128,128]{2,1,0:T(8,128)(2,1)S(1)} %get-tuple-element.37.tiles_ref, bf16[4,256,128]{2,1,0:T(8,128)(2,1)S(1)} %get-tuple-element.47.gt_ref, f32[128,256]{1,0:T(8,128)S(1)} %get-tuple-element.51.refs_0_.wkeep_ref), custom_call_target="tpu_custom_call" | custom-call | flops 330000000 | bytes 1080000 | tf_op jit(solution)/shard_map/backward_tiles/pallas_call | solution.py:343
  29.3 0.5 collective-permute-start.10
  29.9 0.5 collective-permute-done.13.got_ref
  30.4 0.1 pair_sum_weights.1
  30.5 0.8 %collective-permute-start.14 = (bf16[640,128]{1,0:T(8,128)(2,1)S(1)}, bf16[640,128]{1,0:T(8,128)(2,1)S(1)}, u32[]{:S(2)}, u32[]{:S(2)}) collective-permute-start(bf16[640,128]{1,0:T(8,128)(2,1)S(1)} %get-tuple-element.61), channel_id=1, source_target_pairs={{0,6},{1,7},{2,4},{3,5},{4,2},{5,3},{6,0},{7,1},{8,14},{9,15},{10,... | collective-permute-start | bytes 491528 | tf_op jit(solution)/shard_map/ppermute | solution.py:21
  31.3 1.0 %collective-permute-start.15 = (bf16[640,128]{1,0:T(8,128)(2,1)S(1)}, bf16[640,128]{1,0:T(8,128)(2,1)S(1)}, u32[]{:S(2)}, u32[]{:S(2)}) collective-permute-start(bf16[640,128]{1,0:T(8,128)(2,1)S(1)} %get-tuple-element.62), channel_id=1, source_target_pairs={{0,2},{1,3},{2,0},{3,1},{4,6},{5,7},{6,4},{7,5},{8,10},{9,11},{10,... | collective-permute-start | bytes 491528 | tf_op jit(solution)/shard_map/ppermute | solution.py:21
  32.3 1.8 %collective-permute-start.16 = (bf16[640,128]{1,0:T(8,128)(2,1)S(1)}, bf16[640,128]{1,0:T(8,128)(2,1)S(1)}, u32[]{:S(2)}, u32[]{:S(2)}) collective-permute-start(bf16[640,128]{1,0:T(8,128)(2,1)S(1)} %get-tuple-element.63), channel_id=1, source_target_pairs={{0,4},{1,5},{2,6},{3,7},{4,0},{5,1},{6,2},{7,3},{8,12},{9,13},{10,... | collective-permute-start | bytes 491528 | tf_op jit(solution)/shard_map/ppermute | solution.py:21
  34.1 0.1 pair_sum.1
  34.1 0.8 %collective-permute-start.11 = (bf16[512,128]{1,0:T(8,128)(2,1)S(1)}, bf16[512,128]{1,0:T(8,128)(2,1)S(1)}, u32[]{:S(2)}, u32[]{:S(2)}) collective-permute-start(bf16[512,128]{1,0:T(8,128)(2,1)S(1)} %get-tuple-element.55), channel_id=1, source_target_pairs={{0,6},{1,7},{2,4},{3,5},{4,2},{5,3},{6,0},{7,1},{8,14},{9,15},{10,... | collective-permute-start | bytes 393224 | tf_op jit(solution)/shard_map/ppermute | solution.py:21
  34.9 1.0 %collective-permute-start.12 = (bf16[512,128]{1,0:T(8,128)(2,1)S(1)}, bf16[512,128]{1,0:T(8,128)(2,1)S(1)}, u32[]{:S(2)}, u32[]{:S(2)}) collective-permute-start(bf16[512,128]{1,0:T(8,128)(2,1)S(1)} %get-tuple-element.56), channel_id=1, source_target_pairs={{0,2},{1,3},{2,0},{3,1},{4,6},{5,7},{6,4},{7,5},{8,10},{9,11},{10,... | collective-permute-start | bytes 393224 | tf_op jit(solution)/shard_map/ppermute | solution.py:21
  35.9 2.6 %collective-permute-done.14.refs_0_ = bf16[640,128]{1,0:T(8,128)(2,1)S(1)} collective-permute-done((bf16[640,128]{1,0:T(8,128)(2,1)S(1)}, bf16[640,128]{1,0:T(8,128)(2,1)S(1)}, u32[]{:S(2)}, u32[]{:S(2)}) %collective-permute-start.14) | collective-permute-done | bytes 163872 | tf_op jit(solution)/shard_map/ppermute | solution.py:21
  38.5 3.6 %collective-permute-done.15.refs_1_ = bf16[640,128]{1,0:T(8,128)(2,1)S(1)} collective-permute-done((bf16[640,128]{1,0:T(8,128)(2,1)S(1)}, bf16[640,128]{1,0:T(8,128)(2,1)S(1)}, u32[]{:S(2)}, u32[]{:S(2)}) %collective-permute-start.15) | collective-permute-done | bytes 163872 | tf_op jit(solution)/shard_map/ppermute | solution.py:21
  42.1 0.1 square_sum_weights.1
  42.2 1.8 %collective-permute-start.19 = (f32[32,256]{1,0:T(8,128)S(1)}, f32[32,256]{1,0:T(8,128)S(1)}, u32[]{:S(2)}, u32[]{:S(2)}) collective-permute-start(f32[32,256]{1,0:T(8,128)S(1)} %get-tuple-element.65.own_ref), channel_id=1, source_target_pairs={{0,8},{1,9},{2,10},{3,11},{4,12},{5,13},{6,14},{7,15},{8,0},{9,1},... | collective-permute-start | bytes 98312 | tf_op jit(solution)/shard_map/ppermute | solution.py:21
  44.0 1.9 %collective-permute-start.17 = (bf16[512,128]{1,0:T(8,128)(2,1)S(1)}, bf16[512,128]{1,0:T(8,128)(2,1)S(1)}, u32[]{:S(2)}, u32[]{:S(2)}) collective-permute-start(bf16[512,128]{1,0:T(8,128)(2,1)S(1)} %pair_sum_later.1), channel_id=1, source_target_pairs={{0,4},{1,5},{2,6},{3,7},{4,0},{5,1},{6,2},{7,3},{8,12},{9,13},{10,... | collective-permute-start | bytes 393224 | tf_op jit(solution)/shard_map/ppermute | solution.py:21
  45.8 1.7 %collective-permute-done.19.got_ref = f32[32,256]{1,0:T(8,128)S(1)} collective-permute-done((f32[32,256]{1,0:T(8,128)S(1)}, f32[32,256]{1,0:T(8,128)S(1)}, u32[]{:S(2)}, u32[]{:S(2)}) %collective-permute-start.19) | collective-permute-done | bytes 32800 | tf_op jit(solution)/shard_map/ppermute | solution.py:21
  47.5 0.4 collective-permute-start.20
  47.9 2.9 %collective-permute-start.18 = (bf16[512,128]{1,0:T(8,128)(2,1)S(1)}, bf16[512,128]{1,0:T(8,128)(2,1)S(1)}, u32[]{:S(2)}, u32[]{:S(2)}) collective-permute-start(bf16[512,128]{1,0:T(8,128)(2,1)S(1)} %get-tuple-element.64.refs_0_), channel_id=1, source_target_pairs={{0,8},{1,9},{2,10},{3,11},{4,12},{5,13},{6,14},{7,15},{8,0},{9,1},... | collective-permute-start | bytes 393224 | tf_op jit(solution)/shard_map/ppermute | solution.py:21
  50.8 0.6 %collective-permute-done.20.refs_1_ = f32[32,256]{1,0:T(8,128)S(1)} collective-permute-done((f32[32,256]{1,0:T(8,128)S(1)}, f32[32,256]{1,0:T(8,128)S(1)}, u32[]{:S(2)}, u32[]{:S(2)}) %collective-permute-start.20) | collective-permute-done | bytes 32800 | tf_op jit(solution)/shard_map/ppermute | solution.py:21
  51.4 0.9 %collective-permute-start.21 = (f32[2,32,256]{2,1,0:T(8,128)S(1)}, f32[2,32,256]{2,1,0:T(8,128)S(1)}, u32[]{:S(2)}, u32[]{:S(2)}) collective-permute-start(f32[2,32,256]{2,1,0:T(8,128)S(1)} %pack_weights.2.refs_0_), channel_id=1, source_target_pairs={{0,2},{1,3},{2,0},{3,1},{4,6},{5,7},{6,4},{7,5},{8,10},{9,11},{10,... | collective-permute-start | bytes 196616 | tf_op jit(solution)/shard_map/ppermute | solution.py:21
  52.4 0.3 near_sum.1.near_ref.refs_2_
  52.7 3.0 %collective-permute-done.21.refs_1_ = f32[2,32,256]{2,1,0:T(8,128)S(1)} collective-permute-done((f32[2,32,256]{2,1,0:T(8,128)S(1)}, f32[2,32,256]{2,1,0:T(8,128)S(1)}, u32[]{:S(2)}, u32[]{:S(2)}) %collective-permute-start.21) | collective-permute-done | bytes 65568 | tf_op jit(solution)/shard_map/ppermute | solution.py:21
  55.7 0.1 collective-permute-start.22
  55.8 0.8 %grad_input_sum.1 = bf16[512,128]{1,0:T(8,128)(2,1)} custom-call(f32[512,128]{1,0:T(8,128)S(1)} %near_sum.1.near_ref.refs_2_, bf16[512,128]{1,0:T(8,128)(2,1)S(1)} %collective-permute-done.18.refs_0_), custom_call_target="tpu_custom_call" | custom-call | flops 11000000512 | bytes 36000000 | tf_op jit(solution)/shard_map/grad_input_sum/pallas_call | solution.py:343
  56.6 0.6 collective-permute-done.22.other_ref
  57.1 0.7 %write_weights.1 = (f32[128,256]{1,0:T(8,128)}, f32[128,256]{1,0:T(8,128)}) custom-call(s32[363]{0:T(512)S(4)} %get-tuple-element.36.index_ref, f32[2,2,32,256]{3,2,1,0:T(8,128)S(1)} %pack_weights.3.weight_ref, f32[2,2,32,256]{3,2,1,0:T(8,128)S(1)} %collective-permute-done.22.other_ref), custom_call_target="tpu_custom_call" | custom-call | flops 220000000 | bytes 720000 | tf_op jit(solution)/shard_map/write_weights/pallas_call | solution.py:343
  (23 shorter events, 0.4 us)
Async XLA Ops:
  0.6 10.7 %collective-permute-start.4 = (bf16[512,128]{1,0:T(8,128)(2,1)}, bf16[512,128]{1,0:T(8,128)(2,1)S(1)}, u32[]{:S(2)}, u32[]{:S(2)}) collective-permute-start(bf16[512,128]{1,0:T(8,128)(2,1)} %feat_ref.1), channel_id=1, source_target_pairs={{0,8},{1,9},{2,10},{3,11},{4,12},{5,13},{6,14},{7,15},{8,0},{9,1},... | collective-permute-start | bytes 393224 | tf_op jit(solution)/shard_map/ppermute | solution.py:21
  4.7 8.9 %collective-permute-start = (bf16[512,128]{1,0:T(8,128)(2,1)}, bf16[512,128]{1,0:T(8,128)(2,1)S(1)}, u32[]{:S(2)}, u32[]{:S(2)}) collective-permute-start(bf16[512,128]{1,0:T(8,128)(2,1)} %feat_ref.1), channel_id=1, source_target_pairs={{0,2},{1,3},{2,0},{3,1},{4,6},{5,7},{6,4},{7,5},{8,10},{9,11},{10,... | collective-permute-start | bytes 393224 | tf_op jit(solution)/shard_map/ppermute | solution.py:21
  6.3 13.0 %collective-permute-start.1 = (bf16[512,128]{1,0:T(8,128)(2,1)}, bf16[512,128]{1,0:T(8,128)(2,1)S(1)}, u32[]{:S(2)}, u32[]{:S(2)}) collective-permute-start(bf16[512,128]{1,0:T(8,128)(2,1)} %feat_ref.1), channel_id=1, source_target_pairs={{0,6},{1,7},{2,4},{3,5},{4,2},{5,3},{6,0},{7,1},{8,14},{9,15},{10,... | collective-permute-start | bytes 393224 | tf_op jit(solution)/shard_map/ppermute | solution.py:21
  7.8 11.5 %collective-permute-start.2 = (bf16[512,128]{1,0:T(8,128)(2,1)}, bf16[512,128]{1,0:T(8,128)(2,1)S(1)}, u32[]{:S(2)}, u32[]{:S(2)}) collective-permute-start(bf16[512,128]{1,0:T(8,128)(2,1)} %feat_ref.1), channel_id=1, source_target_pairs={{0,4},{1,5},{2,6},{3,7},{4,0},{5,1},{6,2},{7,3},{8,12},{9,13},{10,... | collective-permute-start | bytes 393224 | tf_op jit(solution)/shard_map/ppermute | solution.py:21
  11.4 9.1 %collective-permute-start.5 = (bf16[512,128]{1,0:T(8,128)(2,1)S(1)}, bf16[512,128]{1,0:T(8,128)(2,1)S(1)}, u32[]{:S(2)}, u32[]{:S(2)}) collective-permute-start(bf16[512,128]{1,0:T(8,128)(2,1)S(1)} %collective-permute-done.4.refs_0_), channel_id=1, source_target_pairs={{0,6},{1,7},{2,4},{3,5},{4,2},{5,3},{6,0},{7,1},{8,14},{9,15},{10,... | collective-permute-start | bytes 393224 | tf_op jit(solution)/shard_map/ppermute | solution.py:21
  13.1 7.9 %collective-permute-start.6 = (bf16[512,128]{1,0:T(8,128)(2,1)S(1)}, bf16[512,128]{1,0:T(8,128)(2,1)S(1)}, u32[]{:S(2)}, u32[]{:S(2)}) collective-permute-start(bf16[512,128]{1,0:T(8,128)(2,1)S(1)} %collective-permute-done.4.refs_0_), channel_id=1, source_target_pairs={{0,2},{1,3},{2,0},{3,1},{4,6},{5,7},{6,4},{7,5},{8,10},{9,11},{10,... | collective-permute-start | bytes 393224 | tf_op jit(solution)/shard_map/ppermute | solution.py:21
  13.6 7.6 %collective-permute-start.7 = (bf16[512,128]{1,0:T(8,128)(2,1)S(1)}, bf16[512,128]{1,0:T(8,128)(2,1)S(1)}, u32[]{:S(2)}, u32[]{:S(2)}) collective-permute-start(bf16[512,128]{1,0:T(8,128)(2,1)S(1)} %collective-permute-done.4.refs_0_), channel_id=1, source_target_pairs={{0,4},{1,5},{2,6},{3,7},{4,0},{5,1},{6,2},{7,3},{8,12},{9,13},{10,... | collective-permute-start | bytes 393224 | tf_op jit(solution)/shard_map/ppermute | solution.py:21
  14.8 0.7 %copy-start = (s32[60]{0:T(128)S(1)}, s32[60]{0:T(128)}, u32[]{:S(2)}) copy-start(s32[60]{0:T(128)} %trow_ref.1) | copy-start | bytes 724
  15.5 0.7 %copy-start.1 = (s32[60]{0:T(128)S(1)}, s32[60]{0:T(128)}, u32[]{:S(2)}) copy-start(s32[60]{0:T(128)} %tcol_ref.1) | copy-start | bytes 724
  19.3 2.0 %collective-permute-start.3 = (bf16[4,512,128]{2,1,0:T(8,128)(2,1)S(1)}, bf16[4,512,128]{2,1,0:T(8,128)(2,1)S(1)}, u32[]{:S(2)}, u32[]{:S(2)}) collective-permute-start(bf16[4,512,128]{2,1,0:T(8,128)(2,1)S(1)} %pack_square.2.same_ref), channel_id=1, source_target_pairs={{0,1},{1,0},{2,3},{3,2},{4,5},{5,4},{6,7},{7,6},{8,9},{9,8},{10,11... | collective-permute-start | bytes 1572872 | tf_op jit(solution)/shard_map/ppermute | solution.py:21
  21.2 2.0 %collective-permute-start.8 = (bf16[4,512,128]{2,1,0:T(8,128)(2,1)S(1)}, bf16[4,512,128]{2,1,0:T(8,128)(2,1)S(1)}, u32[]{:S(2)}, u32[]{:S(2)}) collective-permute-start(bf16[4,512,128]{2,1,0:T(8,128)(2,1)S(1)} %pack_square.3.refs_0_), channel_id=1, source_target_pairs={{0,1},{1,0},{2,3},{3,2},{4,5},{5,4},{6,7},{7,6},{8,9},{9,8},{10,11... | collective-permute-start | bytes 1572872 | tf_op jit(solution)/shard_map/ppermute | solution.py:21
  26.2 3.0 %collective-permute-start.9 = (f32[128,256]{1,0:T(8,128)S(1)}, f32[128,256]{1,0:T(8,128)S(1)}, u32[]{:S(2)}, u32[]{:S(2)}) collective-permute-start(f32[128,256]{1,0:T(8,128)S(1)} %get-tuple-element.52), channel_id=1, source_target_pairs={{0,1},{1,0},{2,3},{3,2},{4,5},{5,4},{6,7},{7,6},{8,9},{9,8},{10,11... | collective-permute-start | bytes 393224 | tf_op jit(solution)/shard_map/ppermute | solution.py:21
  27.7 2.7 %collective-permute-start.13 = (f32[4,512,128]{2,1,0:T(8,128)S(1)}, f32[4,512,128]{2,1,0:T(8,128)S(1)}, u32[]{:S(2)}, u32[]{:S(2)}) collective-permute-start(f32[4,512,128]{2,1,0:T(8,128)S(1)} %send.3), channel_id=1, source_target_pairs={{0,1},{1,0},{2,3},{3,2},{4,5},{5,4},{6,7},{7,6},{8,9},{9,8},{10,11... | collective-permute-start | bytes 3145736 | tf_op jit(solution)/shard_map/ppermute | solution.py:21
  29.3 4.7 %collective-permute-start.10 = (f32[4,512,128]{2,1,0:T(8,128)S(1)}, f32[4,512,128]{2,1,0:T(8,128)S(1)}, u32[]{:S(2)}, u32[]{:S(2)}) collective-permute-start(f32[4,512,128]{2,1,0:T(8,128)S(1)} %send.2), channel_id=1, source_target_pairs={{0,1},{1,0},{2,3},{3,2},{4,5},{5,4},{6,7},{7,6},{8,9},{9,8},{10,11... | collective-permute-start | bytes 3145736 | tf_op jit(solution)/shard_map/ppermute | solution.py:21
  30.5 8.0 %collective-permute-start.14 = (bf16[640,128]{1,0:T(8,128)(2,1)S(1)}, bf16[640,128]{1,0:T(8,128)(2,1)S(1)}, u32[]{:S(2)}, u32[]{:S(2)}) collective-permute-start(bf16[640,128]{1,0:T(8,128)(2,1)S(1)} %get-tuple-element.61), channel_id=1, source_target_pairs={{0,6},{1,7},{2,4},{3,5},{4,2},{5,3},{6,0},{7,1},{8,14},{9,15},{10,... | collective-permute-start | bytes 491528 | tf_op jit(solution)/shard_map/ppermute | solution.py:21
  31.3 10.8 %collective-permute-start.15 = (bf16[640,128]{1,0:T(8,128)(2,1)S(1)}, bf16[640,128]{1,0:T(8,128)(2,1)S(1)}, u32[]{:S(2)}, u32[]{:S(2)}) collective-permute-start(bf16[640,128]{1,0:T(8,128)(2,1)S(1)} %get-tuple-element.62), channel_id=1, source_target_pairs={{0,2},{1,3},{2,0},{3,1},{4,6},{5,7},{6,4},{7,5},{8,10},{9,11},{10,... | collective-permute-start | bytes 491528 | tf_op jit(solution)/shard_map/ppermute | solution.py:21
  32.3 9.8 %collective-permute-start.16 = (bf16[640,128]{1,0:T(8,128)(2,1)S(1)}, bf16[640,128]{1,0:T(8,128)(2,1)S(1)}, u32[]{:S(2)}, u32[]{:S(2)}) collective-permute-start(bf16[640,128]{1,0:T(8,128)(2,1)S(1)} %get-tuple-element.63), channel_id=1, source_target_pairs={{0,4},{1,5},{2,6},{3,7},{4,0},{5,1},{6,2},{7,3},{8,12},{9,13},{10,... | collective-permute-start | bytes 491528 | tf_op jit(solution)/shard_map/ppermute | solution.py:21
  34.1 18.2 %collective-permute-start.11 = (bf16[512,128]{1,0:T(8,128)(2,1)S(1)}, bf16[512,128]{1,0:T(8,128)(2,1)S(1)}, u32[]{:S(2)}, u32[]{:S(2)}) collective-permute-start(bf16[512,128]{1,0:T(8,128)(2,1)S(1)} %get-tuple-element.55), channel_id=1, source_target_pairs={{0,6},{1,7},{2,4},{3,5},{4,2},{5,3},{6,0},{7,1},{8,14},{9,15},{10,... | collective-permute-start | bytes 393224 | tf_op jit(solution)/shard_map/ppermute | solution.py:21
  34.9 17.4 %collective-permute-start.12 = (bf16[512,128]{1,0:T(8,128)(2,1)S(1)}, bf16[512,128]{1,0:T(8,128)(2,1)S(1)}, u32[]{:S(2)}, u32[]{:S(2)}) collective-permute-start(bf16[512,128]{1,0:T(8,128)(2,1)S(1)} %get-tuple-element.56), channel_id=1, source_target_pairs={{0,2},{1,3},{2,0},{3,1},{4,6},{5,7},{6,4},{7,5},{8,10},{9,11},{10,... | collective-permute-start | bytes 393224 | tf_op jit(solution)/shard_map/ppermute | solution.py:21
  42.2 5.3 %collective-permute-start.19 = (f32[32,256]{1,0:T(8,128)S(1)}, f32[32,256]{1,0:T(8,128)S(1)}, u32[]{:S(2)}, u32[]{:S(2)}) collective-permute-start(f32[32,256]{1,0:T(8,128)S(1)} %get-tuple-element.65.own_ref), channel_id=1, source_target_pairs={{0,8},{1,9},{2,10},{3,11},{4,12},{5,13},{6,14},{7,15},{8,0},{9,1},... | collective-permute-start | bytes 98312 | tf_op jit(solution)/shard_map/ppermute | solution.py:21
  44.0 8.4 %collective-permute-start.17 = (bf16[512,128]{1,0:T(8,128)(2,1)S(1)}, bf16[512,128]{1,0:T(8,128)(2,1)S(1)}, u32[]{:S(2)}, u32[]{:S(2)}) collective-permute-start(bf16[512,128]{1,0:T(8,128)(2,1)S(1)} %pair_sum_later.1), channel_id=1, source_target_pairs={{0,4},{1,5},{2,6},{3,7},{4,0},{5,1},{6,2},{7,3},{8,12},{9,13},{10,... | collective-permute-start | bytes 393224 | tf_op jit(solution)/shard_map/ppermute | solution.py:21
  47.5 3.9 %collective-permute-start.20 = (f32[32,256]{1,0:T(8,128)S(1)}, f32[32,256]{1,0:T(8,128)S(1)}, u32[]{:S(2)}, u32[]{:S(2)}) collective-permute-start(f32[32,256]{1,0:T(8,128)S(1)} %weight_sum.1.refs_0_), channel_id=1, source_target_pairs={{0,4},{1,5},{2,6},{3,7},{4,0},{5,1},{6,2},{7,3},{8,12},{9,13},{10,... | collective-permute-start | bytes 98312 | tf_op jit(solution)/shard_map/ppermute | solution.py:21
  47.9 7.9 %collective-permute-start.18 = (bf16[512,128]{1,0:T(8,128)(2,1)S(1)}, bf16[512,128]{1,0:T(8,128)(2,1)S(1)}, u32[]{:S(2)}, u32[]{:S(2)}) collective-permute-start(bf16[512,128]{1,0:T(8,128)(2,1)S(1)} %get-tuple-element.64.refs_0_), channel_id=1, source_target_pairs={{0,8},{1,9},{2,10},{3,11},{4,12},{5,13},{6,14},{7,15},{8,0},{9,1},... | collective-permute-start | bytes 393224 | tf_op jit(solution)/shard_map/ppermute | solution.py:21
  51.4 4.3 %collective-permute-start.21 = (f32[2,32,256]{2,1,0:T(8,128)S(1)}, f32[2,32,256]{2,1,0:T(8,128)S(1)}, u32[]{:S(2)}, u32[]{:S(2)}) collective-permute-start(f32[2,32,256]{2,1,0:T(8,128)S(1)} %pack_weights.2.refs_0_), channel_id=1, source_target_pairs={{0,2},{1,3},{2,0},{3,1},{4,6},{5,7},{6,4},{7,5},{8,10},{9,11},{10,... | collective-permute-start | bytes 196616 | tf_op jit(solution)/shard_map/ppermute | solution.py:21
  55.7 1.4 %collective-permute-start.22 = (f32[2,2,32,256]{3,2,1,0:T(8,128)S(1)}, f32[2,2,32,256]{3,2,1,0:T(8,128)S(1)}, u32[]{:S(2)}, u32[]{:S(2)}) collective-permute-start(f32[2,2,32,256]{3,2,1,0:T(8,128)S(1)} %pack_weights.3.weight_ref), channel_id=1, source_target_pairs={{0,1},{1,0},{2,3},{3,2},{4,5},{5,4},{6,7},{7,6},{8,9},{9,8},{10,11... | collective-permute-start | bytes 393224 | tf_op jit(solution)/shard_map/ppermute | solution.py:21

commit v14 on v13

--- a/solution.py
+++ b/solution.py
@@ -444,9 +444,8 @@
         terms.append([own, *[swap(pieces[q - 1], n, 2 * q) for q in (3, 1, 2)]])
     near_operands = (sums[0], got[0])
     own, *pieces = call(
-        functools.partial(pair_kernel, 0, (0, 3, 1)), "pair_sum", (wide, piece, piece),
-        near_operands)
-    near = [own, swap(pieces[0], n, 6), swap(pieces[1], n, 2)]
+        functools.partial(pair_kernel, 0, (0, 3)), "pair_sum", (wide, piece), near_operands)
+    near = [own, swap(pieces[0], n, 6)]
     distance = 1
     while distance < squares:
         for s in range(squares - distance, 0, -2 * distance):
@@ -458,9 +457,10 @@
                 total = call(add_kernel, "square_sum", piece, terms[s], cost_us=SQUARE_COST)
             terms[s - distance].append(swap(total, n, 8 * distance))
         distance *= 2
-    later = call(
-        functools.partial(pair_kernel, 0, (2,)), "pair_sum_later", piece, near_operands + (total,))
-    near.append(swap(later, n, 4))
+    along_z, along_y = call(
+        functools.partial(pair_kernel, 0, (2, 1)), "pair_sum_later", (piece, piece),
+        near_operands + (total,))
+    near += [swap(along_z, n, 4), swap(along_y, n, 2)]
     near_total = call(near_kernel, "near_sum", wide, (high, low, ws, *near), cost_us=NEAR_COST)
     terms[0].insert(0, near_total)
     bit = 8

time: 58 us -> 57.9 us (level)
  starting transfers between devices: 25.7 us -> 24.4 us
  waiting for transfers between devices: 18.5 us -> 19.6 us
    ppermute x23, starting transfers between devices: 25.7 us -> 24.4 us  [swap(): return lax.ppermute(x, 'row', [(i, i ^ offset) for i in range(n)])]
    ppermute x23, waiting for transfers between devices: 18.5 us -> 19.6 us  [swap(): return lax.ppermute(x, 'row', [(i, i ^ offset) for i in range(n)])]
  transfers between devices with their start and end apart: 23 -> 23, of which waited for: 12 -> 13; matrix products, arithmetic and copies ran while one was open for 0% -> 0% of each run, Pallas kernels for 13% -> 13%
where the time goes in v14:
time: 57.9 us; the launch traced here: 57.6 us
  starting transfers between devices  24.4 us (42%)
  waiting for transfers between devices  19.6 us (34%)
  Pallas kernels  11.6 us (20%)
  local copies, waits for them, and re-layouts  1.31 us (2%)
  between operations  0.81 us (1%)
    ppermute x23, starting transfers between devices, swap(): return lax.ppermute(x, 'row', [(i, i ^ offset) for i in range(n)])  24.4 us
    ppermute x23, waiting for transfers between devices, swap(): return lax.ppermute(x, 'row', [(i, i ^ offset) for i in range(n)])  19.6 us
    pallas_call x20, Pallas kernels, call(): pl.pallas_call(kernel, out_shape=out_shape, in_specs=specs, out_specs=out...  8.49 us
    pallas_call x1, Pallas kernels, body(): pl.pallas_call(functools.partial(stage_kernel, (8 * block_local, (n - 8)...  3.09 us
    unnamed x4, local copies, waits for them, and re-layouts  1.31 us
  transfers between devices with their start and end apart: 23, of which 13 were waited for; matrix products, arithmetic and copies ran while one was open for 0% of the time, Pallas kernels for 13%

profile of v14, /device:TPU:0, one launch (start us, length us, event | category | flops | bytes accessed | tf_op | source)
XLA Modules:
  0.0 57.6 jit_solution(14591455226778309215)
XLA Ops:
  0.6 4.1 %collective-permute-start.4 = (bf16[512,128]{1,0:T(8,128)(2,1)}, bf16[512,128]{1,0:T(8,128)(2,1)S(1)}, u32[]{:S(2)}, u32[]{:S(2)}) collective-permute-start(bf16[512,128]{1,0:T(8,128)(2,1)} %feat_ref.1), channel_id=1, source_target_pairs={{0,8},{1,9},{2,10},{3,11},{4,12},{5,13},{6,14},{7,15},{8,0},{9,1},... | collective-permute-start | bytes 393224 | tf_op jit(solution)/shard_map/ppermute | solution.py:21
  4.7 1.5 %collective-permute-start = (bf16[512,128]{1,0:T(8,128)(2,1)}, bf16[512,128]{1,0:T(8,128)(2,1)S(1)}, u32[]{:S(2)}, u32[]{:S(2)}) collective-permute-start(bf16[512,128]{1,0:T(8,128)(2,1)} %feat_ref.1), channel_id=1, source_target_pairs={{0,2},{1,3},{2,0},{3,1},{4,6},{5,7},{6,4},{7,5},{8,10},{9,11},{10,... | collective-permute-start | bytes 393224 | tf_op jit(solution)/shard_map/ppermute | solution.py:21
  6.3 1.5 %collective-permute-start.1 = (bf16[512,128]{1,0:T(8,128)(2,1)}, bf16[512,128]{1,0:T(8,128)(2,1)S(1)}, u32[]{:S(2)}, u32[]{:S(2)}) collective-permute-start(bf16[512,128]{1,0:T(8,128)(2,1)} %feat_ref.1), channel_id=1, source_target_pairs={{0,6},{1,7},{2,4},{3,5},{4,2},{5,3},{6,0},{7,1},{8,14},{9,15},{10,... | collective-permute-start | bytes 393224 | tf_op jit(solution)/shard_map/ppermute | solution.py:21
  7.8 0.4 collective-permute-start.2
  8.2 3.1 %collective-permute-done.4.refs_0_ = bf16[512,128]{1,0:T(8,128)(2,1)S(1)} collective-permute-done((bf16[512,128]{1,0:T(8,128)(2,1)}, bf16[512,128]{1,0:T(8,128)(2,1)S(1)}, u32[]{:S(2)}, u32[]{:S(2)}) %collective-permute-start.4) | collective-permute-done | bytes 131104 | tf_op jit(solution)/shard_map/ppermute | solution.py:21
  11.4 1.7 %collective-permute-start.5 = (bf16[512,128]{1,0:T(8,128)(2,1)S(1)}, bf16[512,128]{1,0:T(8,128)(2,1)S(1)}, u32[]{:S(2)}, u32[]{:S(2)}) collective-permute-start(bf16[512,128]{1,0:T(8,128)(2,1)S(1)} %collective-permute-done.4.refs_0_), channel_id=1, source_target_pairs={{0,6},{1,7},{2,4},{3,5},{4,2},{5,3},{6,0},{7,1},{8,14},{9,15},{10,... | collective-permute-start | bytes 393224 | tf_op jit(solution)/shard_map/ppermute | solution.py:21
  13.1 0.5 collective-permute-start.6
  13.6 1.3 %collective-permute-start.7 = (bf16[512,128]{1,0:T(8,128)(2,1)S(1)}, bf16[512,128]{1,0:T(8,128)(2,1)S(1)}, u32[]{:S(2)}, u32[]{:S(2)}) collective-permute-start(bf16[512,128]{1,0:T(8,128)(2,1)S(1)} %collective-permute-done.4.refs_0_), channel_id=1, source_target_pairs={{0,4},{1,5},{2,6},{3,7},{4,0},{5,1},{6,2},{7,3},{8,12},{9,13},{10,... | collective-permute-start | bytes 393224 | tf_op jit(solution)/shard_map/ppermute | solution.py:21
  14.9 0.7 %copy-done = s32[60]{0:T(128)S(1)} copy-done((s32[60]{0:T(128)S(1)}, s32[60]{0:T(128)}, u32[]{:S(2)}) %copy-start) | copy-done | bytes 264
  15.5 0.7 %copy-done.1 = s32[60]{0:T(128)S(1)} copy-done((s32[60]{0:T(128)S(1)}, s32[60]{0:T(128)}, u32[]{:S(2)}) %copy-start.1) | copy-done | bytes 264
  16.2 3.1 %stage_arguments.1 = (bf16[60,128,128]{2,1,0:T(8,128)(2,1)S(1)}, bf16[128,256]{1,0:T(8,128)(2,1)S(1)}, bf16[128,256]{1,0:T(8,128)(2,1)S(1)}, f32[4,128,128]{2,1,...) custom-call(s32[1]{0:T(128)} %bitcast.me_ref, ...), custom_call_target="tpu_custom_call" | custom-call | flops 3300000000 | bytes 10800000 | tf_op jit(solution)/shard_map/stage_arguments/pallas_call | solution.py:366
  19.4 1.0 %collective-permute-done.5.refs_1_ = bf16[512,128]{1,0:T(8,128)(2,1)S(1)} collective-permute-done((bf16[512,128]{1,0:T(8,128)(2,1)S(1)}, bf16[512,128]{1,0:T(8,128)(2,1)S(1)}, u32[]{:S(2)}, u32[]{:S(2)}) %collective-permute-start.5) | collective-permute-done | bytes 131104 | tf_op jit(solution)/shard_map/ppermute | solution.py:21
  20.4 0.6 %collective-permute-done.6.refs_2_ = bf16[512,128]{1,0:T(8,128)(2,1)S(1)} collective-permute-done((bf16[512,128]{1,0:T(8,128)(2,1)S(1)}, bf16[512,128]{1,0:T(8,128)(2,1)S(1)}, u32[]{:S(2)}, u32[]{:S(2)}) %collective-permute-start.6) | collective-permute-done | bytes 131104 | tf_op jit(solution)/shard_map/ppermute | solution.py:21
  21.0 0.1 collective-permute-done.7.refs_3_
  21.2 0.1 collective-permute-start.8
  21.3 0.8 %forward_near.1.near_ref = f32[5,128,128]{2,1,0:T(8,128)S(1)} custom-call(s32[363]{0:T(512)S(4)} %get-tuple-element.37.index_ref, bf16[60,128,128]{2,1,0:T(8,128)(2,1)S(1)} %get-tuple-element.38.tiles_ref, bf16[4,512,128]{2,1,0:T(8,128)(2,1)S(1)} %pack_square.2.same_ref, bf16[4,512,128]{2,1,0:T(8,128)(2,1)S(1)} %collective-permute-done.3.other_ref), custom_call_target="tpu_custom_call" | custom-call | flops 110000000 | bytes 360000 | tf_op jit(solution)/shard_map/forward_near/pallas_call | solution.py:343
  22.2 1.0 %collective-permute-done.8.refs_1_ = bf16[4,512,128]{2,1,0:T(8,128)(2,1)S(1)} collective-permute-done((bf16[4,512,128]{2,1,0:T(8,128)(2,1)S(1)}, bf16[4,512,128]{2,1,0:T(8,128)(2,1)S(1)}, u32[]{:S(2)}, u32[]{:S(2)}) %collective-permute-start.8) | collective-permute-done | bytes 524320 | tf_op jit(solution)/shard_map/ppermute | solution.py:21
  23.2 2.6 %forward_layer.1 = (bf16[512,256]{1,0:T(8,128)(2,1)}, bf16[512,256]{1,0:T(8,128)(2,1)S(1)}, bf16[512,256]{1,0:T(8,128)(2,1)S(1)}, bf16[512,256]{1,0:T(8,128)(2,1...) custom-call(s32[363]{0:T(512)S(4)} %get-tuple-element.37.index_ref, ...), custom_call_target="tpu_custom_call" | custom-call | flops 3300000000 | bytes 10800000 | tf_op jit(solution)/shard_map/forward_layer/pallas_call | solution.py:343
  25.7 0.5 weights.1
  26.2 0.2 collective-permute-start.9
  26.5 1.1 %backward_tiles.3.acc_ref = f32[33,128,128]{2,1,0:T(8,128)S(1)} custom-call(s32[363]{0:T(512)S(4)} %get-tuple-element.37.index_ref, bf16[60,128,128]{2,1,0:T(8,128)(2,1)S(1)} %get-tuple-element.38.tiles_ref, bf16[4,256,128]{2,1,0:T(8,128)(2,1)S(1)} %get-tuple-element.48.gt_ref, f32[128,256]{1,0:T(8,128)S(1)} %get-tuple-element.52.refs_0_.wkeep_ref), custom_call_target="tpu_custom_call" | custom-call | flops 1650000000 | bytes 5400000 | tf_op jit(solution)/shard_map/backward_tiles/pallas_call | solution.py:343
  27.7 0.4 collective-permute-start.12
  28.1 1.1 %backward_tiles.2.acc_ref = f32[33,128,128]{2,1,0:T(8,128)S(1)} custom-call(s32[363]{0:T(512)S(4)} %get-tuple-element.37.index_ref, bf16[60,128,128]{2,1,0:T(8,128)(2,1)S(1)} %get-tuple-element.38.tiles_ref, bf16[4,256,128]{2,1,0:T(8,128)(2,1)S(1)} %get-tuple-element.48.gt_ref, f32[128,256]{1,0:T(8,128)S(1)} %get-tuple-element.52.refs_0_.wkeep_ref), custom_call_target="tpu_custom_call" | custom-call | flops 330000000 | bytes 1080000 | tf_op jit(solution)/shard_map/backward_tiles/pallas_call | solution.py:343
  29.3 0.2 collective-permute-start.10
  29.6 0.8 %collective-permute-done.12.got_ref = f32[4,512,128]{2,1,0:T(8,128)S(1)} collective-permute-done((f32[4,512,128]{2,1,0:T(8,128)S(1)}, f32[4,512,128]{2,1,0:T(8,128)S(1)}, u32[]{:S(2)}, u32[]{:S(2)}) %collective-permute-start.12) | collective-permute-done | bytes 1048608 | tf_op jit(solution)/shard_map/ppermute | solution.py:21
  30.4 0.1 pair_sum_weights.1
  30.5 0.8 %collective-permute-start.13 = (bf16[640,128]{1,0:T(8,128)(2,1)S(1)}, bf16[640,128]{1,0:T(8,128)(2,1)S(1)}, u32[]{:S(2)}, u32[]{:S(2)}) collective-permute-start(bf16[640,128]{1,0:T(8,128)(2,1)S(1)} %get-tuple-element.61), channel_id=1, source_target_pairs={{0,6},{1,7},{2,4},{3,5},{4,2},{5,3},{6,0},{7,1},{8,14},{9,15},{10,... | collective-permute-start | bytes 491528 | tf_op jit(solution)/shard_map/ppermute | solution.py:21
  31.3 1.0 %collective-permute-start.14 = (bf16[640,128]{1,0:T(8,128)(2,1)S(1)}, bf16[640,128]{1,0:T(8,128)(2,1)S(1)}, u32[]{:S(2)}, u32[]{:S(2)}) collective-permute-start(bf16[640,128]{1,0:T(8,128)(2,1)S(1)} %get-tuple-element.62), channel_id=1, source_target_pairs={{0,2},{1,3},{2,0},{3,1},{4,6},{5,7},{6,4},{7,5},{8,10},{9,11},{10,... | collective-permute-start | bytes 491528 | tf_op jit(solution)/shard_map/ppermute | solution.py:21
  32.3 1.8 %collective-permute-start.15 = (bf16[640,128]{1,0:T(8,128)(2,1)S(1)}, bf16[640,128]{1,0:T(8,128)(2,1)S(1)}, u32[]{:S(2)}, u32[]{:S(2)}) collective-permute-start(bf16[640,128]{1,0:T(8,128)(2,1)S(1)} %get-tuple-element.63), channel_id=1, source_target_pairs={{0,4},{1,5},{2,6},{3,7},{4,0},{5,1},{6,2},{7,3},{8,12},{9,13},{10,... | collective-permute-start | bytes 491528 | tf_op jit(solution)/shard_map/ppermute | solution.py:21
  34.1 0.9 %collective-permute-start.11 = (bf16[512,128]{1,0:T(8,128)(2,1)S(1)}, bf16[512,128]{1,0:T(8,128)(2,1)S(1)}, u32[]{:S(2)}, u32[]{:S(2)}) collective-permute-start(bf16[512,128]{1,0:T(8,128)(2,1)S(1)} %get-tuple-element.56), channel_id=1, source_target_pairs={{0,6},{1,7},{2,4},{3,5},{4,2},{5,3},{6,0},{7,1},{8,14},{9,15},{10,... | collective-permute-start | bytes 393224 | tf_op jit(solution)/shard_map/ppermute | solution.py:21
  35.1 3.5 %collective-permute-done.13.refs_0_ = bf16[640,128]{1,0:T(8,128)(2,1)S(1)} collective-permute-done((bf16[640,128]{1,0:T(8,128)(2,1)S(1)}, bf16[640,128]{1,0:T(8,128)(2,1)S(1)}, u32[]{:S(2)}, u32[]{:S(2)}) %collective-permute-start.13) | collective-permute-done | bytes 163872 | tf_op jit(solution)/shard_map/ppermute | solution.py:21
  38.5 2.5 %collective-permute-done.14.refs_1_ = bf16[640,128]{1,0:T(8,128)(2,1)S(1)} collective-permute-done((bf16[640,128]{1,0:T(8,128)(2,1)S(1)}, bf16[640,128]{1,0:T(8,128)(2,1)S(1)}, u32[]{:S(2)}, u32[]{:S(2)}) %collective-permute-start.14) | collective-permute-done | bytes 163872 | tf_op jit(solution)/shard_map/ppermute | solution.py:21
  41.1 1.0 %collective-permute-done.15.refs_2_ = bf16[640,128]{1,0:T(8,128)(2,1)S(1)} collective-permute-done((bf16[640,128]{1,0:T(8,128)(2,1)S(1)}, bf16[640,128]{1,0:T(8,128)(2,1)S(1)}, u32[]{:S(2)}, u32[]{:S(2)}) %collective-permute-start.15) | collective-permute-done | bytes 163872 | tf_op jit(solution)/shard_map/ppermute | solution.py:21
  42.0 0.1 square_sum_weights.1
  42.1 1.5 %collective-permute-start.19 = (f32[32,256]{1,0:T(8,128)S(1)}, f32[32,256]{1,0:T(8,128)S(1)}, u32[]{:S(2)}, u32[]{:S(2)}) collective-permute-start(f32[32,256]{1,0:T(8,128)S(1)} %get-tuple-element.67.own_ref), channel_id=1, source_target_pairs={{0,8},{1,9},{2,10},{3,11},{4,12},{5,13},{6,14},{7,15},{8,0},{9,1},... | collective-permute-start | bytes 98312 | tf_op jit(solution)/shard_map/ppermute | solution.py:21
  43.6 1.8 %collective-permute-start.16 = (bf16[512,128]{1,0:T(8,128)(2,1)S(1)}, bf16[512,128]{1,0:T(8,128)(2,1)S(1)}, u32[]{:S(2)}, u32[]{:S(2)}) collective-permute-start(bf16[512,128]{1,0:T(8,128)(2,1)S(1)} %get-tuple-element.65), channel_id=1, source_target_pairs={{0,4},{1,5},{2,6},{3,7},{4,0},{5,1},{6,2},{7,3},{8,12},{9,13},{10,... | collective-permute-start | bytes 393224 | tf_op jit(solution)/shard_map/ppermute | solution.py:21
  45.5 0.6 %collective-permute-start.17 = (bf16[512,128]{1,0:T(8,128)(2,1)S(1)}, bf16[512,128]{1,0:T(8,128)(2,1)S(1)}, u32[]{:S(2)}, u32[]{:S(2)}) collective-permute-start(bf16[512,128]{1,0:T(8,128)(2,1)S(1)} %get-tuple-element.66), channel_id=1, source_target_pairs={{0,2},{1,3},{2,0},{3,1},{4,6},{5,7},{6,4},{7,5},{8,10},{9,11},{10,... | collective-permute-start | bytes 393224 | tf_op jit(solution)/shard_map/ppermute | solution.py:21
  46.1 1.2 %collective-permute-done.19.got_ref = f32[32,256]{1,0:T(8,128)S(1)} collective-permute-done((f32[32,256]{1,0:T(8,128)S(1)}, f32[32,256]{1,0:T(8,128)S(1)}, u32[]{:S(2)}, u32[]{:S(2)}) %collective-permute-start.19) | collective-permute-done | bytes 32800 | tf_op jit(solution)/shard_map/ppermute | solution.py:21
  47.3 0.3 collective-permute-start.20
  47.6 2.9 %collective-permute-start.18 = (bf16[512,128]{1,0:T(8,128)(2,1)S(1)}, bf16[512,128]{1,0:T(8,128)(2,1)S(1)}, u32[]{:S(2)}, u32[]{:S(2)}) collective-permute-start(bf16[512,128]{1,0:T(8,128)(2,1)S(1)} %get-tuple-element.64.refs_0_), channel_id=1, source_target_pairs={{0,8},{1,9},{2,10},{3,11},{4,12},{5,13},{6,14},{7,15},{8,0},{9,1},... | collective-permute-start | bytes 393224 | tf_op jit(solution)/shard_map/ppermute | solution.py:21
  50.4 0.8 %collective-permute-done.20.refs_1_ = f32[32,256]{1,0:T(8,128)S(1)} collective-permute-done((f32[32,256]{1,0:T(8,128)S(1)}, f32[32,256]{1,0:T(8,128)S(1)}, u32[]{:S(2)}, u32[]{:S(2)}) %collective-permute-start.20) | collective-permute-done | bytes 32800 | tf_op jit(solution)/shard_map/ppermute | solution.py:21
  51.2 0.6 %collective-permute-start.21 = (f32[2,32,256]{2,1,0:T(8,128)S(1)}, f32[2,32,256]{2,1,0:T(8,128)S(1)}, u32[]{:S(2)}, u32[]{:S(2)}) collective-permute-start(f32[2,32,256]{2,1,0:T(8,128)S(1)} %pack_weights.2.refs_0_), channel_id=1, source_target_pairs={{0,2},{1,3},{2,0},{3,1},{4,6},{5,7},{6,4},{7,5},{8,10},{9,11},{10,... | collective-permute-start | bytes 196616 | tf_op jit(solution)/shard_map/ppermute | solution.py:21
  51.8 0.3 near_sum.1.near_ref.refs_2_
  52.2 3.3 %collective-permute-done.21.refs_1_ = f32[2,32,256]{2,1,0:T(8,128)S(1)} collective-permute-done((f32[2,32,256]{2,1,0:T(8,128)S(1)}, f32[2,32,256]{2,1,0:T(8,128)S(1)}, u32[]{:S(2)}, u32[]{:S(2)}) %collective-permute-start.21) | collective-permute-done | bytes 65568 | tf_op jit(solution)/shard_map/ppermute | solution.py:21
  55.5 0.1 collective-permute-start.22
  55.6 0.8 %grad_input_sum.1 = bf16[512,128]{1,0:T(8,128)(2,1)} custom-call(f32[512,128]{1,0:T(8,128)S(1)} %near_sum.1.near_ref.refs_2_, bf16[512,128]{1,0:T(8,128)(2,1)S(1)} %collective-permute-done.18.refs_0_), custom_call_target="tpu_custom_call" | custom-call | flops 11000000512 | bytes 36000000 | tf_op jit(solution)/shard_map/grad_input_sum/pallas_call | solution.py:343
  56.3 0.6 collective-permute-done.22.other_ref
  56.9 0.7 %write_weights.1 = (f32[128,256]{1,0:T(8,128)}, f32[128,256]{1,0:T(8,128)}) custom-call(s32[363]{0:T(512)S(4)} %get-tuple-element.37.index_ref, f32[2,2,32,256]{3,2,1,0:T(8,128)S(1)} %pack_weights.3.weight_ref, f32[2,2,32,256]{3,2,1,0:T(8,128)S(1)} %collective-permute-done.22.other_ref), custom_call_target="tpu_custom_call" | custom-call | flops 220000000 | bytes 720000 | tf_op jit(solution)/shard_map/write_weights/pallas_call | solution.py:343
  (23 shorter events, 0.5 us)
Async XLA Ops:
  0.6 10.7 %collective-permute-start.4 = (bf16[512,128]{1,0:T(8,128)(2,1)}, bf16[512,128]{1,0:T(8,128)(2,1)S(1)}, u32[]{:S(2)}, u32[]{:S(2)}) collective-permute-start(bf16[512,128]{1,0:T(8,128)(2,1)} %feat_ref.1), channel_id=1, source_target_pairs={{0,8},{1,9},{2,10},{3,11},{4,12},{5,13},{6,14},{7,15},{8,0},{9,1},... | collective-permute-start | bytes 393224 | tf_op jit(solution)/shard_map/ppermute | solution.py:21
  4.7 8.9 %collective-permute-start = (bf16[512,128]{1,0:T(8,128)(2,1)}, bf16[512,128]{1,0:T(8,128)(2,1)S(1)}, u32[]{:S(2)}, u32[]{:S(2)}) collective-permute-start(bf16[512,128]{1,0:T(8,128)(2,1)} %feat_ref.1), channel_id=1, source_target_pairs={{0,2},{1,3},{2,0},{3,1},{4,6},{5,7},{6,4},{7,5},{8,10},{9,11},{10,... | collective-permute-start | bytes 393224 | tf_op jit(solution)/shard_map/ppermute | solution.py:21
  6.3 13.0 %collective-permute-start.1 = (bf16[512,128]{1,0:T(8,128)(2,1)}, bf16[512,128]{1,0:T(8,128)(2,1)S(1)}, u32[]{:S(2)}, u32[]{:S(2)}) collective-permute-start(bf16[512,128]{1,0:T(8,128)(2,1)} %feat_ref.1), channel_id=1, source_target_pairs={{0,6},{1,7},{2,4},{3,5},{4,2},{5,3},{6,0},{7,1},{8,14},{9,15},{10,... | collective-permute-start | bytes 393224 | tf_op jit(solution)/shard_map/ppermute | solution.py:21
  7.8 11.5 %collective-permute-start.2 = (bf16[512,128]{1,0:T(8,128)(2,1)}, bf16[512,128]{1,0:T(8,128)(2,1)S(1)}, u32[]{:S(2)}, u32[]{:S(2)}) collective-permute-start(bf16[512,128]{1,0:T(8,128)(2,1)} %feat_ref.1), channel_id=1, source_target_pairs={{0,4},{1,5},{2,6},{3,7},{4,0},{5,1},{6,2},{7,3},{8,12},{9,13},{10,... | collective-permute-start | bytes 393224 | tf_op jit(solution)/shard_map/ppermute | solution.py:21
  11.4 9.1 %collective-permute-start.5 = (bf16[512,128]{1,0:T(8,128)(2,1)S(1)}, bf16[512,128]{1,0:T(8,128)(2,1)S(1)}, u32[]{:S(2)}, u32[]{:S(2)}) collective-permute-start(bf16[512,128]{1,0:T(8,128)(2,1)S(1)} %collective-permute-done.4.refs_0_), channel_id=1, source_target_pairs={{0,6},{1,7},{2,4},{3,5},{4,2},{5,3},{6,0},{7,1},{8,14},{9,15},{10,... | collective-permute-start | bytes 393224 | tf_op jit(solution)/shard_map/ppermute | solution.py:21
  13.1 7.9 %collective-permute-start.6 = (bf16[512,128]{1,0:T(8,128)(2,1)S(1)}, bf16[512,128]{1,0:T(8,128)(2,1)S(1)}, u32[]{:S(2)}, u32[]{:S(2)}) collective-permute-start(bf16[512,128]{1,0:T(8,128)(2,1)S(1)} %collective-permute-done.4.refs_0_), channel_id=1, source_target_pairs={{0,2},{1,3},{2,0},{3,1},{4,6},{5,7},{6,4},{7,5},{8,10},{9,11},{10,... | collective-permute-start | bytes 393224 | tf_op jit(solution)/shard_map/ppermute | solution.py:21
  13.6 7.6 %collective-permute-start.7 = (bf16[512,128]{1,0:T(8,128)(2,1)S(1)}, bf16[512,128]{1,0:T(8,128)(2,1)S(1)}, u32[]{:S(2)}, u32[]{:S(2)}) collective-permute-start(bf16[512,128]{1,0:T(8,128)(2,1)S(1)} %collective-permute-done.4.refs_0_), channel_id=1, source_target_pairs={{0,4},{1,5},{2,6},{3,7},{4,0},{5,1},{6,2},{7,3},{8,12},{9,13},{10,... | collective-permute-start | bytes 393224 | tf_op jit(solution)/shard_map/ppermute | solution.py:21
  14.8 0.7 %copy-start = (s32[60]{0:T(128)S(1)}, s32[60]{0:T(128)}, u32[]{:S(2)}) copy-start(s32[60]{0:T(128)} %trow_ref.1) | copy-start | bytes 724
  15.5 0.7 %copy-start.1 = (s32[60]{0:T(128)S(1)}, s32[60]{0:T(128)}, u32[]{:S(2)}) copy-start(s32[60]{0:T(128)} %tcol_ref.1) | copy-start | bytes 724
  19.3 2.0 %collective-permute-start.3 = (bf16[4,512,128]{2,1,0:T(8,128)(2,1)S(1)}, bf16[4,512,128]{2,1,0:T(8,128)(2,1)S(1)}, u32[]{:S(2)}, u32[]{:S(2)}) collective-permute-start(bf16[4,512,128]{2,1,0:T(8,128)(2,1)S(1)} %pack_square.2.same_ref), channel_id=1, source_target_pairs={{0,1},{1,0},{2,3},{3,2},{4,5},{5,4},{6,7},{7,6},{8,9},{9,8},{10,11... | collective-permute-start | bytes 1572872 | tf_op jit(solution)/shard_map/ppermute | solution.py:21
  21.2 2.0 %collective-permute-start.8 = (bf16[4,512,128]{2,1,0:T(8,128)(2,1)S(1)}, bf16[4,512,128]{2,1,0:T(8,128)(2,1)S(1)}, u32[]{:S(2)}, u32[]{:S(2)}) collective-permute-start(bf16[4,512,128]{2,1,0:T(8,128)(2,1)S(1)} %pack_square.3.refs_0_), channel_id=1, source_target_pairs={{0,1},{1,0},{2,3},{3,2},{4,5},{5,4},{6,7},{7,6},{8,9},{9,8},{10,11... | collective-permute-start | bytes 1572872 | tf_op jit(solution)/shard_map/ppermute | solution.py:21
  26.2 3.0 %collective-permute-start.9 = (f32[128,256]{1,0:T(8,128)S(1)}, f32[128,256]{1,0:T(8,128)S(1)}, u32[]{:S(2)}, u32[]{:S(2)}) collective-permute-start(f32[128,256]{1,0:T(8,128)S(1)} %get-tuple-element.53), channel_id=1, source_target_pairs={{0,1},{1,0},{2,3},{3,2},{4,5},{5,4},{6,7},{7,6},{8,9},{9,8},{10,11... | collective-permute-start | bytes 393224 | tf_op jit(solution)/shard_map/ppermute | solution.py:21
  27.7 2.7 %collective-permute-start.12 = (f32[4,512,128]{2,1,0:T(8,128)S(1)}, f32[4,512,128]{2,1,0:T(8,128)S(1)}, u32[]{:S(2)}, u32[]{:S(2)}) collective-permute-start(f32[4,512,128]{2,1,0:T(8,128)S(1)} %send.3), channel_id=1, source_target_pairs={{0,1},{1,0},{2,3},{3,2},{4,5},{5,4},{6,7},{7,6},{8,9},{9,8},{10,11... | collective-permute-start | bytes 3145736 | tf_op jit(solution)/shard_map/ppermute | solution.py:21
  29.3 4.7 %collective-permute-start.10 = (f32[4,512,128]{2,1,0:T(8,128)S(1)}, f32[4,512,128]{2,1,0:T(8,128)S(1)}, u32[]{:S(2)}, u32[]{:S(2)}) collective-permute-start(f32[4,512,128]{2,1,0:T(8,128)S(1)} %send.2), channel_id=1, source_target_pairs={{0,1},{1,0},{2,3},{3,2},{4,5},{5,4},{6,7},{7,6},{8,9},{9,8},{10,11... | collective-permute-start | bytes 3145736 | tf_op jit(solution)/shard_map/ppermute | solution.py:21
  30.5 8.0 %collective-permute-start.13 = (bf16[640,128]{1,0:T(8,128)(2,1)S(1)}, bf16[640,128]{1,0:T(8,128)(2,1)S(1)}, u32[]{:S(2)}, u32[]{:S(2)}) collective-permute-start(bf16[640,128]{1,0:T(8,128)(2,1)S(1)} %get-tuple-element.61), channel_id=1, source_target_pairs={{0,6},{1,7},{2,4},{3,5},{4,2},{5,3},{6,0},{7,1},{8,14},{9,15},{10,... | collective-permute-start | bytes 491528 | tf_op jit(solution)/shard_map/ppermute | solution.py:21
  31.3 9.8 %collective-permute-start.14 = (bf16[640,128]{1,0:T(8,128)(2,1)S(1)}, bf16[640,128]{1,0:T(8,128)(2,1)S(1)}, u32[]{:S(2)}, u32[]{:S(2)}) collective-permute-start(bf16[640,128]{1,0:T(8,128)(2,1)S(1)} %get-tuple-element.62), channel_id=1, source_target_pairs={{0,2},{1,3},{2,0},{3,1},{4,6},{5,7},{6,4},{7,5},{8,10},{9,11},{10,... | collective-permute-start | bytes 491528 | tf_op jit(solution)/shard_map/ppermute | solution.py:21
  32.3 9.7 %collective-permute-start.15 = (bf16[640,128]{1,0:T(8,128)(2,1)S(1)}, bf16[640,128]{1,0:T(8,128)(2,1)S(1)}, u32[]{:S(2)}, u32[]{:S(2)}) collective-permute-start(bf16[640,128]{1,0:T(8,128)(2,1)S(1)} %get-tuple-element.63), channel_id=1, source_target_pairs={{0,4},{1,5},{2,6},{3,7},{4,0},{5,1},{6,2},{7,3},{8,12},{9,13},{10,... | collective-permute-start | bytes 491528 | tf_op jit(solution)/shard_map/ppermute | solution.py:21
  34.1 17.7 %collective-permute-start.11 = (bf16[512,128]{1,0:T(8,128)(2,1)S(1)}, bf16[512,128]{1,0:T(8,128)(2,1)S(1)}, u32[]{:S(2)}, u32[]{:S(2)}) collective-permute-start(bf16[512,128]{1,0:T(8,128)(2,1)S(1)} %get-tuple-element.56), channel_id=1, source_target_pairs={{0,6},{1,7},{2,4},{3,5},{4,2},{5,3},{6,0},{7,1},{8,14},{9,15},{10,... | collective-permute-start | bytes 393224 | tf_op jit(solution)/shard_map/ppermute | solution.py:21
  42.1 5.2 %collective-permute-start.19 = (f32[32,256]{1,0:T(8,128)S(1)}, f32[32,256]{1,0:T(8,128)S(1)}, u32[]{:S(2)}, u32[]{:S(2)}) collective-permute-start(f32[32,256]{1,0:T(8,128)S(1)} %get-tuple-element.67.own_ref), channel_id=1, source_target_pairs={{0,8},{1,9},{2,10},{3,11},{4,12},{5,13},{6,14},{7,15},{8,0},{9,1},... | collective-permute-start | bytes 98312 | tf_op jit(solution)/shard_map/ppermute | solution.py:21
  43.6 8.2 %collective-permute-start.16 = (bf16[512,128]{1,0:T(8,128)(2,1)S(1)}, bf16[512,128]{1,0:T(8,128)(2,1)S(1)}, u32[]{:S(2)}, u32[]{:S(2)}) collective-permute-start(bf16[512,128]{1,0:T(8,128)(2,1)S(1)} %get-tuple-element.65), channel_id=1, source_target_pairs={{0,4},{1,5},{2,6},{3,7},{4,0},{5,1},{6,2},{7,3},{8,12},{9,13},{10,... | collective-permute-start | bytes 393224 | tf_op jit(solution)/shard_map/ppermute | solution.py:21
  45.5 6.4 %collective-permute-start.17 = (bf16[512,128]{1,0:T(8,128)(2,1)S(1)}, bf16[512,128]{1,0:T(8,128)(2,1)S(1)}, u32[]{:S(2)}, u32[]{:S(2)}) collective-permute-start(bf16[512,128]{1,0:T(8,128)(2,1)S(1)} %get-tuple-element.66), channel_id=1, source_target_pairs={{0,2},{1,3},{2,0},{3,1},{4,6},{5,7},{6,4},{7,5},{8,10},{9,11},{10,... | collective-permute-start | bytes 393224 | tf_op jit(solution)/shard_map/ppermute | solution.py:21
  47.3 3.9 %collective-permute-start.20 = (f32[32,256]{1,0:T(8,128)S(1)}, f32[32,256]{1,0:T(8,128)S(1)}, u32[]{:S(2)}, u32[]{:S(2)}) collective-permute-start(f32[32,256]{1,0:T(8,128)S(1)} %weight_sum.1.refs_0_), channel_id=1, source_target_pairs={{0,4},{1,5},{2,6},{3,7},{4,0},{5,1},{6,2},{7,3},{8,12},{9,13},{10,... | collective-permute-start | bytes 98312 | tf_op jit(solution)/shard_map/ppermute | solution.py:21
  47.6 8.0 %collective-permute-start.18 = (bf16[512,128]{1,0:T(8,128)(2,1)S(1)}, bf16[512,128]{1,0:T(8,128)(2,1)S(1)}, u32[]{:S(2)}, u32[]{:S(2)}) collective-permute-start(bf16[512,128]{1,0:T(8,128)(2,1)S(1)} %get-tuple-element.64.refs_0_), channel_id=1, source_target_pairs={{0,8},{1,9},{2,10},{3,11},{4,12},{5,13},{6,14},{7,15},{8,0},{9,1},... | collective-permute-start | bytes 393224 | tf_op jit(solution)/shard_map/ppermute | solution.py:21
  51.2 4.3 %collective-permute-start.21 = (f32[2,32,256]{2,1,0:T(8,128)S(1)}, f32[2,32,256]{2,1,0:T(8,128)S(1)}, u32[]{:S(2)}, u32[]{:S(2)}) collective-permute-start(f32[2,32,256]{2,1,0:T(8,128)S(1)} %pack_weights.2.refs_0_), channel_id=1, source_target_pairs={{0,2},{1,3},{2,0},{3,1},{4,6},{5,7},{6,4},{7,5},{8,10},{9,11},{10,... | collective-permute-start | bytes 196616 | tf_op jit(solution)/shard_map/ppermute | solution.py:21
  55.5 1.4 %collective-permute-start.22 = (f32[2,2,32,256]{3,2,1,0:T(8,128)S(1)}, f32[2,2,32,256]{3,2,1,0:T(8,128)S(1)}, u32[]{:S(2)}, u32[]{:S(2)}) collective-permute-start(f32[2,2,32,256]{3,2,1,0:T(8,128)S(1)} %pack_weights.3.weight_ref), channel_id=1, source_target_pairs={{0,1},{1,0},{2,3},{3,2},{4,5},{5,4},{6,7},{7,6},{8,9},{9,8},{10,11... | collective-permute-start | bytes 393224 | tf_op jit(solution)/shard_map/ppermute | solution.py:21

commit v15 on v14

--- a/solution.py
+++ b/solution.py
@@ -14,7 +14,7 @@
 ANY = pl.BlockSpec(memory_space=pl.ANY)
 MIB = 1024 * 1024
 LAST = ((1,), (1,))
-NEAR_COST, SQUARE_COST, MAIN_COST = 0.2, 4, 10
+NEAR_COST, SQUARE_COST, MAIN_COST, FAR_COST = 0.2, 4, 0.2, 10
 
 
 def swap(x, n, offset):
@@ -260,15 +260,15 @@
                 start += rows
 
 
-def add_two_kernel(own_ref, got_ref, out_ref):
-    out_ref[...] = own_ref[...] + got_ref[...]
+def add_two_kernel(own_ref, got_ref, *refs):
+    refs[-1][...] = own_ref[...] + got_ref[...]
 
 
 def add_kernel(own_ref, *refs):
-    total = own_ref[...]
+    total = own_ref[...].astype(F32)
     for got_ref in refs[:-1]:
         total = total + got_ref[...].astype(F32)
-    refs[-1][...] = total.astype(BF16)
+    refs[-1][...] = total.astype(refs[-1].dtype)
 
 
 def add_weights_kernel(weight_ref, own_ref, *refs):
@@ -457,22 +457,23 @@
                 total = call(add_kernel, "square_sum", piece, terms[s], cost_us=SQUARE_COST)
             terms[s - distance].append(swap(total, n, 8 * distance))
         distance *= 2
-    along_z, along_y = call(
-        functools.partial(pair_kernel, 0, (2, 1)), "pair_sum_later", (piece, piece),
-        near_operands + (total,))
-    near += [swap(along_z, n, 4), swap(along_y, n, 2)]
-    near_total = call(near_kernel, "near_sum", wide, (high, low, ws, *near), cost_us=NEAR_COST)
-    terms[0].insert(0, near_total)
     bit = 8
     while bit < n:
-        wsum = call(add_two_kernel, "weight_sum", chunk, (wsum, swap(wsum, n, bit)))
+        wsum = call(add_two_kernel, "weight_sum", chunk, (wsum, swap(wsum, n, bit), near[1]))
         bit *= 2
     rows = chunk.shape[0]
     two = call(functools.partial(pack_kernel, (0, 1)), "pack_weights", result((2, rows, hidden), F32), (wsum, swap(wsum, n, 4)))
+    along_z, along_y = call(
+        functools.partial(pair_kernel, 0, (2, 1)), "pair_sum_later", (piece, piece),
+        near_operands + (two,))
+    near += [swap(along_z, n, 4), swap(along_y, n, 2)]
+    near_total = call(near_kernel, "near_sum", wide, (high, low, ws, *near), cost_us=NEAR_COST)
     mine = call(
-        functools.partial(pack_kernel, (0, 1)), "pack_weights", result((2, 2, rows, hidden), F32), (two, swap(two, n, 2), near_total))
+        functools.partial(pack_kernel, (0, 1)), "pack_weights", result((2, 2, rows, hidden), F32), (two, swap(two, n, 2)))
+    from_far = [
+        call(add_kernel, "far_sum", wide, (x,), cost_us=FAR_COST) for x in terms[0]]
     grad_input = call(
-        main_kernel, "grad_input_sum", result((nodes, feat_in), BF16, False), terms[0],
+        main_kernel, "grad_input_sum", result((nodes, feat_in), BF16, False), (near_total, *from_far),
         cost_us=MAIN_COST)
     full = result((feat_in, hidden), F32, False)
     grad_self, grad_neigh = call(

time: 57.9 us -> 60.4 us (1.043)
  waiting for transfers between devices: 19.6 us -> 22 us
    ppermute x23, waiting for transfers between devices: 19.6 us -> 22 us  [swap(): return lax.ppermute(x, 'row', [(i, i ^ offset) for i in range(n)])]
    pallas_call x20 -> x21, Pallas kernels: 8.49 us -> 7.98 us  [call(): pl.pallas_call(kernel, out_shape=out_shape, in_specs=specs, out_specs=out...]
  transfers between devices with their start and end apart: 23 -> 23, of which waited for: 13 -> 14; matrix products, arithmetic and copies ran while one was open for 0% -> 0% of each run, Pallas kernels for 13% -> 12%
where the time goes in v15:
time: 60.4 us; the launch traced here: 59.9 us
  starting transfers between devices  24.8 us (41%)
  waiting for transfers between devices  22 us (36%)
  Pallas kernels  11.1 us (18%)
  local copies, waits for them, and re-layouts  1.31 us (2%)
  between operations  0.82 us (1%)
    ppermute x23, starting transfers between devices, swap(): return lax.ppermute(x, 'row', [(i, i ^ offset) for i in range(n)])  24.8 us
    ppermute x23, waiting for transfers between devices, swap(): return lax.ppermute(x, 'row', [(i, i ^ offset) for i in range(n)])  22 us
    pallas_call x21, Pallas kernels, call(): pl.pallas_call(kernel, out_shape=out_shape, in_specs=specs, out_specs=out...  7.98 us
    pallas_call x1, Pallas kernels, body(): pl.pallas_call(functools.partial(stage_kernel, (8 * block_local, (n - 8)...  3.09 us
    unnamed x4, local copies, waits for them, and re-layouts  1.31 us
  transfers between devices with their start and end apart: 23, of which 14 were waited for; matrix products, arithmetic and copies ran while one was open for 0% of the time, Pallas kernels for 12%

profile of v15, /device:TPU:0, one launch (start us, length us, event | category | flops | bytes accessed | tf_op | source)
XLA Modules:
  0.0 59.9 jit_solution(2004024562056296691)
XLA Ops:
  0.6 4.1 %collective-permute-start.4 = (bf16[512,128]{1,0:T(8,128)(2,1)}, bf16[512,128]{1,0:T(8,128)(2,1)S(1)}, u32[]{:S(2)}, u32[]{:S(2)}) collective-permute-start(bf16[512,128]{1,0:T(8,128)(2,1)} %feat_ref.1), channel_id=1, source_target_pairs={{0,8},{1,9},{2,10},{3,11},{4,12},{5,13},{6,14},{7,15},{8,0},{9,1},... | collective-permute-start | bytes 393224 | tf_op jit(solution)/shard_map/ppermute | solution.py:21
  4.7 1.5 %collective-permute-start = (bf16[512,128]{1,0:T(8,128)(2,1)}, bf16[512,128]{1,0:T(8,128)(2,1)S(1)}, u32[]{:S(2)}, u32[]{:S(2)}) collective-permute-start(bf16[512,128]{1,0:T(8,128)(2,1)} %feat_ref.1), channel_id=1, source_target_pairs={{0,2},{1,3},{2,0},{3,1},{4,6},{5,7},{6,4},{7,5},{8,10},{9,11},{10,... | collective-permute-start | bytes 393224 | tf_op jit(solution)/shard_map/ppermute | solution.py:21
  6.3 1.5 %collective-permute-start.1 = (bf16[512,128]{1,0:T(8,128)(2,1)}, bf16[512,128]{1,0:T(8,128)(2,1)S(1)}, u32[]{:S(2)}, u32[]{:S(2)}) collective-permute-start(bf16[512,128]{1,0:T(8,128)(2,1)} %feat_ref.1), channel_id=1, source_target_pairs={{0,6},{1,7},{2,4},{3,5},{4,2},{5,3},{6,0},{7,1},{8,14},{9,15},{10,... | collective-permute-start | bytes 393224 | tf_op jit(solution)/shard_map/ppermute | solution.py:21
  7.8 0.4 collective-permute-start.2
  8.2 3.1 %collective-permute-done.4.refs_0_ = bf16[512,128]{1,0:T(8,128)(2,1)S(1)} collective-permute-done((bf16[512,128]{1,0:T(8,128)(2,1)}, bf16[512,128]{1,0:T(8,128)(2,1)S(1)}, u32[]{:S(2)}, u32[]{:S(2)}) %collective-permute-start.4) | collective-permute-done | bytes 131104 | tf_op jit(solution)/shard_map/ppermute | solution.py:21
  11.4 1.7 %collective-permute-start.5 = (bf16[512,128]{1,0:T(8,128)(2,1)S(1)}, bf16[512,128]{1,0:T(8,128)(2,1)S(1)}, u32[]{:S(2)}, u32[]{:S(2)}) collective-permute-start(bf16[512,128]{1,0:T(8,128)(2,1)S(1)} %collective-permute-done.4.refs_0_), channel_id=1, source_target_pairs={{0,6},{1,7},{2,4},{3,5},{4,2},{5,3},{6,0},{7,1},{8,14},{9,15},{10,... | collective-permute-start | bytes 393224 | tf_op jit(solution)/shard_map/ppermute | solution.py:21
  13.1 0.5 collective-permute-start.6
  13.6 1.3 %collective-permute-start.7 = (bf16[512,128]{1,0:T(8,128)(2,1)S(1)}, bf16[512,128]{1,0:T(8,128)(2,1)S(1)}, u32[]{:S(2)}, u32[]{:S(2)}) collective-permute-start(bf16[512,128]{1,0:T(8,128)(2,1)S(1)} %collective-permute-done.4.refs_0_), channel_id=1, source_target_pairs={{0,4},{1,5},{2,6},{3,7},{4,0},{5,1},{6,2},{7,3},{8,12},{9,13},{10,... | collective-permute-start | bytes 393224 | tf_op jit(solution)/shard_map/ppermute | solution.py:21
  14.9 0.7 %copy-done = s32[60]{0:T(128)S(1)} copy-done((s32[60]{0:T(128)S(1)}, s32[60]{0:T(128)}, u32[]{:S(2)}) %copy-start) | copy-done | bytes 264
  15.5 0.7 %copy-done.1 = s32[60]{0:T(128)S(1)} copy-done((s32[60]{0:T(128)S(1)}, s32[60]{0:T(128)}, u32[]{:S(2)}) %copy-start.1) | copy-done | bytes 264
  16.2 3.1 %stage_arguments.1 = (bf16[60,128,128]{2,1,0:T(8,128)(2,1)S(1)}, bf16[128,256]{1,0:T(8,128)(2,1)S(1)}, bf16[128,256]{1,0:T(8,128)(2,1)S(1)}, f32[4,128,128]{2,1,...) custom-call(s32[1]{0:T(128)} %bitcast.me_ref, ...), custom_call_target="tpu_custom_call" | custom-call | flops 3300000000 | bytes 10800000 | tf_op jit(solution)/shard_map/stage_arguments/pallas_call | solution.py:366
  19.3 0.1 collective-permute-start.3
  19.4 1.0 %collective-permute-done.5.refs_1_ = bf16[512,128]{1,0:T(8,128)(2,1)S(1)} collective-permute-done((bf16[512,128]{1,0:T(8,128)(2,1)S(1)}, bf16[512,128]{1,0:T(8,128)(2,1)S(1)}, u32[]{:S(2)}, u32[]{:S(2)}) %collective-permute-start.5) | collective-permute-done | bytes 131104 | tf_op jit(solution)/shard_map/ppermute | solution.py:21
  20.4 0.6 %collective-permute-done.6.refs_2_ = bf16[512,128]{1,0:T(8,128)(2,1)S(1)} collective-permute-done((bf16[512,128]{1,0:T(8,128)(2,1)S(1)}, bf16[512,128]{1,0:T(8,128)(2,1)S(1)}, u32[]{:S(2)}, u32[]{:S(2)}) %collective-permute-start.6) | collective-permute-done | bytes 131104 | tf_op jit(solution)/shard_map/ppermute | solution.py:21
  21.0 0.1 collective-permute-done.7.refs_3_
  21.2 0.1 collective-permute-start.8
  21.3 0.8 %forward_near.1.near_ref = f32[5,128,128]{2,1,0:T(8,128)S(1)} custom-call(s32[363]{0:T(512)S(4)} %get-tuple-element.37.index_ref, bf16[60,128,128]{2,1,0:T(8,128)(2,1)S(1)} %get-tuple-element.38.tiles_ref, bf16[4,512,128]{2,1,0:T(8,128)(2,1)S(1)} %pack_square.2.same_ref, bf16[4,512,128]{2,1,0:T(8,128)(2,1)S(1)} %collective-permute-done.3.other_ref), custom_call_target="tpu_custom_call" | custom-call | flops 110000000 | bytes 360000 | tf_op jit(solution)/shard_map/forward_near/pallas_call | solution.py:343
  22.2 1.0 %collective-permute-done.8.refs_1_ = bf16[4,512,128]{2,1,0:T(8,128)(2,1)S(1)} collective-permute-done((bf16[4,512,128]{2,1,0:T(8,128)(2,1)S(1)}, bf16[4,512,128]{2,1,0:T(8,128)(2,1)S(1)}, u32[]{:S(2)}, u32[]{:S(2)}) %collective-permute-start.8) | collective-permute-done | bytes 524320 | tf_op jit(solution)/shard_map/ppermute | solution.py:21
  23.2 2.3 %forward_layer.1 = (bf16[512,256]{1,0:T(8,128)(2,1)}, bf16[512,256]{1,0:T(8,128)(2,1)S(1)}, bf16[512,256]{1,0:T(8,128)(2,1)S(1)}, bf16[512,256]{1,0:T(8,128)(2,1...) custom-call(s32[363]{0:T(512)S(4)} %get-tuple-element.37.index_ref, ...), custom_call_target="tpu_custom_call" | custom-call | flops 3300000000 | bytes 10800000 | tf_op jit(solution)/shard_map/forward_layer/pallas_call | solution.py:343
  25.5 0.5 weights.1
  26.0 0.2 collective-permute-start.9
  26.2 0.8 %backward_tiles.3.acc_ref = f32[33,128,128]{2,1,0:T(8,128)S(1)} custom-call(s32[363]{0:T(512)S(4)} %get-tuple-element.37.index_ref, bf16[60,128,128]{2,1,0:T(8,128)(2,1)S(1)} %get-tuple-element.38.tiles_ref, bf16[4,256,128]{2,1,0:T(8,128)(2,1)S(1)} %get-tuple-element.48.gt_ref, f32[128,256]{1,0:T(8,128)S(1)} %get-tuple-element.52.refs_0_.wkeep_ref), custom_call_target="tpu_custom_call" | custom-call | flops 1650000000 | bytes 5400000 | tf_op jit(solution)/shard_map/backward_tiles/pallas_call | solution.py:343
  27.1 0.4 collective-permute-start.12
  27.5 1.1 %backward_tiles.2.acc_ref = f32[33,128,128]{2,1,0:T(8,128)S(1)} custom-call(s32[363]{0:T(512)S(4)} %get-tuple-element.37.index_ref, bf16[60,128,128]{2,1,0:T(8,128)(2,1)S(1)} %get-tuple-element.38.tiles_ref, bf16[4,256,128]{2,1,0:T(8,128)(2,1)S(1)} %get-tuple-element.48.gt_ref, f32[128,256]{1,0:T(8,128)S(1)} %get-tuple-element.52.refs_0_.wkeep_ref), custom_call_target="tpu_custom_call" | custom-call | flops 330000000 | bytes 1080000 | tf_op jit(solution)/shard_map/backward_tiles/pallas_call | solution.py:343
  28.9 1.0 %collective-permute-done.12.got_ref = f32[4,512,128]{2,1,0:T(8,128)S(1)} collective-permute-done((f32[4,512,128]{2,1,0:T(8,128)S(1)}, f32[4,512,128]{2,1,0:T(8,128)S(1)}, u32[]{:S(2)}, u32[]{:S(2)}) %collective-permute-start.12) | collective-permute-done | bytes 1048608 | tf_op jit(solution)/shard_map/ppermute | solution.py:21
  29.8 0.1 pair_sum_weights.1
  29.9 2.0 %collective-permute-start.13 = (bf16[640,128]{1,0:T(8,128)(2,1)S(1)}, bf16[640,128]{1,0:T(8,128)(2,1)S(1)}, u32[]{:S(2)}, u32[]{:S(2)}) collective-permute-start(bf16[640,128]{1,0:T(8,128)(2,1)S(1)} %get-tuple-element.61), channel_id=1, source_target_pairs={{0,6},{1,7},{2,4},{3,5},{4,2},{5,3},{6,0},{7,1},{8,14},{9,15},{10,... | collective-permute-start | bytes 491528 | tf_op jit(solution)/shard_map/ppermute | solution.py:21
  31.9 0.6 collective-permute-start.14
  32.4 1.0 %collective-permute-start.15 = (bf16[640,128]{1,0:T(8,128)(2,1)S(1)}, bf16[640,128]{1,0:T(8,128)(2,1)S(1)}, u32[]{:S(2)}, u32[]{:S(2)}) collective-permute-start(bf16[640,128]{1,0:T(8,128)(2,1)S(1)} %get-tuple-element.63), channel_id=1, source_target_pairs={{0,4},{1,5},{2,6},{3,7},{4,0},{5,1},{6,2},{7,3},{8,12},{9,13},{10,... | collective-permute-start | bytes 491528 | tf_op jit(solution)/shard_map/ppermute | solution.py:21
  33.5 1.9 %collective-permute-start.11 = (bf16[512,128]{1,0:T(8,128)(2,1)S(1)}, bf16[512,128]{1,0:T(8,128)(2,1)S(1)}, u32[]{:S(2)}, u32[]{:S(2)}) collective-permute-start(bf16[512,128]{1,0:T(8,128)(2,1)S(1)} %get-tuple-element.56), channel_id=1, source_target_pairs={{0,6},{1,7},{2,4},{3,5},{4,2},{5,3},{6,0},{7,1},{8,14},{9,15},{10,... | collective-permute-start | bytes 393224 | tf_op jit(solution)/shard_map/ppermute | solution.py:21
  35.5 2.5 %collective-permute-done.13.refs_0_ = bf16[640,128]{1,0:T(8,128)(2,1)S(1)} collective-permute-done((bf16[640,128]{1,0:T(8,128)(2,1)S(1)}, bf16[640,128]{1,0:T(8,128)(2,1)S(1)}, u32[]{:S(2)}, u32[]{:S(2)}) %collective-permute-start.13) | collective-permute-done | bytes 163872 | tf_op jit(solution)/shard_map/ppermute | solution.py:21
  38.0 3.4 %collective-permute-done.14.refs_1_ = bf16[640,128]{1,0:T(8,128)(2,1)S(1)} collective-permute-done((bf16[640,128]{1,0:T(8,128)(2,1)S(1)}, bf16[640,128]{1,0:T(8,128)(2,1)S(1)}, u32[]{:S(2)}, u32[]{:S(2)}) %collective-permute-start.14) | collective-permute-done | bytes 163872 | tf_op jit(solution)/shard_map/ppermute | solution.py:21
  41.4 0.7 %collective-permute-done.15.refs_2_ = bf16[640,128]{1,0:T(8,128)(2,1)S(1)} collective-permute-done((bf16[640,128]{1,0:T(8,128)(2,1)S(1)}, bf16[640,128]{1,0:T(8,128)(2,1)S(1)}, u32[]{:S(2)}, u32[]{:S(2)}) %collective-permute-start.15) | collective-permute-done | bytes 163872 | tf_op jit(solution)/shard_map/ppermute | solution.py:21
  42.0 0.1 square_sum_weights.1
  42.1 1.6 %collective-permute-start.16 = (f32[32,256]{1,0:T(8,128)S(1)}, f32[32,256]{1,0:T(8,128)S(1)}, u32[]{:S(2)}, u32[]{:S(2)}) collective-permute-start(f32[32,256]{1,0:T(8,128)S(1)} %get-tuple-element.64.own_ref), channel_id=1, source_target_pairs={{0,8},{1,9},{2,10},{3,11},{4,12},{5,13},{6,14},{7,15},{8,0},{9,1},... | collective-permute-start | bytes 98312 | tf_op jit(solution)/shard_map/ppermute | solution.py:21
  43.7 3.5 %collective-permute-done.16.got_ref = f32[32,256]{1,0:T(8,128)S(1)} collective-permute-done((f32[32,256]{1,0:T(8,128)S(1)}, f32[32,256]{1,0:T(8,128)S(1)}, u32[]{:S(2)}, u32[]{:S(2)}) %collective-permute-start.16) | collective-permute-done | bytes 32800 | tf_op jit(solution)/shard_map/ppermute | solution.py:21
  47.2 0.3 collective-permute-start.17
  47.5 2.9 %collective-permute-start.20 = (bf16[512,128]{1,0:T(8,128)(2,1)S(1)}, bf16[512,128]{1,0:T(8,128)(2,1)S(1)}, u32[]{:S(2)}, u32[]{:S(2)}) collective-permute-start(bf16[512,128]{1,0:T(8,128)(2,1)S(1)} %get-tuple-element.67), channel_id=1, source_target_pairs={{0,8},{1,9},{2,10},{3,11},{4,12},{5,13},{6,14},{7,15},{8,0},{9,1},... | collective-permute-start | bytes 393224 | tf_op jit(solution)/shard_map/ppermute | solution.py:21
  50.4 0.8 %collective-permute-done.17.refs_1_ = f32[32,256]{1,0:T(8,128)S(1)} collective-permute-done((f32[32,256]{1,0:T(8,128)S(1)}, f32[32,256]{1,0:T(8,128)S(1)}, u32[]{:S(2)}, u32[]{:S(2)}) %collective-permute-start.17) | collective-permute-done | bytes 32800 | tf_op jit(solution)/shard_map/ppermute | solution.py:21
  51.2 0.3 collective-permute-start.21
  51.5 1.6 %collective-permute-start.18 = (bf16[512,128]{1,0:T(8,128)(2,1)S(1)}, bf16[512,128]{1,0:T(8,128)(2,1)S(1)}, u32[]{:S(2)}, u32[]{:S(2)}) collective-permute-start(bf16[512,128]{1,0:T(8,128)(2,1)S(1)} %get-tuple-element.65), channel_id=1, source_target_pairs={{0,4},{1,5},{2,6},{3,7},{4,0},{5,1},{6,2},{7,3},{8,12},{9,13},{10,... | collective-permute-start | bytes 393224 | tf_op jit(solution)/shard_map/ppermute | solution.py:21
  53.1 0.6 collective-permute-start.19
  53.7 1.8 %collective-permute-done.21.refs_1_ = f32[2,32,256]{2,1,0:T(8,128)S(1)} collective-permute-done((f32[2,32,256]{2,1,0:T(8,128)S(1)}, f32[2,32,256]{2,1,0:T(8,128)S(1)}, u32[]{:S(2)}, u32[]{:S(2)}) %collective-permute-start.21) | collective-permute-done | bytes 65568 | tf_op jit(solution)/shard_map/ppermute | solution.py:21
  55.6 1.0 %collective-permute-done.18.refs_1_ = bf16[512,128]{1,0:T(8,128)(2,1)S(1)} collective-permute-done((bf16[512,128]{1,0:T(8,128)(2,1)S(1)}, bf16[512,128]{1,0:T(8,128)(2,1)S(1)}, u32[]{:S(2)}, u32[]{:S(2)}) %collective-permute-start.18) | collective-permute-done | bytes 131104 | tf_op jit(solution)/shard_map/ppermute | solution.py:21
  56.6 1.5 %collective-permute-done.19.refs_2_ = bf16[512,128]{1,0:T(8,128)(2,1)S(1)} collective-permute-done((bf16[512,128]{1,0:T(8,128)(2,1)S(1)}, bf16[512,128]{1,0:T(8,128)(2,1)S(1)}, u32[]{:S(2)}, u32[]{:S(2)}) %collective-permute-start.19) | collective-permute-done | bytes 131104 | tf_op jit(solution)/shard_map/ppermute | solution.py:21
  58.1 0.3 near_sum.1.near_ref
  58.4 0.8 %grad_input_sum.1 = bf16[512,128]{1,0:T(8,128)(2,1)} custom-call(f32[512,128]{1,0:T(8,128)S(1)} %near_sum.1.near_ref, f32[512,128]{1,0:T(8,128)S(1)} %far_sum.1.refs_0_), custom_call_target="tpu_custom_call" | custom-call | flops 220000000 | bytes 720000 | tf_op jit(solution)/shard_map/grad_input_sum/pallas_call | solution.py:343
  59.2 0.7 %write_weights.1 = (f32[128,256]{1,0:T(8,128)}, f32[128,256]{1,0:T(8,128)}) custom-call(s32[363]{0:T(512)S(4)} %get-tuple-element.37.index_ref, f32[2,2,32,256]{3,2,1,0:T(8,128)S(1)} %pack_weights.3.weight_ref, f32[2,2,32,256]{3,2,1,0:T(8,128)S(1)} %collective-permute-done.22.other_ref), custom_call_target="tpu_custom_call" | custom-call | flops 220000000 | bytes 720000 | tf_op jit(solution)/shard_map/write_weights/pallas_call | solution.py:343
  (24 shorter events, 0.6 us)
Async XLA Ops:
  0.6 10.7 %collective-permute-start.4 = (bf16[512,128]{1,0:T(8,128)(2,1)}, bf16[512,128]{1,0:T(8,128)(2,1)S(1)}, u32[]{:S(2)}, u32[]{:S(2)}) collective-permute-start(bf16[512,128]{1,0:T(8,128)(2,1)} %feat_ref.1), channel_id=1, source_target_pairs={{0,8},{1,9},{2,10},{3,11},{4,12},{5,13},{6,14},{7,15},{8,0},{9,1},... | collective-permute-start | bytes 393224 | tf_op jit(solution)/shard_map/ppermute | solution.py:21
  4.7 8.9 %collective-permute-start = (bf16[512,128]{1,0:T(8,128)(2,1)}, bf16[512,128]{1,0:T(8,128)(2,1)S(1)}, u32[]{:S(2)}, u32[]{:S(2)}) collective-permute-start(bf16[512,128]{1,0:T(8,128)(2,1)} %feat_ref.1), channel_id=1, source_target_pairs={{0,2},{1,3},{2,0},{3,1},{4,6},{5,7},{6,4},{7,5},{8,10},{9,11},{10,... | collective-permute-start | bytes 393224 | tf_op jit(solution)/shard_map/ppermute | solution.py:21
  6.3 13.0 %collective-permute-start.1 = (bf16[512,128]{1,0:T(8,128)(2,1)}, bf16[512,128]{1,0:T(8,128)(2,1)S(1)}, u32[]{:S(2)}, u32[]{:S(2)}) collective-permute-start(bf16[512,128]{1,0:T(8,128)(2,1)} %feat_ref.1), channel_id=1, source_target_pairs={{0,6},{1,7},{2,4},{3,5},{4,2},{5,3},{6,0},{7,1},{8,14},{9,15},{10,... | collective-permute-start | bytes 393224 | tf_op jit(solution)/shard_map/ppermute | solution.py:21
  7.8 11.5 %collective-permute-start.2 = (bf16[512,128]{1,0:T(8,128)(2,1)}, bf16[512,128]{1,0:T(8,128)(2,1)S(1)}, u32[]{:S(2)}, u32[]{:S(2)}) collective-permute-start(bf16[512,128]{1,0:T(8,128)(2,1)} %feat_ref.1), channel_id=1, source_target_pairs={{0,4},{1,5},{2,6},{3,7},{4,0},{5,1},{6,2},{7,3},{8,12},{9,13},{10,... | collective-permute-start | bytes 393224 | tf_op jit(solution)/shard_map/ppermute | solution.py:21
  11.4 9.1 %collective-permute-start.5 = (bf16[512,128]{1,0:T(8,128)(2,1)S(1)}, bf16[512,128]{1,0:T(8,128)(2,1)S(1)}, u32[]{:S(2)}, u32[]{:S(2)}) collective-permute-start(bf16[512,128]{1,0:T(8,128)(2,1)S(1)} %collective-permute-done.4.refs_0_), channel_id=1, source_target_pairs={{0,6},{1,7},{2,4},{3,5},{4,2},{5,3},{6,0},{7,1},{8,14},{9,15},{10,... | collective-permute-start | bytes 393224 | tf_op jit(solution)/shard_map/ppermute | solution.py:21
  13.1 7.9 %collective-permute-start.6 = (bf16[512,128]{1,0:T(8,128)(2,1)S(1)}, bf16[512,128]{1,0:T(8,128)(2,1)S(1)}, u32[]{:S(2)}, u32[]{:S(2)}) collective-permute-start(bf16[512,128]{1,0:T(8,128)(2,1)S(1)} %collective-permute-done.4.refs_0_), channel_id=1, source_target_pairs={{0,2},{1,3},{2,0},{3,1},{4,6},{5,7},{6,4},{7,5},{8,10},{9,11},{10,... | collective-permute-start | bytes 393224 | tf_op jit(solution)/shard_map/ppermute | solution.py:21
  13.6 7.6 %collective-permute-start.7 = (bf16[512,128]{1,0:T(8,128)(2,1)S(1)}, bf16[512,128]{1,0:T(8,128)(2,1)S(1)}, u32[]{:S(2)}, u32[]{:S(2)}) collective-permute-start(bf16[512,128]{1,0:T(8,128)(2,1)S(1)} %collective-permute-done.4.refs_0_), channel_id=1, source_target_pairs={{0,4},{1,5},{2,6},{3,7},{4,0},{5,1},{6,2},{7,3},{8,12},{9,13},{10,... | collective-permute-start | bytes 393224 | tf_op jit(solution)/shard_map/ppermute | solution.py:21
  14.8 0.7 %copy-start = (s32[60]{0:T(128)S(1)}, s32[60]{0:T(128)}, u32[]{:S(2)}) copy-start(s32[60]{0:T(128)} %trow_ref.1) | copy-start | bytes 724
  15.5 0.7 %copy-start.1 = (s32[60]{0:T(128)S(1)}, s32[60]{0:T(128)}, u32[]{:S(2)}) copy-start(s32[60]{0:T(128)} %tcol_ref.1) | copy-start | bytes 724
  19.3 2.0 %collective-permute-start.3 = (bf16[4,512,128]{2,1,0:T(8,128)(2,1)S(1)}, bf16[4,512,128]{2,1,0:T(8,128)(2,1)S(1)}, u32[]{:S(2)}, u32[]{:S(2)}) collective-permute-start(bf16[4,512,128]{2,1,0:T(8,128)(2,1)S(1)} %pack_square.2.same_ref), channel_id=1, source_target_pairs={{0,1},{1,0},{2,3},{3,2},{4,5},{5,4},{6,7},{7,6},{8,9},{9,8},{10,11... | collective-permute-start | bytes 1572872 | tf_op jit(solution)/shard_map/ppermute | solution.py:21
  21.2 2.0 %collective-permute-start.8 = (bf16[4,512,128]{2,1,0:T(8,128)(2,1)S(1)}, bf16[4,512,128]{2,1,0:T(8,128)(2,1)S(1)}, u32[]{:S(2)}, u32[]{:S(2)}) collective-permute-start(bf16[4,512,128]{2,1,0:T(8,128)(2,1)S(1)} %pack_square.3.refs_0_), channel_id=1, source_target_pairs={{0,1},{1,0},{2,3},{3,2},{4,5},{5,4},{6,7},{7,6},{8,9},{9,8},{10,11... | collective-permute-start | bytes 1572872 | tf_op jit(solution)/shard_map/ppermute | solution.py:21
  26.0 2.6 %collective-permute-start.9 = (f32[128,256]{1,0:T(8,128)S(1)}, f32[128,256]{1,0:T(8,128)S(1)}, u32[]{:S(2)}, u32[]{:S(2)}) collective-permute-start(f32[128,256]{1,0:T(8,128)S(1)} %get-tuple-element.53), channel_id=1, source_target_pairs={{0,1},{1,0},{2,3},{3,2},{4,5},{5,4},{6,7},{7,6},{8,9},{9,8},{10,11... | collective-permute-start | bytes 393224 | tf_op jit(solution)/shard_map/ppermute | solution.py:21
  27.1 2.7 %collective-permute-start.12 = (f32[4,512,128]{2,1,0:T(8,128)S(1)}, f32[4,512,128]{2,1,0:T(8,128)S(1)}, u32[]{:S(2)}, u32[]{:S(2)}) collective-permute-start(f32[4,512,128]{2,1,0:T(8,128)S(1)} %send.3), channel_id=1, source_target_pairs={{0,1},{1,0},{2,3},{3,2},{4,5},{5,4},{6,7},{7,6},{8,9},{9,8},{10,11... | collective-permute-start | bytes 3145736 | tf_op jit(solution)/shard_map/ppermute | solution.py:21
  28.8 4.7 %collective-permute-start.10 = (f32[4,512,128]{2,1,0:T(8,128)S(1)}, f32[4,512,128]{2,1,0:T(8,128)S(1)}, u32[]{:S(2)}, u32[]{:S(2)}) collective-permute-start(f32[4,512,128]{2,1,0:T(8,128)S(1)} %send.2), channel_id=1, source_target_pairs={{0,1},{1,0},{2,3},{3,2},{4,5},{5,4},{6,7},{7,6},{8,9},{9,8},{10,11... | collective-permute-start | bytes 3145736 | tf_op jit(solution)/shard_map/ppermute | solution.py:21
  29.9 8.0 %collective-permute-start.13 = (bf16[640,128]{1,0:T(8,128)(2,1)S(1)}, bf16[640,128]{1,0:T(8,128)(2,1)S(1)}, u32[]{:S(2)}, u32[]{:S(2)}) collective-permute-start(bf16[640,128]{1,0:T(8,128)(2,1)S(1)} %get-tuple-element.61), channel_id=1, source_target_pairs={{0,6},{1,7},{2,4},{3,5},{4,2},{5,3},{6,0},{7,1},{8,14},{9,15},{10,... | collective-permute-start | bytes 491528 | tf_op jit(solution)/shard_map/ppermute | solution.py:21
  31.9 9.5 %collective-permute-start.14 = (bf16[640,128]{1,0:T(8,128)(2,1)S(1)}, bf16[640,128]{1,0:T(8,128)(2,1)S(1)}, u32[]{:S(2)}, u32[]{:S(2)}) collective-permute-start(bf16[640,128]{1,0:T(8,128)(2,1)S(1)} %get-tuple-element.62), channel_id=1, source_target_pairs={{0,2},{1,3},{2,0},{3,1},{4,6},{5,7},{6,4},{7,5},{8,10},{9,11},{10,... | collective-permute-start | bytes 491528 | tf_op jit(solution)/shard_map/ppermute | solution.py:21
  32.4 9.6 %collective-permute-start.15 = (bf16[640,128]{1,0:T(8,128)(2,1)S(1)}, bf16[640,128]{1,0:T(8,128)(2,1)S(1)}, u32[]{:S(2)}, u32[]{:S(2)}) collective-permute-start(bf16[640,128]{1,0:T(8,128)(2,1)S(1)} %get-tuple-element.63), channel_id=1, source_target_pairs={{0,4},{1,5},{2,6},{3,7},{4,0},{5,1},{6,2},{7,3},{8,12},{9,13},{10,... | collective-permute-start | bytes 491528 | tf_op jit(solution)/shard_map/ppermute | solution.py:21
  33.5 13.6 %collective-permute-start.11 = (bf16[512,128]{1,0:T(8,128)(2,1)S(1)}, bf16[512,128]{1,0:T(8,128)(2,1)S(1)}, u32[]{:S(2)}, u32[]{:S(2)}) collective-permute-start(bf16[512,128]{1,0:T(8,128)(2,1)S(1)} %get-tuple-element.56), channel_id=1, source_target_pairs={{0,6},{1,7},{2,4},{3,5},{4,2},{5,3},{6,0},{7,1},{8,14},{9,15},{10,... | collective-permute-start | bytes 393224 | tf_op jit(solution)/shard_map/ppermute | solution.py:21
  42.1 5.1 %collective-permute-start.16 = (f32[32,256]{1,0:T(8,128)S(1)}, f32[32,256]{1,0:T(8,128)S(1)}, u32[]{:S(2)}, u32[]{:S(2)}) collective-permute-start(f32[32,256]{1,0:T(8,128)S(1)} %get-tuple-element.64.own_ref), channel_id=1, source_target_pairs={{0,8},{1,9},{2,10},{3,11},{4,12},{5,13},{6,14},{7,15},{8,0},{9,1},... | collective-permute-start | bytes 98312 | tf_op jit(solution)/shard_map/ppermute | solution.py:21
  47.2 4.0 %collective-permute-start.17 = (f32[32,256]{1,0:T(8,128)S(1)}, f32[32,256]{1,0:T(8,128)S(1)}, u32[]{:S(2)}, u32[]{:S(2)}) collective-permute-start(f32[32,256]{1,0:T(8,128)S(1)} %weight_sum.1.refs_0_), channel_id=1, source_target_pairs={{0,4},{1,5},{2,6},{3,7},{4,0},{5,1},{6,2},{7,3},{8,12},{9,13},{10,... | collective-permute-start | bytes 98312 | tf_op jit(solution)/shard_map/ppermute | solution.py:21
  47.5 8.1 %collective-permute-start.20 = (bf16[512,128]{1,0:T(8,128)(2,1)S(1)}, bf16[512,128]{1,0:T(8,128)(2,1)S(1)}, u32[]{:S(2)}, u32[]{:S(2)}) collective-permute-start(bf16[512,128]{1,0:T(8,128)(2,1)S(1)} %get-tuple-element.67), channel_id=1, source_target_pairs={{0,8},{1,9},{2,10},{3,11},{4,12},{5,13},{6,14},{7,15},{8,0},{9,1},... | collective-permute-start | bytes 393224 | tf_op jit(solution)/shard_map/ppermute | solution.py:21
  51.2 4.3 %collective-permute-start.21 = (f32[2,32,256]{2,1,0:T(8,128)S(1)}, f32[2,32,256]{2,1,0:T(8,128)S(1)}, u32[]{:S(2)}, u32[]{:S(2)}) collective-permute-start(f32[2,32,256]{2,1,0:T(8,128)S(1)} %pack_weights.2.refs_0_), channel_id=1, source_target_pairs={{0,2},{1,3},{2,0},{3,1},{4,6},{5,7},{6,4},{7,5},{8,10},{9,11},{10,... | collective-permute-start | bytes 196616 | tf_op jit(solution)/shard_map/ppermute | solution.py:21
  51.5 5.0 %collective-permute-start.18 = (bf16[512,128]{1,0:T(8,128)(2,1)S(1)}, bf16[512,128]{1,0:T(8,128)(2,1)S(1)}, u32[]{:S(2)}, u32[]{:S(2)}) collective-permute-start(bf16[512,128]{1,0:T(8,128)(2,1)S(1)} %get-tuple-element.65), channel_id=1, source_target_pairs={{0,4},{1,5},{2,6},{3,7},{4,0},{5,1},{6,2},{7,3},{8,12},{9,13},{10,... | collective-permute-start | bytes 393224 | tf_op jit(solution)/shard_map/ppermute | solution.py:21
  53.1 5.0 %collective-permute-start.19 = (bf16[512,128]{1,0:T(8,128)(2,1)S(1)}, bf16[512,128]{1,0:T(8,128)(2,1)S(1)}, u32[]{:S(2)}, u32[]{:S(2)}) collective-permute-start(bf16[512,128]{1,0:T(8,128)(2,1)S(1)} %get-tuple-element.66), channel_id=1, source_target_pairs={{0,2},{1,3},{2,0},{3,1},{4,6},{5,7},{6,4},{7,5},{8,10},{9,11},{10,... | collective-permute-start | bytes 393224 | tf_op jit(solution)/shard_map/ppermute | solution.py:21
  55.5 3.7 %collective-permute-start.22 = (f32[2,2,32,256]{3,2,1,0:T(8,128)S(1)}, f32[2,2,32,256]{3,2,1,0:T(8,128)S(1)}, u32[]{:S(2)}, u32[]{:S(2)}) collective-permute-start(f32[2,2,32,256]{3,2,1,0:T(8,128)S(1)} %pack_weights.3.weight_ref), channel_id=1, source_target_pairs={{0,1},{1,0},{2,3},{3,2},{4,5},{5,4},{6,7},{7,6},{8,9},{9,8},{10,11... | collective-permute-start | bytes 393224 | tf_op jit(solution)/shard_map/ppermute | solution.py:21

commit v16 on v13

--- a/solution.py
+++ b/solution.py
@@ -254,10 +254,9 @@
     for weight_ref, ref in zip((w1, w2, w3), pieces):
         rows, columns = weight_ref.shape
         start = nodes
-        for part in split_bf16(weight_ref[...]):
-            for column in range(0, columns, lanes):
-                ref[pl.ds(start, rows), :] = part[:, column:column + lanes]
-                start += rows
+        for column in range(0, columns, lanes):
+            ref[pl.ds(start, rows), :] = weight_ref[:, column:column + lanes].astype(BF16)
+            start += rows
 
 
 def add_two_kernel(own_ref, got_ref, out_ref):
@@ -276,14 +275,11 @@
     nodes, lanes = own_ref.shape
     add_kernel(own_ref, *[ref.at[pl.ds(0, nodes), :] for ref in got_refs], out_ref)
     rows, columns = weight_ref.shape
-    cuts = columns // lanes
-    for cut in range(cuts):
+    for cut in range(columns // lanes):
         span = pl.ds(cut * lanes, lanes)
         total = weight_ref[:, span]
         for ref in got_refs[:3]:
-            high = ref[pl.ds(nodes + cut * rows, rows), :]
-            low = ref[pl.ds(nodes + (cuts + cut) * rows, rows), :]
-            total = total + (high.astype(F32) + low.astype(F32))
+            total = total + ref[pl.ds(nodes + cut * rows, rows), :].astype(F32)
         weight_out[:, span] = total
 
 
@@ -429,7 +425,7 @@
             send = call(functools.partial(send_kernel, s - section), "send", send_shape, operands)
             got[s] = swap(send, n, 1)
 
-    extra = result((nodes + 2 * chunk.shape[0] * (hidden // feat_in), feat_in), BF16)
+    extra = result((nodes + chunk.shape[0] * (hidden // feat_in), feat_in), BF16)
     terms = [[]]
     for s in range(1, squares):
         operands = (sums[1], got[s])

time: 58 us -> 57.4 us (0.990)
  starting transfers between devices: 25.7 us -> 22.3 us
  waiting for transfers between devices: 18.5 us -> 20.7 us
  Pallas kernels: 11.6 us -> 12.2 us
    ppermute x23, starting transfers between devices: 25.7 us -> 22.3 us  [swap(): return lax.ppermute(x, 'row', [(i, i ^ offset) for i in range(n)])]
    ppermute x23, waiting for transfers between devices: 18.5 us -> 20.7 us  [swap(): return lax.ppermute(x, 'row', [(i, i ^ offset) for i in range(n)])]
    pallas_call x20, Pallas kernels: 8.49 us -> 9.07 us  [call(): pl.pallas_call(kernel, out_shape=out_shape, in_specs=specs, out_specs=out...]
  transfers between devices with their start and end apart: 23 -> 23, of which waited for: 12 -> 12; matrix products, arithmetic and copies ran while one was open for 0% -> 0% of each run, Pallas kernels for 13% -> 14%
where the time goes in v16:
time: 57.4 us
  starting transfers between devices  22.3 us (39%)
  waiting for transfers between devices  20.7 us (36%)
  Pallas kernels  12.2 us (21%)
  local copies, waits for them, and re-layouts  1.31 us (2%)
  between operations  0.83 us (1%)
    ppermute x23, starting transfers between devices, swap(): return lax.ppermute(x, 'row', [(i, i ^ offset) for i in range(n)])  22.3 us
    ppermute x23, waiting for transfers between devices, swap(): return lax.ppermute(x, 'row', [(i, i ^ offset) for i in range(n)])  20.7 us
    pallas_call x20, Pallas kernels, call(): pl.pallas_call(kernel, out_shape=out_shape, in_specs=specs, out_specs=out...  9.07 us
    pallas_call x1, Pallas kernels, body(): pl.pallas_call(functools.partial(stage_kernel, (8 * block_local, (n - 8)...  3.09 us
    unnamed x4, local copies, waits for them, and re-layouts  1.31 us
  transfers between devices with their start and end apart: 23, of which 12 were waited for; matrix products, arithmetic and copies ran while one was open for 0% of the time, Pallas kernels for 14%

profile of v16, /device:TPU:0, one launch (start us, length us, event | category | flops | bytes accessed | tf_op | source)
XLA Modules:
  0.0 57.4 jit_solution(10155292366899124828)
XLA Ops:
  0.6 4.1 %collective-permute-start.4 = (bf16[512,128]{1,0:T(8,128)(2,1)}, bf16[512,128]{1,0:T(8,128)(2,1)S(1)}, u32[]{:S(2)}, u32[]{:S(2)}) collective-permute-start(bf16[512,128]{1,0:T(8,128)(2,1)} %feat_ref.1), channel_id=1, source_target_pairs={{0,8},{1,9},{2,10},{3,11},{4,12},{5,13},{6,14},{7,15},{8,0},{9,1},... | collective-permute-start | bytes 393224 | tf_op jit(solution)/shard_map/ppermute | solution.py:21
  4.7 1.5 %collective-permute-start = (bf16[512,128]{1,0:T(8,128)(2,1)}, bf16[512,128]{1,0:T(8,128)(2,1)S(1)}, u32[]{:S(2)}, u32[]{:S(2)}) collective-permute-start(bf16[512,128]{1,0:T(8,128)(2,1)} %feat_ref.1), channel_id=1, source_target_pairs={{0,2},{1,3},{2,0},{3,1},{4,6},{5,7},{6,4},{7,5},{8,10},{9,11},{10,... | collective-permute-start | bytes 393224 | tf_op jit(solution)/shard_map/ppermute | solution.py:21
  6.3 1.5 %collective-permute-start.1 = (bf16[512,128]{1,0:T(8,128)(2,1)}, bf16[512,128]{1,0:T(8,128)(2,1)S(1)}, u32[]{:S(2)}, u32[]{:S(2)}) collective-permute-start(bf16[512,128]{1,0:T(8,128)(2,1)} %feat_ref.1), channel_id=1, source_target_pairs={{0,6},{1,7},{2,4},{3,5},{4,2},{5,3},{6,0},{7,1},{8,14},{9,15},{10,... | collective-permute-start | bytes 393224 | tf_op jit(solution)/shard_map/ppermute | solution.py:21
  7.8 0.4 collective-permute-start.2
  8.2 3.1 %collective-permute-done.4.refs_0_ = bf16[512,128]{1,0:T(8,128)(2,1)S(1)} collective-permute-done((bf16[512,128]{1,0:T(8,128)(2,1)}, bf16[512,128]{1,0:T(8,128)(2,1)S(1)}, u32[]{:S(2)}, u32[]{:S(2)}) %collective-permute-start.4) | collective-permute-done | bytes 131104 | tf_op jit(solution)/shard_map/ppermute | solution.py:21
  11.4 1.7 %collective-permute-start.5 = (bf16[512,128]{1,0:T(8,128)(2,1)S(1)}, bf16[512,128]{1,0:T(8,128)(2,1)S(1)}, u32[]{:S(2)}, u32[]{:S(2)}) collective-permute-start(bf16[512,128]{1,0:T(8,128)(2,1)S(1)} %collective-permute-done.4.refs_0_), channel_id=1, source_target_pairs={{0,6},{1,7},{2,4},{3,5},{4,2},{5,3},{6,0},{7,1},{8,14},{9,15},{10,... | collective-permute-start | bytes 393224 | tf_op jit(solution)/shard_map/ppermute | solution.py:21
  13.1 0.5 collective-permute-start.6
  13.6 1.3 %collective-permute-start.7 = (bf16[512,128]{1,0:T(8,128)(2,1)S(1)}, bf16[512,128]{1,0:T(8,128)(2,1)S(1)}, u32[]{:S(2)}, u32[]{:S(2)}) collective-permute-start(bf16[512,128]{1,0:T(8,128)(2,1)S(1)} %collective-permute-done.4.refs_0_), channel_id=1, source_target_pairs={{0,4},{1,5},{2,6},{3,7},{4,0},{5,1},{6,2},{7,3},{8,12},{9,13},{10,... | collective-permute-start | bytes 393224 | tf_op jit(solution)/shard_map/ppermute | solution.py:21
  14.9 0.7 %copy-done = s32[60]{0:T(128)S(1)} copy-done((s32[60]{0:T(128)S(1)}, s32[60]{0:T(128)}, u32[]{:S(2)}) %copy-start) | copy-done | bytes 264
  15.5 0.7 %copy-done.1 = s32[60]{0:T(128)S(1)} copy-done((s32[60]{0:T(128)S(1)}, s32[60]{0:T(128)}, u32[]{:S(2)}) %copy-start.1) | copy-done | bytes 264
  16.2 3.1 %stage_arguments.1 = (bf16[60,128,128]{2,1,0:T(8,128)(2,1)S(1)}, bf16[128,256]{1,0:T(8,128)(2,1)S(1)}, bf16[128,256]{1,0:T(8,128)(2,1)S(1)}, f32[4,128,128]{2,1,...) custom-call(s32[1]{0:T(128)} %bitcast.me_ref, ...), custom_call_target="tpu_custom_call" | custom-call | flops 3300000000 | bytes 10800000 | tf_op jit(solution)/shard_map/stage_arguments/pallas_call | solution.py:362
  19.3 0.1 collective-permute-start.3
  19.4 1.0 %collective-permute-done.5.refs_1_ = bf16[512,128]{1,0:T(8,128)(2,1)S(1)} collective-permute-done((bf16[512,128]{1,0:T(8,128)(2,1)S(1)}, bf16[512,128]{1,0:T(8,128)(2,1)S(1)}, u32[]{:S(2)}, u32[]{:S(2)}) %collective-permute-start.5) | collective-permute-done | bytes 131104 | tf_op jit(solution)/shard_map/ppermute | solution.py:21
  20.4 0.6 %collective-permute-done.6.refs_2_ = bf16[512,128]{1,0:T(8,128)(2,1)S(1)} collective-permute-done((bf16[512,128]{1,0:T(8,128)(2,1)S(1)}, bf16[512,128]{1,0:T(8,128)(2,1)S(1)}, u32[]{:S(2)}, u32[]{:S(2)}) %collective-permute-start.6) | collective-permute-done | bytes 131104 | tf_op jit(solution)/shard_map/ppermute | solution.py:21
  21.0 0.1 collective-permute-done.7.refs_3_
  21.2 0.1 collective-permute-start.8
  21.3 0.8 %forward_near.1.near_ref = f32[5,128,128]{2,1,0:T(8,128)S(1)} custom-call(s32[363]{0:T(512)S(4)} %get-tuple-element.36.index_ref, bf16[60,128,128]{2,1,0:T(8,128)(2,1)S(1)} %get-tuple-element.37.tiles_ref, bf16[4,512,128]{2,1,0:T(8,128)(2,1)S(1)} %pack_square.2.same_ref, bf16[4,512,128]{2,1,0:T(8,128)(2,1)S(1)} %collective-permute-done.3.other_ref), custom_call_target="tpu_custom_call" | custom-call | flops 110000000 | bytes 360000 | tf_op jit(solution)/shard_map/forward_near/pallas_call | solution.py:339
  22.2 1.0 %collective-permute-done.8.refs_1_ = bf16[4,512,128]{2,1,0:T(8,128)(2,1)S(1)} collective-permute-done((bf16[4,512,128]{2,1,0:T(8,128)(2,1)S(1)}, bf16[4,512,128]{2,1,0:T(8,128)(2,1)S(1)}, u32[]{:S(2)}, u32[]{:S(2)}) %collective-permute-start.8) | collective-permute-done | bytes 524320 | tf_op jit(solution)/shard_map/ppermute | solution.py:21
  23.2 2.8 %forward_layer.1 = (bf16[512,256]{1,0:T(8,128)(2,1)}, bf16[512,256]{1,0:T(8,128)(2,1)S(1)}, bf16[512,256]{1,0:T(8,128)(2,1)S(1)}, bf16[512,256]{1,0:T(8,128)(2,1...) custom-call(s32[363]{0:T(512)S(4)} %get-tuple-element.36.index_ref, ...), custom_call_target="tpu_custom_call" | custom-call | flops 3300000000 | bytes 10800000 | tf_op jit(solution)/shard_map/forward_layer/pallas_call | solution.py:339
  26.0 0.5 weights.1
  26.5 0.1 collective-permute-start.9
  26.6 1.4 %backward_tiles.3.acc_ref = f32[33,128,128]{2,1,0:T(8,128)S(1)} custom-call(s32[363]{0:T(512)S(4)} %get-tuple-element.36.index_ref, bf16[60,128,128]{2,1,0:T(8,128)(2,1)S(1)} %get-tuple-element.37.tiles_ref, bf16[4,256,128]{2,1,0:T(8,128)(2,1)S(1)} %get-tuple-element.47.gt_ref, f32[128,256]{1,0:T(8,128)S(1)} %get-tuple-element.51.refs_0_.wkeep_ref), custom_call_target="tpu_custom_call" | custom-call | flops 1650000000 | bytes 5400000 | tf_op jit(solution)/shard_map/backward_tiles/pallas_call | solution.py:339
  28.1 0.1 collective-permute-start.13
  28.2 1.1 %backward_tiles.2.acc_ref = f32[33,128,128]{2,1,0:T(8,128)S(1)} custom-call(s32[363]{0:T(512)S(4)} %get-tuple-element.36.index_ref, bf16[60,128,128]{2,1,0:T(8,128)(2,1)S(1)} %get-tuple-element.37.tiles_ref, bf16[4,256,128]{2,1,0:T(8,128)(2,1)S(1)} %get-tuple-element.47.gt_ref, f32[128,256]{1,0:T(8,128)S(1)} %get-tuple-element.51.refs_0_.wkeep_ref), custom_call_target="tpu_custom_call" | custom-call | flops 330000000 | bytes 1080000 | tf_op jit(solution)/shard_map/backward_tiles/pallas_call | solution.py:339
  29.5 0.2 collective-permute-start.10
  29.7 1.2 %collective-permute-done.13.got_ref = f32[4,512,128]{2,1,0:T(8,128)S(1)} collective-permute-done((f32[4,512,128]{2,1,0:T(8,128)S(1)}, f32[4,512,128]{2,1,0:T(8,128)S(1)}, u32[]{:S(2)}, u32[]{:S(2)}) %collective-permute-start.13) | collective-permute-done | bytes 1048608 | tf_op jit(solution)/shard_map/ppermute | solution.py:21
  30.8 0.1 pair_sum_weights.1
  31.0 0.7 %collective-permute-start.14 = (bf16[576,128]{1,0:T(8,128)(2,1)S(1)}, bf16[576,128]{1,0:T(8,128)(2,1)S(1)}, u32[]{:S(2)}, u32[]{:S(2)}) collective-permute-start(bf16[576,128]{1,0:T(8,128)(2,1)S(1)} %get-tuple-element.61), channel_id=1, source_target_pairs={{0,6},{1,7},{2,4},{3,5},{4,2},{5,3},{6,0},{7,1},{8,14},{9,15},{10,... | collective-permute-start | bytes 442376 | tf_op jit(solution)/shard_map/ppermute | solution.py:21
  31.6 0.7 %collective-permute-start.15 = (bf16[576,128]{1,0:T(8,128)(2,1)S(1)}, bf16[576,128]{1,0:T(8,128)(2,1)S(1)}, u32[]{:S(2)}, u32[]{:S(2)}) collective-permute-start(bf16[576,128]{1,0:T(8,128)(2,1)S(1)} %get-tuple-element.62), channel_id=1, source_target_pairs={{0,2},{1,3},{2,0},{3,1},{4,6},{5,7},{6,4},{7,5},{8,10},{9,11},{10,... | collective-permute-start | bytes 442376 | tf_op jit(solution)/shard_map/ppermute | solution.py:21
  32.3 2.2 %collective-permute-start.16 = (bf16[576,128]{1,0:T(8,128)(2,1)S(1)}, bf16[576,128]{1,0:T(8,128)(2,1)S(1)}, u32[]{:S(2)}, u32[]{:S(2)}) collective-permute-start(bf16[576,128]{1,0:T(8,128)(2,1)S(1)} %get-tuple-element.63), channel_id=1, source_target_pairs={{0,4},{1,5},{2,6},{3,7},{4,0},{5,1},{6,2},{7,3},{8,12},{9,13},{10,... | collective-permute-start | bytes 442376 | tf_op jit(solution)/shard_map/ppermute | solution.py:21
  34.5 0.1 pair_sum.1
  34.6 0.7 %collective-permute-start.11 = (bf16[512,128]{1,0:T(8,128)(2,1)S(1)}, bf16[512,128]{1,0:T(8,128)(2,1)S(1)}, u32[]{:S(2)}, u32[]{:S(2)}) collective-permute-start(bf16[512,128]{1,0:T(8,128)(2,1)S(1)} %get-tuple-element.55), channel_id=1, source_target_pairs={{0,6},{1,7},{2,4},{3,5},{4,2},{5,3},{6,0},{7,1},{8,14},{9,15},{10,... | collective-permute-start | bytes 393224 | tf_op jit(solution)/shard_map/ppermute | solution.py:21
  35.3 0.9 %collective-permute-start.12 = (bf16[512,128]{1,0:T(8,128)(2,1)S(1)}, bf16[512,128]{1,0:T(8,128)(2,1)S(1)}, u32[]{:S(2)}, u32[]{:S(2)}) collective-permute-start(bf16[512,128]{1,0:T(8,128)(2,1)S(1)} %get-tuple-element.56), channel_id=1, source_target_pairs={{0,2},{1,3},{2,0},{3,1},{4,6},{5,7},{6,4},{7,5},{8,10},{9,11},{10,... | collective-permute-start | bytes 393224 | tf_op jit(solution)/shard_map/ppermute | solution.py:21
  36.1 2.5 %collective-permute-done.14.refs_0_ = bf16[576,128]{1,0:T(8,128)(2,1)S(1)} collective-permute-done((bf16[576,128]{1,0:T(8,128)(2,1)S(1)}, bf16[576,128]{1,0:T(8,128)(2,1)S(1)}, u32[]{:S(2)}, u32[]{:S(2)}) %collective-permute-start.14) | collective-permute-done | bytes 147488 | tf_op jit(solution)/shard_map/ppermute | solution.py:21
  38.7 3.2 %collective-permute-done.15.refs_1_ = bf16[576,128]{1,0:T(8,128)(2,1)S(1)} collective-permute-done((bf16[576,128]{1,0:T(8,128)(2,1)S(1)}, bf16[576,128]{1,0:T(8,128)(2,1)S(1)}, u32[]{:S(2)}, u32[]{:S(2)}) %collective-permute-start.15) | collective-permute-done | bytes 147488 | tf_op jit(solution)/shard_map/ppermute | solution.py:21
  41.9 1.3 %collective-permute-start.19 = (f32[32,256]{1,0:T(8,128)S(1)}, f32[32,256]{1,0:T(8,128)S(1)}, u32[]{:S(2)}, u32[]{:S(2)}) collective-permute-start(f32[32,256]{1,0:T(8,128)S(1)} %get-tuple-element.65.own_ref), channel_id=1, source_target_pairs={{0,8},{1,9},{2,10},{3,11},{4,12},{5,13},{6,14},{7,15},{8,0},{9,1},... | collective-permute-start | bytes 98312 | tf_op jit(solution)/shard_map/ppermute | solution.py:21
  43.2 1.2 %collective-permute-start.17 = (bf16[512,128]{1,0:T(8,128)(2,1)S(1)}, bf16[512,128]{1,0:T(8,128)(2,1)S(1)}, u32[]{:S(2)}, u32[]{:S(2)}) collective-permute-start(bf16[512,128]{1,0:T(8,128)(2,1)S(1)} %pair_sum_later.1), channel_id=1, source_target_pairs={{0,4},{1,5},{2,6},{3,7},{4,0},{5,1},{6,2},{7,3},{8,12},{9,13},{10,... | collective-permute-start | bytes 393224 | tf_op jit(solution)/shard_map/ppermute | solution.py:21
  44.5 2.5 %collective-permute-done.19.got_ref = f32[32,256]{1,0:T(8,128)S(1)} collective-permute-done((f32[32,256]{1,0:T(8,128)S(1)}, f32[32,256]{1,0:T(8,128)S(1)}, u32[]{:S(2)}, u32[]{:S(2)}) %collective-permute-start.19) | collective-permute-done | bytes 32800 | tf_op jit(solution)/shard_map/ppermute | solution.py:21
  47.0 0.2 collective-permute-start.20
  47.2 2.1 %collective-permute-start.18 = (bf16[512,128]{1,0:T(8,128)(2,1)S(1)}, bf16[512,128]{1,0:T(8,128)(2,1)S(1)}, u32[]{:S(2)}, u32[]{:S(2)}) collective-permute-start(bf16[512,128]{1,0:T(8,128)(2,1)S(1)} %get-tuple-element.64.refs_0_), channel_id=1, source_target_pairs={{0,8},{1,9},{2,10},{3,11},{4,12},{5,13},{6,14},{7,15},{8,0},{9,1},... | collective-permute-start | bytes 393224 | tf_op jit(solution)/shard_map/ppermute | solution.py:21
  49.3 1.6 %collective-permute-done.20.refs_1_ = f32[32,256]{1,0:T(8,128)S(1)} collective-permute-done((f32[32,256]{1,0:T(8,128)S(1)}, f32[32,256]{1,0:T(8,128)S(1)}, u32[]{:S(2)}, u32[]{:S(2)}) %collective-permute-start.20) | collective-permute-done | bytes 32800 | tf_op jit(solution)/shard_map/ppermute | solution.py:21
  50.9 0.8 %collective-permute-start.21 = (f32[2,32,256]{2,1,0:T(8,128)S(1)}, f32[2,32,256]{2,1,0:T(8,128)S(1)}, u32[]{:S(2)}, u32[]{:S(2)}) collective-permute-start(f32[2,32,256]{2,1,0:T(8,128)S(1)} %pack_weights.2.refs_0_), channel_id=1, source_target_pairs={{0,2},{1,3},{2,0},{3,1},{4,6},{5,7},{6,4},{7,5},{8,10},{9,11},{10,... | collective-permute-start | bytes 196616 | tf_op jit(solution)/shard_map/ppermute | solution.py:21
  51.7 0.3 near_sum.1.near_ref.refs_2_
  52.0 3.2 %collective-permute-done.21.refs_1_ = f32[2,32,256]{2,1,0:T(8,128)S(1)} collective-permute-done((f32[2,32,256]{2,1,0:T(8,128)S(1)}, f32[2,32,256]{2,1,0:T(8,128)S(1)}, u32[]{:S(2)}, u32[]{:S(2)}) %collective-permute-start.21) | collective-permute-done | bytes 65568 | tf_op jit(solution)/shard_map/ppermute | solution.py:21
  55.2 0.1 collective-permute-start.22
  55.3 0.8 %grad_input_sum.1 = bf16[512,128]{1,0:T(8,128)(2,1)} custom-call(f32[512,128]{1,0:T(8,128)S(1)} %near_sum.1.near_ref.refs_2_, bf16[512,128]{1,0:T(8,128)(2,1)S(1)} %collective-permute-done.18.refs_0_), custom_call_target="tpu_custom_call" | custom-call | flops 11000000512 | bytes 36000000 | tf_op jit(solution)/shard_map/grad_input_sum/pallas_call | solution.py:339
  56.1 0.6 collective-permute-done.22.other_ref
  56.6 0.7 %write_weights.1 = (f32[128,256]{1,0:T(8,128)}, f32[128,256]{1,0:T(8,128)}) custom-call(s32[363]{0:T(512)S(4)} %get-tuple-element.36.index_ref, f32[2,2,32,256]{3,2,1,0:T(8,128)S(1)} %pack_weights.3.weight_ref, f32[2,2,32,256]{3,2,1,0:T(8,128)S(1)} %collective-permute-done.22.other_ref), custom_call_target="tpu_custom_call" | custom-call | flops 220000000 | bytes 720000 | tf_op jit(solution)/shard_map/write_weights/pallas_call | solution.py:339
  (23 shorter events, 0.4 us)
Async XLA Ops:
  0.6 10.7 %collective-permute-start.4 = (bf16[512,128]{1,0:T(8,128)(2,1)}, bf16[512,128]{1,0:T(8,128)(2,1)S(1)}, u32[]{:S(2)}, u32[]{:S(2)}) collective-permute-start(bf16[512,128]{1,0:T(8,128)(2,1)} %feat_ref.1), channel_id=1, source_target_pairs={{0,8},{1,9},{2,10},{3,11},{4,12},{5,13},{6,14},{7,15},{8,0},{9,1},... | collective-permute-start | bytes 393224 | tf_op jit(solution)/shard_map/ppermute | solution.py:21
  4.7 8.9 %collective-permute-start = (bf16[512,128]{1,0:T(8,128)(2,1)}, bf16[512,128]{1,0:T(8,128)(2,1)S(1)}, u32[]{:S(2)}, u32[]{:S(2)}) collective-permute-start(bf16[512,128]{1,0:T(8,128)(2,1)} %feat_ref.1), channel_id=1, source_target_pairs={{0,2},{1,3},{2,0},{3,1},{4,6},{5,7},{6,4},{7,5},{8,10},{9,11},{10,... | collective-permute-start | bytes 393224 | tf_op jit(solution)/shard_map/ppermute | solution.py:21
  6.3 13.0 %collective-permute-start.1 = (bf16[512,128]{1,0:T(8,128)(2,1)}, bf16[512,128]{1,0:T(8,128)(2,1)S(1)}, u32[]{:S(2)}, u32[]{:S(2)}) collective-permute-start(bf16[512,128]{1,0:T(8,128)(2,1)} %feat_ref.1), channel_id=1, source_target_pairs={{0,6},{1,7},{2,4},{3,5},{4,2},{5,3},{6,0},{7,1},{8,14},{9,15},{10,... | collective-permute-start | bytes 393224 | tf_op jit(solution)/shard_map/ppermute | solution.py:21
  7.8 11.5 %collective-permute-start.2 = (bf16[512,128]{1,0:T(8,128)(2,1)}, bf16[512,128]{1,0:T(8,128)(2,1)S(1)}, u32[]{:S(2)}, u32[]{:S(2)}) collective-permute-start(bf16[512,128]{1,0:T(8,128)(2,1)} %feat_ref.1), channel_id=1, source_target_pairs={{0,4},{1,5},{2,6},{3,7},{4,0},{5,1},{6,2},{7,3},{8,12},{9,13},{10,... | collective-permute-start | bytes 393224 | tf_op jit(solution)/shard_map/ppermute | solution.py:21
  11.4 9.1 %collective-permute-start.5 = (bf16[512,128]{1,0:T(8,128)(2,1)S(1)}, bf16[512,128]{1,0:T(8,128)(2,1)S(1)}, u32[]{:S(2)}, u32[]{:S(2)}) collective-permute-start(bf16[512,128]{1,0:T(8,128)(2,1)S(1)} %collective-permute-done.4.refs_0_), channel_id=1, source_target_pairs={{0,6},{1,7},{2,4},{3,5},{4,2},{5,3},{6,0},{7,1},{8,14},{9,15},{10,... | collective-permute-start | bytes 393224 | tf_op jit(solution)/shard_map/ppermute | solution.py:21
  13.1 7.9 %collective-permute-start.6 = (bf16[512,128]{1,0:T(8,128)(2,1)S(1)}, bf16[512,128]{1,0:T(8,128)(2,1)S(1)}, u32[]{:S(2)}, u32[]{:S(2)}) collective-permute-start(bf16[512,128]{1,0:T(8,128)(2,1)S(1)} %collective-permute-done.4.refs_0_), channel_id=1, source_target_pairs={{0,2},{1,3},{2,0},{3,1},{4,6},{5,7},{6,4},{7,5},{8,10},{9,11},{10,... | collective-permute-start | bytes 393224 | tf_op jit(solution)/shard_map/ppermute | solution.py:21
  13.6 7.6 %collective-permute-start.7 = (bf16[512,128]{1,0:T(8,128)(2,1)S(1)}, bf16[512,128]{1,0:T(8,128)(2,1)S(1)}, u32[]{:S(2)}, u32[]{:S(2)}) collective-permute-start(bf16[512,128]{1,0:T(8,128)(2,1)S(1)} %collective-permute-done.4.refs_0_), channel_id=1, source_target_pairs={{0,4},{1,5},{2,6},{3,7},{4,0},{5,1},{6,2},{7,3},{8,12},{9,13},{10,... | collective-permute-start | bytes 393224 | tf_op jit(solution)/shard_map/ppermute | solution.py:21
  14.8 0.7 %copy-start = (s32[60]{0:T(128)S(1)}, s32[60]{0:T(128)}, u32[]{:S(2)}) copy-start(s32[60]{0:T(128)} %trow_ref.1) | copy-start | bytes 724
  15.5 0.7 %copy-start.1 = (s32[60]{0:T(128)S(1)}, s32[60]{0:T(128)}, u32[]{:S(2)}) copy-start(s32[60]{0:T(128)} %tcol_ref.1) | copy-start | bytes 724
  19.3 2.0 %collective-permute-start.3 = (bf16[4,512,128]{2,1,0:T(8,128)(2,1)S(1)}, bf16[4,512,128]{2,1,0:T(8,128)(2,1)S(1)}, u32[]{:S(2)}, u32[]{:S(2)}) collective-permute-start(bf16[4,512,128]{2,1,0:T(8,128)(2,1)S(1)} %pack_square.2.same_ref), channel_id=1, source_target_pairs={{0,1},{1,0},{2,3},{3,2},{4,5},{5,4},{6,7},{7,6},{8,9},{9,8},{10,11... | collective-permute-start | bytes 1572872 | tf_op jit(solution)/shard_map/ppermute | solution.py:21
  21.2 2.0 %collective-permute-start.8 = (bf16[4,512,128]{2,1,0:T(8,128)(2,1)S(1)}, bf16[4,512,128]{2,1,0:T(8,128)(2,1)S(1)}, u32[]{:S(2)}, u32[]{:S(2)}) collective-permute-start(bf16[4,512,128]{2,1,0:T(8,128)(2,1)S(1)} %pack_square.3.refs_0_), channel_id=1, source_target_pairs={{0,1},{1,0},{2,3},{3,2},{4,5},{5,4},{6,7},{7,6},{8,9},{9,8},{10,11... | collective-permute-start | bytes 1572872 | tf_op jit(solution)/shard_map/ppermute | solution.py:21
  26.5 2.8 %collective-permute-start.9 = (f32[128,256]{1,0:T(8,128)S(1)}, f32[128,256]{1,0:T(8,128)S(1)}, u32[]{:S(2)}, u32[]{:S(2)}) collective-permute-start(f32[128,256]{1,0:T(8,128)S(1)} %get-tuple-element.52), channel_id=1, source_target_pairs={{0,1},{1,0},{2,3},{3,2},{4,5},{5,4},{6,7},{7,6},{8,9},{9,8},{10,11... | collective-permute-start | bytes 393224 | tf_op jit(solution)/shard_map/ppermute | solution.py:21
  28.1 2.7 %collective-permute-start.13 = (f32[4,512,128]{2,1,0:T(8,128)S(1)}, f32[4,512,128]{2,1,0:T(8,128)S(1)}, u32[]{:S(2)}, u32[]{:S(2)}) collective-permute-start(f32[4,512,128]{2,1,0:T(8,128)S(1)} %send.3), channel_id=1, source_target_pairs={{0,1},{1,0},{2,3},{3,2},{4,5},{5,4},{6,7},{7,6},{8,9},{9,8},{10,11... | collective-permute-start | bytes 3145736 | tf_op jit(solution)/shard_map/ppermute | solution.py:21
  29.5 5.1 %collective-permute-start.10 = (f32[4,512,128]{2,1,0:T(8,128)S(1)}, f32[4,512,128]{2,1,0:T(8,128)S(1)}, u32[]{:S(2)}, u32[]{:S(2)}) collective-permute-start(f32[4,512,128]{2,1,0:T(8,128)S(1)} %send.2), channel_id=1, source_target_pairs={{0,1},{1,0},{2,3},{3,2},{4,5},{5,4},{6,7},{7,6},{8,9},{9,8},{10,11... | collective-permute-start | bytes 3145736 | tf_op jit(solution)/shard_map/ppermute | solution.py:21
  31.0 7.7 %collective-permute-start.14 = (bf16[576,128]{1,0:T(8,128)(2,1)S(1)}, bf16[576,128]{1,0:T(8,128)(2,1)S(1)}, u32[]{:S(2)}, u32[]{:S(2)}) collective-permute-start(bf16[576,128]{1,0:T(8,128)(2,1)S(1)} %get-tuple-element.61), channel_id=1, source_target_pairs={{0,6},{1,7},{2,4},{3,5},{4,2},{5,3},{6,0},{7,1},{8,14},{9,15},{10,... | collective-permute-start | bytes 442376 | tf_op jit(solution)/shard_map/ppermute | solution.py:21
  31.6 10.2 %collective-permute-start.15 = (bf16[576,128]{1,0:T(8,128)(2,1)S(1)}, bf16[576,128]{1,0:T(8,128)(2,1)S(1)}, u32[]{:S(2)}, u32[]{:S(2)}) collective-permute-start(bf16[576,128]{1,0:T(8,128)(2,1)S(1)} %get-tuple-element.62), channel_id=1, source_target_pairs={{0,2},{1,3},{2,0},{3,1},{4,6},{5,7},{6,4},{7,5},{8,10},{9,11},{10,... | collective-permute-start | bytes 442376 | tf_op jit(solution)/shard_map/ppermute | solution.py:21
  32.3 9.6 %collective-permute-start.16 = (bf16[576,128]{1,0:T(8,128)(2,1)S(1)}, bf16[576,128]{1,0:T(8,128)(2,1)S(1)}, u32[]{:S(2)}, u32[]{:S(2)}) collective-permute-start(bf16[576,128]{1,0:T(8,128)(2,1)S(1)} %get-tuple-element.63), channel_id=1, source_target_pairs={{0,4},{1,5},{2,6},{3,7},{4,0},{5,1},{6,2},{7,3},{8,12},{9,13},{10,... | collective-permute-start | bytes 442376 | tf_op jit(solution)/shard_map/ppermute | solution.py:21
  34.6 17.1 %collective-permute-start.11 = (bf16[512,128]{1,0:T(8,128)(2,1)S(1)}, bf16[512,128]{1,0:T(8,128)(2,1)S(1)}, u32[]{:S(2)}, u32[]{:S(2)}) collective-permute-start(bf16[512,128]{1,0:T(8,128)(2,1)S(1)} %get-tuple-element.55), channel_id=1, source_target_pairs={{0,6},{1,7},{2,4},{3,5},{4,2},{5,3},{6,0},{7,1},{8,14},{9,15},{10,... | collective-permute-start | bytes 393224 | tf_op jit(solution)/shard_map/ppermute | solution.py:21
  35.3 16.5 %collective-permute-start.12 = (bf16[512,128]{1,0:T(8,128)(2,1)S(1)}, bf16[512,128]{1,0:T(8,128)(2,1)S(1)}, u32[]{:S(2)}, u32[]{:S(2)}) collective-permute-start(bf16[512,128]{1,0:T(8,128)(2,1)S(1)} %get-tuple-element.56), channel_id=1, source_target_pairs={{0,2},{1,3},{2,0},{3,1},{4,6},{5,7},{6,4},{7,5},{8,10},{9,11},{10,... | collective-permute-start | bytes 393224 | tf_op jit(solution)/shard_map/ppermute | solution.py:21
  41.9 5.1 %collective-permute-start.19 = (f32[32,256]{1,0:T(8,128)S(1)}, f32[32,256]{1,0:T(8,128)S(1)}, u32[]{:S(2)}, u32[]{:S(2)}) collective-permute-start(f32[32,256]{1,0:T(8,128)S(1)} %get-tuple-element.65.own_ref), channel_id=1, source_target_pairs={{0,8},{1,9},{2,10},{3,11},{4,12},{5,13},{6,14},{7,15},{8,0},{9,1},... | collective-permute-start | bytes 98312 | tf_op jit(solution)/shard_map/ppermute | solution.py:21
  43.2 8.5 %collective-permute-start.17 = (bf16[512,128]{1,0:T(8,128)(2,1)S(1)}, bf16[512,128]{1,0:T(8,128)(2,1)S(1)}, u32[]{:S(2)}, u32[]{:S(2)}) collective-permute-start(bf16[512,128]{1,0:T(8,128)(2,1)S(1)} %pair_sum_later.1), channel_id=1, source_target_pairs={{0,4},{1,5},{2,6},{3,7},{4,0},{5,1},{6,2},{7,3},{8,12},{9,13},{10,... | collective-permute-start | bytes 393224 | tf_op jit(solution)/shard_map/ppermute | solution.py:21
  47.0 3.9 %collective-permute-start.20 = (f32[32,256]{1,0:T(8,128)S(1)}, f32[32,256]{1,0:T(8,128)S(1)}, u32[]{:S(2)}, u32[]{:S(2)}) collective-permute-start(f32[32,256]{1,0:T(8,128)S(1)} %weight_sum.1.refs_0_), channel_id=1, source_target_pairs={{0,4},{1,5},{2,6},{3,7},{4,0},{5,1},{6,2},{7,3},{8,12},{9,13},{10,... | collective-permute-start | bytes 98312 | tf_op jit(solution)/shard_map/ppermute | solution.py:21
  47.2 8.1 %collective-permute-start.18 = (bf16[512,128]{1,0:T(8,128)(2,1)S(1)}, bf16[512,128]{1,0:T(8,128)(2,1)S(1)}, u32[]{:S(2)}, u32[]{:S(2)}) collective-permute-start(bf16[512,128]{1,0:T(8,128)(2,1)S(1)} %get-tuple-element.64.refs_0_), channel_id=1, source_target_pairs={{0,8},{1,9},{2,10},{3,11},{4,12},{5,13},{6,14},{7,15},{8,0},{9,1},... | collective-permute-start | bytes 393224 | tf_op jit(solution)/shard_map/ppermute | solution.py:21
  50.9 4.3 %collective-permute-start.21 = (f32[2,32,256]{2,1,0:T(8,128)S(1)}, f32[2,32,256]{2,1,0:T(8,128)S(1)}, u32[]{:S(2)}, u32[]{:S(2)}) collective-permute-start(f32[2,32,256]{2,1,0:T(8,128)S(1)} %pack_weights.2.refs_0_), channel_id=1, source_target_pairs={{0,2},{1,3},{2,0},{3,1},{4,6},{5,7},{6,4},{7,5},{8,10},{9,11},{10,... | collective-permute-start | bytes 196616 | tf_op jit(solution)/shard_map/ppermute | solution.py:21
  55.2 1.4 %collective-permute-start.22 = (f32[2,2,32,256]{3,2,1,0:T(8,128)S(1)}, f32[2,2,32,256]{3,2,1,0:T(8,128)S(1)}, u32[]{:S(2)}, u32[]{:S(2)}) collective-permute-start(f32[2,2,32,256]{3,2,1,0:T(8,128)S(1)} %pack_weights.3.weight_ref), channel_id=1, source_target_pairs={{0,1},{1,0},{2,3},{3,2},{4,5},{5,4},{6,7},{7,6},{8,9},{9,8},{10,11... | collective-permute-start | bytes 393224 | tf_op jit(solution)/shard_map/ppermute | solution.py:21

commit v17 on v13

--- a/solution.py
+++ b/solution.py
@@ -441,7 +441,7 @@
             own, *pieces = call(
                 functools.partial(pair_kernel, s - 1, range(4)), "pair_sum",
                 (wide, piece, piece, piece), operands)
-        terms.append([own, *[swap(pieces[q - 1], n, 2 * q) for q in (3, 1, 2)]])
+        terms.append([own, *[swap(pieces[q - 1], n, 2 * q) for q in (1, 3, 2)]])
     near_operands = (sums[0], got[0])
     own, *pieces = call(
         functools.partial(pair_kernel, 0, (0, 3, 1)), "pair_sum", (wide, piece, piece),

time: 58 us -> 58.2 us (level)
  starting transfers between devices: 25.7 us -> 26.6 us
  Pallas kernels: 11.6 us -> 11 us
    ppermute x23, starting transfers between devices: 25.7 us -> 26.6 us  [swap(): return lax.ppermute(x, 'row', [(i, i ^ offset) for i in range(n)])]
where the time goes in v17:
time: 58.2 us; the launch traced here: 57.9 us
  starting transfers between devices  26.6 us (46%)
  waiting for transfers between devices  18.2 us (31%)
  Pallas kernels  11 us (19%)
  local copies, waits for them, and re-layouts  1.31 us (2%)
  between operations  0.8 us (1%)
    ppermute x23, starting transfers between devices, swap(): return lax.ppermute(x, 'row', [(i, i ^ offset) for i in range(n)])  26.6 us
    ppermute x23, waiting for transfers between devices, swap(): return lax.ppermute(x, 'row', [(i, i ^ offset) for i in range(n)])  18.2 us
    pallas_call x20, Pallas kernels, call(): pl.pallas_call(kernel, out_shape=out_shape, in_specs=specs, out_specs=out...  7.92 us
    pallas_call x1, Pallas kernels, body(): pl.pallas_call(functools.partial(stage_kernel, (8 * block_local, (n - 8)...  3.09 us
    unnamed x4, local copies, waits for them, and re-layouts  1.31 us
  transfers between devices with their start and end apart: 23, of which 12 were waited for; matrix products, arithmetic and copies ran while one was open for 0% of the time, Pallas kernels for 13%

profile of v17, /device:TPU:0, one launch (start us, length us, event | category | flops | bytes accessed | tf_op | source)
XLA Modules:
  0.0 57.9 jit_solution(7327668751311698499)
XLA Ops:
  0.6 4.1 %collective-permute-start.4 = (bf16[512,128]{1,0:T(8,128)(2,1)}, bf16[512,128]{1,0:T(8,128)(2,1)S(1)}, u32[]{:S(2)}, u32[]{:S(2)}) collective-permute-start(bf16[512,128]{1,0:T(8,128)(2,1)} %feat_ref.1), channel_id=1, source_target_pairs={{0,8},{1,9},{2,10},{3,11},{4,12},{5,13},{6,14},{7,15},{8,0},{9,1},... | collective-permute-start | bytes 393224 | tf_op jit(solution)/shard_map/ppermute | solution.py:21
  4.7 1.5 %collective-permute-start = (bf16[512,128]{1,0:T(8,128)(2,1)}, bf16[512,128]{1,0:T(8,128)(2,1)S(1)}, u32[]{:S(2)}, u32[]{:S(2)}) collective-permute-start(bf16[512,128]{1,0:T(8,128)(2,1)} %feat_ref.1), channel_id=1, source_target_pairs={{0,2},{1,3},{2,0},{3,1},{4,6},{5,7},{6,4},{7,5},{8,10},{9,11},{10,... | collective-permute-start | bytes 393224 | tf_op jit(solution)/shard_map/ppermute | solution.py:21
  6.3 1.5 %collective-permute-start.1 = (bf16[512,128]{1,0:T(8,128)(2,1)}, bf16[512,128]{1,0:T(8,128)(2,1)S(1)}, u32[]{:S(2)}, u32[]{:S(2)}) collective-permute-start(bf16[512,128]{1,0:T(8,128)(2,1)} %feat_ref.1), channel_id=1, source_target_pairs={{0,6},{1,7},{2,4},{3,5},{4,2},{5,3},{6,0},{7,1},{8,14},{9,15},{10,... | collective-permute-start | bytes 393224 | tf_op jit(solution)/shard_map/ppermute | solution.py:21
  7.8 0.4 collective-permute-start.2
  8.2 3.1 %collective-permute-done.4.refs_0_ = bf16[512,128]{1,0:T(8,128)(2,1)S(1)} collective-permute-done((bf16[512,128]{1,0:T(8,128)(2,1)}, bf16[512,128]{1,0:T(8,128)(2,1)S(1)}, u32[]{:S(2)}, u32[]{:S(2)}) %collective-permute-start.4) | collective-permute-done | bytes 131104 | tf_op jit(solution)/shard_map/ppermute | solution.py:21
  11.4 1.7 %collective-permute-start.5 = (bf16[512,128]{1,0:T(8,128)(2,1)S(1)}, bf16[512,128]{1,0:T(8,128)(2,1)S(1)}, u32[]{:S(2)}, u32[]{:S(2)}) collective-permute-start(bf16[512,128]{1,0:T(8,128)(2,1)S(1)} %collective-permute-done.4.refs_0_), channel_id=1, source_target_pairs={{0,6},{1,7},{2,4},{3,5},{4,2},{5,3},{6,0},{7,1},{8,14},{9,15},{10,... | collective-permute-start | bytes 393224 | tf_op jit(solution)/shard_map/ppermute | solution.py:21
  13.1 0.5 collective-permute-start.6
  13.6 1.3 %collective-permute-start.7 = (bf16[512,128]{1,0:T(8,128)(2,1)S(1)}, bf16[512,128]{1,0:T(8,128)(2,1)S(1)}, u32[]{:S(2)}, u32[]{:S(2)}) collective-permute-start(bf16[512,128]{1,0:T(8,128)(2,1)S(1)} %collective-permute-done.4.refs_0_), channel_id=1, source_target_pairs={{0,4},{1,5},{2,6},{3,7},{4,0},{5,1},{6,2},{7,3},{8,12},{9,13},{10,... | collective-permute-start | bytes 393224 | tf_op jit(solution)/shard_map/ppermute | solution.py:21
  14.9 0.7 %copy-done = s32[60]{0:T(128)S(1)} copy-done((s32[60]{0:T(128)S(1)}, s32[60]{0:T(128)}, u32[]{:S(2)}) %copy-start) | copy-done | bytes 264
  15.5 0.7 %copy-done.1 = s32[60]{0:T(128)S(1)} copy-done((s32[60]{0:T(128)S(1)}, s32[60]{0:T(128)}, u32[]{:S(2)}) %copy-start.1) | copy-done | bytes 264
  16.2 3.1 %stage_arguments.1 = (bf16[60,128,128]{2,1,0:T(8,128)(2,1)S(1)}, bf16[128,256]{1,0:T(8,128)(2,1)S(1)}, bf16[128,256]{1,0:T(8,128)(2,1)S(1)}, f32[4,128,128]{2,1,...) custom-call(s32[1]{0:T(128)} %bitcast.me_ref, ...), custom_call_target="tpu_custom_call" | custom-call | flops 3300000000 | bytes 10800000 | tf_op jit(solution)/shard_map/stage_arguments/pallas_call | solution.py:366
  19.3 0.1 collective-permute-start.3
  19.4 1.0 %collective-permute-done.5.refs_1_ = bf16[512,128]{1,0:T(8,128)(2,1)S(1)} collective-permute-done((bf16[512,128]{1,0:T(8,128)(2,1)S(1)}, bf16[512,128]{1,0:T(8,128)(2,1)S(1)}, u32[]{:S(2)}, u32[]{:S(2)}) %collective-permute-start.5) | collective-permute-done | bytes 131104 | tf_op jit(solution)/shard_map/ppermute | solution.py:21
  20.4 0.6 %collective-permute-done.6.refs_2_ = bf16[512,128]{1,0:T(8,128)(2,1)S(1)} collective-permute-done((bf16[512,128]{1,0:T(8,128)(2,1)S(1)}, bf16[512,128]{1,0:T(8,128)(2,1)S(1)}, u32[]{:S(2)}, u32[]{:S(2)}) %collective-permute-start.6) | collective-permute-done | bytes 131104 | tf_op jit(solution)/shard_map/ppermute | solution.py:21
  21.0 0.1 collective-permute-done.7.refs_3_
  21.2 0.1 collective-permute-start.8
  21.3 0.8 %forward_near.1.near_ref = f32[5,128,128]{2,1,0:T(8,128)S(1)} custom-call(s32[363]{0:T(512)S(4)} %get-tuple-element.36.index_ref, bf16[60,128,128]{2,1,0:T(8,128)(2,1)S(1)} %get-tuple-element.37.tiles_ref, bf16[4,512,128]{2,1,0:T(8,128)(2,1)S(1)} %pack_square.2.same_ref, bf16[4,512,128]{2,1,0:T(8,128)(2,1)S(1)} %collective-permute-done.3.other_ref), custom_call_target="tpu_custom_call" | custom-call | flops 110000000 | bytes 360000 | tf_op jit(solution)/shard_map/forward_near/pallas_call | solution.py:343
  22.2 1.0 %collective-permute-done.8.refs_1_ = bf16[4,512,128]{2,1,0:T(8,128)(2,1)S(1)} collective-permute-done((bf16[4,512,128]{2,1,0:T(8,128)(2,1)S(1)}, bf16[4,512,128]{2,1,0:T(8,128)(2,1)S(1)}, u32[]{:S(2)}, u32[]{:S(2)}) %collective-permute-start.8) | collective-permute-done | bytes 524320 | tf_op jit(solution)/shard_map/ppermute | solution.py:21
  23.2 2.3 %forward_layer.1 = (bf16[512,256]{1,0:T(8,128)(2,1)}, bf16[512,256]{1,0:T(8,128)(2,1)S(1)}, bf16[512,256]{1,0:T(8,128)(2,1)S(1)}, bf16[512,256]{1,0:T(8,128)(2,1...) custom-call(s32[363]{0:T(512)S(4)} %get-tuple-element.36.index_ref, ...), custom_call_target="tpu_custom_call" | custom-call | flops 3300000000 | bytes 10800000 | tf_op jit(solution)/shard_map/forward_layer/pallas_call | solution.py:343
  25.5 0.5 weights.1
  26.0 0.5 collective-permute-start.9
  26.5 0.8 %backward_tiles.3.acc_ref = f32[33,128,128]{2,1,0:T(8,128)S(1)} custom-call(s32[363]{0:T(512)S(4)} %get-tuple-element.36.index_ref, bf16[60,128,128]{2,1,0:T(8,128)(2,1)S(1)} %get-tuple-element.37.tiles_ref, bf16[4,256,128]{2,1,0:T(8,128)(2,1)S(1)} %get-tuple-element.47.gt_ref, f32[128,256]{1,0:T(8,128)S(1)} %get-tuple-element.51.refs_0_.wkeep_ref), custom_call_target="tpu_custom_call" | custom-call | flops 1650000000 | bytes 5400000 | tf_op jit(solution)/shard_map/backward_tiles/pallas_call | solution.py:343
  27.3 0.5 collective-permute-start.13
  27.8 1.1 %backward_tiles.2.acc_ref = f32[33,128,128]{2,1,0:T(8,128)S(1)} custom-call(s32[363]{0:T(512)S(4)} %get-tuple-element.36.index_ref, bf16[60,128,128]{2,1,0:T(8,128)(2,1)S(1)} %get-tuple-element.37.tiles_ref, bf16[4,256,128]{2,1,0:T(8,128)(2,1)S(1)} %get-tuple-element.47.gt_ref, f32[128,256]{1,0:T(8,128)S(1)} %get-tuple-element.51.refs_0_.wkeep_ref), custom_call_target="tpu_custom_call" | custom-call | flops 330000000 | bytes 1080000 | tf_op jit(solution)/shard_map/backward_tiles/pallas_call | solution.py:343
  29.1 0.1 collective-permute-start.10
  29.2 0.9 %collective-permute-done.13.got_ref = f32[4,512,128]{2,1,0:T(8,128)S(1)} collective-permute-done((f32[4,512,128]{2,1,0:T(8,128)S(1)}, f32[4,512,128]{2,1,0:T(8,128)S(1)}, u32[]{:S(2)}, u32[]{:S(2)}) %collective-permute-start.13) | collective-permute-done | bytes 1048608 | tf_op jit(solution)/shard_map/ppermute | solution.py:21
  30.1 0.1 pair_sum_weights.1
  30.2 1.3 %collective-permute-start.14 = (bf16[640,128]{1,0:T(8,128)(2,1)S(1)}, bf16[640,128]{1,0:T(8,128)(2,1)S(1)}, u32[]{:S(2)}, u32[]{:S(2)}) collective-permute-start(bf16[640,128]{1,0:T(8,128)(2,1)S(1)} %get-tuple-element.61), channel_id=1, source_target_pairs={{0,2},{1,3},{2,0},{3,1},{4,6},{5,7},{6,4},{7,5},{8,10},{9,11},{10,... | collective-permute-start | bytes 491528 | tf_op jit(solution)/shard_map/ppermute | solution.py:21
  31.6 0.3 collective-permute-start.15
  31.9 2.0 %collective-permute-start.16 = (bf16[640,128]{1,0:T(8,128)(2,1)S(1)}, bf16[640,128]{1,0:T(8,128)(2,1)S(1)}, u32[]{:S(2)}, u32[]{:S(2)}) collective-permute-start(bf16[640,128]{1,0:T(8,128)(2,1)S(1)} %get-tuple-element.63), channel_id=1, source_target_pairs={{0,4},{1,5},{2,6},{3,7},{4,0},{5,1},{6,2},{7,3},{8,12},{9,13},{10,... | collective-permute-start | bytes 491528 | tf_op jit(solution)/shard_map/ppermute | solution.py:21
  33.8 0.1 pair_sum.1
  33.9 1.4 %collective-permute-start.11 = (bf16[512,128]{1,0:T(8,128)(2,1)S(1)}, bf16[512,128]{1,0:T(8,128)(2,1)S(1)}, u32[]{:S(2)}, u32[]{:S(2)}) collective-permute-start(bf16[512,128]{1,0:T(8,128)(2,1)S(1)} %get-tuple-element.55), channel_id=1, source_target_pairs={{0,6},{1,7},{2,4},{3,5},{4,2},{5,3},{6,0},{7,1},{8,14},{9,15},{10,... | collective-permute-start | bytes 393224 | tf_op jit(solution)/shard_map/ppermute | solution.py:21
  35.3 0.2 collective-permute-start.12
  35.5 5.4 %collective-permute-done.14.refs_0_ = bf16[640,128]{1,0:T(8,128)(2,1)S(1)} collective-permute-done((bf16[640,128]{1,0:T(8,128)(2,1)S(1)}, bf16[640,128]{1,0:T(8,128)(2,1)S(1)}, u32[]{:S(2)}, u32[]{:S(2)}) %collective-permute-start.14) | collective-permute-done | bytes 163872 | tf_op jit(solution)/shard_map/ppermute | solution.py:21
  40.9 1.5 %collective-permute-done.16.refs_2_ = bf16[640,128]{1,0:T(8,128)(2,1)S(1)} collective-permute-done((bf16[640,128]{1,0:T(8,128)(2,1)S(1)}, bf16[640,128]{1,0:T(8,128)(2,1)S(1)}, u32[]{:S(2)}, u32[]{:S(2)}) %collective-permute-start.16) | collective-permute-done | bytes 163872 | tf_op jit(solution)/shard_map/ppermute | solution.py:21
  42.4 0.1 square_sum_weights.1
  42.5 2.0 %collective-permute-start.19 = (f32[32,256]{1,0:T(8,128)S(1)}, f32[32,256]{1,0:T(8,128)S(1)}, u32[]{:S(2)}, u32[]{:S(2)}) collective-permute-start(f32[32,256]{1,0:T(8,128)S(1)} %get-tuple-element.65.own_ref), channel_id=1, source_target_pairs={{0,8},{1,9},{2,10},{3,11},{4,12},{5,13},{6,14},{7,15},{8,0},{9,1},... | collective-permute-start | bytes 98312 | tf_op jit(solution)/shard_map/ppermute | solution.py:21
  44.5 1.9 %collective-permute-start.17 = (bf16[512,128]{1,0:T(8,128)(2,1)S(1)}, bf16[512,128]{1,0:T(8,128)(2,1)S(1)}, u32[]{:S(2)}, u32[]{:S(2)}) collective-permute-start(bf16[512,128]{1,0:T(8,128)(2,1)S(1)} %pair_sum_later.1), channel_id=1, source_target_pairs={{0,4},{1,5},{2,6},{3,7},{4,0},{5,1},{6,2},{7,3},{8,12},{9,13},{10,... | collective-permute-start | bytes 393224 | tf_op jit(solution)/shard_map/ppermute | solution.py:21
  46.4 1.0 %collective-permute-done.19.got_ref = f32[32,256]{1,0:T(8,128)S(1)} collective-permute-done((f32[32,256]{1,0:T(8,128)S(1)}, f32[32,256]{1,0:T(8,128)S(1)}, u32[]{:S(2)}, u32[]{:S(2)}) %collective-permute-start.19) | collective-permute-done | bytes 32800 | tf_op jit(solution)/shard_map/ppermute | solution.py:21
  47.4 1.0 %collective-permute-start.20 = (f32[32,256]{1,0:T(8,128)S(1)}, f32[32,256]{1,0:T(8,128)S(1)}, u32[]{:S(2)}, u32[]{:S(2)}) collective-permute-start(f32[32,256]{1,0:T(8,128)S(1)} %weight_sum.1.refs_0_), channel_id=1, source_target_pairs={{0,4},{1,5},{2,6},{3,7},{4,0},{5,1},{6,2},{7,3},{8,12},{9,13},{10,... | collective-permute-start | bytes 98312 | tf_op jit(solution)/shard_map/ppermute | solution.py:21
  48.4 3.0 %collective-permute-start.18 = (bf16[512,128]{1,0:T(8,128)(2,1)S(1)}, bf16[512,128]{1,0:T(8,128)(2,1)S(1)}, u32[]{:S(2)}, u32[]{:S(2)}) collective-permute-start(bf16[512,128]{1,0:T(8,128)(2,1)S(1)} %get-tuple-element.64.refs_0_), channel_id=1, source_target_pairs={{0,8},{1,9},{2,10},{3,11},{4,12},{5,13},{6,14},{7,15},{8,0},{9,1},... | collective-permute-start | bytes 393224 | tf_op jit(solution)/shard_map/ppermute | solution.py:21
  51.5 1.2 %collective-permute-start.21 = (f32[2,32,256]{2,1,0:T(8,128)S(1)}, f32[2,32,256]{2,1,0:T(8,128)S(1)}, u32[]{:S(2)}, u32[]{:S(2)}) collective-permute-start(f32[2,32,256]{2,1,0:T(8,128)S(1)} %pack_weights.2.refs_0_), channel_id=1, source_target_pairs={{0,2},{1,3},{2,0},{3,1},{4,6},{5,7},{6,4},{7,5},{8,10},{9,11},{10,... | collective-permute-start | bytes 196616 | tf_op jit(solution)/shard_map/ppermute | solution.py:21
  52.7 0.3 near_sum.1.near_ref.refs_2_
  53.0 2.7 %collective-permute-done.21.refs_1_ = f32[2,32,256]{2,1,0:T(8,128)S(1)} collective-permute-done((f32[2,32,256]{2,1,0:T(8,128)S(1)}, f32[2,32,256]{2,1,0:T(8,128)S(1)}, u32[]{:S(2)}, u32[]{:S(2)}) %collective-permute-start.21) | collective-permute-done | bytes 65568 | tf_op jit(solution)/shard_map/ppermute | solution.py:21
  55.8 0.1 collective-permute-start.22
  55.8 0.8 %grad_input_sum.1 = bf16[512,128]{1,0:T(8,128)(2,1)} custom-call(f32[512,128]{1,0:T(8,128)S(1)} %near_sum.1.near_ref.refs_2_, bf16[512,128]{1,0:T(8,128)(2,1)S(1)} %collective-permute-done.18.refs_0_), custom_call_target="tpu_custom_call" | custom-call | flops 11000000512 | bytes 36000000 | tf_op jit(solution)/shard_map/grad_input_sum/pallas_call | solution.py:343
  56.6 0.6 collective-permute-done.22.other_ref
  57.2 0.7 %write_weights.1 = (f32[128,256]{1,0:T(8,128)}, f32[128,256]{1,0:T(8,128)}) custom-call(s32[363]{0:T(512)S(4)} %get-tuple-element.36.index_ref, f32[2,2,32,256]{3,2,1,0:T(8,128)S(1)} %pack_weights.3.weight_ref, f32[2,2,32,256]{3,2,1,0:T(8,128)S(1)} %collective-permute-done.22.other_ref), custom_call_target="tpu_custom_call" | custom-call | flops 220000000 | bytes 720000 | tf_op jit(solution)/shard_map/write_weights/pallas_call | solution.py:343
  (23 shorter events, 0.4 us)
Async XLA Ops:
  0.6 10.7 %collective-permute-start.4 = (bf16[512,128]{1,0:T(8,128)(2,1)}, bf16[512,128]{1,0:T(8,128)(2,1)S(1)}, u32[]{:S(2)}, u32[]{:S(2)}) collective-permute-start(bf16[512,128]{1,0:T(8,128)(2,1)} %feat_ref.1), channel_id=1, source_target_pairs={{0,8},{1,9},{2,10},{3,11},{4,12},{5,13},{6,14},{7,15},{8,0},{9,1},... | collective-permute-start | bytes 393224 | tf_op jit(solution)/shard_map/ppermute | solution.py:21
  4.7 8.9 %collective-permute-start = (bf16[512,128]{1,0:T(8,128)(2,1)}, bf16[512,128]{1,0:T(8,128)(2,1)S(1)}, u32[]{:S(2)}, u32[]{:S(2)}) collective-permute-start(bf16[512,128]{1,0:T(8,128)(2,1)} %feat_ref.1), channel_id=1, source_target_pairs={{0,2},{1,3},{2,0},{3,1},{4,6},{5,7},{6,4},{7,5},{8,10},{9,11},{10,... | collective-permute-start | bytes 393224 | tf_op jit(solution)/shard_map/ppermute | solution.py:21
  6.3 13.0 %collective-permute-start.1 = (bf16[512,128]{1,0:T(8,128)(2,1)}, bf16[512,128]{1,0:T(8,128)(2,1)S(1)}, u32[]{:S(2)}, u32[]{:S(2)}) collective-permute-start(bf16[512,128]{1,0:T(8,128)(2,1)} %feat_ref.1), channel_id=1, source_target_pairs={{0,6},{1,7},{2,4},{3,5},{4,2},{5,3},{6,0},{7,1},{8,14},{9,15},{10,... | collective-permute-start | bytes 393224 | tf_op jit(solution)/shard_map/ppermute | solution.py:21
  7.8 11.5 %collective-permute-start.2 = (bf16[512,128]{1,0:T(8,128)(2,1)}, bf16[512,128]{1,0:T(8,128)(2,1)S(1)}, u32[]{:S(2)}, u32[]{:S(2)}) collective-permute-start(bf16[512,128]{1,0:T(8,128)(2,1)} %feat_ref.1), channel_id=1, source_target_pairs={{0,4},{1,5},{2,6},{3,7},{4,0},{5,1},{6,2},{7,3},{8,12},{9,13},{10,... | collective-permute-start | bytes 393224 | tf_op jit(solution)/shard_map/ppermute | solution.py:21
  11.4 9.1 %collective-permute-start.5 = (bf16[512,128]{1,0:T(8,128)(2,1)S(1)}, bf16[512,128]{1,0:T(8,128)(2,1)S(1)}, u32[]{:S(2)}, u32[]{:S(2)}) collective-permute-start(bf16[512,128]{1,0:T(8,128)(2,1)S(1)} %collective-permute-done.4.refs_0_), channel_id=1, source_target_pairs={{0,6},{1,7},{2,4},{3,5},{4,2},{5,3},{6,0},{7,1},{8,14},{9,15},{10,... | collective-permute-start | bytes 393224 | tf_op jit(solution)/shard_map/ppermute | solution.py:21
  13.1 7.9 %collective-permute-start.6 = (bf16[512,128]{1,0:T(8,128)(2,1)S(1)}, bf16[512,128]{1,0:T(8,128)(2,1)S(1)}, u32[]{:S(2)}, u32[]{:S(2)}) collective-permute-start(bf16[512,128]{1,0:T(8,128)(2,1)S(1)} %collective-permute-done.4.refs_0_), channel_id=1, source_target_pairs={{0,2},{1,3},{2,0},{3,1},{4,6},{5,7},{6,4},{7,5},{8,10},{9,11},{10,... | collective-permute-start | bytes 393224 | tf_op jit(solution)/shard_map/ppermute | solution.py:21
  13.6 7.6 %collective-permute-start.7 = (bf16[512,128]{1,0:T(8,128)(2,1)S(1)}, bf16[512,128]{1,0:T(8,128)(2,1)S(1)}, u32[]{:S(2)}, u32[]{:S(2)}) collective-permute-start(bf16[512,128]{1,0:T(8,128)(2,1)S(1)} %collective-permute-done.4.refs_0_), channel_id=1, source_target_pairs={{0,4},{1,5},{2,6},{3,7},{4,0},{5,1},{6,2},{7,3},{8,12},{9,13},{10,... | collective-permute-start | bytes 393224 | tf_op jit(solution)/shard_map/ppermute | solution.py:21
  14.8 0.7 %copy-start = (s32[60]{0:T(128)S(1)}, s32[60]{0:T(128)}, u32[]{:S(2)}) copy-start(s32[60]{0:T(128)} %trow_ref.1) | copy-start | bytes 724
  15.5 0.7 %copy-start.1 = (s32[60]{0:T(128)S(1)}, s32[60]{0:T(128)}, u32[]{:S(2)}) copy-start(s32[60]{0:T(128)} %tcol_ref.1) | copy-start | bytes 724
  19.3 2.0 %collective-permute-start.3 = (bf16[4,512,128]{2,1,0:T(8,128)(2,1)S(1)}, bf16[4,512,128]{2,1,0:T(8,128)(2,1)S(1)}, u32[]{:S(2)}, u32[]{:S(2)}) collective-permute-start(bf16[4,512,128]{2,1,0:T(8,128)(2,1)S(1)} %pack_square.2.same_ref), channel_id=1, source_target_pairs={{0,1},{1,0},{2,3},{3,2},{4,5},{5,4},{6,7},{7,6},{8,9},{9,8},{10,11... | collective-permute-start | bytes 1572872 | tf_op jit(solution)/shard_map/ppermute | solution.py:21
  21.2 2.0 %collective-permute-start.8 = (bf16[4,512,128]{2,1,0:T(8,128)(2,1)S(1)}, bf16[4,512,128]{2,1,0:T(8,128)(2,1)S(1)}, u32[]{:S(2)}, u32[]{:S(2)}) collective-permute-start(bf16[4,512,128]{2,1,0:T(8,128)(2,1)S(1)} %pack_square.3.refs_0_), channel_id=1, source_target_pairs={{0,1},{1,0},{2,3},{3,2},{4,5},{5,4},{6,7},{7,6},{8,9},{9,8},{10,11... | collective-permute-start | bytes 1572872 | tf_op jit(solution)/shard_map/ppermute | solution.py:21
  26.0 3.0 %collective-permute-start.9 = (f32[128,256]{1,0:T(8,128)S(1)}, f32[128,256]{1,0:T(8,128)S(1)}, u32[]{:S(2)}, u32[]{:S(2)}) collective-permute-start(f32[128,256]{1,0:T(8,128)S(1)} %get-tuple-element.52), channel_id=1, source_target_pairs={{0,1},{1,0},{2,3},{3,2},{4,5},{5,4},{6,7},{7,6},{8,9},{9,8},{10,11... | collective-permute-start | bytes 393224 | tf_op jit(solution)/shard_map/ppermute | solution.py:21
  27.3 2.8 %collective-permute-start.13 = (f32[4,512,128]{2,1,0:T(8,128)S(1)}, f32[4,512,128]{2,1,0:T(8,128)S(1)}, u32[]{:S(2)}, u32[]{:S(2)}) collective-permute-start(f32[4,512,128]{2,1,0:T(8,128)S(1)} %send.3), channel_id=1, source_target_pairs={{0,1},{1,0},{2,3},{3,2},{4,5},{5,4},{6,7},{7,6},{8,9},{9,8},{10,11... | collective-permute-start | bytes 3145736 | tf_op jit(solution)/shard_map/ppermute | solution.py:21
  29.1 4.7 %collective-permute-start.10 = (f32[4,512,128]{2,1,0:T(8,128)S(1)}, f32[4,512,128]{2,1,0:T(8,128)S(1)}, u32[]{:S(2)}, u32[]{:S(2)}) collective-permute-start(f32[4,512,128]{2,1,0:T(8,128)S(1)} %send.2), channel_id=1, source_target_pairs={{0,1},{1,0},{2,3},{3,2},{4,5},{5,4},{6,7},{7,6},{8,9},{9,8},{10,11... | collective-permute-start | bytes 3145736 | tf_op jit(solution)/shard_map/ppermute | solution.py:21
  30.2 10.6 %collective-permute-start.14 = (bf16[640,128]{1,0:T(8,128)(2,1)S(1)}, bf16[640,128]{1,0:T(8,128)(2,1)S(1)}, u32[]{:S(2)}, u32[]{:S(2)}) collective-permute-start(bf16[640,128]{1,0:T(8,128)(2,1)S(1)} %get-tuple-element.61), channel_id=1, source_target_pairs={{0,2},{1,3},{2,0},{3,1},{4,6},{5,7},{6,4},{7,5},{8,10},{9,11},{10,... | collective-permute-start | bytes 491528 | tf_op jit(solution)/shard_map/ppermute | solution.py:21
  31.6 9.3 %collective-permute-start.15 = (bf16[640,128]{1,0:T(8,128)(2,1)S(1)}, bf16[640,128]{1,0:T(8,128)(2,1)S(1)}, u32[]{:S(2)}, u32[]{:S(2)}) collective-permute-start(bf16[640,128]{1,0:T(8,128)(2,1)S(1)} %get-tuple-element.62), channel_id=1, source_target_pairs={{0,6},{1,7},{2,4},{3,5},{4,2},{5,3},{6,0},{7,1},{8,14},{9,15},{10,... | collective-permute-start | bytes 491528 | tf_op jit(solution)/shard_map/ppermute | solution.py:21
  31.9 10.5 %collective-permute-start.16 = (bf16[640,128]{1,0:T(8,128)(2,1)S(1)}, bf16[640,128]{1,0:T(8,128)(2,1)S(1)}, u32[]{:S(2)}, u32[]{:S(2)}) collective-permute-start(bf16[640,128]{1,0:T(8,128)(2,1)S(1)} %get-tuple-element.63), channel_id=1, source_target_pairs={{0,4},{1,5},{2,6},{3,7},{4,0},{5,1},{6,2},{7,3},{8,12},{9,13},{10,... | collective-permute-start | bytes 491528 | tf_op jit(solution)/shard_map/ppermute | solution.py:21
  33.9 18.8 %collective-permute-start.11 = (bf16[512,128]{1,0:T(8,128)(2,1)S(1)}, bf16[512,128]{1,0:T(8,128)(2,1)S(1)}, u32[]{:S(2)}, u32[]{:S(2)}) collective-permute-start(bf16[512,128]{1,0:T(8,128)(2,1)S(1)} %get-tuple-element.55), channel_id=1, source_target_pairs={{0,6},{1,7},{2,4},{3,5},{4,2},{5,3},{6,0},{7,1},{8,14},{9,15},{10,... | collective-permute-start | bytes 393224 | tf_op jit(solution)/shard_map/ppermute | solution.py:21
  35.3 17.4 %collective-permute-start.12 = (bf16[512,128]{1,0:T(8,128)(2,1)S(1)}, bf16[512,128]{1,0:T(8,128)(2,1)S(1)}, u32[]{:S(2)}, u32[]{:S(2)}) collective-permute-start(bf16[512,128]{1,0:T(8,128)(2,1)S(1)} %get-tuple-element.56), channel_id=1, source_target_pairs={{0,2},{1,3},{2,0},{3,1},{4,6},{5,7},{6,4},{7,5},{8,10},{9,11},{10,... | collective-permute-start | bytes 393224 | tf_op jit(solution)/shard_map/ppermute | solution.py:21
  42.5 4.9 %collective-permute-start.19 = (f32[32,256]{1,0:T(8,128)S(1)}, f32[32,256]{1,0:T(8,128)S(1)}, u32[]{:S(2)}, u32[]{:S(2)}) collective-permute-start(f32[32,256]{1,0:T(8,128)S(1)} %get-tuple-element.65.own_ref), channel_id=1, source_target_pairs={{0,8},{1,9},{2,10},{3,11},{4,12},{5,13},{6,14},{7,15},{8,0},{9,1},... | collective-permute-start | bytes 98312 | tf_op jit(solution)/shard_map/ppermute | solution.py:21
  44.5 8.2 %collective-permute-start.17 = (bf16[512,128]{1,0:T(8,128)(2,1)S(1)}, bf16[512,128]{1,0:T(8,128)(2,1)S(1)}, u32[]{:S(2)}, u32[]{:S(2)}) collective-permute-start(bf16[512,128]{1,0:T(8,128)(2,1)S(1)} %pair_sum_later.1), channel_id=1, source_target_pairs={{0,4},{1,5},{2,6},{3,7},{4,0},{5,1},{6,2},{7,3},{8,12},{9,13},{10,... | collective-permute-start | bytes 393224 | tf_op jit(solution)/shard_map/ppermute | solution.py:21
  47.4 4.0 %collective-permute-start.20 = (f32[32,256]{1,0:T(8,128)S(1)}, f32[32,256]{1,0:T(8,128)S(1)}, u32[]{:S(2)}, u32[]{:S(2)}) collective-permute-start(f32[32,256]{1,0:T(8,128)S(1)} %weight_sum.1.refs_0_), channel_id=1, source_target_pairs={{0,4},{1,5},{2,6},{3,7},{4,0},{5,1},{6,2},{7,3},{8,12},{9,13},{10,... | collective-permute-start | bytes 98312 | tf_op jit(solution)/shard_map/ppermute | solution.py:21
  48.4 7.4 %collective-permute-start.18 = (bf16[512,128]{1,0:T(8,128)(2,1)S(1)}, bf16[512,128]{1,0:T(8,128)(2,1)S(1)}, u32[]{:S(2)}, u32[]{:S(2)}) collective-permute-start(bf16[512,128]{1,0:T(8,128)(2,1)S(1)} %get-tuple-element.64.refs_0_), channel_id=1, source_target_pairs={{0,8},{1,9},{2,10},{3,11},{4,12},{5,13},{6,14},{7,15},{8,0},{9,1},... | collective-permute-start | bytes 393224 | tf_op jit(solution)/shard_map/ppermute | solution.py:21
  51.5 4.3 %collective-permute-start.21 = (f32[2,32,256]{2,1,0:T(8,128)S(1)}, f32[2,32,256]{2,1,0:T(8,128)S(1)}, u32[]{:S(2)}, u32[]{:S(2)}) collective-permute-start(f32[2,32,256]{2,1,0:T(8,128)S(1)} %pack_weights.2.refs_0_), channel_id=1, source_target_pairs={{0,2},{1,3},{2,0},{3,1},{4,6},{5,7},{6,4},{7,5},{8,10},{9,11},{10,... | collective-permute-start | bytes 196616 | tf_op jit(solution)/shard_map/ppermute | solution.py:21
  55.8 1.4 %collective-permute-start.22 = (f32[2,2,32,256]{3,2,1,0:T(8,128)S(1)}, f32[2,2,32,256]{3,2,1,0:T(8,128)S(1)}, u32[]{:S(2)}, u32[]{:S(2)}) collective-permute-start(f32[2,2,32,256]{3,2,1,0:T(8,128)S(1)} %pack_weights.3.weight_ref), channel_id=1, source_target_pairs={{0,1},{1,0},{2,3},{3,2},{4,5},{5,4},{6,7},{7,6},{8,9},{9,8},{10,11... | collective-permute-start | bytes 393224 | tf_op jit(solution)/shard_map/ppermute | solution.py:21
